TPU v7x, 32 devices: a whole 2x2x4 slice. The times are simulated.
32 devices in a mesh: dp: 8 (over z, x), row: 2 (over core), col: 2 (over y).
Axes of the slice: x: 2, y: 2, z: 4, core: 2. Of those that a mesh axis runs over, the one named last changes fastest.
Arguments:
- block_input: bfloat16 [8192, 1536], P(('dp', 'row'), 'col'), may hold values from -6 to 6
- segment_ids: int32 [8192], P('dp'), may hold values from 0 to 2, as said below
- first_gain: float32 [1536], P('col'), may hold values from 0.25 to 1.75
- qkv_weight: bfloat16 [2, 2, 768, 1024], P('col', 'row'), may hold values from -0.15625 to 0.15625
- qkv_bias: float32 [2, 1024], P('row'), may hold values from -3 to 3
- output_weight: bfloat16 [2, 2, 768, 768], P('row', 'col'), may hold values from -0.625 to 0.625
- second_gain: float32 [1536], P('col'), may hold values from 0.25 to 1.75
- gate_up_weight: bfloat16 [2, 2, 768, 8960], P('col', 'row'), may hold values from -0.15625 to 0.15625
- down_weight: bfloat16 [2, 2, 4480, 768], P('row', 'col'), may hold values from -0.0625 to 0.0625
- output_grad: bfloat16 [8192, 1536], P(('dp', 'row'), 'col'), may hold values from -6 to 6
Outputs:
- block_output: bfloat16 [8192, 1536], P(('dp', 'row'), 'col')
- input_grad: float32 [8192, 1536], P(('dp', 'row'), 'col')
- first_gain_grad: float32 [1536], P('col')
- qkv_weight_grad: float32 [2, 2, 768, 1024], P('col', 'row', 'dp')
- qkv_bias_grad: float32 [2, 1024], P('row', 'dp')
- output_weight_grad: float32 [2, 2, 768, 768], P('row', 'col', 'dp')
- second_gain_grad: float32 [1536], P('col')
- gate_up_grad: float32 [2, 2, 768, 8960], P('col', 'row', 'dp')
- down_grad: float32 [2, 2, 4480, 768], P('row', 'col', 'dp')
Inputs may be any that keep to these rules, and one draw needn't show every extreme that they name: `segment_ids`: in each sequence of 1024 tokens the segment numbers start at 0, never fall, and rise by one at exactly 2 tokens; no document starts within 64 tokens of the sequence's middle token 512.
All inputs are finite; a program needn't handle non-finite values.
Results may differ from a plain program's by a relative error of at most 0.012.
Values may be sent and summed in bfloat16 or wider, within the bound.
No kernel may reach another device: no remote copies, remote signals or barrier semaphores. Data moves between devices by JAX's collectives and lax.ppermute only.
A program may use at most 256 MiB of HBM per device.

v0:
```python
import jax
import jax.numpy as jnp
from jax import lax
from jax.sharding import PartitionSpec as P

HEADS = 12
KV_HEADS = 2
HEAD_DIM = 128


EPSILON = 1e-06
ROPE_BASE = 1000000.0
MASKED = -1e30


def row_gather(local_part):
    return lax.all_gather(local_part, "row", axis=0, tiled=True)


def col_gather(local_part):
    return lax.all_gather(local_part, "col", axis=0, tiled=True)


def contract_rows(row_block, weight, contract):
    return lax.dot_general(
        row_block, weight, (((1,), (contract,)), ((), ())), preferred_element_type=jnp.float32
    )


def through_rows(local_part, weight, contract):
    gathered = row_gather(local_part)
    share_rows = gathered.shape[0] // lax.axis_size("col")

    def partial_term(start, count):
        return contract_rows(gathered, weight, contract)

    return (
        lax.psum_scatter(
            partial_term(jnp.int32(0), lax.axis_size("col") * share_rows),
            "col",
            scatter_dimension=0,
            tiled=True,
        ),
        gathered,
    )


def through_cols(local_part, weight, contract):
    gathered = col_gather(local_part)
    share_rows = gathered.shape[0] // lax.axis_size("row")

    def partial_term(start, count):
        return contract_rows(gathered, weight, contract)

    return (
        lax.psum_scatter(
            partial_term(jnp.int32(0), lax.axis_size("row") * share_rows),
            "row",
            scatter_dimension=0,
            tiled=True,
        ),
        gathered,
    )


def gate_up_partials(gathered, weight):
    share_rows = gathered.shape[0] // lax.axis_size("col")

    def partial_term(start, count):
        return contract_rows(gathered, weight, 0)

    return lax.psum_scatter(
        partial_term(jnp.int32(0), lax.axis_size("col") * share_rows),
        "col",
        scatter_dimension=0,
        tiled=True,
    )


def weight_grad(left_side, right_side):
    return lax.dot_general(
        left_side, right_side, (((0,), (0,)), ((), ())), preferred_element_type=jnp.float32
    )


def feature_sum(per_token):
    return lax.psum(per_token, "col")


def norm_forward(stream, gain_vector, model_width):
    scaling = lax.rsqrt(feature_sum(jnp.sum(stream * stream, axis=1)) / model_width + EPSILON)[
        :, None
    ]
    return (stream * scaling * gain_vector, scaling)


def norm_backward(cotangent, stream, scaling, gain_vector, model_width):
    gain_part = jnp.sum(cotangent * stream * scaling, axis=0)
    weighted = cotangent * gain_vector
    inner_sum = feature_sum(jnp.sum(weighted * stream, axis=1))[:, None]
    return (
        scaling * (weighted - stream * (scaling * scaling) * (inner_sum / model_width)),
        gain_part,
    )


def rope_tables(positions, head_size):
    frequency = ROPE_BASE ** (-jnp.arange(0, head_size, 2, dtype=jnp.float32) / head_size)
    angles = positions.astype(jnp.float32)[:, None] * frequency[None, :]
    angles = jnp.concatenate([angles, angles], axis=1)
    return (jnp.cos(angles)[:, None, :], jnp.sin(angles)[:, None, :])


def rotate(values, cosine, sine):
    half_dim = values.shape[-1] // 2
    turned = jnp.concatenate([-values[..., half_dim:], values[..., :half_dim]], axis=-1)
    return values * cosine + turned * sine


def unrotate(cotangent, cosine, sine):
    half_dim = cotangent.shape[-1] // 2
    sine_part = cotangent * sine
    turned = jnp.concatenate([sine_part[..., half_dim:], -sine_part[..., :half_dim]], axis=-1)
    return cotangent * cosine + turned


def allowed_mask(query_index, query_segment, segment_all):
    key_index = jnp.arange(segment_all.shape[0], dtype=jnp.int32)
    return (key_index[None, :] <= query_index[:, None]) & (
        segment_all[None, :] == query_segment[:, None]
    )


def block_scores(queries, key_rows, allowed, scaling):
    scores = (
        jnp.einsum("qkgd,skd->kgqs", queries, key_rows, preferred_element_type=jnp.float32)
        * scaling
    )
    return jnp.where(allowed[None, None], scores, MASKED)


def shards(
    block_input,
    segment_ids,
    first_gain,
    qkv_weight,
    qkv_bias,
    output_weight,
    second_gain,
    gate_up_weight,
    down_weight,
    output_grad,
):
    half_width = block_input.shape[1]
    model_width = half_width * lax.axis_size("col")
    qkv_block = qkv_weight[0, 0]
    out_block = output_weight[0, 0]
    gate_up_block = gate_up_weight[0, 0]
    down_block = down_weight[0, 0]
    bias_row = qkv_bias[0]
    seq_len = segment_ids.shape[0]
    col_index = lax.axis_index("col")
    query_rows = seq_len // lax.axis_size("col")
    head_size = HEAD_DIM
    query_heads = HEADS // lax.axis_size("row")
    key_heads = KV_HEADS // lax.axis_size("row")
    groups = query_heads // key_heads
    query_width = query_heads * head_size
    key_width = key_heads * head_size
    block_count = query_rows // query_rows
    scaling = head_size ** (-0.5)
    position_index = jnp.arange(seq_len, dtype=jnp.int32)
    doc_first = jnp.concatenate([jnp.ones((1,), jnp.bool_), segment_ids[1:] != segment_ids[:-1]])
    positions = position_index - lax.cummax(jnp.where(doc_first, position_index, 0), axis=0)
    row_start = col_index * query_rows
    cosine, sine = rope_tables(
        lax.dynamic_slice_in_dim(positions, row_start, query_rows, 0), head_size
    )
    own_segment = lax.dynamic_slice_in_dim(segment_ids, row_start, query_rows, 0)
    query_index = (row_start + jnp.arange(query_rows, dtype=jnp.int32)).reshape(
        block_count, query_rows
    )
    query_segment = own_segment.reshape(block_count, query_rows)
    stream = block_input.astype(jnp.float32)
    first_normed, first_scale = norm_forward(stream, first_gain, model_width)
    projected, first_full = through_rows(first_normed.astype(jnp.bfloat16), qkv_block, 0)
    projected = projected + bias_row
    query = rotate(
        projected[:, :query_width].reshape(query_rows, query_heads, head_size), cosine, sine
    ).astype(jnp.bfloat16)
    key_local = rotate(
        projected[:, query_width : query_width + key_width].reshape(
            query_rows, key_heads, head_size
        ),
        cosine,
        sine,
    )
    value_local = projected[:, query_width + key_width :]
    key_value = lax.all_gather(
        jnp.concatenate([key_local.reshape(query_rows, key_width), value_local], axis=1).astype(
            jnp.bfloat16
        ),
        "col",
        axis=0,
        tiled=True,
    )
    key_rows = key_value[:, :key_width].reshape(seq_len, key_heads, head_size)
    value_rows = key_value[:, key_width:].reshape(seq_len, key_heads, head_size)
    query_blocks = query.reshape(block_count, query_rows, key_heads, groups, head_size)

    def forward_block(block_item):
        query_part, index_part, segment_part = block_item
        scores = block_scores(
            query_part, key_rows, allowed_mask(index_part, segment_part, segment_ids), scaling
        )
        row_top = jnp.max(scores, axis=-1, keepdims=True)
        exponent = jnp.exp(scores - row_top)
        row_total = jnp.sum(exponent, axis=-1, keepdims=True)
        attn_probs = (exponent / row_total).astype(jnp.bfloat16)
        attended = jnp.einsum(
            "kgqs,skd->qkgd", attn_probs, value_rows, preferred_element_type=jnp.float32
        )
        return (attended, (row_top + jnp.log(row_total))[..., 0])

    attended, log_total = lax.map(forward_block, (query_blocks, query_index, query_segment))
    attended = attended.reshape(query_rows, query_width).astype(jnp.bfloat16)
    attn_branch, attended_full = through_cols(attended, out_block, 0)
    hidden_one = stream + attn_branch
    second_normed, second_scale = norm_forward(hidden_one, second_gain, model_width)
    second_full = row_gather(second_normed.astype(jnp.bfloat16))
    gate_up = gate_up_partials(second_full, gate_up_block)
    half_units = gate_up.shape[1] // 2
    gate_part = gate_up[:, :half_units]
    up_part = gate_up[:, half_units:]
    sigmoid_gate = jax.nn.sigmoid(gate_part)
    activated = (gate_part * sigmoid_gate * up_part).astype(jnp.bfloat16)
    mlp_branch, activated_full = through_cols(activated, down_block, 0)
    block_output = (hidden_one + mlp_branch).astype(jnp.bfloat16)
    d_activated, grad_full = through_rows(output_grad, down_block, 1)
    down_sum = weight_grad(activated_full, grad_full)
    d_gate = d_activated * up_part * (sigmoid_gate * (1.0 + gate_part * (1.0 - sigmoid_gate)))
    d_up = d_activated * gate_part * sigmoid_gate
    d_gate_up = jnp.concatenate([d_gate, d_up], axis=1).astype(jnp.bfloat16)
    d_second, gate_up_full = through_cols(d_gate_up, gate_up_block, 1)
    gate_up_sum = weight_grad(second_full, gate_up_full)
    d_hidden_norm, second_gain_part = norm_backward(
        d_second, hidden_one, second_scale, second_gain, model_width
    )
    d_hidden = output_grad.astype(jnp.float32) + d_hidden_norm
    d_attended, hidden_grad_full = through_rows(d_hidden.astype(jnp.bfloat16), out_block, 1)
    out_sum = weight_grad(attended_full, hidden_grad_full)
    d_attended_blocks = d_attended.astype(jnp.bfloat16).reshape(
        block_count, query_rows, key_heads, groups, head_size
    )

    def backward_block(grad_carry, block_item):
        query_part, index_part, segment_part, d_part, total_part = block_item
        scores = block_scores(
            query_part, key_rows, allowed_mask(index_part, segment_part, segment_ids), scaling
        )
        attn_probs = jnp.exp(scores - total_part[..., None])
        probs_low = attn_probs.astype(jnp.bfloat16)
        d_probs = jnp.einsum(
            "qkgd,skd->kgqs", d_part, value_rows, preferred_element_type=jnp.float32
        )
        d_scores = (
            attn_probs * (d_probs - jnp.sum(d_probs * attn_probs, axis=-1, keepdims=True))
        ).astype(jnp.bfloat16)
        d_query = (
            jnp.einsum("kgqs,skd->qkgd", d_scores, key_rows, preferred_element_type=jnp.float32)
            * scaling
        )
        d_key = (
            grad_carry[0]
            + jnp.einsum("kgqs,qkgd->skd", d_scores, query_part, preferred_element_type=jnp.float32)
            * scaling
        )
        d_value = grad_carry[1] + jnp.einsum(
            "kgqs,qkgd->skd", probs_low, d_part, preferred_element_type=jnp.float32
        )
        return ((d_key, d_value), d_query)

    zero_rows = jnp.zeros((seq_len, key_heads, head_size), jnp.float32)
    key_grads, query_grads = lax.scan(
        backward_block,
        (zero_rows, zero_rows),
        (query_blocks, query_index, query_segment, d_attended_blocks, log_total),
    )
    own_key_grad, own_value_grad = (
        lax.psum_scatter(key_grads[0], "col", scatter_dimension=0, tiled=True),
        lax.psum_scatter(key_grads[1], "col", scatter_dimension=0, tiled=True),
    )
    query_grad = unrotate(query_grads.reshape(query_rows, query_heads, head_size), cosine, sine)
    own_key_grad = unrotate(own_key_grad, cosine, sine)
    d_projected = jnp.concatenate(
        [
            query_grad.reshape(query_rows, query_width),
            own_key_grad.reshape(query_rows, key_width),
            own_value_grad.reshape(query_rows, key_width),
        ],
        axis=1,
    ).astype(jnp.bfloat16)
    d_first, projected_full = through_cols(d_projected, qkv_block, 1)
    qkv_sum = weight_grad(first_full, projected_full)
    bias_part = jnp.sum(projected_full, axis=0, dtype=jnp.float32)
    d_input_norm, first_gain_part = norm_backward(
        d_first, stream, first_scale, first_gain, model_width
    )
    input_grad = d_hidden + d_input_norm
    gain_sums = lax.psum((first_gain_part, second_gain_part), ("dp", "row"))
    grad_sums = (
        lax.psum_scatter(qkv_sum, "dp", scatter_dimension=0, tiled=True),
        lax.psum_scatter(bias_part, "dp", scatter_dimension=0, tiled=True),
        lax.psum_scatter(out_sum, "dp", scatter_dimension=0, tiled=True),
        lax.psum_scatter(gate_up_sum, "dp", scatter_dimension=0, tiled=True),
        lax.psum_scatter(down_sum, "dp", scatter_dimension=0, tiled=True),
    )
    return (
        block_output,
        input_grad,
        gain_sums[0],
        grad_sums[0][None, None],
        grad_sums[1][None],
        grad_sums[2][None, None],
        gain_sums[1],
        grad_sums[3][None, None],
        grad_sums[4][None, None],
    )


def solution(mesh):
    placed = (
        P(("dp", "row"), "col"),
        P("dp"),
        P("col"),
        P("col", "row", None, None),
        P("row", None),
        P("row", "col", None, None),
        P("col"),
        P("col", "row", None, None),
        P("row", "col", None, None),
        P(("dp", "row"), "col"),
    )
    return jax.shard_map(
        shards,
        mesh=mesh,
        in_specs=placed,
        out_specs=(
            P(("dp", "row"), "col"),
            P(("dp", "row"), "col"),
            P("col"),
            P("col", "row", "dp", None),
            P("row", "dp"),
            P("row", "col", "dp", None),
            P("col"),
            P("col", "row", "dp", None),
            P("row", "col", "dp", None),
        ),
        check_vma=False,
    )
```

profile of v0, /device:TPU:0, one launch (start us, length us, event | category | flops | bytes accessed | tf_op | source)
XLA Modules:
  0.0 2198.5 jit_solution(4059293805016383092)
XLA Ops:
  8.7 5.9 psum.42
  15.8 2.3 fusion.23
  18.1 11.7 all-gather.9.cloned.1.call-done
  29.8 5.1 fusion.35
  38.7 52.0 %reduce-scatter.15.cloned.1.call-done = f32[512,1024]{1,0:T(8,128)} async-done(((f32[1024,1024]{1,0:T(8,128)}), f32[512,1024]{1,0:T(8,128)}) %reduce-scatter.15.cloned.1.call-update) | async-done | bytes 2097168 | tf_op jit(solution)/shard_map/reduce_scatter | solution.py:38
  90.6 1.8 broadcast_add_fusion
  94.3 1.8 fusion.52
  96.3 2.0 copy.58
  99.9 3.1 copy.60
  105.0 3.5 add_convert_fusion.2
  110.0 8.7 all_gather.28
  118.7 2.3 fusion.64
  121.1 1.8 fusion.7
  122.8 2.8 copy-done.1
  125.7 3.4 fusion.37
  129.4 27.1 %all-gather.11.cloned.1.call-done = bf16[1024,768]{0,1:T(8,128)(2,1)} async-done(((bf16[512,768]{0,1:T(8,128)(2,1)}), bf16[1024,768]{0,1:T(8,128)(2,1)}) %all-gather.11.cloned.1.call-update) | async-done | bytes 1572880 | tf_op jit(solution)/shard_map/all_gather | solution.py:21
  156.4 4.5 fusion.47
  161.6 10.4 reduce-scatter.17.cloned.1.call-done
  172.0 1.9 multiply_reduce_fusion.2
  173.9 4.9 psum.43
  180.0 4.4 all-gather.17.cloned.1.call-done
  184.4 14.5 fusion.9
  199.0 26.2 %fusion.2 = f32[1024,8960]{1,0:T(8,128)} fusion(bf16[1024,768]{1,0:T(8,128)(2,1)} %all-gather.13.cloned.1.call-done, bf16[1,1,768,8960]{3,2,1,0:T(8,128)(2,1)} %param.17), kind=kOutput, calls=%fused_computation.2 | convolution fusion | flops 14092861440 | bytes 52035584 | tf_op jit(solution)/shard_map/dot_general | solution.py:25
  225.6 181.3 %reduce-scatter.23.cloned.1.call-done = f32[512,4480]{1,0:T(8,128)} async-done(((f32[1024,4480]{1,0:T(8,128)}), f32[512,4480]{1,0:T(8,128)}) %reduce-scatter.23.cloned.1.call-update) | async-done | bytes 9175056 | tf_op jit(solution)/shard_map/reduce_scatter | solution.py:38
  406.9 405.0 %reduce-scatter.19.cloned.1.call-done = f32[512,8960]{1,0:T(8,128)} async-done(((f32[1024,8960]{1,0:T(8,128)}), f32[512,8960]{1,0:T(8,128)}) %reduce-scatter.19.cloned.1.call-update) | async-done | bytes 18350096 | tf_op jit(solution)/shard_map/reduce_scatter | solution.py:72
  812.0 13.9 multiply_convert_fusion.1
  825.9 3.9 pad_maximum_fusion
  830.4 218.1 %all-gather.19.cloned.1.call-done = bf16[1024,8960]{1,0:T(8,128)(2,1)} async-done(((bf16[512,8960]{1,0:T(8,128)(2,1)}), bf16[1024,8960]{1,0:T(8,128)(2,1)}) %all-gather.19.cloned.1.call-update) | async-done | bytes 18350096 | tf_op jit(solution)/shard_map/all_gather | solution.py:21
  1048.5 21.7 fusion
  1070.3 94.7 %all-gather.15.cloned.1.call-done = bf16[1024,4480]{1,0:T(8,128)(2,1)} async-done(((bf16[512,4480]{1,0:T(8,128)(2,1)}), bf16[1024,4480]{1,0:T(8,128)(2,1)}) %all-gather.15.cloned.1.call-update) | async-done | bytes 9175056 | tf_op jit(solution)/shard_map/all_gather | solution.py:21
  1165.1 13.2 fusion.11
  1178.8 1.8 multiply_reduce_fusion
  1180.7 4.9 psum.44
  1185.6 7.5 reduce-scatter.21.cloned.1.call-done
  1193.1 4.3 fusion.61
  1197.5 11.1 all-gather.21.cloned.1.call-done
  1208.6 4.8 fusion.45
  1214.2 44.0 %reduce-scatter.27.cloned.1.call-done = f32[512,768]{1,0:T(8,128)} async-done(((f32[1024,768]{1,0:T(8,128)}), f32[512,768]{1,0:T(8,128)}) %reduce-scatter.27.cloned.1.call-update) | async-done | bytes 1572880 | tf_op jit(solution)/shard_map/reduce_scatter | solution.py:38
  1258.1 2.4 convert_element_type.83
  1261.9 10.3 fusion.4
  1274.5 6.9 fusion.16
  1281.5 2.6 copy-done.2
  1284.1 2.7 fusion.44
  1286.8 5.5 bitcast_multiply_fusion.1
  1292.3 7.6 fusion.40
  1304.0 1.9 sine_multiply_fusion
  1306.0 2.0 fusion.57
  1308.1 10.7 reduce-scatter.31.cloned.1.call-done
  1321.0 33.0 %all-gather.23.cloned.1.call-done = bf16[1024,1024]{0,1:T(8,128)(2,1)} async-done(((bf16[512,1024]{0,1:T(8,128)(2,1)}), bf16[1024,1024]{0,1:T(8,128)(2,1)}) %all-gather.23.cloned.1.call-update) | async-done | bytes 2097168 | tf_op jit(solution)/shard_map/all_gather | solution.py:21
  1354.0 5.1 fusion.33
  1360.6 4.2 fusion.66
  1364.9 1.8 copy-done.32
  1366.7 14.1 fusion.68
  1382.2 5.1 fusion.65
  1388.7 23.7 %fusion.67 = f32[768,8960]{1,0:T(8,128)} fusion(bf16[1024,768]{1,0:T(8,128)(2,1)S(1)} %copy-done.33, bf16[1024,8960]{1,0:T(8,128)(2,1)} %all-gather.19.cloned.1.call-done), kind=kOutput, calls=%fused_computation.128 | convolution fusion | flops 14092861440 | bytes 47448064 | tf_op jit(solution)/shard_map/dot_general | solution.py:81
  1414.3 2.0 convert_reduce_fusion
  1416.3 21.8 all-reduce
  1438.7 2.0 fusion.30
  1440.7 31.4 %all-reduce.1 = (f32[768]{0:T(1024)}, f32[768]{0:T(1024)}) all-reduce(f32[768]{0:T(1024)S(1)} %get-tuple-element.62, f32[768]{0:T(1024)S(1)} %get-tuple-element.60), channel_id=1, replica_groups=mesh['dp'=8,'row'=2,'col'=2] {'dp','row'}, use_global_device_ids=true, to_apply=%region_24.25 | all-reduce | flops 1536 | bytes 12288 | tf_op jit(solution)/shard_map/psum | solution.py:310
  1472.1 4.9 psum.45
  1477.0 3.5 fusion.27
  1480.4 190.6 %reduce-scatter.41.cloned.1.call-done = f32[560,768]{1,0:T(8,128)} async-done(((f32[4480,768]{1,0:T(8,128)}), f32[560,768]{1,0:T(8,128)}) %reduce-scatter.41.cloned.1.call-update) | async-done | bytes 1720336 | tf_op jit(solution)/shard_map/reduce_scatter | solution.py:316
  1671.0 78.3 %reduce-scatter.35.cloned.1.call-done = f32[96,1024]{1,0:T(8,128)} async-done(((f32[768,1024]{1,0:T(8,128)}), f32[96,1024]{1,0:T(8,128)}) %reduce-scatter.35.cloned.1.call-update) | async-done | bytes 393232 | tf_op jit(solution)/shard_map/reduce_scatter | solution.py:312
  1749.3 441.9 %reduce-scatter.39.cloned.1.call-done = f32[96,8960]{1,0:T(8,128)} async-done(((f32[768,8960]{1,0:T(8,128)}), f32[96,8960]{1,0:T(8,128)}) %reduce-scatter.39.cloned.1.call-update) | async-done | bytes 3440656 | tf_op jit(solution)/shard_map/reduce_scatter | solution.py:315
  (167 shorter events, 34.4 us)
Async XLA Ops:
  7.2 22.6 %copy-start = (bf16[1,1,768,1024]{3,2,1,0:T(8,128)(2,1)S(1)}, bf16[1,1,768,1024]{3,2,1,0:T(8,128)(2,1)}, u32[]{:S(2)}) copy-start(bf16[1,1,768,1024]{3,2,1,0:T(8,128)(2,1)} %param.13) | copy-start | bytes 4718596
  7.2 22.6 %all-gather.9.cloned.1.call-start = ((), (), s32[]{:S(2)}) async-start(), calls=%async_computation.14 | async-start | bytes 2359296 | tf_op jit(solution)/shard_map/all_gather | solution.py:17
  15.2 0.6 copy-start.26
  18.0 72.6 %reduce-scatter.15.cloned.1.call-start = ((), (), s32[]{:S(2)}) async-start(), calls=%async_computation.15 | async-start | bytes 6291456 | tf_op jit(solution)/shard_map/reduce_scatter | solution.py:38
  34.9 0.7 copy-start.23
  34.9 55.7 %copy-start.29 = (f32[1,1024]{1,0:T(1,128)S(1)}, f32[1,1024]{1,0:T(1,128)}, u32[]{:S(2)}) copy-start(f32[1,1024]{1,0:T(1,128)} %param.14) | copy-start | bytes 12292
  35.0 121.5 %all-gather.11.cloned.1.call-start = ((), (), s32[]{:S(2)}) async-start(), calls=%async_computation.16 | async-start | bytes 2359296 | tf_op jit(solution)/shard_map/all_gather | solution.py:21
  92.5 1.8 copy-start.7
  96.3 2.2 copy-start.15
  98.3 1.7 copy-start.3
  99.9 3.1 copy-start.17
  103.1 1.8 copy-start.8
  105.0 5.0 copy-start.18
  108.5 10.3 copy-start.11
  118.7 4.1 copy-start.12
  121.0 4.7 copy-start.1
  121.0 4.6 copy-start.19
  125.7 3.4 copy-start.21
  125.7 30.8 %copy-start.34 = (bf16[1,1,768,768]{3,2,1,0:T(8,128)(2,1)S(1)}, bf16[1,1,768,768]{3,2,1,0:T(8,128)(2,1)}, u32[]{:S(2)}) copy-start(bf16[1,1,768,768]{3,2,1,0:T(8,128)(2,1)} %param.15) | copy-start | bytes 3538948
  129.1 42.9 %reduce-scatter.17.cloned.1.call-start = ((), (), s32[]{:S(2)}) async-start(), calls=%async_computation.17 | async-start | bytes 4718592 | tf_op jit(solution)/shard_map/reduce_scatter | solution.py:56
  161.0 23.4 %all-gather.17.cloned.1.call-start = ((), (), s32[]{:S(2)}) async-start(), calls=%async_computation.22 | async-start | bytes 2359296 | tf_op jit(solution)/shard_map/all_gather | solution.py:17
  161.6 17.3 copy-start.24
  161.6 37.4 %all-gather.13.cloned.1.call-start = ((), (), s32[]{:S(2)}) async-start(), calls=%async_computation.18 | async-start | bytes 2359296 | tf_op jit(solution)/shard_map/all_gather | solution.py:17
  180.0 227.0 %reduce-scatter.23.cloned.1.call-start = ((), (), s32[]{:S(2)}) async-start(), calls=%async_computation.23 | async-start | bytes 27525120 | tf_op jit(solution)/shard_map/reduce_scatter | solution.py:38
  198.9 613.0 %reduce-scatter.19.cloned.1.call-start = ((), (), s32[]{:S(2)}) async-start(), calls=%async_computation.19 | async-start | bytes 55050240 | tf_op jit(solution)/shard_map/reduce_scatter | solution.py:72
  225.2 823.3 %all-gather.19.cloned.1.call-start = ((), (), s32[]{:S(2)}) async-start(), calls=%async_computation.24 | async-start | bytes 27525120 | tf_op jit(solution)/shard_map/all_gather | solution.py:21
  829.8 335.3 %all-gather.15.cloned.1.call-start = ((), (), s32[]{:S(2)}) async-start(), calls=%async_computation.20 | async-start | bytes 13762560 | tf_op jit(solution)/shard_map/all_gather | solution.py:21
  830.4 348.5 %reduce-scatter.25.cloned.1.call-start = ((), (), s32[]{:S(2)}) async-start(), calls=%async_computation.25 | async-start | bytes 4718592 | tf_op jit(solution)/shard_map/reduce_scatter | solution.py:56
  1070.3 122.8 %reduce-scatter.21.cloned.1.call-start = ((), (), s32[]{:S(2)}) async-start(), calls=%async_computation.21 | async-start | bytes 4718592 | tf_op jit(solution)/shard_map/reduce_scatter | solution.py:56
  1178.3 30.3 %all-gather.21.cloned.1.call-start = ((), (), s32[]{:S(2)}) async-start(), calls=%async_computation.26 | async-start | bytes 2359296 | tf_op jit(solution)/shard_map/all_gather | solution.py:17
  1197.5 60.7 %reduce-scatter.27.cloned.1.call-start = ((), (), s32[]{:S(2)}) async-start(), calls=%async_computation.27 | async-start | bytes 4718592 | tf_op jit(solution)/shard_map/reduce_scatter | solution.py:38
  1213.4 0.7 copy-start.20
  1213.4 0.7 copy-start.22
  1213.4 48.5 %copy-start.13 = (bf16[1024,256]{1,0:T(8,128)(2,1)S(1)}, bf16[1024,256]{1,0:T(8,128)(2,1)}, u32[]{:S(2)}) copy-start(bf16[1024,256]{1,0:T(8,128)(2,1)} %copy-done.12) | copy-start | bytes 1572868
  1213.5 90.0 %reduce-scatter.29.cloned.1.call-start = ((), (), s32[]{:S(2)}) async-start(), calls=%async_computation.28 | async-start | bytes 786432 | tf_op jit(solution)/shard_map/reduce_scatter | solution.py:290
  1261.9 10.4 slice-start
  1261.9 11.4 slice-start.1
  1261.9 12.6 slice-start.2
  1274.5 9.5 copy-start.4
  1274.5 9.5 copy-start.5
  1274.5 9.5 copy-start.9
  1281.5 2.6 copy-start.2
  1284.1 2.7 copy-start.16
  1286.8 32.0 %reduce-scatter.31.cloned.1.call-start = ((), (), s32[]{:S(2)}) async-start(), calls=%async_computation.29 | async-start | bytes 786432 | tf_op jit(solution)/shard_map/reduce_scatter | solution.py:291
  1300.0 54.0 %all-gather.23.cloned.1.call-start = ((), (), s32[]{:S(2)}) async-start(), calls=%async_computation.30 | async-start | bytes 3145728 | tf_op jit(solution)/shard_map/all_gather | solution.py:21
  1301.6 1.4 copy-start.10
  1303.0 0.9 copy-start.14
  1320.8 117.9 %reduce-scatter.33.cloned.1.call-start = ((), (), s32[]{:S(2)}) async-start(), calls=%async_computation.31 | async-start | bytes 4718592 | tf_op jit(solution)/shard_map/reduce_scatter | solution.py:56
  1359.2 1.4 copy-start.31
  1359.2 121.2 %reduce-scatter.37.cloned.1.call-start = ((), (), s32[]{:S(2)}) async-start(), calls=%async_computation.33 | async-start | bytes 2654208 | tf_op jit(solution)/shard_map/reduce_scatter | solution.py:314
  1364.8 1.9 copy-start.32
  1364.8 306.2 %reduce-scatter.41.cloned.1.call-start = ((), (), s32[]{:S(2)}) async-start(), calls=%async_computation.35 | async-start | bytes 15482880 | tf_op jit(solution)/shard_map/reduce_scatter | solution.py:316
  1380.8 1.4 copy-start.30
  1380.8 368.5 %reduce-scatter.35.cloned.1.call-start = ((), (), s32[]{:S(2)}) async-start(), calls=%async_computation.32 | async-start | bytes 3538944 | tf_op jit(solution)/shard_map/reduce_scatter | solution.py:312
  1387.3 1.4 copy-start.33
  1387.3 803.9 %reduce-scatter.39.cloned.1.call-start = ((), (), s32[]{:S(2)}) async-start(), calls=%async_computation.34 | async-start | bytes 30965760 | tf_op jit(solution)/shard_map/reduce_scatter | solution.py:315
  1412.4 0.7 copy-start.35
  1412.4 26.2 %copy-start.6 = (bf16[512,768]{1,0:T(8,128)(2,1)S(1)}, bf16[512,768]{1,0:T(8,128)(2,1)}, u32[]{:S(2)}) copy-start(bf16[512,768]{1,0:T(8,128)(2,1)} %param.10) | copy-start | bytes 2359300
  1412.5 26.2 %copy-start.25 = (f32[768]{0:T(1024)S(1)}, f32[768]{0:T(1024)}, u32[]{:S(2)}) copy-start(f32[768]{0:T(1024)} %param.12) | copy-start | bytes 9220
  1412.5 26.2 %copy-start.27 = (f32[512]{0:T(512)S(1)}, f32[512]{0:T(512)}, u32[]{:S(2)}) copy-start(f32[512]{0:T(512)} %copy-done.26) | copy-start | bytes 6148
  1414.3 62.7 %copy-start.28 = (f32[512]{0:T(512)S(1)}, f32[512]{0:T(512)}, u32[]{:S(2)}) copy-start(f32[512]{0:T(512)} %get-tuple-element.99) | copy-start | bytes 6148
Sparse Core Ops, SparseCore 0:
  18.2 11.5 all-gather.8
  35.1 55.5 reduce-scatter.14
  129.2 27.1 all-gather.10
  161.1 10.8 reduce-scatter.16
  173.4 10.9 all-gather.16
  186.4 10.9 all-gather.12
  199.7 207.1 reduce-scatter.22
  409.2 402.6 reduce-scatter.18
  829.9 218.5 all-gather.18
  1049.9 115.1 all-gather.14
  1167.9 10.8 reduce-scatter.24
  1181.0 12.0 reduce-scatter.20
  1197.6 10.9 all-gather.20
  1213.6 44.5 reduce-scatter.26
  1286.9 14.5 reduce-scatter.28
  1304.1 14.5 reduce-scatter.30
  1320.9 33.1 all-gather.22
  1359.3 10.8 reduce-scatter.32
  1374.3 70.2 reduce-scatter.36
  1448.6 222.3 reduce-scatter.40
  1675.6 73.6 reduce-scatter.34
  1754.3 436.9 reduce-scatter.38
where the time goes:
time: 2210 us; the launch traced here: 2200 us
  waiting for transfers between devices  1820 us (82%)
  matrix products  174 us (8%)
  blocking collectives  82.6 us (4%)
  other arithmetic  69.6 us (3%)
  local copies, waits for them, and re-layouts  30.6 us (1%)
    reduce_scatter x1, waiting for transfers between devices, shards(): lax.psum_scatter(gate_up_sum, 'dp', scatter_dimension=0, tiled=True)  442 us
    reduce_scatter x1, waiting for transfers between devices, gate_up_partials(): lax.psum_scatter(partial_term(jnp.int32(0), lax.axis_size('col') * share_...  405 us
    all_gather x4, waiting for transfers between devices, col_gather(): return lax.all_gather(local_part, 'col', axis=0, tiled=True)  373 us
    reduce_scatter x3, waiting for transfers between devices, through_rows(): lax.psum_scatter(partial_term(jnp.int32(0), lax.axis_size('col') * share_...  277 us
    reduce_scatter x1, waiting for transfers between devices, shards(): lax.psum_scatter(down_sum, 'dp', scatter_dimension=0, tiled=True)  191 us
    dot_general x8, matrix products, contract_rows(): lax.dot_general(row_block, weight, (((1,), (contract,)), ((), ())), prefe...  95.2 us
    reduce_scatter x1, waiting for transfers between devices, shards(): lax.psum_scatter(qkv_sum, 'dp', scatter_dimension=0, tiled=True)  78.3 us
    dot_general x4, matrix products, weight_grad(): lax.dot_general(left_side, right_side, (((0,), (0,)), ((), ())), preferre...  47.1 us
  transfers between devices with their start and end apart: 22, of which 18 were waited for; matrix products, arithmetic and copies ran while one was open for 7% of the time, Pallas kernels for 0%

commit v1 on v0

v1 whole, which is shorter than its diff:
```python
import jax
import jax.numpy as jnp
from jax import lax
from jax.sharding import PartitionSpec as P

HEADS = 12
KV_HEADS = 2
HEAD_DIM = 128
EPSILON = 1e-06
ROPE_BASE = 1000000.0
MASKED = -1e30
F32 = jnp.float32
BF16 = jnp.bfloat16


def dot(left, right, left_dim, right_dim):
    return lax.dot_general(
        left, right, (((left_dim,), (right_dim,)), ((), ())), preferred_element_type=F32
    )


def swap(part, axis_name):
    return lax.ppermute(part, axis_name, [(0, 1), (1, 0)])


def pick(array, index, axis):
    return lax.dynamic_index_in_dim(array, index, axis, keepdims=False)


def in_order(index, own, other, axis):
    first = jnp.where(index == 0, own, other)
    second = jnp.where(index == 0, other, own)
    return jnp.concatenate([first, second], axis=axis)


def ring_of(count):
    return list(range(0, count, 2)) + list(range(count - 1, 0, -2))


def ring_gather(part, rank):
    count = lax.axis_size("dp")
    ring = ring_of(count)
    place = [0] * count
    for position, device in enumerate(ring):
        place[device] = position
    onward = [(ring[i], ring[(i + 1) % count]) for i in range(count)]
    back = [(b, a) for a, b in onward]
    ring_table = jnp.array(ring, jnp.int32)
    here = jnp.array(place, jnp.int32)[rank]
    gathered = jnp.zeros((count,) + part.shape, part.dtype)
    gathered = lax.dynamic_update_index_in_dim(gathered, part, rank, 0)
    right, left = part, part
    for step in range(1, count // 2 + 1):
        right = lax.ppermute(right, "dp", onward)
        source = ring_table[(here - step) % count]
        gathered = lax.dynamic_update_index_in_dim(gathered, right, source, 0)
        if step < count - count // 2:
            left = lax.ppermute(left, "dp", back)
            source = ring_table[(here + step) % count]
            gathered = lax.dynamic_update_index_in_dim(gathered, left, source, 0)
    return gathered


def line_scatter(terms, place, axis):
    length = terms.shape[axis]
    count = 2 * length

    def term(index):
        return pick(terms, jnp.clip(index, 0, length - 1), axis).astype(F32)

    up = down = None
    for step in range(1, length):
        up_send = term(place + length - step)
        down_send = term(place - length + step)
        if step > 1:
            up_send = up_send + up.astype(F32)
            down_send = down_send + down.astype(F32)
        up_pairs = [
            (i, i + 2) for i in range(count - 2) if i // 2 <= step - 1
        ]
        down_pairs = [
            (i, i - 2) for i in range(2, count) if i // 2 >= length - step
        ]
        up = lax.ppermute(up_send.astype(BF16), "dp", up_pairs)
        down = lax.ppermute(down_send.astype(BF16), "dp", down_pairs)
    total = term(place)
    if length > 1:
        total = total + (up.astype(F32) + down.astype(F32))
    return total


def pair_scatter(terms, side, axis):
    count = lax.axis_size("dp")
    pairs = [(i, i ^ 1) for i in range(count)]
    arrived = lax.ppermute(pick(terms, 1 - side, axis).astype(BF16), "dp", pairs)
    return pick(terms, side, axis).astype(F32) + arrived.astype(F32)


def dp_scatter(terms, rank, axis, pair_first=True):
    shape = terms.shape
    half = shape[axis] // 2
    split = terms.reshape(shape[:axis] + (half, 2) + shape[axis + 1 :])
    if pair_first:
        return line_scatter(
            pair_scatter(split, rank % 2, axis + 1).astype(BF16), rank // 2, axis
        )
    return pair_scatter(line_scatter(split, rank // 2, axis).astype(BF16), rank % 2, axis)


def dp_sum(part):
    count = lax.axis_size("dp")
    distance = 1
    while distance < count:
        part = part + lax.ppermute(part, "dp", [(i, i ^ distance) for i in range(count)])
        distance *= 2
    return part


def rope_tables(positions, head_size):
    frequency = ROPE_BASE ** (-jnp.arange(0, head_size, 2, dtype=F32) / head_size)
    angles = positions.astype(F32)[:, None] * frequency[None, :]
    angles = jnp.concatenate([angles, angles], axis=1)
    return (jnp.cos(angles)[:, None, :], jnp.sin(angles)[:, None, :])


def rotate(values, cosine, sine):
    half_dim = values.shape[-1] // 2
    turned = jnp.concatenate([-values[..., half_dim:], values[..., :half_dim]], axis=-1)
    return values * cosine + turned * sine


def unrotate(cotangent, cosine, sine):
    half_dim = cotangent.shape[-1] // 2
    sine_part = cotangent * sine
    turned = jnp.concatenate([sine_part[..., half_dim:], -sine_part[..., :half_dim]], axis=-1)
    return cotangent * cosine + turned


def masked_scores(query, key, allowed):
    scores = jnp.einsum("qhd,sd->hqs", query, key, preferred_element_type=F32) * HEAD_DIM ** (-0.5)
    return jnp.where(allowed[None], scores, MASKED)


def shards(
    block_input,
    segment_ids,
    first_gain,
    qkv_weight,
    qkv_bias,
    output_weight,
    second_gain,
    gate_up_weight,
    down_weight,
    output_grad,
):
    count = lax.axis_size("dp")
    rank = lax.axis_index("dp")
    row = lax.axis_index("row")
    col = lax.axis_index("col")
    qkv_block = qkv_weight[0, 0]
    out_block = output_weight[0, 0]
    gate_up_block = gate_up_weight[0, 0]
    down_block = down_weight[0, 0]
    seq_len = segment_ids.shape[0]
    own_rows, half_width = block_input.shape
    model_width = 2 * half_width
    head_size = HEAD_DIM
    own_heads = HEADS // 4
    query_width = own_heads * head_size
    key_width = (KV_HEADS // 2) * head_size
    group_units = down_block.shape[0]
    own_units = group_units // 2
    segment = own_units // count

    def own_tokens(array):
        return lax.dynamic_slice_in_dim(array, row * own_rows, own_rows, 0)

    def other_tokens(array):
        return lax.dynamic_slice_in_dim(array, (1 - row) * own_rows, own_rows, 0)

    def gather_block(part):
        far = swap(part, "col")
        near = swap(part, "row")
        far_near = swap(far, "row")
        return jnp.concatenate(
            [in_order(row, part, near, 0), in_order(row, far, far_near, 0)], axis=1
        )

    def row_sum_own(partial_sum, kind):
        arrived = swap(other_tokens(partial_sum).astype(kind), "row")
        return own_tokens(partial_sum).astype(F32) + arrived.astype(F32)

    def qkv_columns(side):
        heads = lax.dynamic_slice_in_dim(qkv_block, side * query_width, query_width, 1)
        return jnp.concatenate([heads, qkv_block[:, 2 * query_width :]], axis=1)

    stream_bf = gather_block(block_input)
    qkv_own = jnp.concatenate([qkv_columns(col), swap(qkv_columns(1 - col), "col")], axis=0)
    bias = qkv_bias[0]
    bias_own = jnp.concatenate(
        [lax.dynamic_slice_in_dim(bias, col * query_width, query_width, 0), bias[2 * query_width :]]
    )
    gains = jnp.stack([first_gain, second_gain])
    gains = jnp.concatenate([gains, swap(gains, "col")], axis=1)

    out_far = swap(out_block, "col")
    out_wide = jnp.concatenate([out_block, out_far], axis=1)
    out_full = jnp.concatenate([out_wide, swap(out_wide, "row")], axis=0)

    feature_rows = half_width // count

    def unit_columns(array, side):
        split = array.reshape(array.shape[0], 2, count, 2, segment)
        return pick(split, side, 3).reshape(array.shape[0], 2 * own_units)

    gate_up_slice = lax.dynamic_slice_in_dim(gate_up_block, rank * feature_rows, feature_rows, 0)
    gate_up_far = ring_gather(swap(unit_columns(gate_up_slice, 1 - col), "col"), rank)
    gate_up_own = jnp.concatenate(
        [unit_columns(gate_up_block, col), gate_up_far.reshape(half_width, 2 * own_units)], axis=0
    )
    down_split = down_block.reshape(count, 2, segment, half_width)
    down_far = ring_gather(swap(pick(pick(down_split, rank, 0), 1 - col, 0), "col"), rank)
    down_own = jnp.concatenate(
        [
            pick(down_split, col, 1).reshape(own_units, half_width),
            down_far.reshape(own_units, half_width),
        ],
        axis=1,
    )
    grad_bf = gather_block(output_grad)

    position_index = jnp.arange(seq_len, dtype=jnp.int32)
    doc_first = jnp.concatenate([jnp.ones((1,), jnp.bool_), segment_ids[1:] != segment_ids[:-1]])
    positions = position_index - lax.cummax(jnp.where(doc_first, position_index, 0), axis=0)
    cosine, sine = rope_tables(positions, head_size)
    allowed = (position_index[None, :] <= position_index[:, None]) & (
        segment_ids[None, :] == segment_ids[:, None]
    )
    stream = stream_bf.astype(F32)
    first_scale = lax.rsqrt(jnp.sum(stream * stream, axis=1) / model_width + EPSILON)[:, None]
    first_normed = (stream * first_scale * gains[0]).astype(BF16)
    projected = dot(first_normed, qkv_own, 1, 0) + bias_own
    query = rotate(
        projected[:, :query_width].reshape(seq_len, own_heads, head_size), cosine, sine
    ).astype(BF16)
    key = rotate(
        projected[:, query_width : query_width + key_width].reshape(seq_len, 1, head_size),
        cosine,
        sine,
    ).astype(BF16)[:, 0]
    value = projected[:, query_width + key_width :].astype(BF16)
    scores = masked_scores(query, key, allowed)
    row_top = jnp.max(scores, axis=-1, keepdims=True)
    exponent = jnp.exp(scores - row_top)
    row_total = jnp.sum(exponent, axis=-1, keepdims=True)
    attn_probs = (exponent / row_total).astype(BF16)
    attended = (
        jnp.einsum("hqs,sd->qhd", attn_probs, value, preferred_element_type=F32)
        .reshape(seq_len, query_width)
        .astype(BF16)
    )
    log_total = row_top + jnp.log(row_total)
    attended_group = in_order(col, attended, swap(attended, "col"), 1)
    attended_full = jnp.concatenate([attended_group, swap(attended_group, "row")], axis=1)
    hidden_one = stream + dot(attended_full, out_full, 1, 0)
    second_scale = lax.rsqrt(jnp.sum(hidden_one * hidden_one, axis=1) / model_width + EPSILON)[
        :, None
    ]
    second_normed = (hidden_one * second_scale * gains[1]).astype(BF16)

    gate_up = dot(second_normed, gate_up_own, 1, 0)
    gate_part = gate_up[:, :own_units]
    up_part = gate_up[:, own_units:]
    sigmoid_gate = jax.nn.sigmoid(gate_part)
    activated = (gate_part * sigmoid_gate * up_part).astype(BF16)
    down_terms = dot(activated, grad_bf, 0, 0).astype(BF16).reshape(count, segment, model_width)
    down_sum = dp_scatter(down_terms, rank, 0)

    d_activated = dot(grad_bf, down_own, 1, 1)
    d_gate = (
        d_activated * up_part * (sigmoid_gate * (1.0 + gate_part * (1.0 - sigmoid_gate)))
    ).astype(BF16)
    d_up = (d_activated * gate_part * sigmoid_gate).astype(BF16)
    gate_terms = dot(second_normed, d_gate, 0, 0).astype(BF16)
    gate_sum = dp_scatter(gate_terms.reshape(2, count, feature_rows, own_units), rank, 1)
    up_terms = dot(second_normed, d_up, 0, 0).astype(BF16)
    up_sum = dp_scatter(up_terms.reshape(2, count, feature_rows, own_units), rank, 1)
    d_gate_up = jnp.concatenate([d_gate, d_up], axis=1)
    d_second_chip = row_sum_own(dot(d_gate_up, gate_up_own, 1, 1), BF16)
    d_second_far = swap(d_second_chip.astype(BF16), "col").astype(F32)
    d_second = d_second_chip + jnp.concatenate(
        [d_second_far[:, half_width:], d_second_far[:, :half_width]], axis=1
    )

    hidden_own = own_tokens(hidden_one)
    scale_own = own_tokens(second_scale)
    weighted = d_second * gains[1]
    inner = jnp.sum(weighted * hidden_own, axis=1, keepdims=True)
    d_hidden = own_tokens(grad_bf).astype(F32) + scale_own * (
        weighted - hidden_own * (scale_own * scale_own) * (inner / model_width)
    )
    second_gain_part = jnp.sum(
        d_second[:, :half_width] * hidden_own[:, :half_width] * scale_own, axis=0
    )
    d_hidden_low = d_hidden.astype(BF16)
    d_hidden_full = in_order(row, d_hidden_low, swap(d_hidden_low, "row"), 0)

    out_terms = dot(attended_group, d_hidden_full[:, :half_width], 0, 0).astype(BF16)
    out_sum = dp_scatter(out_terms.reshape(count, feature_rows, half_width), rank, 0)

    out_rows = lax.dynamic_slice_in_dim(out_full, col * query_width, query_width, 0)
    d_attended = dot(d_hidden_full, out_rows, 1, 1).astype(BF16)
    d_attended = d_attended.reshape(seq_len, own_heads, head_size)
    probs = jnp.exp(masked_scores(query, key, allowed) - log_total)
    probs_low = probs.astype(BF16)
    d_probs = jnp.einsum("qhd,sd->hqs", d_attended, value, preferred_element_type=F32)
    d_scores = (probs * (d_probs - jnp.sum(d_probs * probs, axis=-1, keepdims=True))).astype(BF16)
    scaling = head_size ** (-0.5)
    d_query = jnp.einsum("hqs,sd->qhd", d_scores, key, preferred_element_type=F32) * scaling
    d_key = jnp.einsum("hqs,qhd->sd", d_scores, query, preferred_element_type=F32) * scaling
    d_value = jnp.einsum("hqs,qhd->sd", probs_low, d_attended, preferred_element_type=F32)
    d_query = unrotate(d_query, cosine, sine).reshape(seq_len, query_width).astype(BF16)
    d_key = unrotate(d_key[:, None, :], cosine, sine)[:, 0]
    d_key_value = jnp.concatenate([d_key, d_value], axis=1)
    arrived = swap(jnp.concatenate([d_query, d_key_value.astype(BF16)], axis=1), "col")
    d_key_value = (d_key_value + arrived[:, query_width:].astype(F32)).astype(BF16)
    d_projected = jnp.concatenate(
        [in_order(col, d_query, arrived[:, :query_width], 1), d_key_value], axis=1
    )
    qkv_terms = dot(first_normed[:, :half_width], d_projected, 0, 0).astype(BF16)
    qkv_sum = dp_scatter(qkv_terms.reshape(count, feature_rows, -1), rank, 0)
    bias_part = jnp.sum(d_projected, axis=0, dtype=F32)
    d_first = row_sum_own(dot(d_projected, qkv_block, 1, 1), F32)
    stream_own = block_input.astype(F32)
    first_scale_own = own_tokens(first_scale)
    first_gain_part = jnp.sum(d_first * stream_own * first_scale_own, axis=0)
    weighted = d_first * first_gain
    inner = jnp.sum(weighted * stream_own, axis=1)
    inner = (inner + swap(inner, "col"))[:, None]
    input_grad = d_hidden[:, :half_width] + first_scale_own * (
        weighted - stream_own * (first_scale_own * first_scale_own) * (inner / model_width)
    )

    mlp_chip = row_sum_own(dot(activated, down_own, 1, 0), BF16)
    mlp_far = swap(mlp_chip[:, half_width:].astype(BF16), "col").astype(F32)
    block_output = (hidden_own[:, :half_width] + (mlp_chip[:, :half_width] + mlp_far)).astype(BF16)

    gain_parts = jnp.concatenate([first_gain_part, second_gain_part])
    gain_parts = gain_parts + swap(gain_parts, "row")
    small = dp_sum(jnp.concatenate([gain_parts, bias_part]))
    bias_width = bias.shape[0] // count
    bias_grad = lax.dynamic_slice_in_dim(small[model_width:], rank * bias_width, bias_width, 0)

    down_far_sum = swap(down_sum[:, half_width:].astype(BF16), "col").astype(F32)
    down_grad = in_order(col, down_sum[:, :half_width], down_far_sum, 0)
    gate_up_sum = jnp.stack([gate_sum, up_sum], axis=2)
    far_sum = swap(gate_up_sum[1].astype(BF16), "col").astype(F32)
    own_sum = gate_up_sum[0].reshape(feature_rows, 2, count, segment)
    far_sum = far_sum.reshape(feature_rows, 2, count, segment)
    gate_up_grad = jnp.stack(
        [jnp.where(col == 0, own_sum, far_sum), jnp.where(col == 0, far_sum, own_sum)], axis=3
    ).reshape(feature_rows, 2 * group_units)

    return (
        block_output,
        input_grad,
        small[:half_width],
        qkv_sum[None, None],
        bias_grad[None],
        out_sum[None, None],
        small[half_width:model_width],
        gate_up_grad[None, None],
        down_grad[None, None],
    )


def solution(mesh):
    placed = (
        P(("dp", "row"), "col"),
        P("dp"),
        P("col"),
        P("col", "row", None, None),
        P("row", None),
        P("row", "col", None, None),
        P("col"),
        P("col", "row", None, None),
        P("row", "col", None, None),
        P(("dp", "row"), "col"),
    )
    return jax.shard_map(
        shards,
        mesh=mesh,
        in_specs=placed,
        out_specs=(
            P(("dp", "row"), "col"),
            P(("dp", "row"), "col"),
            P("col"),
            P("col", "row", "dp", None),
            P("row", "dp"),
            P("row", "col", "dp", None),
            P("col"),
            P("col", "row", "dp", None),
            P("row", "col", "dp", None),
        ),
        check_vma=False,
    )
```

time: 2210 us -> 873 us (0.40)
  waiting for transfers between devices: 1820 us -> 242 us
  starting transfers between devices: 2.16 us -> 169 us
  local copies, waits for them, and re-layouts: 30.6 us -> 154 us
  blocking collectives: 82.6 us -> 0 us
  other arithmetic: 69.6 us -> 136 us
  matrix products: 174 us -> 141 us
    reduce_scatter x14 -> x0, waiting for transfers between devices: 1420 us -> none  [the longest x1 442 us: shards(): lax.psum_scatter(gate_up_sum, 'dp', scatter_dimension=0, tiled=True)]
    all_gather x8 -> x0, waiting for transfers between devices: 400 us -> none  [the longest x4 373 us: col_gather(): return lax.all_gather(local_part, 'col', axis=0, tiled=True)]
    ppermute x0 -> x77, waiting for transfers between devices: none -> 242 us  [the longest x5 96.1 us: pair_scatter(): lax.ppermute(pick(terms, 1 - side, axis).astype(BF16), 'dp', pairs)]
    ppermute x0 -> x77, starting transfers between devices: none -> 169 us  [the longest x15 107 us: line_scatter(): up = lax.ppermute(up_send.astype(BF16), 'dp', up_pairs)]
    psum x5 -> x0, blocking collectives: 52 us -> none  [the longest x1 31.4 us: shards(): gain_sums = lax.psum((first_gain_part, second_gain_part), ('dp', 'row'))]
    convert_element_type x6 -> x31, other arithmetic: 13.6 us -> 54.2 us  [the longest x1 13.8 us: shards(): first_normed = (stream * first_scale * gains[0]).astype(BF16)]
    dot_general x18 -> x19, matrix products: 174 us -> 141 us  [the longest x13 123 us: dot(): lax.dot_general(left, right, (((left_dim,), (right_dim,)), ((), ())), pre...]
    dynamic_slice x1 -> x11, local copies, waits for them, and re-layouts: 0.08 us -> 27.3 us  [the longest x5 20.2 us: pick(): return lax.dynamic_index_in_dim(array, index, axis, keepdims=False)]
  transfers between devices with their start and end apart: 22 -> 77, of which waited for: 18 -> 18; matrix products, arithmetic and copies ran while one was open for 7% -> 39% of each run, Pallas kernels for 0% -> 0%
where the time goes in v1:
time: 873 us; the launch traced here: 861 us
  waiting for transfers between devices  242 us (28%)
  starting transfers between devices  169 us (19%)
  local copies, waits for them, and re-layouts  154 us (18%)
  matrix products  141 us (16%)
  other arithmetic  136 us (16%)
  between operations  20.2 us (2%)
    dot_general x13, matrix products, dot(): lax.dot_general(left, right, (((left_dim,), (right_dim,)), ((), ())), pre...  123 us
    ppermute x15, starting transfers between devices, line_scatter(): up = lax.ppermute(up_send.astype(BF16), 'dp', up_pairs)  107 us
    ppermute x5, waiting for transfers between devices, pair_scatter(): lax.ppermute(pick(terms, 1 - side, axis).astype(BF16), 'dp', pairs)  96.1 us
    ppermute x25, waiting for transfers between devices, swap(): return lax.ppermute(part, axis_name, [(0, 1), (1, 0)])  46.6 us
    ppermute x8, waiting for transfers between devices, ring_gather(): right = lax.ppermute(right, 'dp', onward)  39.7 us
    ppermute x15, waiting for transfers between devices, line_scatter(): up = lax.ppermute(up_send.astype(BF16), 'dp', up_pairs)  32.5 us
    unnamed x173, local copies, waits for them, and re-layouts  25.4 us
    dynamic_slice x5, local copies, waits for them, and re-layouts, pick(): return lax.dynamic_index_in_dim(array, index, axis, keepdims=False)  20.2 us
  transfers between devices with their start and end apart: 77, of which 18 were waited for; matrix products, arithmetic and copies ran while one was open for 39% of the time, Pallas kernels for 0%

profile of v1, /device:TPU:0, one launch (start us, length us, event | category | flops | bytes accessed | tf_op | source)
XLA Modules:
  0.0 861.2 jit_solution(3375092057842630668)
XLA Ops:
  0.6 3.0 collective-permute-start.1
  3.7 2.8 constant_dynamic-slice_fusion.4
  6.4 5.6 reshape.374
  12.1 7.4 dynamic-slice_reduce_fusion
  34.2 18.8 %copy.83 = bf16[1,1,768,8960]{2,3,1,0:T(8,128)(2,1)} copy(bf16[1,1,768,8960]{3,2,1,0:T(8,128)(2,1)} %param.21) | data formatting | bytes 27525120 | tf_op args[7]
  55.5 4.0 constant_dynamic-slice_fusion.3
  59.6 6.2 constant_dynamic-slice_fusion.5
  90.4 3.4 broadcast_in_dim.111
  97.8 5.3 collective-permute-done.28
  105.7 22.6 %collective-permute-done.7 = bf16[768,768]{1,0:T(8,128)(2,1)S(1)} collective-permute-done((bf16[768,768]{1,0:T(8,128)(2,1)S(1)}, bf16[768,768]{1,0:T(8,128)(2,1)S(1)}, u32[]{:S(2)}, u32[]{:S(2)}) %collective-permute-start.7) | collective-permute-done | bytes 1179680 | tf_op jit(solution)/shard_map/ppermute | solution.py:23
  133.0 6.6 collective-permute-done.21
  143.2 10.5 %fusion.13 = f32[1024]{0:T(1024)S(1)} fusion(bf16[512,768]{1,0:T(8,128)(2,1)S(1)} %get-tuple-element.66, bf16[512,768]{1,0:T(8,128)(2,1)S(1)} %get-tuple-element.65, bf16[512,768]{1,0:T(8,128)(2,1)S(1)} %get-tuple-element.64, bf16[512,768]{1,0:T(8,128)(2,1)S(1)} %get-tuple-element.63), kind=kLoop, calls=%fused_computation.34 | loop fusion | flops 15727616 | bytes 3149824 | tf_op jit(solution)/shard_map/reduce_sum | solution.py:240
  153.8 13.8 %fusion.15 = bf16[1024,1536]{1,0:T(8,128)(2,1)S(1)} fusion(f32[1536]{0:T(1024)S(1)} %get-tuple-element.12, f32[1024]{0:T(1024)S(1)} %add_rsqrt_fusion.1, bf16[512,768]{1,0:T(8,128)(2,1)S(1)} %get-tuple-element.66, bf16[512,768]{1,0:T(8,128)(2,1)S(1)} %get-tuple-element.65, bf16[512,768]{1,0:T(8,128)(2,1)S(1)} %get-tuple-element.64, ...), kind=kLoop, calls=%fused_computation.36 | loop fusion | flops 17301504 | bytes 6301696 | tf_op jit(solution)/shard_map/convert_element_type | solution.py:241
  180.4 2.8 copy-done
  190.2 14.3 %maximum_maximum_fusion.1 = bf16[1024,1536]{1,0:T(8,128)(2,1)} fusion(bf16[512,768]{1,0:T(8,128)(2,1)S(1)} %get-tuple-element.56, bf16[512,768]{1,0:T(8,128)(2,1)S(1)} %get-tuple-element.55, bf16[512,768]{1,0:T(8,128)(2,1)S(1)} %copy-done.34, bf16[512,768]{1,0:T(8,128)(2,1)S(1)} %copy-done.32), kind=kLoop, calls=%fused_computation.61 | loop fusion | flops 12582912 | bytes 6291456 | tf_op jit(solution)/shard_map/concatenate | solution.py:185
  215.6 22.2 %collective-permute-done.24 = bf16[280,768]{1,0:T(8,128)(2,1)S(1)} collective-permute-done((bf16[280,768]{1,0:T(8,128)(2,1)}, bf16[280,768]{1,0:T(8,128)(2,1)S(1)}, u32[]{:S(2)}, u32[]{:S(2)}) %collective-permute-start.24) | collective-permute-done | bytes 430112 | tf_op jit(solution)/shard_map/ppermute | solution.py:54
  243.0 17.5 %collective-permute-done.14 = bf16[96,4480]{1,0:T(8,128)(2,1)S(1)} collective-permute-done((bf16[96,4480]{1,0:T(8,128)(2,1)S(1)}, bf16[96,4480]{1,0:T(8,128)(2,1)S(1)}, u32[]{:S(2)}, u32[]{:S(2)}) %collective-permute-start.14) | collective-permute-done | bytes 860192 | tf_op jit(solution)/shard_map/ppermute | solution.py:54
  263.1 11.9 %pad_maximum_fusion.4 = bf16[1536,1536]{1,0:T(8,128)(2,1)} fusion(bf16[768,1536]{1,0:T(8,128)(2,1)} %collective-permute-done.8, bf16[768,768]{1,0:T(8,128)(2,1)S(1)} %copy-done.19, bf16[768,768]{1,0:T(8,128)(2,1)S(1)} %bitcast.340), kind=kLoop, calls=%fused_computation.42 | loop fusion | flops 14155776 | bytes 9437184 | tf_op jit(solution)/shard_map/concatenate | solution.py:208
  275.1 7.4 multiply_reduce_fusion
  287.1 10.0 %copy.84 = bf16[768,4480]{0,1:T(8,128)(2,1)} copy(bf16[768,4480]{1,0:T(8,128)(2,1)} %bitcast.44) | data formatting | bytes 13762560 | tf_op jit(solution)/shard_map/reshape | solution.py:219
  297.1 21.6 %fusion.9 = f32[1024,4480]{1,0:T(8,128)} fusion(bf16[1024,1536]{1,0:T(8,128)(2,1)} %multiply_convert_fusion.3, bf16[768,4480]{0,1:T(8,128)(2,1)} %copy.84, bf16[768,4480]{0,1:T(8,128)(2,1)} %bitcast.334), kind=kOutput, calls=%fused_computation.26 | convolution fusion | flops 14120386560 | bytes 35258368 | tf_op jit(solution)/shard_map/dot_general | solution.py:17
  318.7 18.3 %multiply_convert_fusion.1 = (bf16[1024,2240]{1,0:T(8,128)(2,1)}, bf16[1024,2240]{1,0:T(8,128)(2,1)}, bf16[1024,2240]{1,0:T(8,128)(2,1)}) fusion(f32[1024,4480]{1,0:T(8,128)} %fusion.9, bf16[2240,768]{1,0:T(8,128)(2,1)S(1)} %bitcast.346, bf16[2240,768]{1,0:T(8,128)(2,1)S(1)} %bitcast.344, bf16[512,768]{1,0:T(8,128)(2,1)} %copy-done.36, ...), kind=kOutput, calls=%fused_computation.19 | convolution fusion | flops 7109476352 | bytes 42139648 | tf_op jit(solution)/shard_map/dot_general | solution.py:17
  337.0 10.3 %convolution_convert_fusion = bf16[2240,1536]{1,0:T(8,128)(2,1)S(1)} fusion(bf16[1024,2240]{1,0:T(8,128)(2,1)} %get-tuple-element.24, bf16[512,768]{1,0:T(8,128)(2,1)} %copy-done.36, bf16[512,768]{1,0:T(8,128)(2,1)} %copy-done.35, bf16[512,768]{1,0:T(8,128)(2,1)} %get-tuple-element.54, bf16[512,768]{1,0:T(8,128)(2,1)S(1)} %copy-done.33), kind=kOutput, calls=%fused_computation.10 | convolution fusion | flops 7062454272 | bytes 14614528 | tf_op jit(solution)/shard_map/dot_general | solution.py:17
  347.4 9.9 %fusion.21 = f32[1024,1536]{1,0:T(8,128)} fusion(bf16[1024,2240]{1,0:T(8,128)(2,1)S(1)} %copy-done.70, bf16[2240,768]{1,0:T(8,128)(2,1)S(1)} %bitcast.347, bf16[2240,768]{1,0:T(8,128)(2,1)S(1)} %bitcast.345), kind=kOutput, calls=%fused_computation.45 | convolution fusion | flops 7060193280 | bytes 17760256 | tf_op jit(solution)/shard_map/dot_general | solution.py:17
  360.8 9.2 %convolution_convert_fusion.1 = bf16[1536,2240]{0,1:T(8,128)(2,1)} fusion(bf16[1024,1536]{1,0:T(8,128)(2,1)S(1)} %copy-done.27, bf16[1024,2240]{1,0:T(8,128)(2,1)S(1)} %bitcast.359), kind=kOutput, calls=%fused_computation.11 | convolution fusion | flops 7049871360 | bytes 14614528 | tf_op jit(solution)/shard_map/dot_general | solution.py:17
  370.0 9.8 %copy.99 = bf16[1536,2240]{1,0:T(8,128)(2,1)} copy(bf16[1536,2240]{0,1:T(8,128)(2,1)} %convolution_convert_fusion.1) | data formatting | bytes 13762560 | tf_op jit(solution)/shard_map/convert_element_type | solution.py:286
  379.8 23.4 %fusion.5 = f32[1024,1536]{1,0:T(8,128)} fusion(bf16[1024,2240]{1,0:T(8,128)(2,1)} %get-tuple-element.23, bf16[1024,2240]{1,0:T(8,128)(2,1)} %get-tuple-element.22, bf16[768,4480]{0,1:T(8,128)(2,1)} %copy.84, bf16[768,4480]{0,1:T(8,128)(2,1)} %bitcast.335), kind=kOutput, calls=%fused_computation.22 | convolution fusion | flops 14138736640 | bytes 29229056 | tf_op jit(solution)/shard_map/dot_general | solution.py:17
  405.4 3.4 dynamic-slice_convert_fusion.1
  409.3 12.3 %convolution_convert_fusion.2 = bf16[1536,2240]{0,1:T(8,128)(2,1)} fusion(bf16[1024,1536]{1,0:T(8,128)(2,1)S(1)} %copy-done.27, bf16[1024,2240]{1,0:T(8,128)(2,1)} %get-tuple-element.22), kind=kOutput, calls=%fused_computation.12 | convolution fusion | flops 7049871360 | bytes 14614528 | tf_op jit(solution)/shard_map/dot_general | solution.py:17
  427.4 9.8 %copy.94 = bf16[1536,2240]{1,0:T(8,128)(2,1)} copy(bf16[1536,2240]{0,1:T(8,128)(2,1)} %convolution_convert_fusion.2) | data formatting | bytes 13762560 | tf_op jit(solution)/shard_map/convert_element_type | solution.py:284
  437.2 4.2 dynamic-slice_bitcast_fusion
  442.3 3.0 convert_add_fusion.5
  447.8 13.1 %collective-permute-done.31 = bf16[512,1536]{1,0:T(8,128)(2,1)} collective-permute-done((bf16[512,1536]{1,0:T(8,128)(2,1)}, bf16[512,1536]{1,0:T(8,128)(2,1)}, u32[]{:S(2)}, u32[]{:S(2)}) %collective-permute-start.31) | collective-permute-done | bytes 1572896 | tf_op jit(solution)/shard_map/ppermute | solution.py:23
  460.9 3.3 fusion.133
  467.0 4.1 fusion.130
  471.1 5.5 collective-permute-done.26
  479.0 3.9 fusion.12
  484.1 3.7 collective-permute-start.70
  489.5 23.3 %collective-permute-done.61 = bf16[2,4,96,2240]{3,2,0,1:T(8,128)(2,1)} collective-permute-done((bf16[2,4,96,2240]{3,2,0,1:T(8,128)(2,1)}, bf16[2,4,96,2240]{3,2,0,1:T(8,128)(2,1)}, u32[]{:S(2)}, u32[]{:S(2)}) %collective-permute-start.61) | collective-permute-done | bytes 3440672 | tf_op jit(solution)/shard_map/ppermute | solution.py:95
  512.8 3.0 fusion.10
  516.8 3.4 collective-permute-start.62
  520.3 66.7 %collective-permute-done.54 = bf16[2,4,96,2240]{3,2,1,0:T(8,128)(2,1)} collective-permute-done((bf16[2,4,96,2240]{3,2,1,0:T(8,128)(2,1)}, bf16[2,4,96,2240]{3,2,1,0:T(8,128)(2,1)}, u32[]{:S(2)}, u32[]{:S(2)}) %collective-permute-start.54) | collective-permute-done | bytes 3440672 | tf_op jit(solution)/shard_map/ppermute | solution.py:95
  588.6 2.9 fusion.11
  592.5 3.4 collective-permute-start.55
  599.8 13.6 %collective-permute-done.55 = bf16[2,96,2240]{2,1,0:T(8,128)(2,1)S(1)} collective-permute-done((bf16[2,96,2240]{2,1,0:T(8,128)(2,1)S(1)}, bf16[2,96,2240]{2,1,0:T(8,128)(2,1)S(1)}, u32[]{:S(2)}, u32[]{:S(2)}) %collective-permute-start.55) | collective-permute-done | bytes 860192 | tf_op jit(solution)/shard_map/ppermute | solution.py:84
  613.4 5.4 collective-permute-start.71
  625.2 2.8 fusion.81
  628.0 6.8 fusion
  634.9 6.9 fusion.2
  657.4 4.4 collective-permute-start.63
  668.5 16.5 %collective-permute-done.49 = bf16[96,768]{1,0:T(8,128)(2,1)S(1)} collective-permute-done((bf16[96,768]{1,0:T(8,128)(2,1)S(1)}, bf16[96,768]{1,0:T(8,128)(2,1)S(1)}, u32[]{:S(2)}, u32[]{:S(2)}) %collective-permute-start.49) | collective-permute-done | bytes 147488 | tf_op jit(solution)/shard_map/ppermute | solution.py:84
  689.5 24.4 %collective-permute-start.50 = (bf16[96,768]{1,0:T(8,128)(2,1)S(1)}, bf16[96,768]{1,0:T(8,128)(2,1)S(1)}, u32[]{:S(2)}, u32[]{:S(2)}) collective-permute-start(bf16[96,768]{1,0:T(8,128)(2,1)S(1)} %get-tuple-element.71), channel_id=1, source_target_pairs={{0,8},{4,12},{8,16},{12,20},{16,24},{20,28},{1,9},{5,13},{9,17},{1... | collective-permute-start | bytes 442376 | tf_op jit(solution)/shard_map/ppermute | solution.py:84
  716.8 5.2 collective-permute-start.72
  722.0 10.4 %collective-permute-start.64 = (bf16[2,96,2240]{2,1,0:T(8,128)(2,1)S(1)}, bf16[2,96,2240]{2,1,0:T(8,128)(2,1)S(1)}, u32[]{:S(2)}, u32[]{:S(2)}) collective-permute-start(bf16[2,96,2240]{2,1,0:T(8,128)(2,1)S(1)} %get-tuple-element.35), channel_id=1, source_target_pairs={{0,8},{4,12},{8,16},{12,20},{16,24},{20,28},{1,9},{5,13},{9,17},{1... | collective-permute-start | bytes 2580488 | tf_op jit(solution)/shard_map/ppermute | solution.py:84
  734.2 3.1 collective-permute-start.57
  747.8 6.0 collective-permute-done.40
  758.7 20.8 %collective-permute-start.41 = (bf16[96,1024]{1,0:T(8,128)(2,1)S(1)}, bf16[96,1024]{1,0:T(8,128)(2,1)S(1)}, u32[]{:S(2)}, u32[]{:S(2)}) collective-permute-start(bf16[96,1024]{1,0:T(8,128)(2,1)S(1)} %get-tuple-element.69), channel_id=1, source_target_pairs={{0,8},{4,12},{1,9},{5,13},{2,10},{6,14},{3,11},{7,15}} | collective-permute-start | bytes 589832 | tf_op jit(solution)/shard_map/ppermute | solution.py:84
  779.5 3.4 collective-permute-done.67
  786.2 6.2 collective-permute-done.60
  793.6 12.8 %collective-permute-start.42 = (bf16[96,1024]{1,0:T(8,128)(2,1)}, bf16[96,1024]{1,0:T(8,128)(2,1)}, u32[]{:S(2)}, u32[]{:S(2)}) collective-permute-start(bf16[96,1024]{1,0:T(8,128)(2,1)} %fusion.99), channel_id=1, source_target_pairs={{0,8},{4,12},{8,16},{12,20},{1,9},{5,13},{9,17},{13,21},{2,10},{6,... | collective-permute-start | bytes 589832 | tf_op jit(solution)/shard_map/ppermute | solution.py:84
  813.6 4.4 collective-permute-start.43
  826.0 7.4 collective-permute-done.46
  847.4 5.8 copy.102
  853.2 7.6 broadcast_in_dim_reshape.3
  (448 shorter events, 199.0 us)
Async XLA Ops:
  0.6 95.2 %collective-permute-start.1 = (bf16[512,768]{1,0:T(8,128)(2,1)}, bf16[512,768]{1,0:T(8,128)(2,1)}, u32[]{:S(2)}, u32[]{:S(2)}) collective-permute-start(bf16[512,768]{1,0:T(8,128)(2,1)} %param.14), channel_id=1, source_target_pairs={{0,1},{1,0},{2,3},{3,2},{4,5},{5,4},{6,7},{7,6},{8,9},{9,8},{10,11... | collective-permute-start | bytes 2359304 | tf_op jit(solution)/shard_map/ppermute | solution.py:23
  3.7 81.9 %collective-permute-start = (bf16[512,768]{1,0:T(8,128)(2,1)}, bf16[512,768]{1,0:T(8,128)(2,1)}, u32[]{:S(2)}, u32[]{:S(2)}) collective-permute-start(bf16[512,768]{1,0:T(8,128)(2,1)} %param.14), channel_id=1, source_target_pairs={{0,2},{2,0},{1,3},{3,1},{4,6},{6,4},{5,7},{7,5},{8,10},{10,8},{9,1... | collective-permute-start | bytes 2359304 | tf_op jit(solution)/shard_map/ppermute | solution.py:23
  21.6 68.7 %collective-permute-start.9 = (bf16[96,4480]{1,0:T(8,128)(2,1)}, bf16[96,4480]{1,0:T(8,128)(2,1)}, u32[]{:S(2)}, u32[]{:S(2)}) collective-permute-start(bf16[96,4480]{1,0:T(8,128)(2,1)} %reshape.375), channel_id=1, source_target_pairs={{0,1},{1,0},{2,3},{3,2},{4,5},{5,4},{6,7},{7,6},{8,9},{9,8},{10,11... | collective-permute-start | bytes 2580488 | tf_op jit(solution)/shard_map/ppermute | solution.py:23
  22.3 59.1 %collective-permute-start.3 = (f32[2,768]{1,0:T(2,128)}, f32[2,768]{1,0:T(2,128)}, u32[]{:S(2)}, u32[]{:S(2)}) collective-permute-start(f32[2,768]{1,0:T(2,128)} %pad_maximum_fusion.19), channel_id=1, source_target_pairs={{0,1},{1,0},{2,3},{3,2},{4,5},{5,4},{6,7},{7,6},{8,9},{9,8},{10,11... | collective-permute-start | bytes 18440 | tf_op jit(solution)/shard_map/ppermute | solution.py:23
  26.1 56.2 %collective-permute-start.17 = (bf16[280,768]{1,0:T(8,128)(2,1)}, bf16[280,768]{1,0:T(8,128)(2,1)}, u32[]{:S(2)}, u32[]{:S(2)}) collective-permute-start(bf16[280,768]{1,0:T(8,128)(2,1)} %dynamic-slice_bitcast_fusion.12), channel_id=1, source_target_pairs={{0,1},{1,0},{2,3},{3,2},{4,5},{5,4},{6,7},{7,6},{8,9},{9,8},{10,11... | collective-permute-start | bytes 1290248 | tf_op jit(solution)/shard_map/ppermute | solution.py:23
  82.3 20.8 %collective-permute-start.28 = (bf16[512,768]{1,0:T(8,128)(2,1)}, bf16[512,768]{1,0:T(8,128)(2,1)}, u32[]{:S(2)}, u32[]{:S(2)}) collective-permute-start(bf16[512,768]{1,0:T(8,128)(2,1)} %param.23), channel_id=1, source_target_pairs={{0,1},{1,0},{2,3},{3,2},{4,5},{5,4},{6,7},{7,6},{8,9},{9,8},{10,11... | collective-permute-start | bytes 2359304 | tf_op jit(solution)/shard_map/ppermute | solution.py:23
  85.6 42.7 %collective-permute-start.7 = (bf16[768,768]{1,0:T(8,128)(2,1)S(1)}, bf16[768,768]{1,0:T(8,128)(2,1)S(1)}, u32[]{:S(2)}, u32[]{:S(2)}) collective-permute-start(bf16[768,768]{1,0:T(8,128)(2,1)S(1)} %bitcast.338), channel_id=1, source_target_pairs={{0,1},{1,0},{2,3},{3,2},{4,5},{5,4},{6,7},{7,6},{8,9},{9,8},{10,11... | collective-permute-start | bytes 3538952 | tf_op jit(solution)/shard_map/ppermute | solution.py:23
  87.0 16.1 %collective-permute-start.18 = (bf16[280,768]{1,0:T(8,128)(2,1)}, bf16[280,768]{1,0:T(8,128)(2,1)S(1)}, u32[]{:S(2)}, u32[]{:S(2)}) collective-permute-start(bf16[280,768]{1,0:T(8,128)(2,1)} %collective-permute-done.17), channel_id=1, source_target_pairs={{0,8},{8,16},{16,24},{24,28},{28,20},{20,12},{12,4},{4,0},{1,9},{9... | collective-permute-start | bytes 1290248 | tf_op jit(solution)/shard_map/ppermute | solution.py:54
  90.3 13.3 %collective-permute-start.19 = (bf16[280,768]{1,0:T(8,128)(2,1)}, bf16[280,768]{1,0:T(8,128)(2,1)S(1)}, u32[]{:S(2)}, u32[]{:S(2)}) collective-permute-start(bf16[280,768]{1,0:T(8,128)(2,1)} %collective-permute-done.17), channel_id=1, source_target_pairs={{8,0},{16,8},{24,16},{28,24},{20,28},{12,20},{4,12},{0,4},{9,1},{1... | collective-permute-start | bytes 1290248 | tf_op jit(solution)/shard_map/ppermute | solution.py:58
  95.9 71.7 %collective-permute-start.4 = (bf16[768,640]{1,0:T(8,128)(2,1)S(1)}, bf16[768,640]{1,0:T(8,128)(2,1)S(1)}, u32[]{:S(2)}, u32[]{:S(2)}) collective-permute-start(bf16[768,640]{1,0:T(8,128)(2,1)S(1)} %copy-done.49), channel_id=1, source_target_pairs={{0,1},{1,0},{2,3},{3,2},{4,5},{5,4},{6,7},{7,6},{8,9},{9,8},{10,11... | collective-permute-start | bytes 2949128 | tf_op jit(solution)/shard_map/ppermute | solution.py:23
  103.1 38.2 %collective-permute-start.2 = (bf16[512,768]{1,0:T(8,128)(2,1)}, bf16[512,768]{1,0:T(8,128)(2,1)S(1)}, u32[]{:S(2)}, u32[]{:S(2)}) collective-permute-start(bf16[512,768]{1,0:T(8,128)(2,1)} %collective-permute-done.1), channel_id=1, source_target_pairs={{0,2},{2,0},{1,3},{3,1},{4,6},{6,4},{5,7},{7,5},{8,10},{10,8},{9,1... | collective-permute-start | bytes 2359304 | tf_op jit(solution)/shard_map/ppermute | solution.py:23
  103.1 84.0 %collective-permute-start.29 = (bf16[512,768]{1,0:T(8,128)(2,1)}, bf16[512,768]{1,0:T(8,128)(2,1)}, u32[]{:S(2)}, u32[]{:S(2)}) collective-permute-start(bf16[512,768]{1,0:T(8,128)(2,1)} %collective-permute-done.28), channel_id=1, source_target_pairs={{0,2},{2,0},{1,3},{3,1},{4,6},{6,4},{5,7},{7,5},{8,10},{10,8},{9,1... | collective-permute-start | bytes 2359304 | tf_op jit(solution)/shard_map/ppermute | solution.py:23
  103.7 28.0 %collective-permute-start.20 = (bf16[280,768]{1,0:T(8,128)(2,1)S(1)}, bf16[280,768]{1,0:T(8,128)(2,1)}, u32[]{:S(2)}, u32[]{:S(2)}) collective-permute-start(bf16[280,768]{1,0:T(8,128)(2,1)S(1)} %collective-permute-done.18), channel_id=1, source_target_pairs={{0,8},{8,16},{16,24},{24,28},{28,20},{20,12},{12,4},{4,0},{1,9},{9... | collective-permute-start | bytes 1290248 | tf_op jit(solution)/shard_map/ppermute | solution.py:54
  131.7 72.9 %collective-permute-start.10 = (bf16[96,4480]{1,0:T(8,128)(2,1)}, bf16[96,4480]{1,0:T(8,128)(2,1)}, u32[]{:S(2)}, u32[]{:S(2)}) collective-permute-start(bf16[96,4480]{1,0:T(8,128)(2,1)} %collective-permute-done.9), channel_id=1, source_target_pairs={{0,8},{8,16},{16,24},{24,28},{28,20},{20,12},{12,4},{4,0},{1,9},{9... | collective-permute-start | bytes 2580488 | tf_op jit(solution)/shard_map/ppermute | solution.py:54
  139.6 68.6 %collective-permute-start.11 = (bf16[96,4480]{1,0:T(8,128)(2,1)}, bf16[96,4480]{1,0:T(8,128)(2,1)}, u32[]{:S(2)}, u32[]{:S(2)}) collective-permute-start(bf16[96,4480]{1,0:T(8,128)(2,1)} %collective-permute-done.9), channel_id=1, source_target_pairs={{8,0},{16,8},{24,16},{28,24},{20,28},{12,20},{4,12},{0,4},{9,1},{1... | collective-permute-start | bytes 2580488 | tf_op jit(solution)/shard_map/ppermute | solution.py:58
  141.3 121.8 %collective-permute-start.8 = (bf16[768,1536]{1,0:T(8,128)(2,1)}, bf16[768,1536]{1,0:T(8,128)(2,1)}, u32[]{:S(2)}, u32[]{:S(2)}) collective-permute-start(bf16[768,1536]{1,0:T(8,128)(2,1)} %pad_maximum_fusion.8), channel_id=1, source_target_pairs={{0,2},{2,0},{1,3},{3,1},{4,6},{6,4},{5,7},{7,5},{8,10},{10,8},{9,1... | collective-permute-start | bytes 7077896 | tf_op jit(solution)/shard_map/ppermute | solution.py:23
  167.6 41.2 %collective-permute-start.22 = (bf16[280,768]{1,0:T(8,128)(2,1)}, bf16[280,768]{1,0:T(8,128)(2,1)}, u32[]{:S(2)}, u32[]{:S(2)}) collective-permute-start(bf16[280,768]{1,0:T(8,128)(2,1)} %collective-permute-done.20), channel_id=1, source_target_pairs={{0,8},{8,16},{16,24},{24,28},{28,20},{20,12},{12,4},{4,0},{1,9},{9... | collective-permute-start | bytes 1290248 | tf_op jit(solution)/shard_map/ppermute | solution.py:54
  187.1 27.2 %collective-permute-start.23 = (bf16[280,768]{1,0:T(8,128)(2,1)S(1)}, bf16[280,768]{1,0:T(8,128)(2,1)S(1)}, u32[]{:S(2)}, u32[]{:S(2)}) collective-permute-start(bf16[280,768]{1,0:T(8,128)(2,1)S(1)} %copy-done.55), channel_id=1, source_target_pairs={{8,0},{16,8},{24,16},{28,24},{20,28},{12,20},{4,12},{0,4},{9,1},{1... | collective-permute-start | bytes 1290248 | tf_op jit(solution)/shard_map/ppermute | solution.py:58
  204.5 34.0 %collective-permute-start.5 = (bf16[1024,384]{0,1:T(8,128)(2,1)S(1)}, bf16[1024,384]{0,1:T(8,128)(2,1)S(1)}, u32[]{:S(2)}, u32[]{:S(2)}) collective-permute-start(bf16[1024,384]{0,1:T(8,128)(2,1)S(1)} %bitcast.355), channel_id=1, source_target_pairs={{0,1},{1,0},{2,3},{3,2},{4,5},{5,4},{6,7},{7,6},{8,9},{9,8},{10,11... | collective-permute-start | bytes 2359304 | tf_op jit(solution)/shard_map/ppermute | solution.py:23
  208.2 30.8 %collective-permute-start.12 = (bf16[96,4480]{1,0:T(8,128)(2,1)}, bf16[96,4480]{1,0:T(8,128)(2,1)S(1)}, u32[]{:S(2)}, u32[]{:S(2)}) collective-permute-start(bf16[96,4480]{1,0:T(8,128)(2,1)} %collective-permute-done.10), channel_id=1, source_target_pairs={{0,8},{8,16},{16,24},{24,28},{28,20},{20,12},{12,4},{4,0},{1,9},{9... | collective-permute-start | bytes 2580488 | tf_op jit(solution)/shard_map/ppermute | solution.py:54
  208.8 29.0 %collective-permute-start.24 = (bf16[280,768]{1,0:T(8,128)(2,1)}, bf16[280,768]{1,0:T(8,128)(2,1)S(1)}, u32[]{:S(2)}, u32[]{:S(2)}) collective-permute-start(bf16[280,768]{1,0:T(8,128)(2,1)} %collective-permute-done.22), channel_id=1, source_target_pairs={{0,8},{8,16},{16,24},{24,28},{28,20},{20,12},{12,4},{4,0},{1,9},{9... | collective-permute-start | bytes 1290248 | tf_op jit(solution)/shard_map/ppermute | solution.py:54
  214.3 26.3 %collective-permute-start.13 = (bf16[96,4480]{1,0:T(8,128)(2,1)}, bf16[96,4480]{1,0:T(8,128)(2,1)S(1)}, u32[]{:S(2)}, u32[]{:S(2)}) collective-permute-start(bf16[96,4480]{1,0:T(8,128)(2,1)} %collective-permute-done.11), channel_id=1, source_target_pairs={{8,0},{16,8},{24,16},{28,24},{20,28},{12,20},{4,12},{0,4},{9,1},{1... | collective-permute-start | bytes 2580488 | tf_op jit(solution)/shard_map/ppermute | solution.py:58
  238.9 36.2 %collective-permute-start.6 = (bf16[1024,768]{0,1:T(8,128)(2,1)S(1)}, bf16[1024,768]{0,1:T(8,128)(2,1)S(1)}, u32[]{:S(2)}, u32[]{:S(2)}) collective-permute-start(bf16[1024,768]{0,1:T(8,128)(2,1)S(1)} %pad_maximum_fusion.11), channel_id=1, source_target_pairs={{0,2},{2,0},{1,3},{3,1},{4,6},{6,4},{5,7},{7,5},{8,10},{10,8},{9,1... | collective-permute-start | bytes 4718600 | tf_op jit(solution)/shard_map/ppermute | solution.py:23
  239.0 21.5 %collective-permute-start.14 = (bf16[96,4480]{1,0:T(8,128)(2,1)S(1)}, bf16[96,4480]{1,0:T(8,128)(2,1)S(1)}, u32[]{:S(2)}, u32[]{:S(2)}) collective-permute-start(bf16[96,4480]{1,0:T(8,128)(2,1)S(1)} %collective-permute-done.12), channel_id=1, source_target_pairs={{0,8},{8,16},{16,24},{24,28},{28,20},{20,12},{12,4},{4,0},{1,9},{9... | collective-permute-start | bytes 2580488 | tf_op jit(solution)/shard_map/ppermute | solution.py:54
  240.6 21.4 %collective-permute-start.15 = (bf16[96,4480]{1,0:T(8,128)(2,1)S(1)}, bf16[96,4480]{1,0:T(8,128)(2,1)S(1)}, u32[]{:S(2)}, u32[]{:S(2)}) collective-permute-start(bf16[96,4480]{1,0:T(8,128)(2,1)S(1)} %collective-permute-done.13), channel_id=1, source_target_pairs={{8,0},{16,8},{24,16},{28,24},{20,28},{12,20},{4,12},{0,4},{9,1},{1... | collective-permute-start | bytes 2580488 | tf_op jit(solution)/shard_map/ppermute | solution.py:58
  260.5 25.5 %collective-permute-start.16 = (bf16[96,4480]{1,0:T(8,128)(2,1)S(1)}, bf16[96,4480]{1,0:T(8,128)(2,1)S(1)}, u32[]{:S(2)}, u32[]{:S(2)}) collective-permute-start(bf16[96,4480]{1,0:T(8,128)(2,1)S(1)} %collective-permute-done.14), channel_id=1, source_target_pairs={{0,8},{8,16},{16,24},{24,28},{28,20},{20,12},{12,4},{4,0},{1,9},{9... | collective-permute-start | bytes 2580488 | tf_op jit(solution)/shard_map/ppermute | solution.py:54
  359.3 119.8 %collective-permute-start.69 = (bf16[4,280,1536]{2,1,0:T(8,128)(2,1)}, bf16[4,280,1536]{2,1,0:T(8,128)(2,1)}, u32[]{:S(2)}, u32[]{:S(2)}) collective-permute-start(bf16[4,280,1536]{2,1,0:T(8,128)(2,1)} %dynamic-slice_bitcast_fusion.1), channel_id=1, source_target_pairs={{0,4},{4,0},{8,12},{12,8},{16,20},{20,16},{24,28},{28,24},{1,5},{5... | collective-permute-start | bytes 10321928 | tf_op jit(solution)/shard_map/ppermute | solution.py:95
  405.3 16.3 %collective-permute-start.30 = (bf16[512,1536]{1,0:T(8,128)(2,1)S(1)}, bf16[512,1536]{1,0:T(8,128)(2,1)S(1)}, u32[]{:S(2)}, u32[]{:S(2)}) collective-permute-start(bf16[512,1536]{1,0:T(8,128)(2,1)S(1)} %dynamic-slice_convert_fusion), channel_id=1, source_target_pairs={{0,2},{2,0},{1,3},{3,1},{4,6},{6,4},{5,7},{7,5},{8,10},{10,8},{9,1... | collective-permute-start | bytes 4718600 | tf_op jit(solution)/shard_map/ppermute | solution.py:23
  408.8 33.5 %collective-permute-start.25 = (bf16[512,1536]{1,0:T(8,128)(2,1)}, bf16[512,1536]{1,0:T(8,128)(2,1)}, u32[]{:S(2)}, u32[]{:S(2)}) collective-permute-start(bf16[512,1536]{1,0:T(8,128)(2,1)} %dynamic-slice_convert_fusion.1), channel_id=1, source_target_pairs={{0,2},{2,0},{1,3},{3,1},{4,6},{6,4},{5,7},{7,5},{8,10},{10,8},{9,1... | collective-permute-start | bytes 4718600 | tf_op jit(solution)/shard_map/ppermute | solution.py:23
  423.3 37.6 %collective-permute-start.31 = (bf16[512,1536]{1,0:T(8,128)(2,1)}, bf16[512,1536]{1,0:T(8,128)(2,1)}, u32[]{:S(2)}, u32[]{:S(2)}) collective-permute-start(bf16[512,1536]{1,0:T(8,128)(2,1)} %fusion.32), channel_id=1, source_target_pairs={{0,1},{1,0},{2,3},{3,2},{4,5},{5,4},{6,7},{7,6},{8,9},{9,8},{10,11... | collective-permute-start | bytes 4718600 | tf_op jit(solution)/shard_map/ppermute | solution.py:23
  426.3 86.5 %collective-permute-start.61 = (bf16[2,4,96,2240]{3,2,0,1:T(8,128)(2,1)}, bf16[2,4,96,2240]{3,2,0,1:T(8,128)(2,1)}, u32[]{:S(2)}, u32[]{:S(2)}) collective-permute-start(bf16[2,4,96,2240]{3,2,0,1:T(8,128)(2,1)} %bitcast.314), channel_id=1, source_target_pairs={{0,4},{4,0},{8,12},{12,8},{16,20},{20,16},{24,28},{28,24},{1,5},{5... | collective-permute-start | bytes 10321928 | tf_op jit(solution)/shard_map/ppermute | solution.py:95
  441.3 145.6 %collective-permute-start.54 = (bf16[2,4,96,2240]{3,2,1,0:T(8,128)(2,1)}, bf16[2,4,96,2240]{3,2,1,0:T(8,128)(2,1)}, u32[]{:S(2)}, u32[]{:S(2)}) collective-permute-start(bf16[2,4,96,2240]{3,2,1,0:T(8,128)(2,1)} %dynamic-slice_bitcast_fusion), channel_id=1, source_target_pairs={{0,4},{4,0},{8,12},{12,8},{16,20},{20,16},{24,28},{28,24},{1,5},{5... | collective-permute-start | bytes 10321928 | tf_op jit(solution)/shard_map/ppermute | solution.py:95
  446.3 30.4 %collective-permute-start.26 = (bf16[512,768]{1,0:T(8,128)(2,1)}, bf16[512,768]{1,0:T(8,128)(2,1)}, u32[]{:S(2)}, u32[]{:S(2)}) collective-permute-start(bf16[512,768]{1,0:T(8,128)(2,1)} %slice.257), channel_id=1, source_target_pairs={{0,1},{1,0},{2,3},{3,2},{4,5},{5,4},{6,7},{7,6},{8,9},{9,8},{10,11... | collective-permute-start | bytes 2359304 | tf_op jit(solution)/shard_map/ppermute | solution.py:23
  471.1 148.9 %collective-permute-start.32 = (bf16[512,1536]{1,0:T(8,128)(2,1)S(1)}, bf16[512,1536]{1,0:T(8,128)(2,1)S(1)}, u32[]{:S(2)}, u32[]{:S(2)}) collective-permute-start(bf16[512,1536]{1,0:T(8,128)(2,1)S(1)} %get-tuple-element.16), channel_id=1, source_target_pairs={{0,2},{2,0},{1,3},{3,1},{4,6},{6,4},{5,7},{7,5},{8,10},{10,8},{9,1... | collective-permute-start | bytes 4718600 | tf_op jit(solution)/shard_map/ppermute | solution.py:23
  484.1 108.4 %collective-permute-start.70 = (bf16[280,1536]{1,0:T(8,128)(2,1)S(1)}, bf16[280,1536]{1,0:T(8,128)(2,1)S(1)}, u32[]{:S(2)}, u32[]{:S(2)}) collective-permute-start(bf16[280,1536]{1,0:T(8,128)(2,1)S(1)} %get-tuple-element.41), channel_id=1, source_target_pairs={{0,8},{4,12},{1,9},{5,13},{2,10},{6,14},{3,11},{7,15}} | collective-permute-start | bytes 2580488 | tf_op jit(solution)/shard_map/ppermute | solution.py:84
  487.8 174.0 %collective-permute-start.73 = (bf16[280,1536]{1,0:T(8,128)(2,1)}, bf16[280,1536]{1,0:T(8,128)(2,1)}, u32[]{:S(2)}, u32[]{:S(2)}) collective-permute-start(bf16[280,1536]{1,0:T(8,128)(2,1)} %get-tuple-element.42), channel_id=1, source_target_pairs={{24,16},{28,20},{25,17},{29,21},{26,18},{30,22},{27,19},{31,23}} | collective-permute-start | bytes 2580488 | tf_op jit(solution)/shard_map/ppermute | solution.py:85
  516.8 80.3 %collective-permute-start.62 = (bf16[2,96,2240]{2,1,0:T(8,128)(2,1)S(1)}, bf16[2,96,2240]{2,1,0:T(8,128)(2,1)S(1)}, u32[]{:S(2)}, u32[]{:S(2)}) collective-permute-start(bf16[2,96,2240]{2,1,0:T(8,128)(2,1)S(1)} %get-tuple-element.37), channel_id=1, source_target_pairs={{0,8},{4,12},{1,9},{5,13},{2,10},{6,14},{3,11},{7,15}} | collective-permute-start | bytes 2580488 | tf_op jit(solution)/shard_map/ppermute | solution.py:84
  587.0 98.6 %collective-permute-start.65 = (bf16[2,96,2240]{2,1,0:T(8,128)(2,1)}, bf16[2,96,2240]{2,1,0:T(8,128)(2,1)}, u32[]{:S(2)}, u32[]{:S(2)}) collective-permute-start(bf16[2,96,2240]{2,1,0:T(8,128)(2,1)} %get-tuple-element.38), channel_id=1, source_target_pairs={{24,16},{28,20},{25,17},{29,21},{26,18},{30,22},{27,19},{31,23}} | collective-permute-start | bytes 2580488 | tf_op jit(solution)/shard_map/ppermute | solution.py:85
  592.5 20.9 %collective-permute-start.55 = (bf16[2,96,2240]{2,1,0:T(8,128)(2,1)S(1)}, bf16[2,96,2240]{2,1,0:T(8,128)(2,1)S(1)}, u32[]{:S(2)}, u32[]{:S(2)}) collective-permute-start(bf16[2,96,2240]{2,1,0:T(8,128)(2,1)S(1)} %get-tuple-element.33), channel_id=1, source_target_pairs={{0,8},{4,12},{1,9},{5,13},{2,10},{6,14},{3,11},{7,15}} | collective-permute-start | bytes 2580488 | tf_op jit(solution)/shard_map/ppermute | solution.py:84
  597.1 92.3 %collective-permute-start.58 = (bf16[2,96,2240]{2,1,0:T(8,128)(2,1)}, bf16[2,96,2240]{2,1,0:T(8,128)(2,1)}, u32[]{:S(2)}, u32[]{:S(2)}) collective-permute-start(bf16[2,96,2240]{2,1,0:T(8,128)(2,1)} %get-tuple-element.34), channel_id=1, source_target_pairs={{24,16},{28,20},{25,17},{29,21},{26,18},{30,22},{27,19},{31,23}} | collective-permute-start | bytes 2580488 | tf_op jit(solution)/shard_map/ppermute | solution.py:85
  613.4 49.4 %collective-permute-start.71 = (bf16[280,1536]{1,0:T(8,128)(2,1)}, bf16[280,1536]{1,0:T(8,128)(2,1)}, u32[]{:S(2)}, u32[]{:S(2)}) collective-permute-start(bf16[280,1536]{1,0:T(8,128)(2,1)} %fusion.53), channel_id=1, source_target_pairs={{0,8},{4,12},{8,16},{12,20},{1,9},{5,13},{9,17},{13,21},{2,10},{6,... | collective-permute-start | bytes 2580488 | tf_op jit(solution)/shard_map/ppermute | solution.py:84
  623.6 28.3 %collective-permute-start.47 = (bf16[4,96,768]{2,1,0:T(8,128)(2,1)}, bf16[4,96,768]{2,1,0:T(8,128)(2,1)}, u32[]{:S(2)}, u32[]{:S(2)}) collective-permute-start(bf16[4,96,768]{2,1,0:T(8,128)(2,1)} %dynamic-slice_bitcast_fusion.9), channel_id=1, source_target_pairs={{0,4},{4,0},{8,12},{12,8},{16,20},{20,16},{24,28},{28,24},{1,5},{5... | collective-permute-start | bytes 1769480 | tf_op jit(solution)/shard_map/ppermute | solution.py:95
  657.4 28.9 %collective-permute-start.63 = (bf16[2,96,2240]{2,1,0:T(8,128)(2,1)S(1)}, bf16[2,96,2240]{2,1,0:T(8,128)(2,1)S(1)}, u32[]{:S(2)}, u32[]{:S(2)}) collective-permute-start(bf16[2,96,2240]{2,1,0:T(8,128)(2,1)S(1)} %copy-done.51), channel_id=1, source_target_pairs={{0,8},{4,12},{8,16},{12,20},{1,9},{5,13},{9,17},{13,21},{2,10},{6,... | collective-permute-start | bytes 2580488 | tf_op jit(solution)/shard_map/ppermute | solution.py:84
  662.8 22.2 %collective-permute-start.49 = (bf16[96,768]{1,0:T(8,128)(2,1)S(1)}, bf16[96,768]{1,0:T(8,128)(2,1)S(1)}, u32[]{:S(2)}, u32[]{:S(2)}) collective-permute-start(bf16[96,768]{1,0:T(8,128)(2,1)S(1)} %fusion.104), channel_id=1, source_target_pairs={{0,8},{4,12},{8,16},{12,20},{1,9},{5,13},{9,17},{13,21},{2,10},{6,... | collective-permute-start | bytes 442376 | tf_op jit(solution)/shard_map/ppermute | solution.py:84
  666.6 47.3 %collective-permute-start.56 = (bf16[2,96,2240]{2,1,0:T(8,128)(2,1)S(1)}, bf16[2,96,2240]{2,1,0:T(8,128)(2,1)S(1)}, u32[]{:S(2)}, u32[]{:S(2)}) collective-permute-start(bf16[2,96,2240]{2,1,0:T(8,128)(2,1)S(1)} %copy-done.50), channel_id=1, source_target_pairs={{0,8},{4,12},{8,16},{12,20},{1,9},{5,13},{9,17},{13,21},{2,10},{6,... | collective-permute-start | bytes 2580488 | tf_op jit(solution)/shard_map/ppermute | solution.py:84
  685.0 52.5 %collective-permute-start.33 = (bf16[1024,640]{0,1:T(8,128)(2,1)S(1)}, bf16[1024,640]{0,1:T(8,128)(2,1)S(1)}, u32[]{:S(2)}, u32[]{:S(2)}) collective-permute-start(bf16[1024,640]{0,1:T(8,128)(2,1)S(1)} %pad_maximum_fusion.12), channel_id=1, source_target_pairs={{0,1},{1,0},{2,3},{3,2},{4,5},{5,4},{6,7},{7,6},{8,9},{9,8},{10,11... | collective-permute-start | bytes 3932168 | tf_op jit(solution)/shard_map/ppermute | solution.py:23
  685.6 47.6 %collective-permute-start.74 = (bf16[280,1536]{1,0:T(8,128)(2,1)S(1)}, bf16[280,1536]{1,0:T(8,128)(2,1)S(1)}, u32[]{:S(2)}, u32[]{:S(2)}) collective-permute-start(bf16[280,1536]{1,0:T(8,128)(2,1)S(1)} %get-tuple-element.40), channel_id=1, source_target_pairs={{16,8},{20,12},{24,16},{28,20},{17,9},{21,13},{25,17},{29,21},{18,... | collective-permute-start | bytes 2580488 | tf_op jit(solution)/shard_map/ppermute | solution.py:85
  688.7 45.5 %collective-permute-start.66 = (bf16[2,96,2240]{2,1,0:T(8,128)(2,1)S(1)}, bf16[2,96,2240]{2,1,0:T(8,128)(2,1)S(1)}, u32[]{:S(2)}, u32[]{:S(2)}) collective-permute-start(bf16[2,96,2240]{2,1,0:T(8,128)(2,1)S(1)} %get-tuple-element.36), channel_id=1, source_target_pairs={{16,8},{20,12},{24,16},{28,20},{17,9},{21,13},{25,17},{29,21},{18,... | collective-permute-start | bytes 2580488 | tf_op jit(solution)/shard_map/ppermute | solution.py:85
  689.5 27.3 %collective-permute-start.50 = (bf16[96,768]{1,0:T(8,128)(2,1)S(1)}, bf16[96,768]{1,0:T(8,128)(2,1)S(1)}, u32[]{:S(2)}, u32[]{:S(2)}) collective-permute-start(bf16[96,768]{1,0:T(8,128)(2,1)S(1)} %get-tuple-element.71), channel_id=1, source_target_pairs={{0,8},{4,12},{8,16},{12,20},{16,24},{20,28},{1,9},{5,13},{9,17},{1... | collective-permute-start | bytes 442376 | tf_op jit(solution)/shard_map/ppermute | solution.py:84
  716.8 39.3 %collective-permute-start.72 = (bf16[280,1536]{1,0:T(8,128)(2,1)S(1)}, bf16[280,1536]{1,0:T(8,128)(2,1)S(1)}, u32[]{:S(2)}, u32[]{:S(2)}) collective-permute-start(bf16[280,1536]{1,0:T(8,128)(2,1)S(1)} %get-tuple-element.39), channel_id=1, source_target_pairs={{0,8},{4,12},{8,16},{12,20},{16,24},{20,28},{1,9},{5,13},{9,17},{1... | collective-permute-start | bytes 2580488 | tf_op jit(solution)/shard_map/ppermute | solution.py:84
  722.0 36.7 %collective-permute-start.64 = (bf16[2,96,2240]{2,1,0:T(8,128)(2,1)S(1)}, bf16[2,96,2240]{2,1,0:T(8,128)(2,1)S(1)}, u32[]{:S(2)}, u32[]{:S(2)}) collective-permute-start(bf16[2,96,2240]{2,1,0:T(8,128)(2,1)S(1)} %get-tuple-element.35), channel_id=1, source_target_pairs={{0,8},{4,12},{8,16},{12,20},{16,24},{20,28},{1,9},{5,13},{9,17},{1... | collective-permute-start | bytes 2580488 | tf_op jit(solution)/shard_map/ppermute | solution.py:84
  734.2 50.4 %collective-permute-start.57 = (bf16[2,96,2240]{2,1,0:T(8,128)(2,1)S(1)}, bf16[2,96,2240]{2,1,0:T(8,128)(2,1)S(1)}, u32[]{:S(2)}, u32[]{:S(2)}) collective-permute-start(bf16[2,96,2240]{2,1,0:T(8,128)(2,1)S(1)} %get-tuple-element.31), channel_id=1, source_target_pairs={{0,8},{4,12},{8,16},{12,20},{16,24},{20,28},{1,9},{5,13},{9,17},{1... | collective-permute-start | bytes 2580488 | tf_op jit(solution)/shard_map/ppermute | solution.py:84
  737.5 19.9 %collective-permute-start.75 = (bf16[280,1536]{1,0:T(8,128)(2,1)S(1)}, bf16[280,1536]{1,0:T(8,128)(2,1)S(1)}, u32[]{:S(2)}, u32[]{:S(2)}) collective-permute-start(bf16[280,1536]{1,0:T(8,128)(2,1)S(1)} %fusion.52), channel_id=1, source_target_pairs={{8,0},{12,4},{16,8},{20,12},{24,16},{28,20},{9,1},{13,5},{17,9},{2... | collective-permute-start | bytes 2580488 | tf_op jit(solution)/shard_map/ppermute | solution.py:85
  741.1 12.7 %collective-permute-start.40 = (bf16[4,96,1024]{2,1,0:T(8,128)(2,1)S(1)}, bf16[4,96,1024]{2,1,0:T(8,128)(2,1)S(1)}, u32[]{:S(2)}, u32[]{:S(2)}) collective-permute-start(bf16[4,96,1024]{2,1,0:T(8,128)(2,1)S(1)} %dynamic-slice_bitcast_fusion.8), channel_id=1, source_target_pairs={{0,4},{4,0},{8,12},{12,8},{16,20},{20,16},{24,28},{28,24},{1,5},{5... | collective-permute-start | bytes 2359304 | tf_op jit(solution)/shard_map/ppermute | solution.py:95
  753.8 29.1 %collective-permute-start.67 = (bf16[2,96,2240]{2,1,0:T(8,128)(2,1)S(1)}, bf16[2,96,2240]{2,1,0:T(8,128)(2,1)S(1)}, u32[]{:S(2)}, u32[]{:S(2)}) collective-permute-start(bf16[2,96,2240]{2,1,0:T(8,128)(2,1)S(1)} %fusion.42), channel_id=1, source_target_pairs={{8,0},{12,4},{16,8},{20,12},{24,16},{28,20},{9,1},{13,5},{17,9},{2... | collective-permute-start | bytes 2580488 | tf_op jit(solution)/shard_map/ppermute | solution.py:85
  756.1 36.3 %collective-permute-start.60 = (bf16[2,96,2240]{2,1,0:T(8,128)(2,1)S(1)}, bf16[2,96,2240]{2,1,0:T(8,128)(2,1)S(1)}, u32[]{:S(2)}, u32[]{:S(2)}) collective-permute-start(bf16[2,96,2240]{2,1,0:T(8,128)(2,1)S(1)} %fusion.47), channel_id=1, source_target_pairs={{8,0},{12,4},{16,8},{20,12},{24,16},{28,20},{9,1},{13,5},{17,9},{2... | collective-permute-start | bytes 2580488 | tf_op jit(solution)/shard_map/ppermute | solution.py:85
  757.4 63.4 %collective-permute-start.34 = (f32[512,768]{1,0:T(8,128)}, f32[512,768]{1,0:T(8,128)}, u32[]{:S(2)}, u32[]{:S(2)}) collective-permute-start(f32[512,768]{1,0:T(8,128)} %constant_dynamic-slice_fusion), channel_id=1, source_target_pairs={{0,2},{2,0},{1,3},{3,1},{4,6},{6,4},{5,7},{7,5},{8,10},{10,8},{9,1... | collective-permute-start | bytes 4718600 | tf_op jit(solution)/shard_map/ppermute | solution.py:23
  758.7 34.1 %collective-permute-start.41 = (bf16[96,1024]{1,0:T(8,128)(2,1)S(1)}, bf16[96,1024]{1,0:T(8,128)(2,1)S(1)}, u32[]{:S(2)}, u32[]{:S(2)}) collective-permute-start(bf16[96,1024]{1,0:T(8,128)(2,1)S(1)} %get-tuple-element.69), channel_id=1, source_target_pairs={{0,8},{4,12},{1,9},{5,13},{2,10},{6,14},{3,11},{7,15}} | collective-permute-start | bytes 589832 | tf_op jit(solution)/shard_map/ppermute | solution.py:84
  782.9 28.7 %collective-permute-start.44 = (bf16[96,1024]{1,0:T(8,128)(2,1)}, bf16[96,1024]{1,0:T(8,128)(2,1)}, u32[]{:S(2)}, u32[]{:S(2)}) collective-permute-start(bf16[96,1024]{1,0:T(8,128)(2,1)} %get-tuple-element.70), channel_id=1, source_target_pairs={{24,16},{28,20},{25,17},{29,21},{26,18},{30,22},{27,19},{31,23}} | collective-permute-start | bytes 589832 | tf_op jit(solution)/shard_map/ppermute | solution.py:85
  784.6 33.5 %collective-permute-start.76 = (bf16[280,768]{1,0:T(8,128)(2,1)}, bf16[280,768]{1,0:T(8,128)(2,1)}, u32[]{:S(2)}, u32[]{:S(2)}) collective-permute-start(bf16[280,768]{1,0:T(8,128)(2,1)} %slice.258), channel_id=1, source_target_pairs={{0,1},{1,0},{2,3},{3,2},{4,5},{5,4},{6,7},{7,6},{8,9},{9,8},{10,11... | collective-permute-start | bytes 1290248 | tf_op jit(solution)/shard_map/ppermute | solution.py:23
  793.6 18.0 %collective-permute-start.42 = (bf16[96,1024]{1,0:T(8,128)(2,1)}, bf16[96,1024]{1,0:T(8,128)(2,1)}, u32[]{:S(2)}, u32[]{:S(2)}) collective-permute-start(bf16[96,1024]{1,0:T(8,128)(2,1)} %fusion.99), channel_id=1, source_target_pairs={{0,8},{4,12},{8,16},{12,20},{1,9},{5,13},{9,17},{13,21},{2,10},{6,... | collective-permute-start | bytes 589832 | tf_op jit(solution)/shard_map/ppermute | solution.py:84
  807.4 36.4 %collective-permute-start.68 = (bf16[96,2,2240]{2,0,1:T(8,128)(2,1)}, bf16[96,2,2240]{2,0,1:T(8,128)(2,1)S(1)}, u32[]{:S(2)}, u32[]{:S(2)}) collective-permute-start(bf16[96,2,2240]{2,0,1:T(8,128)(2,1)} %fusion.90), channel_id=1, source_target_pairs={{0,1},{1,0},{2,3},{3,2},{4,5},{5,4},{6,7},{7,6},{8,9},{9,8},{10,11... | collective-permute-start | bytes 2580488 | tf_op jit(solution)/shard_map/ppermute | solution.py:23
  813.6 12.3 %collective-permute-start.43 = (bf16[96,1024]{1,0:T(8,128)(2,1)S(1)}, bf16[96,1024]{1,0:T(8,128)(2,1)S(1)}, u32[]{:S(2)}, u32[]{:S(2)}) collective-permute-start(bf16[96,1024]{1,0:T(8,128)(2,1)S(1)} %get-tuple-element.67), channel_id=1, source_target_pairs={{0,8},{4,12},{8,16},{12,20},{16,24},{20,28},{1,9},{5,13},{9,17},{1... | collective-permute-start | bytes 589832 | tf_op jit(solution)/shard_map/ppermute | solution.py:84
  824.6 11.4 %collective-permute-start.35 = (f32[512]{0:T(512)S(1)}, f32[512]{0:T(512)S(1)}, u32[]{:S(2)}, u32[]{:S(2)}) collective-permute-start(f32[512]{0:T(512)S(1)} %get-tuple-element.10), channel_id=1, source_target_pairs={{0,1},{1,0},{2,3},{3,2},{4,5},{5,4},{6,7},{7,6},{8,9},{9,8},{10,11... | collective-permute-start | bytes 6152 | tf_op jit(solution)/shard_map/ppermute | solution.py:23
  (100 other events, 1554.9 us)

commit v2 on v1

v2 whole, which is shorter than its diff:
```python
import functools
import jax
import jax.numpy as jnp
from jax import lax
from jax.experimental import pallas as pl
from jax.experimental.pallas import tpu as pltpu
from jax.sharding import PartitionSpec as P

HEADS = 12
KV_HEADS = 2
HEAD_DIM = 128
EPSILON = 1e-06
ROPE_BASE = 1000000.0
MASKED = -1e30
F32 = jnp.float32
BF16 = jnp.bfloat16
VMEM_LIMIT = 60 * 1024 * 1024


def dot(left, right, left_dim, right_dim):
    return lax.dot_general(
        left, right, (((left_dim,), (right_dim,)), ((), ())), preferred_element_type=F32
    )


def params(*semantics):
    return pltpu.CompilerParams(
        dimension_semantics=semantics or None, vmem_limit_bytes=VMEM_LIMIT
    )


def cost(flops, moved):
    return pl.CostEstimate(flops=1, bytes_accessed=1, transcendentals=0)


def whole(shape):
    return pl.BlockSpec(shape, lambda *_: (0,) * len(shape))


ROW, COL, LOW, HIGH = range(4)
BITS = 2


def with_bit(index, place, value):
    return ((index >> place) << (place + 1)) | (value << place) | (index & ((1 << place) - 1))


def ordered(table, parts, columns=slice(None)):
    if len(parts) == 1:
        return parts[0][:, columns]
    first, second, first_other, second_other = [part[:, columns] for part in parts]
    high, low = table[HIGH] == 0, table[LOW] == 0
    return jnp.concatenate(
        [
            jnp.where(high, first, first_other),
            jnp.where(high, first_other, first),
            jnp.where(low, second, second_other),
            jnp.where(low, second_other, second),
        ],
        axis=0,
    )


def halves_of(segment, padded):
    first = padded // 2
    return ((0, first), (first, segment - first))


def units_kernel(count, segment, padded, halves, table, block_ref, *out_refs):
    rows = block_ref.shape[0]

    def write(side):
        for out_ref, half in zip(out_refs, halves):
            begin, width = halves_of(segment, padded)[half]
            parts = []
            for kind in range(2):
                for k in range(count):
                    start = ((kind * count + k) * 2 + side) * segment + begin
                    parts.append(block_ref[:, start : start + width])
                    if width < padded // 2:
                        parts.append(jnp.zeros((rows, padded // 2 - width), block_ref.dtype))
            out_ref[0] = jnp.concatenate(parts, axis=1)

    @pl.when(table[0] == 0)
    def _():
        write(0)

    @pl.when(table[0] != 0)
    def _():
        write(1)


def unit_columns(block, side, slots, count, rows, padded, halves=(0, 1)):
    columns = block.shape[1]
    segment = columns // (4 * count)
    units = padded * count
    steps = slots.shape[0]
    table = jnp.concatenate([side.reshape(1), slots]).astype(jnp.int32)
    return pl.pallas_call(
        functools.partial(units_kernel, count, segment, padded, halves),
        grid_spec=pltpu.PrefetchScalarGridSpec(
            num_scalar_prefetch=1,
            grid=(steps,),
            in_specs=[pl.BlockSpec((rows, columns), lambda i, t: (t[1 + i], 0))],
            out_specs=[pl.BlockSpec((1, rows, units), lambda i, t: (i, 0, 0))] * len(halves),
        ),
        out_shape=[jax.ShapeDtypeStruct((steps, rows, units), block.dtype)] * len(halves),
        compiler_params=params("arbitrary"),
        cost_estimate=cost(0, 4 * steps * rows * units * 2),
        name="unit_columns",
    )(table, block)


def unit_rows_kernel(segment, table, block_ref, out_ref):
    half, width = out_ref.shape[1], block_ref.shape[3]
    rows = block_ref[0, 0].astype(F32)
    out_ref[0, :, :width] = rows[:half].astype(out_ref.dtype)
    rest = jnp.concatenate([rows[half:], jnp.zeros((2 * half - segment, width), F32)], axis=0)
    out_ref[0, :, width:] = rest.astype(out_ref.dtype)


def unit_rows(block, side, ranks, count, padded):
    rows, width = block.shape
    segment = rows // (2 * count)
    steps = ranks.shape[0]
    table = jnp.concatenate([side.reshape(1), ranks]).astype(jnp.int32)
    return pl.pallas_call(
        functools.partial(unit_rows_kernel, segment),
        grid_spec=pltpu.PrefetchScalarGridSpec(
            num_scalar_prefetch=1,
            grid=(steps,),
            in_specs=[pl.BlockSpec((1, 1, segment, width), lambda i, t: (t[1 + i], t[0], 0, 0))],
            out_specs=pl.BlockSpec((1, padded // 2, 2 * width), lambda i, t: (i, 0, 0)),
        ),
        out_shape=jax.ShapeDtypeStruct((steps, padded // 2, 2 * width), block.dtype),
        compiler_params=params("arbitrary"),
        cost_estimate=cost(0, 4 * steps * segment * width),
        name="unit_rows",
    )(table, block.reshape(count, 2, segment, width))


def spread_kernel(count, segment, padded, table, own0_ref, own1_ref, far0_ref, far1_ref, out_ref):
    def write(sides):
        pieces = []
        half = padded // 2
        for kind in range(2):
            for k in range(count):
                for side in sides:
                    for ref, (_, width) in zip(side, halves_of(segment, padded)):
                        start = (kind * count + k) * half
                        pieces.append(ref[:, start : start + width].astype(F32))
        out_ref[...] = jnp.concatenate(pieces, axis=1)

    own, far = (own0_ref, own1_ref), (far0_ref, far1_ref)

    @pl.when(table[COL] == 0)
    def _():
        write((own, far))

    @pl.when(table[COL] != 0)
    def _():
        write((far, own))


def spread_columns(table, own, far, count, segment, padded):
    rows, units = own[0].shape
    step = rows // 3 if rows % 24 == 0 else rows
    part = pl.BlockSpec((step, units), lambda i, t: (i, 0))
    columns = 4 * count * segment
    return pl.pallas_call(
        functools.partial(spread_kernel, count, segment, padded),
        grid_spec=pltpu.PrefetchScalarGridSpec(
            num_scalar_prefetch=1,
            grid=(rows // step,),
            in_specs=[part] * 4,
            out_specs=pl.BlockSpec((step, columns), lambda i, t: (i, 0)),
        ),
        out_shape=jax.ShapeDtypeStruct((rows, columns), F32),
        compiler_params=params("arbitrary"),
        cost_estimate=cost(0, 28 * rows * units),
        name="spread_columns",
    )(table, *own, *far)


def project_kernel(
    width, table, own_ref, near_ref, far_ref, far_near_ref, gain_ref, weight_ref, part0_ref, part1_ref, part2_ref,
    part3_ref, bias_ref, cosine_ref, sine_ref, stream_ref, normed_ref, scale_ref, query_ref, key_ref, value_ref,
):
    half = pl.program_id(0) * 2 // pl.num_programs(0)
    mine = half == table[ROW]
    left = jnp.where(mine, own_ref[...], near_ref[...]).astype(F32)
    right = jnp.where(mine, far_ref[...], far_near_ref[...]).astype(F32)
    squares = jnp.sum(left * left, axis=1, keepdims=True) + jnp.sum(
        right * right, axis=1, keepdims=True
    )
    scale = lax.rsqrt(squares / (2 * width) + EPSILON)
    left_normed = (left * scale * gain_ref[:, :width]).astype(BF16)
    right_normed = (right * scale * gain_ref[:, width:]).astype(BF16)
    stream_ref[:, :width] = left.astype(BF16)
    stream_ref[:, width:] = right.astype(BF16)
    normed_ref[...] = left_normed
    scale_ref[...] = jnp.broadcast_to(scale, scale_ref.shape)
    far_weight = ordered(table, (part0_ref, part1_ref, part2_ref, part3_ref))
    projected = (
        dot(left_normed, weight_ref[...], 1, 0) + dot(right_normed, far_weight, 1, 0) + bias_ref[...]
    )
    cosine, sine = cosine_ref[...], sine_ref[...]

    def rotated(values):
        return (values * cosine + pltpu.roll(values, HEAD_DIM // 2, 1) * sine).astype(BF16)

    query_width = query_ref.shape[1]
    for start in range(0, query_width, HEAD_DIM):
        query_ref[:, start : start + HEAD_DIM] = rotated(projected[:, start : start + HEAD_DIM])
    key_ref[...] = rotated(projected[:, query_width : query_width + HEAD_DIM])
    value_ref[...] = projected[:, query_width + HEAD_DIM :].astype(BF16)


def project(table, own, near, far, far_near, gain, weight, far_parts, bias, cosine, sine):
    rows, width = own.shape
    seq_len = 2 * rows
    block = min(256, rows)
    per_half = rows // block
    out_width = weight.shape[1]
    query_width = out_width - 2 * HEAD_DIM
    part = pl.BlockSpec((block, width), lambda i, t: (i % per_half, 0))

    def tokens(columns):
        return pl.BlockSpec((block, columns), lambda i, t: (i, 0))

    return pl.pallas_call(
        functools.partial(project_kernel, width),
        grid_spec=pltpu.PrefetchScalarGridSpec(
            num_scalar_prefetch=1,
            grid=(seq_len // block,),
            in_specs=[part, part, part, part, whole((1, 2 * width)), whole(weight.shape)]
            + [whole((piece.shape[0], out_width)) for piece in far_parts]
            + [whole((1, out_width)), tokens(HEAD_DIM), tokens(HEAD_DIM)],
            out_specs=[
                tokens(2 * width), tokens(width), tokens(128),
                tokens(query_width), tokens(HEAD_DIM), tokens(HEAD_DIM),
            ],
        ),
        out_shape=[
            jax.ShapeDtypeStruct((seq_len, 2 * width), BF16),
            jax.ShapeDtypeStruct((seq_len, width), BF16),
            jax.ShapeDtypeStruct((seq_len, 128), F32),
            jax.ShapeDtypeStruct((seq_len, query_width), BF16),
            jax.ShapeDtypeStruct((seq_len, HEAD_DIM), BF16),
            jax.ShapeDtypeStruct((seq_len, HEAD_DIM), BF16),
        ],
        compiler_params=params("arbitrary"),
        cost_estimate=cost(4 * seq_len * width * out_width, 12 * seq_len * width),
        name="project",
    )(table, own, near, far, far_near, gain, weight, *far_parts, bias, cosine, sine)


def join_kernel(width, table, own_ref, near_ref, far_ref, far_near_ref, out_ref):
    mine = pl.program_id(0) * 2 // pl.num_programs(0) == table[ROW]
    out_ref[:, :width] = jnp.where(mine, own_ref[...], near_ref[...])
    out_ref[:, width:] = jnp.where(mine, far_ref[...], far_near_ref[...])


def join(table, own, near, far, far_near):
    rows, width = own.shape
    block = min(256, rows)
    per_half = rows // block
    part = pl.BlockSpec((block, width), lambda i, t: (i % per_half, 0))
    return pl.pallas_call(
        functools.partial(join_kernel, width),
        grid_spec=pltpu.PrefetchScalarGridSpec(
            num_scalar_prefetch=1,
            grid=(2 * rows // block,),
            in_specs=[part] * 4,
            out_specs=pl.BlockSpec((block, 2 * width), lambda i, t: (i, 0)),
        ),
        out_shape=jax.ShapeDtypeStruct((2 * rows, 2 * width), own.dtype),
        compiler_params=params("arbitrary"),
        cost_estimate=cost(0, 16 * rows * width),
        name="join",
    )(table, own, near, far, far_near)


def block_probs(query, key, seg_col, seg_row, start, stop):
    scores = dot(query, key, 1, 1) * HEAD_DIM ** (-0.5)
    rows = stop - start
    query_index = start + lax.broadcasted_iota(jnp.int32, (rows, stop), 0)
    key_index = lax.broadcasted_iota(jnp.int32, (rows, stop), 1)
    allowed = (key_index <= query_index) & (seg_col == seg_row)
    scores = jnp.where(allowed, scores, MASKED)
    exponent = jnp.exp(scores - jnp.max(scores, axis=1, keepdims=True))
    return exponent / jnp.sum(exponent, axis=1, keepdims=True)


def attend_kernel(block, query_ref, key_ref, value_ref, seg_col_ref, seg_row_ref, out_ref):
    for start in range(0, query_ref.shape[0], block):
        stop = start + block
        probs = block_probs(
            query_ref[start:stop], key_ref[:stop], seg_col_ref[start:stop], seg_row_ref[:, :stop], start, stop
        )
        out_ref[start:stop] = dot(probs.astype(BF16), value_ref[:stop], 1, 0).astype(BF16)


def attend(query, key, value, seg_col, seg_row):
    seq_len, width = query.shape
    head = pl.BlockSpec((seq_len, HEAD_DIM), lambda h: (0, h))
    shared = whole((seq_len, HEAD_DIM))
    return pl.pallas_call(
        functools.partial(attend_kernel, 256),
        grid=(width // HEAD_DIM,),
        in_specs=[head, shared, shared, whole((seq_len, 1)), whole((1, seq_len))],
        out_specs=head,
        out_shape=jax.ShapeDtypeStruct(query.shape, BF16),
        compiler_params=params("arbitrary"),
        cost_estimate=cost(6 * seq_len * seq_len * width, 8 * seq_len * width),
        name="attend",
    )(query, key, value, seg_col, seg_row)


def attend_back_kernel(
    block, width, table, query_ref, key_ref, value_ref, seg_col_ref, seg_row_ref, own_ref, near_ref, weight_ref,
    far_weight_ref, cosine_ref, sine_ref, sent_ref, key_value_ref,
):
    scaling = HEAD_DIM ** (-0.5)
    own_rows = own_ref.shape[0]

    @pl.when(pl.program_id(0) == 0)
    def _():
        key_value_ref[...] = jnp.zeros_like(key_value_ref)

    for start in range(0, query_ref.shape[0], block):
        stop = start + block
        mine = table[ROW] == start // own_rows
        place = slice(start % own_rows, start % own_rows + block)
        d_hidden = jnp.where(mine, own_ref[place], near_ref[place])
        grad = (
            dot(d_hidden[:, :width], weight_ref[...], 1, 1)
            + dot(d_hidden[:, width:], far_weight_ref[...], 1, 1)
        ).astype(BF16)
        query = query_ref[start:stop]
        key, value = key_ref[:stop], value_ref[:stop]
        probs = block_probs(
            query, key, seg_col_ref[start:stop], seg_row_ref[:, :stop], start, stop
        )
        d_probs = dot(grad, value, 1, 1)
        d_scores = probs * (d_probs - jnp.sum(d_probs * probs, axis=1, keepdims=True))
        d_scores = d_scores.astype(BF16)
        d_query = dot(d_scores, key, 1, 0) * scaling
        turned = pltpu.roll(d_query * sine_ref[start:stop], HEAD_DIM // 2, 1)
        sent_ref[start:stop] = (d_query * cosine_ref[start:stop] + turned).astype(BF16)
        key_value_ref[:stop, :HEAD_DIM] += dot(d_scores, query, 0, 0) * scaling
        key_value_ref[:stop, HEAD_DIM:] += dot(probs.astype(BF16), grad, 0, 0)

    @pl.when(pl.program_id(0) == pl.num_programs(0) - 1)
    def _():
        d_key = key_value_ref[:, :HEAD_DIM]
        turned = pltpu.roll(d_key * sine_ref[...], HEAD_DIM // 2, 1)
        key_value_ref[:, :HEAD_DIM] = d_key * cosine_ref[...] + turned


def attend_back(table, query, key, value, seg_col, seg_row, own, near, weight, far_weight, cosine, sine):
    seq_len, width = query.shape
    features = weight.shape[1]
    heads = width // HEAD_DIM
    head = pl.BlockSpec((seq_len, HEAD_DIM), lambda h, t: (0, h))
    rows = pl.BlockSpec((HEAD_DIM, features), lambda h, t: (heads * t[COL] + h, 0))
    shared = whole((seq_len, HEAD_DIM))
    return pl.pallas_call(
        functools.partial(attend_back_kernel, 256, features),
        grid_spec=pltpu.PrefetchScalarGridSpec(
            num_scalar_prefetch=1,
            grid=(heads,),
            in_specs=[
                head, shared, shared, whole((seq_len, 1)), whole((1, seq_len)), whole(own.shape), whole(near.shape),
                rows, rows, shared, shared,
            ],
            out_specs=[head, whole((seq_len, 2 * HEAD_DIM))],
        ),
        out_shape=[
            jax.ShapeDtypeStruct(query.shape, BF16),
            jax.ShapeDtypeStruct((seq_len, 2 * HEAD_DIM), F32),
        ],
        compiler_params=params("arbitrary"),
        cost_estimate=cost(12 * seq_len * seq_len * width, 12 * seq_len * width),
        name="attend_back",
    )(table, query, key, value, seg_col, seg_row, own, near, weight, far_weight, cosine, sine)


def residual_kernel(
    table, stream_ref, own_ref, far_ref, near_ref, near_far_ref, own_w_ref, far_w_ref, near_w_ref, near_far_w_ref,
    gain_ref, hidden_ref, normed_ref, scale_ref, group_ref,
):
    first = table[COL] == 0
    part = own_ref.shape[1]
    group = [jnp.where(first, own_ref[...], far_ref[...]), jnp.where(first, far_ref[...], own_ref[...])]
    other = [jnp.where(first, near_ref[...], near_far_ref[...]), jnp.where(first, near_far_ref[...], near_ref[...])]
    group_ref[:, :part] = group[0]
    group_ref[:, part:] = group[1]
    width = own_w_ref.shape[1]
    halves = []
    for index, (mine, theirs) in enumerate(((own_w_ref, near_w_ref), (far_w_ref, near_far_w_ref))):
        total = stream_ref[:, index * width : (index + 1) * width].astype(F32)
        for place in range(2):
            rows = slice(place * part, (place + 1) * part)
            total = total + dot(group[place], mine[rows], 1, 0)
            total = total + dot(other[place], theirs[rows], 1, 0)
        halves.append(total)
    squares = sum(jnp.sum(total * total, axis=1, keepdims=True) for total in halves)
    scale = lax.rsqrt(squares / (2 * width) + EPSILON)
    scale_ref[...] = jnp.broadcast_to(scale, scale_ref.shape)
    for index, total in enumerate(halves):
        columns = slice(index * width, (index + 1) * width)
        hidden_ref[:, columns] = total
        normed_ref[:, columns] = (total * scale * gain_ref[:, columns]).astype(BF16)


def residual(table, stream, own, far, near, near_far, weights, gain):
    seq_len, width = stream.shape
    part = own.shape[1]
    block = min(256, seq_len)

    def tokens(columns):
        return pl.BlockSpec((block, columns), lambda i, t: (i, 0))

    return pl.pallas_call(
        residual_kernel,
        grid_spec=pltpu.PrefetchScalarGridSpec(
            num_scalar_prefetch=1,
            grid=(seq_len // block,),
            in_specs=[tokens(width)]
            + [tokens(part)] * 4
            + [whole(weights[0].shape)] * 4
            + [whole((1, width))],
            out_specs=[tokens(width), tokens(width), tokens(128), tokens(2 * part)],
        ),
        out_shape=[
            jax.ShapeDtypeStruct((seq_len, width), F32),
            jax.ShapeDtypeStruct((seq_len, width), BF16),
            jax.ShapeDtypeStruct((seq_len, 128), F32),
            jax.ShapeDtypeStruct((seq_len, 2 * part), BF16),
        ],
        compiler_params=params("arbitrary"),
        cost_estimate=cost(2 * seq_len * width * width, 14 * seq_len * width),
        name="residual",
    )(table, stream, own, far, near, near_far, *weights, gain)


def activate_kernel(width, table, normed_ref, own_gate_ref, own_up_ref, *refs):
    (act_ref, gate_factor_ref, up_factor_ref), refs = refs[-3:], refs[:-3]
    gate_parts, up_parts = refs[: len(refs) // 2], refs[len(refs) // 2 :]
    left, right = normed_ref[:, :width], normed_ref[:, width:]
    gate = dot(left, own_gate_ref[...], 1, 0) + dot(right, ordered(table, gate_parts), 1, 0)
    up = dot(left, own_up_ref[...], 1, 0) + dot(right, ordered(table, up_parts), 1, 0)
    sigmoid = jax.nn.sigmoid(gate)
    silu = gate * sigmoid
    act_ref[...] = (silu * up).astype(BF16)
    gate_factor_ref[...] = (up * (sigmoid * (1.0 + gate * (1.0 - sigmoid)))).astype(BF16)
    up_factor_ref[...] = silu.astype(BF16)


def tile_of(units):
    return next(t for t in (384, 256, 128, units) if units % t == 0)


def activate(table, normed, own, far_parts):
    seq_len, width = normed.shape
    units = own.shape[1] // 2
    tile = tile_of(units)
    steps = units // tile

    def gate(rows):
        return pl.BlockSpec((rows, tile), lambda j, t: (0, j))

    def up(rows):
        return pl.BlockSpec((rows, tile), lambda j, t: (0, steps + j))

    rows = far_parts[0].shape[0]
    out = pl.BlockSpec((seq_len, tile), lambda j, t: (0, j))
    return pl.pallas_call(
        functools.partial(activate_kernel, width // 2),
        grid_spec=pltpu.PrefetchScalarGridSpec(
            num_scalar_prefetch=1,
            grid=(steps,),
            in_specs=[whole(normed.shape), gate(width // 2), up(width // 2)]
            + [gate(rows)] * len(far_parts)
            + [up(rows)] * len(far_parts),
            out_specs=[out] * 3,
        ),
        out_shape=[jax.ShapeDtypeStruct((seq_len, units), BF16)] * 3,
        compiler_params=params("arbitrary"),
        cost_estimate=cost(4 * seq_len * width * units, 6 * seq_len * units + 4 * width * units),
        name="activate",
    )(table, normed, own, own, *far_parts, *far_parts)


def activate_back_kernel(tile, width, table, grad_ref, own_ref, *refs):
    part_refs, (gate_factor_ref, up_factor_ref, d_gate_ref, d_up_ref, far_scr) = refs[:4], refs[4:]

    @pl.when(pl.program_id(0) == 0)
    def _():
        far_scr[...] = ordered(table, part_refs)

    far = far_scr[pl.ds(pl.multiple_of(pl.program_id(0) * tile, tile), tile)]
    d_act = dot(grad_ref[:, :width], own_ref[...], 1, 1) + dot(grad_ref[:, width:], far, 1, 1)
    d_gate_ref[...] = (d_act * gate_factor_ref[...].astype(F32)).astype(BF16)
    d_up_ref[...] = (d_act * up_factor_ref[...].astype(F32)).astype(BF16)


def activate_back(table, grad, own, far_parts, half, gate_factor, up_factor):
    seq_len, width = grad.shape
    units = own.shape[0]
    tile = tile_of(units)
    weight = pl.BlockSpec((tile, width // 2), lambda j, t: (j, half))
    out = pl.BlockSpec((seq_len, tile), lambda j, t: (0, j))
    return pl.pallas_call(
        functools.partial(activate_back_kernel, tile, width // 2),
        grid_spec=pltpu.PrefetchScalarGridSpec(
            num_scalar_prefetch=1,
            grid=(units // tile,),
            in_specs=[whole(grad.shape), weight]
            + [pl.BlockSpec((piece.shape[0], width // 2), lambda j, t: (0, half)) for piece in far_parts]
            + [out, out],
            out_specs=[out] * 2,
            scratch_shapes=[pltpu.VMEM((units, width // 2), BF16)],
        ),
        out_shape=[jax.ShapeDtypeStruct((seq_len, units), BF16)] * 2,
        compiler_params=params("arbitrary"),
        cost_estimate=cost(2 * seq_len * width * units, 8 * seq_len * units + 2 * width * units),
        name="activate_back",
    )(table, grad, own, *far_parts, gate_factor, up_factor)


def down_kernel(halves, table, *refs):
    act_refs, own_refs, part_refs = refs[:halves], refs[halves : halves + 1], refs[halves + 1 : -3]
    own_out_ref, other_out_ref, total_scr = refs[-3:]

    def write(weights):
        total_scr[...] = sum(dot(act[...], weight, 1, 0) for act, weight in zip(act_refs, weights))
        rows = own_out_ref.shape[0]
        own_out_ref[...] = total_scr[pl.ds(pl.multiple_of(table[ROW] * rows, rows), rows)]
        other = pl.multiple_of((1 - table[ROW]) * rows, rows)
        other_out_ref[...] = total_scr[pl.ds(other, rows)].astype(BF16)

    def write_halves(weight_refs):
        width = own_out_ref.shape[1]
        write(
            [ordered(table, weight_refs, slice(half * width, (half + 1) * width)) for half in range(halves)]
        )

    @pl.when(pl.program_id(0) == 0)
    def _():
        write_halves(own_refs)

    @pl.when(pl.program_id(0) == 1)
    def _():
        write_halves(part_refs)


def down(table, acts, own, far_parts):
    seq_len, units = acts[0].shape
    features = own.shape[1] // 2
    parts = far_parts
    return pl.pallas_call(
        functools.partial(down_kernel, len(acts)),
        grid_spec=pltpu.PrefetchScalarGridSpec(
            num_scalar_prefetch=1,
            grid=(2,),
            in_specs=[whole(array.shape) for array in (*acts, own, *parts)],
            out_specs=[pl.BlockSpec((seq_len // 2, features), lambda j, t: (0, j))] * 2,
            scratch_shapes=[pltpu.VMEM((seq_len, features), F32)],
        ),
        out_shape=[
            jax.ShapeDtypeStruct((seq_len // 2, 2 * features), F32),
            jax.ShapeDtypeStruct((seq_len // 2, 2 * features), BF16),
        ],
        compiler_params=params("arbitrary"),
        cost_estimate=cost(
            4 * len(acts) * seq_len * units * features, 8 * seq_len * features + 8 * units * (seq_len + features)
        ),
        name="down",
    )(table, *acts, own, *parts)


def split_product(table, left, rights, tile, groups, count, bits):
    seq_len, height = left.shape
    rows = height // (groups * count)
    columns = sum(right.shape[1] for right in rights)
    steps = [right.shape[1] // tile for right in rights]
    starts = [sum(steps[:index]) for index in range(len(rights))]

    def kernel(table, left_ref, *refs):
        right_refs, out_refs, total_scr = refs[: len(rights)], refs[len(rights) : -1], refs[-1]
        step = pl.program_id(0)
        for right_ref, start, length in zip(right_refs, starts, steps):

            @pl.when((step >= start) & (step < start + length))
            def _():
                total_scr[...] = dot(left_ref[...], right_ref[...], 0, 0)

        for group, bit in enumerate(bits):
            side = table[BITS + bit]
            for out_ref, value in ((out_refs[2 * group], 1 - side), (out_refs[2 * group + 1], side)):
                for index in range(count // 2):
                    begin = (group * count + with_bit(index, bit, value)) * rows
                    if rows % 8 == 0:
                        begin = pl.multiple_of(begin, 8)
                    out_ref[index] = total_scr[pl.ds(begin, rows)].astype(BF16)

    def right_spec(start, length):
        return pl.BlockSpec((seq_len, tile), lambda i, t: (0, jnp.clip(i - start, 0, length - 1)))

    return pl.pallas_call(
        kernel,
        grid_spec=pltpu.PrefetchScalarGridSpec(
            num_scalar_prefetch=1,
            grid=(sum(steps),),
            in_specs=[whole(left.shape)]
            + [right_spec(start, length) for start, length in zip(starts, steps)],
            out_specs=[pl.BlockSpec((count // 2, rows, tile), lambda i, t: (0, 0, i))] * (2 * groups),
            scratch_shapes=[pltpu.VMEM((height, tile), F32)],
        ),
        out_shape=[jax.ShapeDtypeStruct((count // 2, rows, columns), BF16)] * (2 * groups),
        compiler_params=params("arbitrary"),
        cost_estimate=cost(
            2 * seq_len * height * columns, 2 * (seq_len * (height + columns) + height * columns)
        ),
        name="split_product",
    )(table, left, *rights)


def relay_kernel(table, kept_sent_ref, arrived_sent_ref, kept_ref, arrived_ref, sent_out_ref, kept_out_ref):
    sent_out_ref[...] = (kept_sent_ref[...].astype(F32) + arrived_sent_ref[...].astype(F32)).astype(BF16)
    kept_out_ref[...] = (kept_ref[...].astype(F32) + arrived_ref[...].astype(F32)).astype(BF16)


def relay(table, kept, arrived, place, bit):
    count, rows, columns = kept.shape

    def block(sent):
        def index(i, t):
            value = t[BITS + bit]
            return (with_bit(i, place, 1 - value if sent else value), 0, 0)

        return pl.BlockSpec((1, rows, columns), index)

    out = pl.BlockSpec((1, rows, columns), lambda i, t: (i, 0, 0))
    return pl.pallas_call(
        relay_kernel,
        grid_spec=pltpu.PrefetchScalarGridSpec(
            num_scalar_prefetch=1,
            grid=(count // 2,),
            in_specs=[block(True), block(True), block(False), block(False)],
            out_specs=[out, out],
        ),
        out_shape=[jax.ShapeDtypeStruct((count // 2, rows, columns), BF16)] * 2,
        compiler_params=params("arbitrary"),
        cost_estimate=cost(0, 6 * count * rows * columns),
        name="relay",
    )(table, kept, arrived, kept, arrived)


def normed_grad_kernel(halves, steps, tile, counts, table, *refs):
    d_refs, own_refs, refs = refs[: 2 * halves], refs[2 * halves : 3 * halves], refs[3 * halves :]
    part_refs = []
    for parts in counts:
        part_refs.append(refs[:parts])
        refs = refs[parts:]
    own_out_ref, other_out_ref, *far_scrs, total_scr = refs
    units = d_refs[0].shape[1]

    @pl.when(pl.program_id(0) == 0)
    def _():
        for half in range(halves):
            far_scrs[half][...] = ordered(table, part_refs[half])

    def write(weights):
        total = None
        for half in range(halves):
            for kind in range(2):
                term = dot(
                    d_refs[2 * half + kind][...], weights[half][:, kind * units : (kind + 1) * units], 1, 1
                )
                total = term if total is None else total + term
        total_scr[...] = total
        rows = own_out_ref.shape[0]
        own_out_ref[...] = total_scr[pl.ds(pl.multiple_of(table[ROW] * rows, rows), rows)]
        other = pl.multiple_of((1 - table[ROW]) * rows, rows)
        other_out_ref[...] = total_scr[pl.ds(other, rows)].astype(BF16)

    @pl.when(pl.program_id(0) < steps)
    def _():
        write(own_refs)

    @pl.when(pl.program_id(0) >= steps)
    def _():
        start = pl.multiple_of((pl.program_id(0) - steps) * tile, tile)
        write([scr.at[pl.ds(start, tile)] for scr in far_scrs])


def normed_grad(table, d_parts, own, far_parts):
    seq_len, units = d_parts[0].shape
    features = own[0].shape[0]
    tile = 256
    steps = features // tile
    halves = len(own)
    parts = [piece for half in far_parts for piece in half]
    own_spec = pl.BlockSpec((tile, 2 * units), lambda j, t: (jnp.minimum(j, steps - 1), 0))
    return pl.pallas_call(
        functools.partial(normed_grad_kernel, halves, steps, tile, [len(half) for half in far_parts]),
        grid_spec=pltpu.PrefetchScalarGridSpec(
            num_scalar_prefetch=1,
            grid=(2 * steps,),
            in_specs=[whole((seq_len, units))] * (2 * halves)
            + [own_spec] * halves
            + [whole(piece.shape) for piece in parts],
            out_specs=[pl.BlockSpec((seq_len // 2, tile), lambda j, t: (0, j))] * 2,
            scratch_shapes=[pltpu.VMEM((features, 2 * units), BF16)] * halves
            + [pltpu.VMEM((seq_len, tile), F32)],
        ),
        out_shape=[
            jax.ShapeDtypeStruct((seq_len // 2, 2 * features), F32),
            jax.ShapeDtypeStruct((seq_len // 2, 2 * features), BF16),
        ],
        compiler_params=params("arbitrary"),
        cost_estimate=cost(
            8 * seq_len * features * units * halves, 8 * units * halves * (seq_len + features)
        ),
        name="normed_grad",
    )(table, *d_parts, *own, *parts)


def chip_sum_kernel(own_ref, near_ref, out_ref, low_ref):
    total = own_ref[...] + near_ref[...].astype(F32)
    out_ref[...] = total
    low_ref[...] = total.astype(BF16)


def chip_sum(own, near):
    rows, width = own.shape
    block = pl.BlockSpec((rows // 4, width), lambda i: (i, 0))
    return pl.pallas_call(
        chip_sum_kernel,
        grid=(4,),
        in_specs=[block, block],
        out_specs=[block, block],
        out_shape=[jax.ShapeDtypeStruct(own.shape, F32), jax.ShapeDtypeStruct(own.shape, BF16)],
        compiler_params=params("arbitrary"),
        cost_estimate=cost(0, 12 * rows * width),
        name="chip_sum",
    )(own, near)


def norm_back_kernel(
    width, table, chip_ref, far_ref, hidden_ref, scale_ref, grad_ref, gain_ref, out_ref, low_ref, gain_grad_ref
):
    @pl.when(pl.program_id(0) == 0)
    def _():
        gain_grad_ref[...] = jnp.zeros_like(gain_grad_ref)

    far = far_ref[...].astype(F32)
    d_left = chip_ref[:, :width] + far[:, width:]
    d_right = chip_ref[:, width:] + far[:, :width]
    left, right = hidden_ref[:, :width], hidden_ref[:, width:]
    scale = scale_ref[:, :1]
    gain_grad_ref[...] += jnp.sum(d_left * left * scale, axis=0, keepdims=True)
    left_weighted, right_weighted = d_left * gain_ref[:, :width], d_right * gain_ref[:, width:]
    inner = jnp.sum(left_weighted * left, axis=1, keepdims=True) + jnp.sum(
        right_weighted * right, axis=1, keepdims=True
    )
    factor = scale * scale * (inner / (2 * width))
    d_left = grad_ref[:, :width].astype(F32) + scale * (left_weighted - left * factor)
    d_right = grad_ref[:, width:].astype(F32) + scale * (right_weighted - right * factor)
    out_ref[...] = d_left
    low_ref[:, :width] = d_left.astype(BF16)
    low_ref[:, width:] = d_right.astype(BF16)


def norm_back(table, chip, far, hidden, scale, grad, gain):
    rows, width = chip.shape
    block = rows // 4

    def own(columns):
        return pl.BlockSpec((block, columns), lambda i, t: (i, 0))

    def tokens(columns):
        return pl.BlockSpec((block, columns), lambda i, t: (4 * t[ROW] + i, 0))

    return pl.pallas_call(
        functools.partial(norm_back_kernel, width // 2),
        grid_spec=pltpu.PrefetchScalarGridSpec(
            num_scalar_prefetch=1,
            grid=(4,),
            in_specs=[own(width), own(width), tokens(width), tokens(128), tokens(width), whole((1, width))],
            out_specs=[own(width // 2), own(width), whole((1, width // 2))],
        ),
        out_shape=[
            jax.ShapeDtypeStruct((rows, width // 2), F32),
            jax.ShapeDtypeStruct((rows, width), BF16),
            jax.ShapeDtypeStruct((1, width // 2), F32),
        ],
        compiler_params=params("arbitrary"),
        cost_estimate=cost(0, 20 * rows * width),
        name="norm_back",
    )(table, chip, far, hidden, scale, grad, gain)


def project_back_kernel(
    count, bit, query_width, table, query_ref, key_value_ref, arrived_ref, normed_ref, weight_ref,
    sent_ref, kept_ref, own_ref, other_ref, bias_ref, d_scr, total_scr,
):
    first = table[COL] == 0
    own, far = query_ref[...], arrived_ref[:, :query_width]
    d_scr[:, :query_width] = jnp.where(first, own, far)
    d_scr[:, query_width : 2 * query_width] = jnp.where(first, far, own)
    d_key_value = key_value_ref[...] + arrived_ref[:, query_width:].astype(F32)
    d_scr[:, 2 * query_width :] = d_key_value.astype(BF16)
    d_projected = d_scr[...]
    bias_ref[...] = jnp.sum(d_projected.astype(F32), axis=0, keepdims=True)
    total_scr[...] = dot(normed_ref[...], d_projected, 0, 0)
    rows = sent_ref.shape[1]
    side = table[BITS + bit]
    for out_ref, value in ((sent_ref, 1 - side), (kept_ref, side)):
        for index in range(count // 2):
            start = with_bit(index, bit, value) * rows
            if rows % 8 == 0:
                start = pl.multiple_of(start, 8)
            out_ref[index] = total_scr[pl.ds(start, rows)].astype(BF16)
    tokens = own_ref.shape[0]
    for out_ref, half in ((own_ref, table[ROW]), (other_ref, 1 - table[ROW])):
        d_half = d_scr[pl.ds(pl.multiple_of(half * tokens, tokens), tokens)]
        out_ref[...] = dot(d_half, weight_ref[...], 1, 1)


def project_back(table, d_query, d_key_value, arrived, normed, weight, count, bit):
    seq_len, query_width = d_query.shape
    width, columns = weight.shape
    rows = width // count
    return pl.pallas_call(
        functools.partial(project_back_kernel, count, bit, query_width),
        grid_spec=pltpu.PrefetchScalarGridSpec(
            num_scalar_prefetch=1,
            grid=(1,),
            in_specs=[
                whole(array.shape) for array in (d_query, d_key_value, arrived, normed, weight)
            ],
            out_specs=[
                whole((count // 2, rows, columns)), whole((count // 2, rows, columns)),
                whole((seq_len // 2, width)), whole((seq_len // 2, width)), whole((1, columns)),
            ],
            scratch_shapes=[pltpu.VMEM((seq_len, columns), BF16), pltpu.VMEM((width, columns), F32)],
        ),
        out_shape=[
            jax.ShapeDtypeStruct((count // 2, rows, columns), BF16),
            jax.ShapeDtypeStruct((count // 2, rows, columns), BF16),
            jax.ShapeDtypeStruct((seq_len // 2, width), F32),
            jax.ShapeDtypeStruct((seq_len // 2, width), F32),
            jax.ShapeDtypeStruct((1, columns), F32),
        ],
        compiler_params=params("arbitrary"),
        cost_estimate=cost(4 * seq_len * width * columns, 8 * seq_len * columns),
        name="project_back",
    )(table, d_query, d_key_value, arrived, normed, weight)


def swap(part, axis_name):
    return lax.ppermute(part, axis_name, [(0, 1), (1, 0)])


def dp_swap(part, bit):
    count = lax.axis_size("dp")
    return lax.ppermute(part, "dp", [(i, i ^ (1 << bit)) for i in range(count)])


def after(value, *earlier):
    return lax.optimization_barrier((value,) + earlier)[0]


def pick(array, index, axis):
    return lax.dynamic_index_in_dim(array, index, axis, keepdims=False)


def in_order(index, own, other, axis):
    first = jnp.where(index == 0, own, other)
    second = jnp.where(index == 0, other, own)
    return jnp.concatenate([first, second], axis=axis)


def quad_slots(rank):
    low, high = rank % 2, rank // 2 % 2
    return jnp.stack([2 * high + low, 4 + 2 * low + high])


class Line:
    def __init__(self):
        self.last = ()

    def step(self, value):
        return after(value, *self.last) if self.last else value

    def mark(self, *values):
        self.last = values


class Quad:
    def __init__(self, part, rank):
        self.part = part
        self.low, self.high = rank % 2, rank // 2 % 2

    def first_round(self, line):
        part = line.step(self.part)
        self.sent = lax.optimization_barrier((part[0], part[1]))
        line.mark(*self.sent)
        self.arriving = dp_swap(self.sent[0], 0), dp_swap(self.sent[1], 1)

    def second_round(self, line):
        arrived = [line.step(value) for value in self.arriving]
        pairs = lax.optimization_barrier(
            (in_order(self.low, self.sent[0], arrived[0], 0), in_order(self.high, self.sent[1], arrived[1], 0))
        )
        line.mark(*pairs)
        self.parts = [*pairs, dp_swap(pairs[0], 1), dp_swap(pairs[1], 0)]
        return self.parts


def laid_out(parts, rank):
    low, high = rank % 2, rank // 2 % 2
    return jnp.concatenate(
        [in_order(high, parts[0], parts[2], 0), in_order(low, parts[1], parts[3], 0)], axis=0
    )


class Scatter:
    def __init__(self, table, sent, kept, order, line):
        self.table, self.kept = table, kept
        bits = lax.axis_size("dp").bit_length() - 1
        self.order = list(order) + [bit for bit in range(bits) if bit not in order]
        self.left = list(range(bits))
        self.pass_on(sent, line)

    def pass_on(self, sent, line):
        bit = self.order.pop(0)
        self.left.remove(bit)
        self.arriving = dp_swap(line.step(sent), bit)

    def relay(self, line):
        bit = self.order[0]
        sent, self.kept = relay(
            self.table, self.kept, line.step(self.arriving), self.left.index(bit), bit
        )
        line.mark(sent)
        self.pass_on(sent, line)

    def finish(self, line):
        while self.order:
            self.relay(line)
        return self.kept[0].astype(F32) + self.arriving[0].astype(F32)


def dp_sum(part):
    for bit in range(lax.axis_size("dp").bit_length() - 1):
        part = part + dp_swap(part, bit)
    return part


def shards(
    block_input,
    segment_ids,
    first_gain,
    qkv_weight,
    qkv_bias,
    output_weight,
    second_gain,
    gate_up_weight,
    down_weight,
    output_grad,
):
    count = lax.axis_size("dp")
    rank = lax.axis_index("dp")
    row = lax.axis_index("row")
    col = lax.axis_index("col")
    qkv_block = qkv_weight[0, 0]
    out_block = output_weight[0, 0]
    gate_up_block = gate_up_weight[0, 0]
    down_block = down_weight[0, 0]
    seq_len = segment_ids.shape[0]
    own_rows, half_width = block_input.shape
    model_width = 2 * half_width
    query_width = HEADS // 4 * HEAD_DIM
    own_units = down_block.shape[0] // 2
    segment = own_units // count
    step = max(16, 128 // count)
    padded = pl.cdiv(segment, 2 * step) * 2 * step
    feature_rows = half_width // count
    slot_rows = half_width // 8
    slots = quad_slots(rank)
    bits = count.bit_length() - 1

    def own_tokens(array):
        return lax.dynamic_slice_in_dim(array, row * own_rows, own_rows, 0)

    def slot_pair(array):
        parts = array.reshape((8, array.shape[0] // 8) + array.shape[1:])
        return jnp.stack([pick(parts, slots[0], 0), pick(parts, slots[1], 0)])

    table = jnp.stack([row, col] + [(rank >> bit) & 1 for bit in range(bits)]).astype(jnp.int32)
    line = Line()
    half_rows = padded // 2
    pair_first, line_first = [0, 1, 2], [1, 2, 0]

    def qkv_columns(side):
        heads = lax.dynamic_slice_in_dim(qkv_block, side * query_width, query_width, 1)
        return jnp.concatenate([heads, qkv_block[:, 2 * query_width :]], axis=1)

    gains = jnp.stack([first_gain, second_gain])
    gains = jnp.concatenate([gains, swap(gains, "col")], axis=1)
    early_send = slot_pair(jnp.concatenate([qkv_columns(1 - col), out_block], axis=1))
    early_quad = Quad(swap(early_send, "col"), rank)
    qkv_own = qkv_columns(col)
    qkv_width = qkv_own.shape[1]
    bias = qkv_bias[0]
    bias_own = jnp.concatenate(
        [lax.dynamic_slice_in_dim(bias, col * query_width, query_width, 0), bias[2 * query_width :]]
    )

    (send,) = unit_columns(
        after(gate_up_block, early_send, gains), 1 - col, slots, count, slot_rows, padded, (0,)
    )
    line.mark(send)

    near = swap(block_input, "row")
    far = swap(line.step(block_input), "col")
    far_near = swap(far, "row")

    position_index = jnp.arange(seq_len, dtype=jnp.int32)
    doc_first = jnp.concatenate([jnp.ones((1,), jnp.bool_), segment_ids[1:] != segment_ids[:-1]])
    positions = position_index - lax.cummax(jnp.where(doc_first, position_index, 0), axis=0)
    frequency = ROPE_BASE ** (-jnp.arange(0, HEAD_DIM, 2, dtype=F32) / HEAD_DIM)
    angles = positions.astype(F32)[:, None] * frequency[None, :]
    cosine, sine = jnp.cos(angles), jnp.sin(angles)
    cosine = jnp.concatenate([cosine, cosine], axis=1)
    sine = jnp.concatenate([-sine, sine], axis=1)
    seg_col, seg_row = segment_ids[:, None], segment_ids[None, :]

    early_quad.first_round(line)
    gate_up_quad = Quad(swap(line.step(send), "col"), rank)
    line.mark(*early_quad.sent, cosine, sine)
    early_far = early_quad.second_round(line)
    gate_up_own = unit_columns(
        line.step(gate_up_block), col, jnp.arange(8), count, slot_rows, padded
    )
    line.mark(*gate_up_own)
    gate_up_own = [part.reshape(half_width, -1) for part in gate_up_own]
    stream, first_normed, first_scale, query, key, value = project(
        table, line.step(block_input), near, far, far_near, gains[:1], qkv_own, early_far,
        bias_own[None], cosine, sine,
    )
    line.mark(query)
    attended = attend(line.step(query), key, value, seg_col, seg_row)
    line.mark(attended)
    attended_far = swap(attended, "col")
    attended_near = swap(attended, "row")

    gate_up_quad.first_round(line)
    out_far = lax.optimization_barrier(
        laid_out([line.step(part)[:, qkv_width:] for part in early_far], rank)
    )
    line.mark(out_far)
    out_near = swap(line.step(out_block), "row")
    out_far_near = swap(out_far, "row")
    share = count // 8
    send_ranks = (slots[:, None] * share + jnp.arange(share)[None, :]).reshape(-1)
    down_send = unit_rows(line.step(down_block), 1 - col, send_ranks, count, padded)
    line.mark(down_send)
    gate_up_far = [gate_up_quad.second_round(line)]
    attended_far = line.step(attended_far)
    line.mark(attended_far)
    attended_far_near = swap(attended_far, "row")
    grad_far = swap(line.step(output_grad), "col")
    down_quad = Quad(
        swap(line.step(down_send).reshape(2, share * half_rows, model_width), "col"), rank
    )
    hidden_one, second_normed, second_scale, attended_group = residual(
        table, line.step(stream), attended, attended_far, attended_near, attended_far_near,
        [out_block, out_far, out_near, out_far_near], gains[1:],
    )
    line.mark(second_normed)
    (send,) = unit_columns(
        line.step(gate_up_block), 1 - col, jnp.arange(8), count, slot_rows, padded, (1,)
    )
    line.mark(send)

    act0, gate_factor0, up_factor0 = activate(
        table, line.step(second_normed), gate_up_own[0], gate_up_far[0]
    )
    line.mark(act0)
    grad_far = line.step(grad_far)
    line.mark(grad_far)
    grad_near = swap(line.step(output_grad), "row")
    grad_far_near = swap(grad_far, "row")
    gate_up_far.append([swap(line.step(send).reshape(half_width, -1), "col")])
    down_quad.first_round(line)
    down_own = unit_rows(line.step(down_block), col, jnp.arange(count), count, padded)
    line.mark(down_own)
    down_own = down_own.reshape(count * half_rows, model_width)
    grad_full = join(table, line.step(output_grad), grad_near, grad_far, grad_far_near)
    line.mark(grad_full)

    def down_terms(act, order):
        sent, kept = split_product(table, line.step(act), [grad_full], 768, 1, count, [order[0]])
        line.mark(sent)
        return sent, kept

    def gate_up_terms(d_gate, d_up, orders):
        bits = [order[0] for order in orders]
        terms = split_product(
            table, line.step(second_normed), [d_gate, d_up], tile_of(d_gate.shape[1]), 2, count, bits
        )
        line.mark(terms[0])
        return terms

    down_far = down_quad.second_round(line)
    sent, kept = down_terms(act0, pair_first)
    down_far = [line.step(part) for part in down_far]
    line.mark(*down_far)
    down_sum0 = Scatter(table, sent, kept, pair_first, line)
    d_gate0, d_up0 = activate_back(
        table, line.step(grad_full), down_own, down_far, 0, gate_factor0, up_factor0
    )
    line.mark(d_gate0)
    own_sent0, own_kept0, far_sent0, far_kept0 = gate_up_terms(d_gate0, d_up0, (pair_first, pair_first))
    act1, gate_factor1, up_factor1 = activate(
        table, line.step(second_normed), gate_up_own[1], gate_up_far[1]
    )
    line.mark(act1)
    down_sum0.relay(line)
    far_sum0 = Scatter(table, far_sent0, far_kept0, pair_first, line)
    sent1, kept1 = down_terms(act1, pair_first)
    d_gate1, d_up1 = activate_back(
        table, line.step(grad_full), down_own, down_far, 1, gate_factor1, up_factor1
    )
    line.mark(d_gate1)
    down_sum0.relay(line)
    own_sent1, own_kept1, far_sent1, far_kept1 = gate_up_terms(d_gate1, d_up1, (line_first, pair_first))
    far_sum0.relay(line)
    own_sum0 = Scatter(table, own_sent0, own_kept0, pair_first, line)
    own_sum1 = Scatter(table, own_sent1, own_kept1, line_first, line)
    d_second_own, d_second_other = normed_grad(
        table, [line.step(d_gate0), d_up0, d_gate1, d_up1], gate_up_own, gate_up_far
    )
    line.mark(d_second_other)
    far_sum0.relay(line)
    d_second_near = swap(line.step(d_second_other), "row")
    mlp_own, mlp_other = down(table, [line.step(act0), act1], down_own, down_far)
    line.mark(mlp_other)
    own_sum0.relay(line)
    down_sum1 = Scatter(table, sent1, kept1, pair_first, line)
    d_second_chip, d_second_low = chip_sum(line.step(d_second_own), d_second_near)
    line.mark(d_second_low)
    d_second_far = swap(d_second_low, "col")
    own_sum1.relay(line)

    d_hidden, d_hidden_low, second_gain_part = norm_back(
        table, line.step(d_second_chip), d_second_far, hidden_one, second_scale, grad_full, gains[1:]
    )
    line.mark(d_hidden_low)
    down_sum1.relay(line)
    far_sum1 = Scatter(table, far_sent1, far_kept1, pair_first, line)
    d_hidden_near = swap(line.step(d_hidden_low), "row")
    own_sum0.relay(line)
    d_hidden_full = in_order(row, d_hidden_low[:, :half_width], d_hidden_near[:, :half_width], 0)
    sent_out, kept_out = split_product(
        table, line.step(attended_group), [d_hidden_full], tile_of(half_width), 1, count, [0]
    )
    line.mark(sent_out)

    d_query, d_key_value = attend_back(
        table, line.step(query), key, value, seg_col, seg_row, d_hidden_low, d_hidden_near,
        out_block, out_far, cosine, sine,
    )
    d_projected_sent = jnp.concatenate([d_query, d_key_value.astype(BF16)], axis=1)
    d_projected_sent = lax.optimization_barrier(d_projected_sent)
    line.mark(d_projected_sent)
    arrived = swap(d_projected_sent, "col")
    down_sum1.relay(line)
    own_sum1.relay(line)
    out_sum = Scatter(table, sent_out, kept_out, pair_first, line)
    far_sum1.relay(line)
    sent, kept, d_first_own, d_first_other, bias_part = project_back(
        table, line.step(d_query), d_key_value, arrived, first_normed, qkv_block, count, 0
    )
    line.mark(sent)
    qkv_sum = Scatter(table, sent, kept, pair_first, line)

    d_first = line.step(d_first_own) + swap(line.step(d_first_other), "row")
    stream_own = block_input.astype(F32)
    first_scale_own = own_tokens(first_scale)[:, :1]
    first_gain_part = jnp.sum(d_first * stream_own * first_scale_own, axis=0)
    weighted = d_first * first_gain
    inner = jnp.sum(weighted * stream_own, axis=1)
    inner = (inner + swap(inner, "col"))[:, None]
    input_grad = d_hidden + first_scale_own * (
        weighted - stream_own * (first_scale_own * first_scale_own) * (inner / model_width)
    )

    mlp_chip = mlp_own + swap(line.step(mlp_other), "row").astype(F32)
    mlp_far = swap(mlp_chip[:, half_width:].astype(BF16), "col").astype(F32)
    hidden_own = own_tokens(hidden_one)[:, :half_width]
    block_output = (hidden_own + (mlp_chip[:, :half_width] + mlp_far)).astype(BF16)

    down_sum0 = down_sum0.finish(line)
    far_sum0 = far_sum0.finish(line)
    own_sum0 = own_sum0.finish(line)
    down_sum0_far = swap(line.step(down_sum0[:, half_width:].astype(BF16)), "col")
    far_sum0 = swap(line.step(far_sum0.astype(BF16)), "col")
    far_sum1.relay(line)
    out_sum.relay(line)
    qkv_sum.relay(line)
    own_sum1 = own_sum1.finish(line)
    down_sum1 = down_sum1.finish(line)
    out_sum.relay(line)
    qkv_sum.relay(line)
    far_sum1 = far_sum1.finish(line)
    out_sum, qkv_sum = out_sum.finish(line), qkv_sum.finish(line)
    down_sum1_far = swap(down_sum1[:, half_width:].astype(BF16), "col")
    far_sum1 = swap(far_sum1.astype(BF16), "col")

    gain_parts = jnp.concatenate([first_gain_part, second_gain_part[0]])
    gain_parts = gain_parts + swap(gain_parts, "row")
    small = dp_sum(jnp.concatenate([gain_parts, bias_part[0]]))
    bias_width = bias.shape[0] // count
    bias_grad = lax.dynamic_slice_in_dim(small[model_width:], rank * bias_width, bias_width, 0)

    widths = [width for _, width in halves_of(segment, padded)]
    own_rows_sum = [
        part[:width, :half_width] for part, width in zip((down_sum0, down_sum1), widths)
    ]
    far_rows_sum = [
        part[:width].astype(F32) for part, width in zip((down_sum0_far, down_sum1_far), widths)
    ]
    down_grad = in_order(
        col, jnp.concatenate(own_rows_sum, axis=0), jnp.concatenate(far_rows_sum, axis=0), 0
    )
    gate_up_grad = spread_columns(
        table, (own_sum0, own_sum1), (far_sum0, far_sum1), count, segment, padded
    )

    return (
        block_output,
        input_grad,
        small[:half_width],
        qkv_sum[None, None],
        bias_grad[None],
        out_sum[None, None],
        small[half_width:model_width],
        gate_up_grad[None, None],
        down_grad[None, None],
    )


def solution(mesh):
    placed = (
        P(("dp", "row"), "col"),
        P("dp"),
        P("col"),
        P("col", "row", None, None),
        P("row", None),
        P("row", "col", None, None),
        P("col"),
        P("col", "row", None, None),
        P("row", "col", None, None),
        P(("dp", "row"), "col"),
    )
    return jax.shard_map(
        shards,
        mesh=mesh,
        in_specs=placed,
        out_specs=(
            P(("dp", "row"), "col"),
            P(("dp", "row"), "col"),
            P("col"),
            P("col", "row", "dp", None),
            P("row", "dp"),
            P("row", "col", "dp", None),
            P("col"),
            P("col", "row", "dp", None),
            P("row", "col", "dp", None),
        ),
        check_vma=False,
    )
```

time: 873 us -> 647 us (0.74)
  Pallas kernels: 0 us -> 321 us
  matrix products: 141 us -> 0 us
  local copies, waits for them, and re-layouts: 154 us -> 30.6 us
  starting transfers between devices: 169 us -> 59 us
  other arithmetic: 136 us -> 40.8 us
  waiting for transfers between devices: 242 us -> 184 us
  between operations: 20.2 us -> 1.84 us
    pallas_call x0 -> x41, Pallas kernels: none -> 321 us  [the longest x5 55.4 us: split_product(): pl.pallas_call(kernel, grid_spec=pltpu.PrefetchScalarGridSpec(num_scalar_...]
    dot_general x19 -> x0, matrix products: 141 us -> none  [the longest x13 123 us: dot(): lax.dot_general(left, right, (((left_dim,), (right_dim,)), ((), ())), pre...]
    ppermute x52 -> x39, starting transfers between devices: 151 us -> 39.3 us  [dp_swap(): return lax.ppermute(part, 'dp', [(i, i ^ 1 << bit) for i in range(count)])]
    ppermute x52 -> x39, waiting for transfers between devices: 195 us -> 107 us  [dp_swap(): return lax.ppermute(part, 'dp', [(i, i ^ 1 << bit) for i in range(count)])]
    convert_element_type x30 -> x4, other arithmetic: 54.1 us -> 5.63 us  [the longest x1 2.65 us: shards(): (hidden_own + (mlp_chip[:, :half_width] + mlp_far)).astype(BF16)]
    ppermute x25 -> x29, waiting for transfers between devices: 46.6 us -> 76.5 us  [swap(): return lax.ppermute(part, axis_name, [(0, 1), (1, 0)])]
    convert_element_type x4 -> x0, local copies, waits for them, and re-layouts: 25.1 us -> none  [the longest x1 9.81 us: shards(): up_terms = dot(second_normed, d_up, 0, 0).astype(BF16)]
    concatenate x7, other arithmetic: 28 us -> 2.92 us  [the longest x1 1.35 us: shards(): cosine = jnp.concatenate([cosine, cosine], axis=1)]
  transfers between devices with their start and end apart: 77 -> 68, of which waited for: 18 -> 22; matrix products, arithmetic and copies ran while one was open for 39% -> 8% of each run, Pallas kernels for 0% -> 49%
where the time goes in v2:
time: 647 us; the launch traced here: 637 us
  Pallas kernels  321 us (50%)
  waiting for transfers between devices  184 us (28%)
  starting transfers between devices  59 us (9%)
  other arithmetic  40.8 us (6%)
  local copies, waits for them, and re-layouts  30.6 us (5%)
    ppermute x39, waiting for transfers between devices, dp_swap(): return lax.ppermute(part, 'dp', [(i, i ^ 1 << bit) for i in range(count)])  107 us
    ppermute x29, waiting for transfers between devices, swap(): return lax.ppermute(part, axis_name, [(0, 1), (1, 0)])  76.5 us
    pallas_call x5, Pallas kernels, split_product(): pl.pallas_call(kernel, grid_spec=pltpu.PrefetchScalarGridSpec(num_scalar_...  55.4 us
    pallas_call x16, Pallas kernels, relay(): pl.pallas_call(relay_kernel, grid_spec=pltpu.PrefetchScalarGridSpec(num_s...  52.4 us
    ppermute x39, starting transfers between devices, dp_swap(): return lax.ppermute(part, 'dp', [(i, i ^ 1 << bit) for i in range(count)])  39.3 us
    pallas_call x2, Pallas kernels, activate(): pl.pallas_call(functools.partial(activate_kernel, width // 2), grid_spec=...  31.3 us
    pallas_call x1, Pallas kernels, normed_grad(): pl.pallas_call(functools.partial(normed_grad_kernel, halves, steps, tile,...  26.6 us
    pallas_call x3, Pallas kernels, unit_columns(): pl.pallas_call(functools.partial(units_kernel, count, segment, padded, ha...  25.7 us
  transfers between devices with their start and end apart: 68, of which 22 were waited for; matrix products, arithmetic and copies ran while one was open for 8% of the time, Pallas kernels for 49%

profile of v2, /device:TPU:0, one launch (start us, length us, event | category | flops | bytes accessed | tf_op | source)
XLA Modules:
  0.0 636.5 jit_solution(14714545736595938998)
XLA Ops:
  2.1 3.0 collective-permute-start.1
  9.6 3.0 fusion.11
  13.4 3.9 unit_columns.3
  21.4 2.8 collective-permute-done
  31.2 9.7 %collective-permute-done.5.far_ref = bf16[512,768]{1,0:T(8,128)(2,1)} collective-permute-done((bf16[512,768]{1,0:T(8,128)(2,1)S(1)}, bf16[512,768]{1,0:T(8,128)(2,1)}, u32[]{:S(2)}, u32[]{:S(2)}) %collective-permute-start.5) | collective-permute-done | bytes 786464 | tf_op jit(solution)/shard_map/ppermute | solution.py:866
  45.7 11.8 %unit_columns.4 = (bf16[8,96,2304]{2,1,0:T(8,128)(2,1)}, bf16[8,96,2304]{2,1,0:T(8,128)(2,1)}) custom-call(s32[9]{0:T(128)} %get-tuple-element.435.table, bf16[768,8960]{1,0:T(8,128)(2,1)} %bitcast.69), custom_call_target="tpu_custom_call" | custom-call | flops 1 | bytes 1 | tf_op jit(solution)/shard_map/unit_columns/pallas_call | solution.py:99
  58.5 8.6 %project.1 = (bf16[1024,1536]{1,0:T(8,128)(2,1)}, bf16[1024,768]{1,0:T(8,128)(2,1)}, f32[1024,128]{1,0:T(8,128)}, bf16[1024,384]{1,0:T(8,128)(2,1)}, bf16[1024,1...) custom-call(s32[5]{0:T(128)} %stack.44.table, bf16[512,768]{1,0:T(8,128)(2,1)} %own_ref, ...), custom_call_target="tpu_custom_call" | custom-call | flops 1 | bytes 1 | tf_op jit(solution)/shard_map/project/pallas_call | solution.py:231
  67.1 9.1 %attend.1.own_ref = bf16[1024,384]{1,0:T(8,128)(2,1)} custom-call(bf16[1024,384]{1,0:T(8,128)(2,1)} %get-tuple-element.328.query_ref, bf16[1024,128]{1,0:T(8,128)(2,1)} %get-tuple-element.217.key_ref, bf16[1024,128]{1,0:T(8,128)(2,1)} %get-tuple-element.218.value_ref, s32[1024,1]{1,0:T(8,128)} %copy.19.seg_col_ref, s32[1,1024]{1,0:T(1,128)} %bitcast.92), custom_call_target="tpu_custom_call" | custom-call | flops 1 | bytes 1 | tf_op jit(solution)/shard_map/attend/pallas_call | solution.py:308
  80.2 2.6 unit_rows.2
  82.9 7.2 %collective-permute-done.12 = bf16[96,2304]{1,0:T(8,128)(2,1)} collective-permute-done((bf16[96,2304]{1,0:T(8,128)(2,1)S(1)}, bf16[96,2304]{1,0:T(8,128)(2,1)}, u32[]{:S(2)}, u32[]{:S(2)}) %collective-permute-start.12) | collective-permute-done | bytes 442400 | tf_op jit(solution)/shard_map/ppermute | solution.py:871
  93.3 6.1 collective-permute-done.9.far_ref
  104.5 13.3 %residual.1 = (f32[1024,1536]{1,0:T(8,128)}, bf16[1024,1536]{1,0:T(8,128)(2,1)}, f32[1024,128]{1,0:T(8,128)}, bf16[1024,768]{1,0:T(8,128)(2,1)}) custom-call(s32[5]{0:T(128)} %stack.44.table, bf16[1024,1536]{1,0:T(8,128)(2,1)} %get-tuple-element.233.stream_ref, bf16[1024,384]{1,0:T(8,128)(2,1)} %attend.1.own_ref, ...), custom_call_target="tpu_custom_call" | custom-call | flops 1 | bytes 1 | tf_op jit(solution)/shard_map/residual/pallas_call | solution.py:425
  117.8 10.1 %unit_columns.5 = bf16[8,96,2304]{2,1,0:T(8,128)(2,1)} custom-call(s32[9]{0:T(128)} %get-tuple-element.434.table, bf16[768,8960]{1,0:T(8,128)(2,1)} %bitcast.70), custom_call_target="tpu_custom_call" | custom-call | flops 1 | bytes 1 | tf_op jit(solution)/shard_map/unit_columns/pallas_call | solution.py:99
  127.9 16.0 %activate.2 = (bf16[1024,1152]{1,0:T(8,128)(2,1)}, bf16[1024,1152]{1,0:T(8,128)(2,1)}, bf16[1024,1152]{1,0:T(8,128)(2,1)}) custom-call(s32[5]{0:T(128)} %stack.44.table, bf16[1024,1536]{1,0:T(8,128)(2,1)} %get-tuple-element.286.normed_ref.left_ref, bf16[768,2304]{1,0:T(8,128)(2,1)} %bitcast.74, bf16[768,2304]{1,0:T(8,128)(2,1)} %bitcast.75, ...), custom_call_target="tpu_custom_call" | custom-call | flops 1 | bytes 1 | tf_op jit(solution)/shard_map/activate/pallas_call | solution.py:479
  150.5 6.9 %unit_rows.3 = bf16[8,144,1536]{2,1,0:T(8,128)(2,1)} custom-call(s32[9]{0:T(128)} %get-tuple-element.435.table, bf16[8,2,280,768]{3,2,1,0:T(8,128)(2,1)} %bitcast.81), custom_call_target="tpu_custom_call" | custom-call | flops 1 | bytes 1 | tf_op jit(solution)/shard_map/unit_rows/pallas_call | solution.py:127
  157.4 5.5 join.1.refs_0_.grad_ref
  168.6 8.6 %split_product.5 = (bf16[4,144,1536]{2,1,0:T(8,128)(2,1)}, bf16[4,144,1536]{2,1,0:T(8,128)(2,1)}) custom-call(s32[5]{0:T(128)} %stack.44.table, bf16[1024,1152]{1,0:T(8,128)(2,1)} %get-tuple-element.297.left_ref.refs_0_, bf16[1024,1536]{1,0:T(8,128)(2,1)} %join.1.refs_0_.grad_ref), custom_call_target="tpu_custom_call" | custom-call | flops 1 | bytes 1 | tf_op jit(solution)/shard_map/split_product/pallas_call | solution.py:612
  177.2 11.2 %collective-permute-done.26.refs_3_.refs_6_ = bf16[288,1536]{1,0:T(8,128)(2,1)} collective-permute-done((bf16[288,1536]{1,0:T(8,128)(2,1)}, bf16[288,1536]{1,0:T(8,128)(2,1)}, u32[]{:S(2)}, u32[]{:S(2)}) %collective-permute-start.26) | collective-permute-done | bytes 884768 | tf_op jit(solution)/shard_map/ppermute | solution.py:871
  190.2 11.0 %activate_back.2 = (bf16[1024,1152]{1,0:T(8,128)(2,1)}, bf16[1024,1152]{1,0:T(8,128)(2,1)}) custom-call(s32[5]{0:T(128)} %stack.44.table, bf16[1024,1536]{1,0:T(8,128)(2,1)} %join.1.refs_0_.grad_ref, bf16[1152,1536]{1,0:T(8,128)(2,1)} %bitcast.71, bf16[288,1536]{1,0:T(8,128)(2,1)} %pad_maximum_fusion.7.refs_0_.refs_3_, ...), custom_call_target="tpu_custom_call" | custom-call | flops 1 | bytes 1 | tf_op jit(solution)/shard_map/activate_back/pallas_call | solution.py:515
  201.2 16.2 %split_product.6 = (bf16[4,96,2304]{2,1,0:T(8,128)(2,1)}, bf16[4,96,2304]{2,1,0:T(8,128)(2,1)}, bf16[4,96,2304]{2,1,0:T(8,128)(2,1)}, bf16[4,96,2304]{2,1,0:T(8,128)(2,1)}) custom-call(s32[5]{0:T(128)} %stack.44.table, bf16[1024,1536]{1,0:T(8,128)(2,1)} %get-tuple-element.286.normed_ref.left_ref, bf16[1024,1152]{1,0:T(8,128)(2,1)} %get-tuple-element.293.refs_0_, ...), custom_call_target="tpu_custom_call" | custom-call | flops 1 | bytes 1 | tf_op jit(solution)/shard_map/split_product/pallas_call | solution.py:612
  217.4 9.1 %collective-permute-done.28.refs_0_.refs_1_.refs_10_ = bf16[768,2304]{1,0:T(8,128)(2,1)S(1)} collective-permute-done((bf16[768,2304]{1,0:T(8,128)(2,1)}, bf16[768,2304]{1,0:T(8,128)(2,1)S(1)}, u32[]{:S(2)}, u32[]{:S(2)}) %collective-permute-start.28) | collective-permute-done | bytes 3538976 | tf_op jit(solution)/shard_map/ppermute | solution.py:866
  228.4 15.3 %activate.3 = (bf16[1024,1152]{1,0:T(8,128)(2,1)}, bf16[1024,1152]{1,0:T(8,128)(2,1)}, bf16[1024,1152]{1,0:T(8,128)(2,1)}) custom-call(s32[5]{0:T(128)} %stack.44.table, bf16[1024,1536]{1,0:T(8,128)(2,1)} %get-tuple-element.286.normed_ref.left_ref, bf16[768,2304]{1,0:T(8,128)(2,1)} %bitcast.77, bf16[768,2304]{1,0:T(8,128)(2,1)} %bitcast.78, ...), custom_call_target="tpu_custom_call" | custom-call | flops 1 | bytes 1 | tf_op jit(solution)/shard_map/activate/pallas_call | solution.py:479
  243.7 3.7 relay.16
  248.8 9.0 %split_product.7 = (bf16[4,144,1536]{2,1,0:T(8,128)(2,1)}, bf16[4,144,1536]{2,1,0:T(8,128)(2,1)}) custom-call(s32[5]{0:T(128)} %stack.44.table, bf16[1024,1152]{1,0:T(8,128)(2,1)} %get-tuple-element.278.left_ref.refs_1_, bf16[1024,1536]{1,0:T(8,128)(2,1)} %join.1.refs_0_.grad_ref), custom_call_target="tpu_custom_call" | custom-call | flops 1 | bytes 1 | tf_op jit(solution)/shard_map/split_product/pallas_call | solution.py:612
  257.8 11.0 %activate_back.3 = (bf16[1024,1152]{1,0:T(8,128)(2,1)}, bf16[1024,1152]{1,0:T(8,128)(2,1)}) custom-call(s32[5]{0:T(128)} %stack.44.table, bf16[1024,1536]{1,0:T(8,128)(2,1)} %join.1.refs_0_.grad_ref, bf16[1152,1536]{1,0:T(8,128)(2,1)} %bitcast.72, bf16[288,1536]{1,0:T(8,128)(2,1)} %pad_maximum_fusion.7.refs_0_.refs_3_, ...), custom_call_target="tpu_custom_call" | custom-call | flops 1 | bytes 1 | tf_op jit(solution)/shard_map/activate_back/pallas_call | solution.py:515
  269.7 3.1 relay.17
  272.8 16.3 %split_product.8 = (bf16[4,96,2304]{2,1,0:T(8,128)(2,1)}, bf16[4,96,2304]{2,1,0:T(8,128)(2,1)}, bf16[4,96,2304]{2,1,0:T(8,128)(2,1)}, bf16[4,96,2304]{2,1,0:T(8,128)(2,1)}) custom-call(s32[5]{0:T(128)} %stack.44.table, bf16[1024,1536]{1,0:T(8,128)(2,1)} %get-tuple-element.286.normed_ref.left_ref, bf16[1024,1152]{1,0:T(8,128)(2,1)} %get-tuple-element.283.refs_0_.refs_2_, ...), custom_call_target="tpu_custom_call" | custom-call | flops 1 | bytes 1 | tf_op jit(solution)/shard_map/split_product/pallas_call | solution.py:612
  290.3 3.7 relay.18
  296.6 26.6 %normed_grad.1 = (f32[512,1536]{1,0:T(8,128)}, bf16[512,1536]{1,0:T(8,128)(2,1)}) custom-call(s32[5]{0:T(128)} %stack.44.table, bf16[1024,1152]{1,0:T(8,128)(2,1)} %get-tuple-element.293.refs_0_, bf16[1024,1152]{1,0:T(8,128)(2,1)} %get-tuple-element.264.refs_1_, bf16[1024,1152]{1,0:T(8,128)(2,1)} %get-tuple-element.283.refs_0_.refs_2_, ...), custom_call_target="tpu_custom_call" | custom-call | flops 1 | bytes 1 | tf_op jit(solution)/shard_map/normed_grad/pallas_call | solution.py:708
  324.2 3.2 relay.19
  327.9 15.6 %down.1 = (f32[512,1536]{1,0:T(8,128)}, bf16[512,1536]{1,0:T(8,128)(2,1)}) custom-call(s32[5]{0:T(128)} %stack.44.table, bf16[1024,1152]{1,0:T(8,128)(2,1)} %get-tuple-element.297.left_ref.refs_0_, bf16[1024,1152]{1,0:T(8,128)(2,1)} %get-tuple-element.278.left_ref.refs_1_, bf16[1152,1536]{1,0:T(8,128)(2,1)} %bitcast.73, ...), custom_call_target="tpu_custom_call" | custom-call | flops 1 | bytes 1 | tf_op jit(solution)/shard_map/down/pallas_call | solution.py:563
  344.7 3.7 relay.20
  349.2 5.0 chip_sum.1
  355.8 12.7 %collective-permute-done.36.arrived_sent_ref.arrived_ref = bf16[4,96,2304]{2,1,0:T(8,128)(2,1)S(1)} collective-permute-done((bf16[4,96,2304]{2,1,0:T(8,128)(2,1)}, bf16[4,96,2304]{2,1,0:T(8,128)(2,1)S(1)}, u32[]{:S(2)}, u32[]{:S(2)}) %collective-permute-start.36) | collective-permute-done | bytes 1769504 | tf_op jit(solution)/shard_map/ppermute | solution.py:871
  369.8 3.7 relay.21
  373.5 17.3 %collective-permute-done.37.far_ref = bf16[512,1536]{1,0:T(8,128)(2,1)} collective-permute-done((bf16[512,1536]{1,0:T(8,128)(2,1)}, bf16[512,1536]{1,0:T(8,128)(2,1)}, u32[]{:S(2)}, u32[]{:S(2)}) %collective-permute-start.37) | collective-permute-done | bytes 1572896 | tf_op jit(solution)/shard_map/ppermute | solution.py:866
  390.8 7.0 %norm_back.1 = (f32[512,768]{1,0:T(8,128)}, bf16[512,1536]{1,0:T(8,128)(2,1)}, f32[1,768]{1,0:T(1,128)}) custom-call(s32[5]{0:T(128)} %stack.44.table, f32[512,1536]{1,0:T(8,128)} %get-tuple-element.318.chip_ref, bf16[512,1536]{1,0:T(8,128)(2,1)} %collective-permute-done.37.far_ref, f32[1024,1536]{1,0:T(8,128)} %get-tuple-element.235.hidden_ref, ...), custom_call_target="tpu_custom_call" | custom-call | flops 1 | bytes 1 | tf_op jit(solution)/shard_map/norm_back/pallas_call | solution.py:788
  399.0 3.9 relay.22
  404.0 2.6 collective-permute-start.64
  408.7 19.0 %collective-permute-done.64 = bf16[1,144,1536]{2,1,0:T(8,128)(2,1)} collective-permute-done((bf16[1,144,1536]{2,1,0:T(8,128)(2,1)S(1)}, bf16[1,144,1536]{2,1,0:T(8,128)(2,1)}, u32[]{:S(2)}, u32[]{:S(2)}) %collective-permute-start.64) | collective-permute-done | bytes 442400 | tf_op jit(solution)/shard_map/ppermute | solution.py:871
  430.4 18.0 %collective-permute-done.33.arrived_sent_ref.arrived_ref = bf16[2,96,2304]{2,1,0:T(8,128)(2,1)} collective-permute-done((bf16[2,96,2304]{2,1,0:T(8,128)(2,1)}, bf16[2,96,2304]{2,1,0:T(8,128)(2,1)}, u32[]{:S(2)}, u32[]{:S(2)}) %collective-permute-start.33) | collective-permute-done | bytes 884768 | tf_op jit(solution)/shard_map/ppermute | solution.py:871
  448.4 3.1 relay.23
  451.5 2.9 collective-permute-start.58
  457.2 5.3 split_product.9
  462.5 19.2 %attend_back.1 = (bf16[1024,384]{1,0:T(8,128)(2,1)}, f32[1024,256]{1,0:T(8,128)}) custom-call(s32[5]{0:T(128)} %stack.44.table, bf16[1024,384]{1,0:T(8,128)(2,1)} %get-tuple-element.328.query_ref, bf16[1024,128]{1,0:T(8,128)(2,1)} %get-tuple-element.217.key_ref, bf16[1024,128]{1,0:T(8,128)(2,1)} %get-tuple-element.218.value_ref, ...), custom_call_target="tpu_custom_call" | custom-call | flops 1 | bytes 1 | tf_op jit(solution)/shard_map/attend_back/pallas_call | solution.py:368
  486.5 3.1 relay.24
  490.5 3.1 relay.25
  494.8 3.9 relay.26
  505.7 9.5 %collective-permute-done.42.arrived_ref = bf16[1024,640]{1,0:T(8,128)(2,1)} collective-permute-done((bf16[1024,640]{1,0:T(8,128)(2,1)}, bf16[1024,640]{1,0:T(8,128)(2,1)}, u32[]{:S(2)}, u32[]{:S(2)}) %collective-permute-start.42) | collective-permute-done | bytes 1310752 | tf_op jit(solution)/shard_map/ppermute | solution.py:866
  515.3 8.5 %project_back.1 = (bf16[4,96,1024]{2,1,0:T(8,128)(2,1)}, bf16[4,96,1024]{2,1,0:T(8,128)(2,1)}, f32[512,768]{1,0:T(8,128)}, f32[512,768]{1,0:T(8,128)}, f32[1,1024]{1,0:T(1,128)}) custom-call(s32[5]{0:T(128)} %stack.44.table, bf16[1024,384]{1,0:T(8,128)(2,1)} %get-tuple-element.344.query_ref, f32[1024,256]{1,0:T(8,128)} %get-tuple-element.337.key_value_ref, ...), custom_call_target="tpu_custom_call" | custom-call | flops 1 | bytes 1 | tf_op jit(solution)/shard_map/project_back/pallas_call | solution.py:838
  524.7 6.4 collective-permute-done.53.arrived_sent_ref.arrived_ref
  531.9 3.2 relay.27
  539.8 2.9 relay.28
  542.7 15.3 %collective-permute-done.62 = bf16[1,96,2304]{2,1,0:T(8,128)(2,1)} collective-permute-done((bf16[1,96,2304]{2,1,0:T(8,128)(2,1)}, bf16[1,96,2304]{2,1,0:T(8,128)(2,1)}, u32[]{:S(2)}, u32[]{:S(2)}) %collective-permute-start.62) | collective-permute-done | bytes 442400 | tf_op jit(solution)/shard_map/ppermute | solution.py:871
  558.0 2.0 fusion.10
  566.4 2.9 relay.29
  570.8 2.5 relay.30
  577.8 4.6 collective-permute-done.63.far1_ref
  582.4 5.9 spread_columns.1
  590.0 2.7 relay.31
  593.5 10.9 %collective-permute-done.56 = bf16[1,96,1024]{2,1,0:T(8,128)(2,1)S(1)} collective-permute-done((bf16[1,96,1024]{2,1,0:T(8,128)(2,1)}, bf16[1,96,1024]{2,1,0:T(8,128)(2,1)S(1)}, u32[]{:S(2)}, u32[]{:S(2)}) %collective-permute-start.56) | collective-permute-done | bytes 196640 | tf_op jit(solution)/shard_map/ppermute | solution.py:871
  610.5 17.1 %collective-permute-done.46 = f32[512]{0:T(512)S(1)} collective-permute-done((f32[512]{0:T(512)S(1)}, f32[512]{0:T(512)S(1)}, u32[]{:S(2)}, u32[]{:S(2)}) %collective-permute-start.46) | collective-permute-done | bytes 2080 | tf_op jit(solution)/shard_map/ppermute | solution.py:866
  629.3 2.9 collective-permute-done.50
  633.4 2.7 fusion.8
  (296 shorter events, 117.8 us)
Async XLA Ops:
  2.1 11.2 %collective-permute-start.1 = (f32[2,768]{1,0:T(2,128)S(1)}, f32[2,768]{1,0:T(2,128)S(1)}, u32[]{:S(2)}, u32[]{:S(2)}) collective-permute-start(f32[2,768]{1,0:T(2,128)S(1)} %pad_maximum_fusion.19), channel_id=1, source_target_pairs={{0,1},{1,0},{2,3},{3,2},{4,5},{5,4},{6,7},{7,6},{8,9},{9,8},{10,11... | collective-permute-start | bytes 18440 | tf_op jit(solution)/shard_map/ppermute | solution.py:866
  5.2 52.2 %collective-permute-start.4 = (bf16[512,768]{1,0:T(8,128)(2,1)}, bf16[512,768]{1,0:T(8,128)(2,1)}, u32[]{:S(2)}, u32[]{:S(2)}) collective-permute-start(bf16[512,768]{1,0:T(8,128)(2,1)} %own_ref), channel_id=1, source_target_pairs={{0,2},{2,0},{1,3},{3,1},{4,6},{6,4},{5,7},{7,5},{8,10},{10,8},{9,1... | collective-permute-start | bytes 2359304 | tf_op jit(solution)/shard_map/ppermute | solution.py:866
  8.7 15.4 %collective-permute-start = (bf16[2,96,1408]{2,1,0:T(8,128)(2,1)}, bf16[2,96,1408]{2,1,0:T(8,128)(2,1)}, u32[]{:S(2)}, u32[]{:S(2)}) collective-permute-start(bf16[2,96,1408]{2,1,0:T(8,128)(2,1)} %pad_maximum_fusion.10), channel_id=1, source_target_pairs={{0,1},{1,0},{2,3},{3,2},{4,5},{5,4},{6,7},{7,6},{8,9},{9,8},{10,11... | collective-permute-start | bytes 1622024 | tf_op jit(solution)/shard_map/ppermute | solution.py:866
  17.2 23.8 %collective-permute-start.5 = (bf16[512,768]{1,0:T(8,128)(2,1)S(1)}, bf16[512,768]{1,0:T(8,128)(2,1)}, u32[]{:S(2)}, u32[]{:S(2)}) collective-permute-start(bf16[512,768]{1,0:T(8,128)(2,1)S(1)} %copy-done.10), channel_id=1, source_target_pairs={{0,1},{1,0},{2,3},{3,2},{4,5},{5,4},{6,7},{7,6},{8,9},{9,8},{10,11... | collective-permute-start | bytes 2359304 | tf_op jit(solution)/shard_map/ppermute | solution.py:866
  25.2 15.8 %collective-permute-start.2 = (bf16[96,1408]{1,0:T(8,128)(2,1)S(1)}, bf16[96,1408]{1,0:T(8,128)(2,1)S(1)}, u32[]{:S(2)}, u32[]{:S(2)}) collective-permute-start(bf16[96,1408]{1,0:T(8,128)(2,1)S(1)} %get-tuple-element.203), channel_id=1, source_target_pairs={{0,4},{4,0},{8,12},{12,8},{16,20},{20,16},{24,28},{28,24},{1,5},{5... | collective-permute-start | bytes 811016 | tf_op jit(solution)/shard_map/ppermute | solution.py:871
  26.8 14.2 %collective-permute-start.3 = (bf16[96,1408]{1,0:T(8,128)(2,1)S(1)}, bf16[96,1408]{1,0:T(8,128)(2,1)S(1)}, u32[]{:S(2)}, u32[]{:S(2)}) collective-permute-start(bf16[96,1408]{1,0:T(8,128)(2,1)S(1)} %get-tuple-element.204), channel_id=1, source_target_pairs={{0,8},{4,12},{8,0},{12,4},{16,24},{20,28},{24,16},{28,20},{1,9},{5... | collective-permute-start | bytes 811016 | tf_op jit(solution)/shard_map/ppermute | solution.py:871
  30.7 45.5 %collective-permute-start.10 = (bf16[2,96,2304]{2,1,0:T(8,128)(2,1)}, bf16[2,96,2304]{2,1,0:T(8,128)(2,1)}, u32[]{:S(2)}, u32[]{:S(2)}) collective-permute-start(bf16[2,96,2304]{2,1,0:T(8,128)(2,1)} %unit_columns.3), channel_id=1, source_target_pairs={{0,1},{1,0},{2,3},{3,2},{4,5},{5,4},{6,7},{7,6},{8,9},{9,8},{10,11... | collective-permute-start | bytes 2654216 | tf_op jit(solution)/shard_map/ppermute | solution.py:866
  41.0 16.5 %collective-permute-start.6 = (bf16[512,768]{1,0:T(8,128)(2,1)}, bf16[512,768]{1,0:T(8,128)(2,1)}, u32[]{:S(2)}, u32[]{:S(2)}) collective-permute-start(bf16[512,768]{1,0:T(8,128)(2,1)} %collective-permute-done.5.far_ref), channel_id=1, source_target_pairs={{0,2},{2,0},{1,3},{3,1},{4,6},{6,4},{5,7},{7,5},{8,10},{10,8},{9,1... | collective-permute-start | bytes 2359304 | tf_op jit(solution)/shard_map/ppermute | solution.py:866
  41.2 16.2 %collective-permute-start.7 = (bf16[192,1408]{1,0:T(8,128)(2,1)S(1)}, bf16[192,1408]{1,0:T(8,128)(2,1)S(1)}, u32[]{:S(2)}, u32[]{:S(2)}) collective-permute-start(bf16[192,1408]{1,0:T(8,128)(2,1)S(1)} %pad_maximum_fusion.11.part0_ref), channel_id=1, source_target_pairs={{0,8},{4,12},{8,0},{12,4},{16,24},{20,28},{24,16},{28,20},{1,9},{5... | collective-permute-start | bytes 1622024 | tf_op jit(solution)/shard_map/ppermute | solution.py:871
  42.9 14.5 %collective-permute-start.8 = (bf16[192,1408]{1,0:T(8,128)(2,1)S(1)}, bf16[192,1408]{1,0:T(8,128)(2,1)S(1)}, u32[]{:S(2)}, u32[]{:S(2)}) collective-permute-start(bf16[192,1408]{1,0:T(8,128)(2,1)S(1)} %pad_maximum_fusion.12.part1_ref), channel_id=1, source_target_pairs={{0,4},{4,0},{8,12},{12,8},{16,20},{20,16},{24,28},{28,24},{1,5},{5... | collective-permute-start | bytes 1622024 | tf_op jit(solution)/shard_map/ppermute | solution.py:871
  77.5 13.7 %collective-permute-start.11 = (bf16[96,2304]{1,0:T(8,128)(2,1)S(1)}, bf16[96,2304]{1,0:T(8,128)(2,1)}, u32[]{:S(2)}, u32[]{:S(2)}) collective-permute-start(bf16[96,2304]{1,0:T(8,128)(2,1)S(1)} %get-tuple-element.221), channel_id=1, source_target_pairs={{0,4},{4,0},{8,12},{12,8},{16,20},{20,16},{24,28},{28,24},{1,5},{5... | collective-permute-start | bytes 1327112 | tf_op jit(solution)/shard_map/ppermute | solution.py:871
  78.7 11.4 %collective-permute-start.12 = (bf16[96,2304]{1,0:T(8,128)(2,1)S(1)}, bf16[96,2304]{1,0:T(8,128)(2,1)}, u32[]{:S(2)}, u32[]{:S(2)}) collective-permute-start(bf16[96,2304]{1,0:T(8,128)(2,1)S(1)} %get-tuple-element.222), channel_id=1, source_target_pairs={{0,8},{4,12},{8,0},{12,4},{16,24},{20,28},{24,16},{28,20},{1,9},{5... | collective-permute-start | bytes 1327112 | tf_op jit(solution)/shard_map/ppermute | solution.py:871
  79.2 21.2 %collective-permute-start.13 = (bf16[1024,384]{1,0:T(8,128)(2,1)}, bf16[1024,384]{1,0:T(8,128)(2,1)}, u32[]{:S(2)}, u32[]{:S(2)}) collective-permute-start(bf16[1024,384]{1,0:T(8,128)(2,1)} %attend.1.own_ref), channel_id=1, source_target_pairs={{0,2},{2,0},{1,3},{3,1},{4,6},{6,4},{5,7},{7,5},{8,10},{10,8},{9,1... | collective-permute-start | bytes 2359304 | tf_op jit(solution)/shard_map/ppermute | solution.py:866
  79.2 20.3 %collective-permute-start.9 = (bf16[1024,384]{1,0:T(8,128)(2,1)}, bf16[1024,384]{1,0:T(8,128)(2,1)}, u32[]{:S(2)}, u32[]{:S(2)}) collective-permute-start(bf16[1024,384]{1,0:T(8,128)(2,1)} %attend.1.own_ref), channel_id=1, source_target_pairs={{0,1},{1,0},{2,3},{3,2},{4,5},{5,4},{6,7},{7,6},{8,9},{9,8},{10,11... | collective-permute-start | bytes 2359304 | tf_op jit(solution)/shard_map/ppermute | solution.py:866
  79.9 21.2 %collective-permute-start.16 = (bf16[768,768]{1,0:T(8,128)(2,1)S(1)}, bf16[768,768]{1,0:T(8,128)(2,1)}, u32[]{:S(2)}, u32[]{:S(2)}) collective-permute-start(bf16[768,768]{1,0:T(8,128)(2,1)S(1)} %pad_maximum_fusion.3.far_w_ref.far_weight_ref), channel_id=1, source_target_pairs={{0,2},{2,0},{1,3},{3,1},{4,6},{6,4},{5,7},{7,5},{8,10},{10,8},{9,1... | collective-permute-start | bytes 3538952 | tf_op jit(solution)/shard_map/ppermute | solution.py:866
  90.1 11.0 %collective-permute-start.15 = (bf16[768,768]{1,0:T(8,128)(2,1)S(1)}, bf16[768,768]{1,0:T(8,128)(2,1)S(1)}, u32[]{:S(2)}, u32[]{:S(2)}) collective-permute-start(bf16[768,768]{1,0:T(8,128)(2,1)S(1)} %bitcast.85), channel_id=1, source_target_pairs={{0,2},{2,0},{1,3},{3,1},{4,6},{6,4},{5,7},{7,5},{8,10},{10,8},{9,1... | collective-permute-start | bytes 3538952 | tf_op jit(solution)/shard_map/ppermute | solution.py:866
  92.4 35.5 %collective-permute-start.17 = (bf16[192,2304]{1,0:T(8,128)(2,1)S(1)}, bf16[192,2304]{1,0:T(8,128)(2,1)}, u32[]{:S(2)}, u32[]{:S(2)}) collective-permute-start(bf16[192,2304]{1,0:T(8,128)(2,1)S(1)} %pad_maximum_fusion.5.refs_0_.refs_4_.refs_6_), channel_id=1, source_target_pairs={{0,8},{4,12},{8,0},{12,4},{16,24},{20,28},{24,16},{28,20},{1,9},{5... | collective-permute-start | bytes 2654216 | tf_op jit(solution)/shard_map/ppermute | solution.py:871
  99.5 28.5 %collective-permute-start.18 = (bf16[192,2304]{1,0:T(8,128)(2,1)S(1)}, bf16[192,2304]{1,0:T(8,128)(2,1)}, u32[]{:S(2)}, u32[]{:S(2)}) collective-permute-start(bf16[192,2304]{1,0:T(8,128)(2,1)S(1)} %pad_maximum_fusion.6.refs_1_.refs_5_.refs_7_), channel_id=1, source_target_pairs={{0,4},{4,0},{8,12},{12,8},{16,20},{20,16},{24,28},{28,24},{1,5},{5... | collective-permute-start | bytes 2654216 | tf_op jit(solution)/shard_map/ppermute | solution.py:871
  100.3 44.2 %collective-permute-start.19 = (bf16[2,144,1536]{2,1,0:T(8,128)(2,1)}, bf16[2,144,1536]{2,1,0:T(8,128)(2,1)}, u32[]{:S(2)}, u32[]{:S(2)}) collective-permute-start(bf16[2,144,1536]{2,1,0:T(8,128)(2,1)} %unit_rows.2), channel_id=1, source_target_pairs={{0,1},{1,0},{2,3},{3,2},{4,5},{5,4},{6,7},{7,6},{8,9},{9,8},{10,11... | collective-permute-start | bytes 2654216 | tf_op jit(solution)/shard_map/ppermute | solution.py:866
  102.1 41.8 %collective-permute-start.20 = (bf16[512,768]{1,0:T(8,128)(2,1)}, bf16[512,768]{1,0:T(8,128)(2,1)}, u32[]{:S(2)}, u32[]{:S(2)}) collective-permute-start(bf16[512,768]{1,0:T(8,128)(2,1)} %own_ref.1), channel_id=1, source_target_pairs={{0,1},{1,0},{2,3},{3,2},{4,5},{5,4},{6,7},{7,6},{8,9},{9,8},{10,11... | collective-permute-start | bytes 2359304 | tf_op jit(solution)/shard_map/ppermute | solution.py:866
  143.9 13.5 %collective-permute-start.22 = (bf16[512,768]{1,0:T(8,128)(2,1)}, bf16[512,768]{1,0:T(8,128)(2,1)}, u32[]{:S(2)}, u32[]{:S(2)}) collective-permute-start(bf16[512,768]{1,0:T(8,128)(2,1)} %collective-permute-done.20.far_ref), channel_id=1, source_target_pairs={{0,2},{2,0},{1,3},{3,1},{4,6},{6,4},{5,7},{7,5},{8,10},{10,8},{9,1... | collective-permute-start | bytes 2359304 | tf_op jit(solution)/shard_map/ppermute | solution.py:866
  144.1 13.3 %collective-permute-start.21 = (bf16[512,768]{1,0:T(8,128)(2,1)}, bf16[512,768]{1,0:T(8,128)(2,1)}, u32[]{:S(2)}, u32[]{:S(2)}) collective-permute-start(bf16[512,768]{1,0:T(8,128)(2,1)} %own_ref.1), channel_id=1, source_target_pairs={{0,2},{2,0},{1,3},{3,1},{4,6},{6,4},{5,7},{7,5},{8,10},{10,8},{9,1... | collective-permute-start | bytes 2359304 | tf_op jit(solution)/shard_map/ppermute | solution.py:866
  146.5 16.5 %collective-permute-start.24 = (bf16[144,1536]{1,0:T(8,128)(2,1)}, bf16[144,1536]{1,0:T(8,128)(2,1)}, u32[]{:S(2)}, u32[]{:S(2)}) collective-permute-start(bf16[144,1536]{1,0:T(8,128)(2,1)} %get-tuple-element.245), channel_id=1, source_target_pairs={{0,8},{4,12},{8,0},{12,4},{16,24},{20,28},{24,16},{28,20},{1,9},{5... | collective-permute-start | bytes 1327112 | tf_op jit(solution)/shard_map/ppermute | solution.py:871
  148.0 78.5 %collective-permute-start.28 = (bf16[768,2304]{1,0:T(8,128)(2,1)}, bf16[768,2304]{1,0:T(8,128)(2,1)S(1)}, u32[]{:S(2)}, u32[]{:S(2)}) collective-permute-start(bf16[768,2304]{1,0:T(8,128)(2,1)} %bitcast.88), channel_id=1, source_target_pairs={{0,1},{1,0},{2,3},{3,2},{4,5},{5,4},{6,7},{7,6},{8,9},{9,8},{10,11... | collective-permute-start | bytes 10616840 | tf_op jit(solution)/shard_map/ppermute | solution.py:866
  149.3 15.9 %collective-permute-start.23 = (bf16[144,1536]{1,0:T(8,128)(2,1)S(1)}, bf16[144,1536]{1,0:T(8,128)(2,1)}, u32[]{:S(2)}, u32[]{:S(2)}) collective-permute-start(bf16[144,1536]{1,0:T(8,128)(2,1)S(1)} %get-tuple-element.244), channel_id=1, source_target_pairs={{0,4},{4,0},{8,12},{12,8},{16,20},{20,16},{24,28},{28,24},{1,5},{5... | collective-permute-start | bytes 1327112 | tf_op jit(solution)/shard_map/ppermute | solution.py:871
  167.3 21.2 %collective-permute-start.26 = (bf16[288,1536]{1,0:T(8,128)(2,1)}, bf16[288,1536]{1,0:T(8,128)(2,1)}, u32[]{:S(2)}, u32[]{:S(2)}) collective-permute-start(bf16[288,1536]{1,0:T(8,128)(2,1)} %pad_maximum_fusion.8.refs_1_.refs_4_), channel_id=1, source_target_pairs={{0,4},{4,0},{8,12},{12,8},{16,20},{20,16},{24,28},{28,24},{1,5},{5... | collective-permute-start | bytes 2654216 | tf_op jit(solution)/shard_map/ppermute | solution.py:871
  168.2 20.9 %collective-permute-start.25 = (bf16[288,1536]{1,0:T(8,128)(2,1)}, bf16[288,1536]{1,0:T(8,128)(2,1)}, u32[]{:S(2)}, u32[]{:S(2)}) collective-permute-start(bf16[288,1536]{1,0:T(8,128)(2,1)} %pad_maximum_fusion.7.refs_0_.refs_3_), channel_id=1, source_target_pairs={{0,8},{4,12},{8,0},{12,4},{16,24},{20,28},{24,16},{28,20},{1,9},{5... | collective-permute-start | bytes 2654216 | tf_op jit(solution)/shard_map/ppermute | solution.py:871
  189.1 54.6 %collective-permute-start.27 = (bf16[4,144,1536]{2,1,0:T(8,128)(2,1)}, bf16[4,144,1536]{2,1,0:T(8,128)(2,1)}, u32[]{:S(2)}, u32[]{:S(2)}) collective-permute-start(bf16[4,144,1536]{2,1,0:T(8,128)(2,1)} %get-tuple-element.268), channel_id=1, source_target_pairs={{0,4},{4,0},{8,12},{12,8},{16,20},{20,16},{24,28},{28,24},{1,5},{5... | collective-permute-start | bytes 5308424 | tf_op jit(solution)/shard_map/ppermute | solution.py:871
  247.4 41.7 %collective-permute-start.29 = (bf16[4,96,2304]{2,1,0:T(8,128)(2,1)}, bf16[4,96,2304]{2,1,0:T(8,128)(2,1)S(1)}, u32[]{:S(2)}, u32[]{:S(2)}) collective-permute-start(bf16[4,96,2304]{2,1,0:T(8,128)(2,1)} %get-tuple-element.275), channel_id=1, source_target_pairs={{0,4},{4,0},{8,12},{12,8},{16,20},{20,16},{24,28},{28,24},{1,5},{5... | collective-permute-start | bytes 5308424 | tf_op jit(solution)/shard_map/ppermute | solution.py:871
  248.3 20.5 %collective-permute-start.30 = (bf16[2,144,1536]{2,1,0:T(8,128)(2,1)}, bf16[2,144,1536]{2,1,0:T(8,128)(2,1)S(1)}, u32[]{:S(2)}, u32[]{:S(2)}) collective-permute-start(bf16[2,144,1536]{2,1,0:T(8,128)(2,1)} %get-tuple-element.277), channel_id=1, source_target_pairs={{0,8},{4,12},{8,0},{12,4},{16,24},{20,28},{24,16},{28,20},{1,9},{5... | collective-permute-start | bytes 2654216 | tf_op jit(solution)/shard_map/ppermute | solution.py:871
  294.0 29.2 %collective-permute-start.31 = (bf16[2,96,2304]{2,1,0:T(8,128)(2,1)}, bf16[2,96,2304]{2,1,0:T(8,128)(2,1)S(1)}, u32[]{:S(2)}, u32[]{:S(2)}) collective-permute-start(bf16[2,96,2304]{2,1,0:T(8,128)(2,1)} %get-tuple-element.292), channel_id=1, source_target_pairs={{0,8},{4,12},{8,0},{12,4},{16,24},{20,28},{24,16},{28,20},{1,9},{5... | collective-permute-start | bytes 2654216 | tf_op jit(solution)/shard_map/ppermute | solution.py:871
  295.5 48.0 %collective-permute-start.32 = (bf16[4,96,2304]{2,1,0:T(8,128)(2,1)}, bf16[4,96,2304]{2,1,0:T(8,128)(2,1)S(1)}, u32[]{:S(2)}, u32[]{:S(2)}) collective-permute-start(bf16[4,96,2304]{2,1,0:T(8,128)(2,1)} %get-tuple-element.302), channel_id=1, source_target_pairs={{0,4},{4,0},{8,12},{12,8},{16,20},{20,16},{24,28},{28,24},{1,5},{5... | collective-permute-start | bytes 5308424 | tf_op jit(solution)/shard_map/ppermute | solution.py:871
  327.3 21.9 %collective-permute-start.35 = (bf16[512,1536]{1,0:T(8,128)(2,1)}, bf16[512,1536]{1,0:T(8,128)(2,1)}, u32[]{:S(2)}, u32[]{:S(2)}) collective-permute-start(bf16[512,1536]{1,0:T(8,128)(2,1)} %get-tuple-element.311), channel_id=1, source_target_pairs={{0,2},{2,0},{1,3},{3,1},{4,6},{6,4},{5,7},{7,5},{8,10},{10,8},{9,1... | collective-permute-start | bytes 4718600 | tf_op jit(solution)/shard_map/ppermute | solution.py:866
  327.3 41.2 %collective-permute-start.36 = (bf16[4,96,2304]{2,1,0:T(8,128)(2,1)}, bf16[4,96,2304]{2,1,0:T(8,128)(2,1)S(1)}, u32[]{:S(2)}, u32[]{:S(2)}) collective-permute-start(bf16[4,96,2304]{2,1,0:T(8,128)(2,1)} %get-tuple-element.314), channel_id=1, source_target_pairs={{0,8},{4,12},{8,0},{12,4},{16,24},{20,28},{24,16},{28,20},{1,9},{5... | collective-permute-start | bytes 5308424 | tf_op jit(solution)/shard_map/ppermute | solution.py:871
  348.4 49.4 %collective-permute-start.34 = (bf16[4,144,1536]{2,1,0:T(8,128)(2,1)}, bf16[4,144,1536]{2,1,0:T(8,128)(2,1)S(1)}, u32[]{:S(2)}, u32[]{:S(2)}) collective-permute-start(bf16[4,144,1536]{2,1,0:T(8,128)(2,1)} %get-tuple-element.308), channel_id=1, source_target_pairs={{0,4},{4,0},{8,12},{12,8},{16,20},{20,16},{24,28},{28,24},{1,5},{5... | collective-permute-start | bytes 5308424 | tf_op jit(solution)/shard_map/ppermute | solution.py:871
  354.2 36.6 %collective-permute-start.37 = (bf16[512,1536]{1,0:T(8,128)(2,1)}, bf16[512,1536]{1,0:T(8,128)(2,1)}, u32[]{:S(2)}, u32[]{:S(2)}) collective-permute-start(bf16[512,1536]{1,0:T(8,128)(2,1)} %get-tuple-element.315), channel_id=1, source_target_pairs={{0,1},{1,0},{2,3},{3,2},{4,5},{5,4},{6,7},{7,6},{8,9},{9,8},{10,11... | collective-permute-start | bytes 4718600 | tf_op jit(solution)/shard_map/ppermute | solution.py:866
  402.8 48.7 %collective-permute-start.38 = (bf16[512,1536]{1,0:T(8,128)(2,1)}, bf16[512,1536]{1,0:T(8,128)(2,1)}, u32[]{:S(2)}, u32[]{:S(2)}) collective-permute-start(bf16[512,1536]{1,0:T(8,128)(2,1)} %get-tuple-element.326.own_ref), channel_id=1, source_target_pairs={{0,2},{2,0},{1,3},{3,1},{4,6},{6,4},{5,7},{7,5},{8,10},{10,8},{9,1... | collective-permute-start | bytes 4718600 | tf_op jit(solution)/shard_map/ppermute | solution.py:866
  402.8 90.8 %collective-permute-start.39 = (bf16[4,96,2304]{2,1,0:T(8,128)(2,1)}, bf16[4,96,2304]{2,1,0:T(8,128)(2,1)S(1)}, u32[]{:S(2)}, u32[]{:S(2)}) collective-permute-start(bf16[4,96,2304]{2,1,0:T(8,128)(2,1)} %get-tuple-element.332), channel_id=1, source_target_pairs={{0,4},{4,0},{8,12},{12,8},{16,20},{20,16},{24,28},{28,24},{1,5},{5... | collective-permute-start | bytes 5308424 | tf_op jit(solution)/shard_map/ppermute | solution.py:871
  404.0 23.6 %collective-permute-start.64 = (bf16[1,144,1536]{2,1,0:T(8,128)(2,1)S(1)}, bf16[1,144,1536]{2,1,0:T(8,128)(2,1)}, u32[]{:S(2)}, u32[]{:S(2)}) collective-permute-start(bf16[1,144,1536]{2,1,0:T(8,128)(2,1)S(1)} %copy-done.48), channel_id=1, source_target_pairs={{0,16},{4,20},{8,24},{12,28},{16,0},{20,4},{24,8},{28,12},{1,17},{... | collective-permute-start | bytes 1327112 | tf_op jit(solution)/shard_map/ppermute | solution.py:871
  406.6 41.8 %collective-permute-start.33 = (bf16[2,96,2304]{2,1,0:T(8,128)(2,1)}, bf16[2,96,2304]{2,1,0:T(8,128)(2,1)}, u32[]{:S(2)}, u32[]{:S(2)}) collective-permute-start(bf16[2,96,2304]{2,1,0:T(8,128)(2,1)} %get-tuple-element.306), channel_id=1, source_target_pairs={{0,8},{4,12},{8,0},{12,4},{16,24},{20,28},{24,16},{28,20},{1,9},{5... | collective-permute-start | bytes 2654216 | tf_op jit(solution)/shard_map/ppermute | solution.py:871
  408.3 81.3 %collective-permute-start.40 = (bf16[2,96,2304]{2,1,0:T(8,128)(2,1)}, bf16[2,96,2304]{2,1,0:T(8,128)(2,1)S(1)}, u32[]{:S(2)}, u32[]{:S(2)}) collective-permute-start(bf16[2,96,2304]{2,1,0:T(8,128)(2,1)} %get-tuple-element.334), channel_id=1, source_target_pairs={{0,16},{4,20},{8,24},{12,28},{16,0},{20,4},{24,8},{28,12},{1,17},{... | collective-permute-start | bytes 2654216 | tf_op jit(solution)/shard_map/ppermute | solution.py:871
  427.6 57.5 %collective-permute-start.41 = (bf16[2,144,1536]{2,1,0:T(8,128)(2,1)}, bf16[2,144,1536]{2,1,0:T(8,128)(2,1)S(1)}, u32[]{:S(2)}, u32[]{:S(2)}) collective-permute-start(bf16[2,144,1536]{2,1,0:T(8,128)(2,1)} %get-tuple-element.336), channel_id=1, source_target_pairs={{0,8},{4,12},{8,0},{12,4},{16,24},{20,28},{24,16},{28,20},{1,9},{5... | collective-permute-start | bytes 2654216 | tf_op jit(solution)/shard_map/ppermute | solution.py:871
  448.4 50.3 %collective-permute-start.60 = (bf16[1,96,2304]{2,1,0:T(8,128)(2,1)}, bf16[1,96,2304]{2,1,0:T(8,128)(2,1)S(1)}, u32[]{:S(2)}, u32[]{:S(2)}) collective-permute-start(bf16[1,96,2304]{2,1,0:T(8,128)(2,1)} %get-tuple-element.384), channel_id=1, source_target_pairs={{0,16},{4,20},{8,24},{12,28},{16,0},{20,4},{24,8},{28,12},{1,17},{... | collective-permute-start | bytes 1327112 | tf_op jit(solution)/shard_map/ppermute | solution.py:871
  451.5 51.6 %collective-permute-start.58 = (bf16[1,96,2304]{2,1,0:T(8,128)(2,1)}, bf16[1,96,2304]{2,1,0:T(8,128)(2,1)}, u32[]{:S(2)}, u32[]{:S(2)}) collective-permute-start(bf16[1,96,2304]{2,1,0:T(8,128)(2,1)} %get-tuple-element.380), channel_id=1, source_target_pairs={{0,16},{4,20},{8,24},{12,28},{16,0},{20,4},{24,8},{28,12},{1,17},{... | collective-permute-start | bytes 1327112 | tf_op jit(solution)/shard_map/ppermute | solution.py:871
  485.2 30.1 %collective-permute-start.42 = (bf16[1024,640]{1,0:T(8,128)(2,1)}, bf16[1024,640]{1,0:T(8,128)(2,1)}, u32[]{:S(2)}, u32[]{:S(2)}) collective-permute-start(bf16[1024,640]{1,0:T(8,128)(2,1)} %pad_maximum_fusion.2), channel_id=1, source_target_pairs={{0,1},{1,0},{2,3},{3,2},{4,5},{5,4},{6,7},{7,6},{8,9},{9,8},{10,11... | collective-permute-start | bytes 3932168 | tf_op jit(solution)/shard_map/ppermute | solution.py:866
  498.7 32.3 %collective-permute-start.53 = (bf16[2,96,2304]{2,1,0:T(8,128)(2,1)}, bf16[2,96,2304]{2,1,0:T(8,128)(2,1)S(1)}, u32[]{:S(2)}, u32[]{:S(2)}) collective-permute-start(bf16[2,96,2304]{2,1,0:T(8,128)(2,1)} %get-tuple-element.361), channel_id=1, source_target_pairs={{0,8},{4,12},{8,0},{12,4},{16,24},{20,28},{24,16},{28,20},{1,9},{5... | collective-permute-start | bytes 2654216 | tf_op jit(solution)/shard_map/ppermute | solution.py:871
  499.6 37.2 %collective-permute-start.65 = (bf16[1,144,1536]{2,1,0:T(8,128)(2,1)}, bf16[1,144,1536]{2,1,0:T(8,128)(2,1)S(1)}, u32[]{:S(2)}, u32[]{:S(2)}) collective-permute-start(bf16[1,144,1536]{2,1,0:T(8,128)(2,1)} %get-tuple-element.391), channel_id=1, source_target_pairs={{0,16},{4,20},{8,24},{12,28},{16,0},{20,4},{24,8},{28,12},{1,17},{... | collective-permute-start | bytes 1327112 | tf_op jit(solution)/shard_map/ppermute | solution.py:871
  501.6 37.4 %collective-permute-start.52 = (bf16[4,96,768]{2,1,0:T(8,128)(2,1)}, bf16[4,96,768]{2,1,0:T(8,128)(2,1)S(1)}, u32[]{:S(2)}, u32[]{:S(2)}) collective-permute-start(bf16[4,96,768]{2,1,0:T(8,128)(2,1)} %get-tuple-element.359), channel_id=1, source_target_pairs={{0,4},{4,0},{8,12},{12,8},{16,20},{20,16},{24,28},{28,24},{1,5},{5... | collective-permute-start | bytes 1769480 | tf_op jit(solution)/shard_map/ppermute | solution.py:871
  505.1 54.9 %collective-permute-start.59 = (bf16[1,96,2304]{2,1,0:T(8,128)(2,1)}, bf16[1,96,2304]{2,1,0:T(8,128)(2,1)}, u32[]{:S(2)}, u32[]{:S(2)}) collective-permute-start(bf16[1,96,2304]{2,1,0:T(8,128)(2,1)} %get-tuple-element.382), channel_id=1, source_target_pairs={{0,4},{4,0},{8,12},{12,8},{16,20},{20,16},{24,28},{28,24},{1,5},{5... | collective-permute-start | bytes 1327112 | tf_op jit(solution)/shard_map/ppermute | solution.py:871
  523.8 37.8 %collective-permute-start.51 = (bf16[4,96,1024]{2,1,0:T(8,128)(2,1)}, bf16[4,96,1024]{2,1,0:T(8,128)(2,1)S(1)}, u32[]{:S(2)}, u32[]{:S(2)}) collective-permute-start(bf16[4,96,1024]{2,1,0:T(8,128)(2,1)} %get-tuple-element.357), channel_id=1, source_target_pairs={{0,4},{4,0},{8,12},{12,8},{16,20},{20,16},{24,28},{28,24},{1,5},{5... | collective-permute-start | bytes 2359304 | tf_op jit(solution)/shard_map/ppermute | solution.py:871
  535.2 22.8 %collective-permute-start.62 = (bf16[1,96,2304]{2,1,0:T(8,128)(2,1)}, bf16[1,96,2304]{2,1,0:T(8,128)(2,1)}, u32[]{:S(2)}, u32[]{:S(2)}) collective-permute-start(bf16[1,96,2304]{2,1,0:T(8,128)(2,1)} %get-tuple-element.387), channel_id=1, source_target_pairs={{0,16},{4,20},{8,24},{12,28},{16,0},{20,4},{24,8},{28,12},{1,17},{... | collective-permute-start | bytes 1327112 | tf_op jit(solution)/shard_map/ppermute | solution.py:871
  537.7 23.7 %collective-permute-start.67 = (bf16[144,768]{1,0:T(8,128)(2,1)}, bf16[144,768]{1,0:T(8,128)(2,1)}, u32[]{:S(2)}, u32[]{:S(2)}) collective-permute-start(bf16[144,768]{1,0:T(8,128)(2,1)} %slice.183), channel_id=1, source_target_pairs={{0,1},{1,0},{2,3},{3,2},{4,5},{5,4},{6,7},{7,6},{8,9},{9,8},{10,11... | collective-permute-start | bytes 663560 | tf_op jit(solution)/shard_map/ppermute | solution.py:866
  539.0 22.4 %collective-permute-start.66 = (bf16[144,768]{1,0:T(8,128)(2,1)}, bf16[144,768]{1,0:T(8,128)(2,1)}, u32[]{:S(2)}, u32[]{:S(2)}) collective-permute-start(bf16[144,768]{1,0:T(8,128)(2,1)} %slice.184), channel_id=1, source_target_pairs={{0,1},{1,0},{2,3},{3,2},{4,5},{5,4},{6,7},{7,6},{8,9},{9,8},{10,11... | collective-permute-start | bytes 663560 | tf_op jit(solution)/shard_map/ppermute | solution.py:866
  558.0 34.7 %collective-permute-start.45 = (f32[512,768]{1,0:T(8,128)}, f32[512,768]{1,0:T(8,128)S(1)}, u32[]{:S(2)}, u32[]{:S(2)}) collective-permute-start(f32[512,768]{1,0:T(8,128)} %get-tuple-element.353), channel_id=1, source_target_pairs={{0,2},{2,0},{1,3},{3,1},{4,6},{6,4},{5,7},{7,5},{8,10},{10,8},{9,1... | collective-permute-start | bytes 4718600 | tf_op jit(solution)/shard_map/ppermute | solution.py:866
  560.0 14.8 %collective-permute-start.61 = (bf16[96,2304]{1,0:T(8,128)(2,1)}, bf16[96,2304]{1,0:T(8,128)(2,1)}, u32[]{:S(2)}, u32[]{:S(2)}) collective-permute-start(bf16[96,2304]{1,0:T(8,128)(2,1)} %fusion.9), channel_id=1, source_target_pairs={{0,1},{1,0},{2,3},{3,2},{4,5},{5,4},{6,7},{7,6},{8,9},{9,8},{10,11... | collective-permute-start | bytes 1327112 | tf_op jit(solution)/shard_map/ppermute | solution.py:866
  561.4 44.9 %collective-permute-start.43 = (bf16[512,1536]{1,0:T(8,128)(2,1)}, bf16[512,1536]{1,0:T(8,128)(2,1)}, u32[]{:S(2)}, u32[]{:S(2)}) collective-permute-start(bf16[512,1536]{1,0:T(8,128)(2,1)} %get-tuple-element.347), channel_id=1, source_target_pairs={{0,2},{2,0},{1,3},{3,1},{4,6},{6,4},{5,7},{7,5},{8,10},{10,8},{9,1... | collective-permute-start | bytes 4718600 | tf_op jit(solution)/shard_map/ppermute | solution.py:866
  561.6 20.7 %collective-permute-start.63 = (bf16[96,2304]{1,0:T(8,128)(2,1)}, bf16[96,2304]{1,0:T(8,128)(2,1)}, u32[]{:S(2)}, u32[]{:S(2)}) collective-permute-start(bf16[96,2304]{1,0:T(8,128)(2,1)} %fusion.10), channel_id=1, source_target_pairs={{0,1},{1,0},{2,3},{3,2},{4,5},{5,4},{6,7},{7,6},{8,9},{9,8},{10,11... | collective-permute-start | bytes 1327112 | tf_op jit(solution)/shard_map/ppermute | solution.py:866
  573.3 15.0 %collective-permute-start.57 = (bf16[1,96,768]{2,1,0:T(8,128)(2,1)}, bf16[1,96,768]{2,1,0:T(8,128)(2,1)}, u32[]{:S(2)}, u32[]{:S(2)}) collective-permute-start(bf16[1,96,768]{2,1,0:T(8,128)(2,1)} %get-tuple-element.378), channel_id=1, source_target_pairs={{0,16},{4,20},{8,24},{12,28},{16,0},{20,4},{24,8},{28,12},{1,17},{... | collective-permute-start | bytes 442376 | tf_op jit(solution)/shard_map/ppermute | solution.py:871
  574.8 15.2 %collective-permute-start.54 = (bf16[2,96,1024]{2,1,0:T(8,128)(2,1)}, bf16[2,96,1024]{2,1,0:T(8,128)(2,1)}, u32[]{:S(2)}, u32[]{:S(2)}) collective-permute-start(bf16[2,96,1024]{2,1,0:T(8,128)(2,1)} %get-tuple-element.369), channel_id=1, source_target_pairs={{0,8},{4,12},{8,0},{12,4},{16,24},{20,28},{24,16},{28,20},{1,9},{5... | collective-permute-start | bytes 1179656 | tf_op jit(solution)/shard_map/ppermute | solution.py:871
  592.7 11.7 %collective-permute-start.56 = (bf16[1,96,1024]{2,1,0:T(8,128)(2,1)}, bf16[1,96,1024]{2,1,0:T(8,128)(2,1)S(1)}, u32[]{:S(2)}, u32[]{:S(2)}) collective-permute-start(bf16[1,96,1024]{2,1,0:T(8,128)(2,1)} %get-tuple-element.376), channel_id=1, source_target_pairs={{0,16},{4,20},{8,24},{12,28},{16,0},{20,4},{24,8},{28,12},{1,17},{... | collective-permute-start | bytes 589832 | tf_op jit(solution)/shard_map/ppermute | solution.py:871
  593.4 11.8 %collective-permute-start.47 = (f32[1536]{0:T(1024)S(1)}, f32[1536]{0:T(1024)S(1)}, u32[]{:S(2)}, u32[]{:S(2)}) collective-permute-start(f32[1536]{0:T(1024)S(1)} %pad_maximum_fusion.18), channel_id=1, source_target_pairs={{0,2},{2,0},{1,3},{3,1},{4,6},{6,4},{5,7},{7,5},{8,10},{10,8},{9,1... | collective-permute-start | bytes 18440 | tf_op jit(solution)/shard_map/ppermute | solution.py:866
  608.3 25.2 %collective-permute-start.44 = (bf16[512,768]{1,0:T(8,128)(2,1)S(1)}, bf16[512,768]{1,0:T(8,128)(2,1)S(1)}, u32[]{:S(2)}, u32[]{:S(2)}) collective-permute-start(bf16[512,768]{1,0:T(8,128)(2,1)S(1)} %slice.182), channel_id=1, source_target_pairs={{0,1},{1,0},{2,3},{3,2},{4,5},{5,4},{6,7},{7,6},{8,9},{9,8},{10,11... | collective-permute-start | bytes 2359304 | tf_op jit(solution)/shard_map/ppermute | solution.py:866
  610.0 17.6 %collective-permute-start.46 = (f32[512]{0:T(512)S(1)}, f32[512]{0:T(512)S(1)}, u32[]{:S(2)}, u32[]{:S(2)}) collective-permute-start(f32[512]{0:T(512)S(1)} %get-tuple-element.394), channel_id=1, source_target_pairs={{0,1},{1,0},{2,3},{3,2},{4,5},{5,4},{6,7},{7,6},{8,9},{9,8},{10,11... | collective-permute-start | bytes 6152 | tf_op jit(solution)/shard_map/ppermute | solution.py:866
  610.4 17.2 %collective-permute-start.49 = (f32[2560]{0:T(1024)S(1)}, f32[2560]{0:T(1024)S(1)}, u32[]{:S(2)}, u32[]{:S(2)}) collective-permute-start(f32[2560]{0:T(1024)S(1)} %fusion.15), channel_id=1, source_target_pairs={{0,8},{4,12},{8,0},{12,4},{16,24},{20,28},{24,16},{28,20},{1,9},{5... | collective-permute-start | bytes 30728 | tf_op jit(solution)/shard_map/ppermute | solution.py:871
  (54 other events, 352.8 us)

commit v3 on v2

--- a/solution.py
+++ b/solution.py
@@ -62,23 +62,24 @@
 
 
 def halves_of(segment, padded):
-    first = padded // 2
-    return ((0, first), (first, segment - first))
-
-
-def units_kernel(count, segment, padded, halves, table, block_ref, *out_refs):
+    first = 2 * padded // 3
+    return ((0, first, first), (first, segment - first, padded - first))
+
+
+def units_kernel(count, segment, padded, halves, table, block_ref, *refs):
     rows = block_ref.shape[0]
+    out_refs = refs[-len(halves) :]
 
     def write(side):
         for out_ref, half in zip(out_refs, halves):
-            begin, width = halves_of(segment, padded)[half]
+            begin, width, full = halves_of(segment, padded)[half]
             parts = []
             for kind in range(2):
                 for k in range(count):
                     start = ((kind * count + k) * 2 + side) * segment + begin
                     parts.append(block_ref[:, start : start + width])
-                    if width < padded // 2:
-                        parts.append(jnp.zeros((rows, padded // 2 - width), block_ref.dtype))
+                    if width < full:
+                        parts.append(jnp.zeros((rows, full - width), block_ref.dtype))
             out_ref[0] = jnp.concatenate(parts, axis=1)
 
     @pl.when(table[0] == 0)
@@ -90,49 +91,57 @@
         write(1)
 
 
-def unit_columns(block, side, slots, count, rows, padded, halves=(0, 1)):
+def unit_columns(block, side, slots, count, rows, padded, halves=(0, 1), places=None, depth=None, begun=None):
     columns = block.shape[1]
     segment = columns // (4 * count)
-    units = padded * count
+    units = [2 * count * halves_of(segment, padded)[half][2] for half in halves]
     steps = slots.shape[0]
-    table = jnp.concatenate([side.reshape(1), slots]).astype(jnp.int32)
+    depth = steps if depth is None else depth
+    places = jnp.arange(steps) if places is None else places
+    begun = [] if begun is None else begun
+    table = jnp.concatenate([side.reshape(1), slots, places]).astype(jnp.int32)
     return pl.pallas_call(
         functools.partial(units_kernel, count, segment, padded, halves),
         grid_spec=pltpu.PrefetchScalarGridSpec(
             num_scalar_prefetch=1,
             grid=(steps,),
-            in_specs=[pl.BlockSpec((rows, columns), lambda i, t: (t[1 + i], 0))],
-            out_specs=[pl.BlockSpec((1, rows, units), lambda i, t: (i, 0, 0))] * len(halves),
-        ),
-        out_shape=[jax.ShapeDtypeStruct((steps, rows, units), block.dtype)] * len(halves),
-        compiler_params=params("arbitrary"),
-        cost_estimate=cost(0, 4 * steps * rows * units * 2),
+            in_specs=[pl.BlockSpec((rows, columns), lambda i, t: (t[1 + i], 0))]
+            + [pl.BlockSpec(memory_space=pl.ANY)] * len(begun),
+            out_specs=[pl.BlockSpec((1, rows, wide), lambda i, t: (t[1 + steps + i], 0, 0)) for wide in units],
+        ),
+        out_shape=[jax.ShapeDtypeStruct((depth, rows, wide), block.dtype) for wide in units],
+        input_output_aliases={2 + index: index for index in range(len(begun))},
+        compiler_params=params("arbitrary"),
+        cost_estimate=cost(0, 4 * steps * rows * sum(units)),
         name="unit_columns",
-    )(table, block)
-
-
-def unit_rows_kernel(segment, table, block_ref, out_ref):
-    half, width = out_ref.shape[1], block_ref.shape[3]
-    rows = block_ref[0, 0].astype(F32)
-    out_ref[0, :, :width] = rows[:half].astype(out_ref.dtype)
-    rest = jnp.concatenate([rows[half:], jnp.zeros((2 * half - segment, width), F32)], axis=0)
-    out_ref[0, :, width:] = rest.astype(out_ref.dtype)
-
-
-def unit_rows(block, side, ranks, count, padded):
+    )(table, block, *begun)
+
+
+def unit_rows_kernel(parts, table, block_ref, *out_refs):
+    for out_ref, (begin, width, full) in zip(out_refs, parts):
+        if width == full and begin % 16 == 0 and full % 16 == 0:
+            out_ref[0] = block_ref[0, 0, begin : begin + width]
+        else:
+            part = block_ref[0, 0].astype(F32)[begin : begin + width]
+            part = jnp.concatenate([part, jnp.zeros((full - width, part.shape[1]), F32)], axis=0)
+            out_ref[0] = part.astype(out_ref.dtype)
+
+
+def unit_rows(block, side, ranks, count, padded, halves=(0, 1)):
     rows, width = block.shape
     segment = rows // (2 * count)
+    parts = [halves_of(segment, padded)[half] for half in halves]
     steps = ranks.shape[0]
     table = jnp.concatenate([side.reshape(1), ranks]).astype(jnp.int32)
     return pl.pallas_call(
-        functools.partial(unit_rows_kernel, segment),
+        functools.partial(unit_rows_kernel, parts),
         grid_spec=pltpu.PrefetchScalarGridSpec(
             num_scalar_prefetch=1,
             grid=(steps,),
             in_specs=[pl.BlockSpec((1, 1, segment, width), lambda i, t: (t[1 + i], t[0], 0, 0))],
-            out_specs=pl.BlockSpec((1, padded // 2, 2 * width), lambda i, t: (i, 0, 0)),
-        ),
-        out_shape=jax.ShapeDtypeStruct((steps, padded // 2, 2 * width), block.dtype),
+            out_specs=[pl.BlockSpec((1, full, width), lambda i, t: (i, 0, 0)) for _, _, full in parts],
+        ),
+        out_shape=[jax.ShapeDtypeStruct((steps, full, width), block.dtype) for _, _, full in parts],
         compiler_params=params("arbitrary"),
         cost_estimate=cost(0, 4 * steps * segment * width),
         name="unit_rows",
@@ -142,12 +151,11 @@
 def spread_kernel(count, segment, padded, table, own0_ref, own1_ref, far0_ref, far1_ref, out_ref):
     def write(sides):
         pieces = []
-        half = padded // 2
         for kind in range(2):
             for k in range(count):
                 for side in sides:
-                    for ref, (_, width) in zip(side, halves_of(segment, padded)):
-                        start = (kind * count + k) * half
+                    for ref, (_, width, full) in zip(side, halves_of(segment, padded)):
+                        start = (kind * count + k) * full
                         pieces.append(ref[:, start : start + width].astype(F32))
         out_ref[...] = jnp.concatenate(pieces, axis=1)
 
@@ -163,33 +171,38 @@
 
 
 def spread_columns(table, own, far, count, segment, padded):
-    rows, units = own[0].shape
+    rows = own[0].shape[0]
     step = rows // 3 if rows % 24 == 0 else rows
-    part = pl.BlockSpec((step, units), lambda i, t: (i, 0))
+    parts = [pl.BlockSpec((step, part.shape[1]), lambda i, t: (i, 0)) for part in (*own, *far)]
     columns = 4 * count * segment
     return pl.pallas_call(
         functools.partial(spread_kernel, count, segment, padded),
         grid_spec=pltpu.PrefetchScalarGridSpec(
             num_scalar_prefetch=1,
             grid=(rows // step,),
-            in_specs=[part] * 4,
+            in_specs=parts,
             out_specs=pl.BlockSpec((step, columns), lambda i, t: (i, 0)),
         ),
         out_shape=jax.ShapeDtypeStruct((rows, columns), F32),
         compiler_params=params("arbitrary"),
-        cost_estimate=cost(0, 28 * rows * units),
+        cost_estimate=cost(0, 7 * rows * columns),
         name="spread_columns",
     )(table, *own, *far)
 
 
 def project_kernel(
-    width, table, own_ref, near_ref, far_ref, far_near_ref, gain_ref, weight_ref, part0_ref, part1_ref, part2_ref,
-    part3_ref, bias_ref, cosine_ref, sine_ref, stream_ref, normed_ref, scale_ref, query_ref, key_ref, value_ref,
+    width, table, own_ref, near_ref, far_ref, far_near0_ref, far_near1_ref, gain_ref, weight_ref,
+    part0_ref, part1_ref, part2_ref, part3_ref, bias_ref, cosine_ref, sine_ref, stream_ref, normed_ref, scale_ref, query_ref, key_ref, value_ref,
 ):
     half = pl.program_id(0) * 2 // pl.num_programs(0)
     mine = half == table[ROW]
     left = jnp.where(mine, own_ref[...], near_ref[...]).astype(F32)
-    right = jnp.where(mine, far_ref[...], far_near_ref[...]).astype(F32)
+    even = pl.program_id(0) % 2 == 0
+    right = jnp.where(
+        mine,
+        far_ref[...],
+        jnp.where(even, far_near0_ref[...], far_near1_ref[...]),
+    ).astype(F32)
     squares = jnp.sum(left * left, axis=1, keepdims=True) + jnp.sum(
         right * right, axis=1, keepdims=True
     )
@@ -219,8 +232,8 @@
 def project(table, own, near, far, far_near, gain, weight, far_parts, bias, cosine, sine):
     rows, width = own.shape
     seq_len = 2 * rows
-    block = min(256, rows)
-    per_half = rows // block
+    block = rows // 2
+    per_half = 2
     out_width = weight.shape[1]
     query_width = out_width - 2 * HEAD_DIM
     part = pl.BlockSpec((block, width), lambda i, t: (i % per_half, 0))
@@ -233,7 +246,9 @@
         grid_spec=pltpu.PrefetchScalarGridSpec(
             num_scalar_prefetch=1,
             grid=(seq_len // block,),
-            in_specs=[part, part, part, part, whole((1, 2 * width)), whole(weight.shape)]
+            in_specs=[part, part, part]
+            + [whole((block, width))] * 2
+            + [whole((1, 2 * width)), whole(weight.shape)]
             + [whole((piece.shape[0], out_width)) for piece in far_parts]
             + [whole((1, out_width)), tokens(HEAD_DIM), tokens(HEAD_DIM)],
             out_specs=[
@@ -252,7 +267,7 @@
         compiler_params=params("arbitrary"),
         cost_estimate=cost(4 * seq_len * width * out_width, 12 * seq_len * width),
         name="project",
-    )(table, own, near, far, far_near, gain, weight, *far_parts, bias, cosine, sine)
+    )(table, own, near, far, *far_near, gain, weight, *far_parts, bias, cosine, sine)
 
 
 def join_kernel(width, table, own_ref, near_ref, far_ref, far_near_ref, out_ref):
@@ -292,25 +307,38 @@
     return exponent / jnp.sum(exponent, axis=1, keepdims=True)
 
 
-def attend_kernel(block, query_ref, key_ref, value_ref, seg_col_ref, seg_row_ref, out_ref):
+def attend_kernel(block, query_ref, key_ref, value_ref, seg_col_ref, seg_row_ref, out_ref, last_ref):
+    last = pl.program_id(0) == pl.num_programs(0) - 1
     for start in range(0, query_ref.shape[0], block):
         stop = start + block
         probs = block_probs(
             query_ref[start:stop], key_ref[:stop], seg_col_ref[start:stop], seg_row_ref[:, :stop], start, stop
         )
-        out_ref[start:stop] = dot(probs.astype(BF16), value_ref[:stop], 1, 0).astype(BF16)
+        out = dot(probs.astype(BF16), value_ref[:stop], 1, 0).astype(BF16)
+
+        @pl.when(last)
+        def _():
+            last_ref[start:stop] = out
+
+        @pl.when(jnp.logical_not(last))
+        def _():
+            out_ref[start:stop] = out
 
 
 def attend(query, key, value, seg_col, seg_row):
     seq_len, width = query.shape
+    heads = width // HEAD_DIM
     head = pl.BlockSpec((seq_len, HEAD_DIM), lambda h: (0, h))
     shared = whole((seq_len, HEAD_DIM))
     return pl.pallas_call(
         functools.partial(attend_kernel, 256),
         grid=(width // HEAD_DIM,),
         in_specs=[head, shared, shared, whole((seq_len, 1)), whole((1, seq_len))],
-        out_specs=head,
-        out_shape=jax.ShapeDtypeStruct(query.shape, BF16),
+        out_specs=[pl.BlockSpec((seq_len, HEAD_DIM), lambda h: (0, jnp.minimum(h, heads - 2))), shared],
+        out_shape=[
+            jax.ShapeDtypeStruct((seq_len, width - HEAD_DIM), BF16),
+            jax.ShapeDtypeStruct((seq_len, HEAD_DIM), BF16),
+        ],
         compiler_params=params("arbitrary"),
         cost_estimate=cost(6 * seq_len * seq_len * width, 8 * seq_len * width),
         name="attend",
@@ -318,11 +346,12 @@
 
 
 def attend_back_kernel(
-    block, width, table, query_ref, key_ref, value_ref, seg_col_ref, seg_row_ref, own_ref, near_ref, weight_ref,
-    far_weight_ref, cosine_ref, sine_ref, sent_ref, key_value_ref,
+    block, table, query_ref, key_ref, value_ref, seg_col_ref, seg_row_ref, own_ref, far_ref, near_ref, far_near_ref,
+    weight_ref, far_top_ref, far_bottom_ref, cosine_ref, sine_ref, sent_ref, key_value_ref,
 ):
     scaling = HEAD_DIM ** (-0.5)
     own_rows = own_ref.shape[0]
+    far_weight = jnp.where(table[COL] == 0, far_top_ref[...], far_bottom_ref[...])
 
     @pl.when(pl.program_id(0) == 0)
     def _():
@@ -332,10 +361,9 @@
         stop = start + block
         mine = table[ROW] == start // own_rows
         place = slice(start % own_rows, start % own_rows + block)
-        d_hidden = jnp.where(mine, own_ref[place], near_ref[place])
         grad = (
-            dot(d_hidden[:, :width], weight_ref[...], 1, 1)
-            + dot(d_hidden[:, width:], far_weight_ref[...], 1, 1)
+            dot(jnp.where(mine, own_ref[place], near_ref[place]), weight_ref[...], 1, 1)
+            + dot(jnp.where(mine, far_ref[place], far_near_ref[place]), far_weight, 1, 1)
         ).astype(BF16)
         query = query_ref[start:stop]
         key, value = key_ref[:stop], value_ref[:stop]
@@ -358,21 +386,22 @@
         key_value_ref[:, :HEAD_DIM] = d_key * cosine_ref[...] + turned
 
 
-def attend_back(table, query, key, value, seg_col, seg_row, own, near, weight, far_weight, cosine, sine):
+def attend_back(table, query, key, value, seg_col, seg_row, d_hidden, weight, far_weights, cosine, sine):
     seq_len, width = query.shape
     features = weight.shape[1]
     heads = width // HEAD_DIM
     head = pl.BlockSpec((seq_len, HEAD_DIM), lambda h, t: (0, h))
     rows = pl.BlockSpec((HEAD_DIM, features), lambda h, t: (heads * t[COL] + h, 0))
+    far_rows = pl.BlockSpec((HEAD_DIM, features), lambda h, t: (h, 0))
     shared = whole((seq_len, HEAD_DIM))
     return pl.pallas_call(
-        functools.partial(attend_back_kernel, 256, features),
+        functools.partial(attend_back_kernel, 256),
         grid_spec=pltpu.PrefetchScalarGridSpec(
             num_scalar_prefetch=1,
             grid=(heads,),
             in_specs=[
-                head, shared, shared, whole((seq_len, 1)), whole((1, seq_len)), whole(own.shape), whole(near.shape),
-                rows, rows, shared, shared,
+                head, shared, shared, whole((seq_len, 1)), whole((1, seq_len)),
+                *[whole(part.shape) for part in d_hidden], rows, far_rows, far_rows, shared, shared,
             ],
             out_specs=[head, whole((seq_len, 2 * HEAD_DIM))],
         ),
@@ -383,27 +412,30 @@
         compiler_params=params("arbitrary"),
         cost_estimate=cost(12 * seq_len * seq_len * width, 12 * seq_len * width),
         name="attend_back",
-    )(table, query, key, value, seg_col, seg_row, own, near, weight, far_weight, cosine, sine)
-
-
-def residual_kernel(
-    table, stream_ref, own_ref, far_ref, near_ref, near_far_ref, own_w_ref, far_w_ref, near_w_ref, near_far_w_ref,
-    gain_ref, hidden_ref, normed_ref, scale_ref, group_ref,
-):
+    )(table, query, key, value, seg_col, seg_row, *d_hidden, weight, *far_weights, cosine, sine)
+
+
+def residual_kernel(table, stream_ref, *refs):
+    pieces, weights, (gain_ref, hidden_ref, normed_ref, scale_ref, group_ref) = refs[:8], refs[8:14], refs[14:]
     first = table[COL] == 0
-    part = own_ref.shape[1]
-    group = [jnp.where(first, own_ref[...], far_ref[...]), jnp.where(first, far_ref[...], own_ref[...])]
-    other = [jnp.where(first, near_ref[...], near_far_ref[...]), jnp.where(first, near_far_ref[...], near_ref[...])]
+    own, far, near, near_far = (
+        jnp.concatenate([pieces[2 * index][...], pieces[2 * index + 1][...]], axis=1) for index in range(4)
+    )
+    part = own.shape[1]
+    group = [jnp.where(first, own, far), jnp.where(first, far, own)]
+    other = [jnp.where(first, near, near_far), jnp.where(first, near_far, near)]
     group_ref[:, :part] = group[0]
     group_ref[:, part:] = group[1]
-    width = own_w_ref.shape[1]
+    own_w, near_w, *far_w = weights
+    width = own_w.shape[1]
     halves = []
-    for index, (mine, theirs) in enumerate(((own_w_ref, near_w_ref), (far_w_ref, near_far_w_ref))):
+    for index in range(2):
         total = stream_ref[:, index * width : (index + 1) * width].astype(F32)
         for place in range(2):
             rows = slice(place * part, (place + 1) * part)
-            total = total + dot(group[place], mine[rows], 1, 0)
-            total = total + dot(other[place], theirs[rows], 1, 0)
+            mine, theirs = (own_w[rows], near_w[rows]) if index == 0 else (far_w[place][...], far_w[2 + place][...])
+            total = total + dot(group[place], mine, 1, 0)
+            total = total + dot(other[place], theirs, 1, 0)
         halves.append(total)
     squares = sum(jnp.sum(total * total, axis=1, keepdims=True) for total in halves)
     scale = lax.rsqrt(squares / (2 * width) + EPSILON)
@@ -414,9 +446,11 @@
         normed_ref[:, columns] = (total * scale * gain_ref[:, columns]).astype(BF16)
 
 
-def residual(table, stream, own, far, near, near_far, weights, gain):
+def residual(table, stream, attended, own_weight, near_weight, far_weights, near_far_weights, gain):
     seq_len, width = stream.shape
-    part = own.shape[1]
+    pieces = [piece for pair in attended for piece in pair]
+    part = attended[0][0].shape[1] + attended[0][1].shape[1]
+    weights = [own_weight, near_weight, *far_weights, *near_far_weights]
     block = min(256, seq_len)
 
     def tokens(columns):
@@ -428,8 +462,8 @@
             num_scalar_prefetch=1,
             grid=(seq_len // block,),
             in_specs=[tokens(width)]
-            + [tokens(part)] * 4
-            + [whole(weights[0].shape)] * 4
+            + [tokens(piece.shape[1]) for piece in pieces]
+            + [whole(weight.shape) for weight in weights]
             + [whole((1, width))],
             out_specs=[tokens(width), tokens(width), tokens(128), tokens(2 * part)],
         ),
@@ -442,7 +476,7 @@
         compiler_params=params("arbitrary"),
         cost_estimate=cost(2 * seq_len * width * width, 14 * seq_len * width),
         name="residual",
-    )(table, stream, own, far, near, near_far, *weights, gain)
+    )(table, stream, *pieces, *weights, gain)
 
 
 def activate_kernel(width, table, normed_ref, own_gate_ref, own_up_ref, *refs):
@@ -494,7 +528,7 @@
 
 
 def activate_back_kernel(tile, width, table, grad_ref, own_ref, *refs):
-    part_refs, (gate_factor_ref, up_factor_ref, d_gate_ref, d_up_ref, far_scr) = refs[:4], refs[4:]
+    (gate_factor_ref, up_factor_ref, d_gate_ref, d_up_ref, far_scr), part_refs = refs[-5:], refs[:-5]
 
     @pl.when(pl.program_id(0) == 0)
     def _():
@@ -506,19 +540,18 @@
     d_up_ref[...] = (d_act * up_factor_ref[...].astype(F32)).astype(BF16)
 
 
-def activate_back(table, grad, own, far_parts, half, gate_factor, up_factor):
+def activate_back(table, grad, own, far_parts, gate_factor, up_factor):
     seq_len, width = grad.shape
     units = own.shape[0]
     tile = tile_of(units)
-    weight = pl.BlockSpec((tile, width // 2), lambda j, t: (j, half))
     out = pl.BlockSpec((seq_len, tile), lambda j, t: (0, j))
     return pl.pallas_call(
         functools.partial(activate_back_kernel, tile, width // 2),
         grid_spec=pltpu.PrefetchScalarGridSpec(
             num_scalar_prefetch=1,
             grid=(units // tile,),
-            in_specs=[whole(grad.shape), weight]
-            + [pl.BlockSpec((piece.shape[0], width // 2), lambda j, t: (0, half)) for piece in far_parts]
+            in_specs=[whole(grad.shape), pl.BlockSpec((tile, width // 2), lambda j, t: (j, 0))]
+            + [whole(piece.shape) for piece in far_parts]
             + [out, out],
             out_specs=[out] * 2,
             scratch_shapes=[pltpu.VMEM((units, width // 2), BF16)],
@@ -530,42 +563,42 @@
     )(table, grad, own, *far_parts, gate_factor, up_factor)
 
 
-def down_kernel(halves, table, *refs):
-    act_refs, own_refs, part_refs = refs[:halves], refs[halves : halves + 1], refs[halves + 1 : -3]
+def down_kernel(counts, table, *refs):
+    halves = len(counts)
+    act_refs, own_refs, refs = refs[:halves], refs[halves : 2 * halves], refs[2 * halves :]
     own_out_ref, other_out_ref, total_scr = refs[-3:]
+    part_refs = []
+    for parts in counts:
+        part_refs.append(refs[:parts])
+        refs = refs[parts:]
 
     def write(weights):
-        total_scr[...] = sum(dot(act[...], weight, 1, 0) for act, weight in zip(act_refs, weights))
+        total_scr[...] = sum(dot(act_ref[...], weight, 1, 0) for act_ref, weight in zip(act_refs, weights))
         rows = own_out_ref.shape[0]
         own_out_ref[...] = total_scr[pl.ds(pl.multiple_of(table[ROW] * rows, rows), rows)]
         other = pl.multiple_of((1 - table[ROW]) * rows, rows)
         other_out_ref[...] = total_scr[pl.ds(other, rows)].astype(BF16)
 
-    def write_halves(weight_refs):
-        width = own_out_ref.shape[1]
-        write(
-            [ordered(table, weight_refs, slice(half * width, (half + 1) * width)) for half in range(halves)]
-        )
-
     @pl.when(pl.program_id(0) == 0)
     def _():
-        write_halves(own_refs)
+        write([own_ref[...] for own_ref in own_refs])
 
     @pl.when(pl.program_id(0) == 1)
     def _():
-        write_halves(part_refs)
+        write([ordered(table, parts) for parts in part_refs])
 
 
 def down(table, acts, own, far_parts):
-    seq_len, units = acts[0].shape
-    features = own.shape[1] // 2
-    parts = far_parts
-    return pl.pallas_call(
-        functools.partial(down_kernel, len(acts)),
+    seq_len = acts[0].shape[0]
+    features = own[0].shape[1]
+    units = sum(part.shape[0] for part in own)
+    arrays = (*acts, *own, *[piece for parts in far_parts for piece in parts])
+    return pl.pallas_call(
+        functools.partial(down_kernel, [len(parts) for parts in far_parts]),
         grid_spec=pltpu.PrefetchScalarGridSpec(
             num_scalar_prefetch=1,
             grid=(2,),
-            in_specs=[whole(array.shape) for array in (*acts, own, *parts)],
+            in_specs=[whole(array.shape) for array in arrays],
             out_specs=[pl.BlockSpec((seq_len // 2, features), lambda j, t: (0, j))] * 2,
             scratch_shapes=[pltpu.VMEM((seq_len, features), F32)],
         ),
@@ -574,18 +607,20 @@
             jax.ShapeDtypeStruct((seq_len // 2, 2 * features), BF16),
         ],
         compiler_params=params("arbitrary"),
-        cost_estimate=cost(
-            4 * len(acts) * seq_len * units * features, 8 * seq_len * features + 8 * units * (seq_len + features)
-        ),
+        cost_estimate=cost(4 * seq_len * units * features, 8 * seq_len * features + 8 * units * (seq_len + features)),
         name="down",
-    )(table, *acts, own, *parts)
-
-
-def split_product(table, left, rights, tile, groups, count, bits):
+    )(table, *arrays)
+
+
+def split_product(table, left, rights, tile, groups, count, bits, merge=False):
     seq_len, height = left.shape
     rows = height // (groups * count)
-    columns = sum(right.shape[1] for right in rights)
-    steps = [right.shape[1] // tile for right in rights]
+    place = [(0, group) if merge else (group, 0) for group in range(groups)]
+    outs, depth = (1, groups * count // 2) if merge else (groups, count // 2)
+    firsts = [first for _, first, _ in rights]
+    steps = [length for _, _, length in rights]
+    rights = [right for right, _, _ in rights]
+    columns = sum(steps) * tile
     starts = [sum(steps[:index]) for index in range(len(rights))]
 
     def kernel(table, left_ref, *refs):
@@ -599,15 +634,16 @@
 
         for group, bit in enumerate(bits):
             side = table[BITS + bit]
-            for out_ref, value in ((out_refs[2 * group], 1 - side), (out_refs[2 * group + 1], side)):
+            sent_ref, kept_ref = out_refs[2 * place[group][0] : 2 * place[group][0] + 2]
+            for out_ref, value in ((sent_ref, 1 - side), (kept_ref, side)):
                 for index in range(count // 2):
                     begin = (group * count + with_bit(index, bit, value)) * rows
                     if rows % 8 == 0:
                         begin = pl.multiple_of(begin, 8)
-                    out_ref[index] = total_scr[pl.ds(begin, rows)].astype(BF16)
-
-    def right_spec(start, length):
-        return pl.BlockSpec((seq_len, tile), lambda i, t: (0, jnp.clip(i - start, 0, length - 1)))
+                    out_ref[place[group][1] * (count // 2) + index] = total_scr[pl.ds(begin, rows)].astype(BF16)
+
+    def right_spec(first, start, length):
+        return pl.BlockSpec((seq_len, tile), lambda i, t: (0, first + jnp.clip(i - start, 0, length - 1)))
 
     return pl.pallas_call(
         kernel,
@@ -615,11 +651,11 @@
             num_scalar_prefetch=1,
             grid=(sum(steps),),
             in_specs=[whole(left.shape)]
-            + [right_spec(start, length) for start, length in zip(starts, steps)],
-            out_specs=[pl.BlockSpec((count // 2, rows, tile), lambda i, t: (0, 0, i))] * (2 * groups),
+            + [right_spec(*place) for place in zip(firsts, starts, steps)],
+            out_specs=[pl.BlockSpec((depth, rows, tile), lambda i, t: (0, 0, i))] * (2 * outs),
             scratch_shapes=[pltpu.VMEM((height, tile), F32)],
         ),
-        out_shape=[jax.ShapeDtypeStruct((count // 2, rows, columns), BF16)] * (2 * groups),
+        out_shape=[jax.ShapeDtypeStruct((depth, rows, columns), BF16)] * (2 * outs),
         compiler_params=params("arbitrary"),
         cost_estimate=cost(
             2 * seq_len * height * columns, 2 * (seq_len * (height + columns) + height * columns)
@@ -665,8 +701,8 @@
     for parts in counts:
         part_refs.append(refs[:parts])
         refs = refs[parts:]
-    own_out_ref, other_out_ref, *far_scrs, total_scr = refs
-    units = d_refs[0].shape[1]
+    own_out_ref, other_refs, far_scrs, total_scr = refs[0], refs[1:4], refs[4:-1], refs[-1]
+    share = 2 * steps // 3
 
     @pl.when(pl.program_id(0) == 0)
     def _():
@@ -676,6 +712,7 @@
     def write(weights):
         total = None
         for half in range(halves):
+            units = d_refs[2 * half].shape[1]
             for kind in range(2):
                 term = dot(
                     d_refs[2 * half + kind][...], weights[half][:, kind * units : (kind + 1) * units], 1, 1
@@ -685,7 +722,11 @@
         rows = own_out_ref.shape[0]
         own_out_ref[...] = total_scr[pl.ds(pl.multiple_of(table[ROW] * rows, rows), rows)]
         other = pl.multiple_of((1 - table[ROW]) * rows, rows)
-        other_out_ref[...] = total_scr[pl.ds(other, rows)].astype(BF16)
+        for index, other_ref in enumerate(other_refs):
+
+            @pl.when(pl.program_id(0) // share == index)
+            def _():
+                other_ref[...] = total_scr[pl.ds(other, rows)].astype(BF16)
 
     @pl.when(pl.program_id(0) < steps)
     def _():
@@ -698,68 +739,86 @@
 
 
 def normed_grad(table, d_parts, own, far_parts):
-    seq_len, units = d_parts[0].shape
+    seq_len = d_parts[0].shape[0]
+    units = [part.shape[1] for part in d_parts[::2]]
     features = own[0].shape[0]
     tile = 256
     steps = features // tile
     halves = len(own)
     parts = [piece for half in far_parts for piece in half]
-    own_spec = pl.BlockSpec((tile, 2 * units), lambda j, t: (jnp.minimum(j, steps - 1), 0))
+    share = 2 * steps // 3
+
+    def third(index):
+        return pl.BlockSpec(
+            (seq_len // 2, tile), lambda j, t: (0, jnp.clip(j - share * index, 0, share - 1))
+        )
+
+    own_specs = [
+        pl.BlockSpec((tile, 2 * wide), lambda j, t: (jnp.minimum(j, steps - 1), 0)) for wide in units
+    ]
     return pl.pallas_call(
         functools.partial(normed_grad_kernel, halves, steps, tile, [len(half) for half in far_parts]),
         grid_spec=pltpu.PrefetchScalarGridSpec(
             num_scalar_prefetch=1,
             grid=(2 * steps,),
-            in_specs=[whole((seq_len, units))] * (2 * halves)
-            + [own_spec] * halves
+            in_specs=[whole(part.shape) for part in d_parts]
+            + own_specs
             + [whole(piece.shape) for piece in parts],
-            out_specs=[pl.BlockSpec((seq_len // 2, tile), lambda j, t: (0, j))] * 2,
-            scratch_shapes=[pltpu.VMEM((features, 2 * units), BF16)] * halves
+            out_specs=[pl.BlockSpec((seq_len // 2, tile), lambda j, t: (0, j))]
+            + [third(index) for index in range(3)],
+            scratch_shapes=[pltpu.VMEM((features, 2 * wide), BF16) for wide in units]
             + [pltpu.VMEM((seq_len, tile), F32)],
         ),
         out_shape=[
             jax.ShapeDtypeStruct((seq_len // 2, 2 * features), F32),
-            jax.ShapeDtypeStruct((seq_len // 2, 2 * features), BF16),
+            *[jax.ShapeDtypeStruct((seq_len // 2, 2 * features // 3), BF16)] * 3,
         ],
         compiler_params=params("arbitrary"),
         cost_estimate=cost(
-            8 * seq_len * features * units * halves, 8 * units * halves * (seq_len + features)
+            8 * seq_len * features * sum(units), 8 * sum(units) * (seq_len + features)
         ),
         name="normed_grad",
     )(table, *d_parts, *own, *parts)
 
 
-def chip_sum_kernel(own_ref, near_ref, out_ref, low_ref):
-    total = own_ref[...] + near_ref[...].astype(F32)
-    out_ref[...] = total
-    low_ref[...] = total.astype(BF16)
-
-
-def chip_sum(own, near):
+def chip_sum_kernel(own_ref, *refs):
+    near_refs, (out_ref, *low_refs) = refs[:-3], refs[-3:]
+    width = low_refs[0].shape[1]
+    start = 0
+    for near_ref in near_refs:
+        columns = slice(start, start + near_ref.shape[1])
+        total = own_ref[:, columns] + near_ref[...].astype(F32)
+        out_ref[:, columns] = total
+        start += near_ref.shape[1]
+    for index, low_ref in enumerate(low_refs):
+        low_ref[...] = out_ref[:, index * width : (index + 1) * width].astype(BF16)
+
+
+def chip_sum(own, nears):
     rows, width = own.shape
     block = pl.BlockSpec((rows // 4, width), lambda i: (i, 0))
     return pl.pallas_call(
         chip_sum_kernel,
         grid=(4,),
-        in_specs=[block, block],
-        out_specs=[block, block],
-        out_shape=[jax.ShapeDtypeStruct(own.shape, F32), jax.ShapeDtypeStruct(own.shape, BF16)],
+        in_specs=[block] + [pl.BlockSpec((rows // 4, near.shape[1]), lambda i: (i, 0)) for near in nears],
+        out_specs=[block] + [pl.BlockSpec((rows // 4, width // 2), lambda i: (i, 0))] * 2,
+        out_shape=[jax.ShapeDtypeStruct(own.shape, F32)]
+        + [jax.ShapeDtypeStruct((rows, width // 2), BF16)] * 2,
         compiler_params=params("arbitrary"),
         cost_estimate=cost(0, 12 * rows * width),
         name="chip_sum",
-    )(own, near)
+    )(own, *nears)
 
 
 def norm_back_kernel(
-    width, table, chip_ref, far_ref, hidden_ref, scale_ref, grad_ref, gain_ref, out_ref, low_ref, gain_grad_ref
+    width, table, chip_ref, far_own_ref, far_other_ref, hidden_ref, scale_ref, grad_ref, gain_ref, out_ref, low0_ref, low1_ref, gain_grad_ref
 ):
     @pl.when(pl.program_id(0) == 0)
     def _():
         gain_grad_ref[...] = jnp.zeros_like(gain_grad_ref)
 
-    far = far_ref[...].astype(F32)
-    d_left = chip_ref[:, :width] + far[:, width:]
-    d_right = chip_ref[:, width:] + far[:, :width]
+    d_left = chip_ref[:, :width] + far_other_ref[...].astype(F32)
+    d_right = chip_ref[:, width:] + far_own_ref[...].astype(F32)
     left, right = hidden_ref[:, :width], hidden_ref[:, width:]
     scale = scale_ref[:, :1]
     gain_grad_ref[...] += jnp.sum(d_left * left * scale, axis=0, keepdims=True)
@@ -771,8 +830,8 @@
     d_left = grad_ref[:, :width].astype(F32) + scale * (left_weighted - left * factor)
     d_right = grad_ref[:, width:].astype(F32) + scale * (right_weighted - right * factor)
     out_ref[...] = d_left
-    low_ref[:, :width] = d_left.astype(BF16)
-    low_ref[:, width:] = d_right.astype(BF16)
+    low0_ref[...] = d_left.astype(BF16)
+    low1_ref[...] = d_right.astype(BF16)
 
 
 def norm_back(table, chip, far, hidden, scale, grad, gain):
@@ -790,76 +849,86 @@
         grid_spec=pltpu.PrefetchScalarGridSpec(
             num_scalar_prefetch=1,
             grid=(4,),
-            in_specs=[own(width), own(width), tokens(width), tokens(128), tokens(width), whole((1, width))],
-            out_specs=[own(width // 2), own(width), whole((1, width // 2))],
+            in_specs=[own(width), own(width // 2), own(width // 2), tokens(width), tokens(128), tokens(width), whole((1, width))],
+            out_specs=[own(width // 2)] * 3 + [whole((1, width // 2))],
         ),
         out_shape=[
             jax.ShapeDtypeStruct((rows, width // 2), F32),
-            jax.ShapeDtypeStruct((rows, width), BF16),
+            jax.ShapeDtypeStruct((rows, width // 2), BF16),
+            jax.ShapeDtypeStruct((rows, width // 2), BF16),
             jax.ShapeDtypeStruct((1, width // 2), F32),
         ],
         compiler_params=params("arbitrary"),
         cost_estimate=cost(0, 20 * rows * width),
         name="norm_back",
-    )(table, chip, far, hidden, scale, grad, gain)
+    )(table, chip, *far, hidden, scale, grad, gain)
 
 
 def project_back_kernel(
-    count, bit, query_width, table, query_ref, key_value_ref, arrived_ref, normed_ref, weight_ref,
-    sent_ref, kept_ref, own_ref, other_ref, bias_ref, d_scr, total_scr,
+    count, bit, table, query_ref, key_value_ref, arrived_query_ref, arrived_ref, normed_ref, weight_ref, group_ref,
+    d_hidden_ref, d_hidden_near_ref, sent_ref, kept_ref, own_ref, other_ref, bias_ref, d_scr, total_scr, hidden_scr, out_scr,
 ):
     first = table[COL] == 0
-    own, far = query_ref[...], arrived_ref[:, :query_width]
+    query_width = query_ref.shape[1]
+    own, far = query_ref[...], arrived_query_ref[...]
     d_scr[:, :query_width] = jnp.where(first, own, far)
     d_scr[:, query_width : 2 * query_width] = jnp.where(first, far, own)
-    d_key_value = key_value_ref[...] + arrived_ref[:, query_width:].astype(F32)
+    d_key_value = key_value_ref[...] + arrived_ref[...].astype(F32)
     d_scr[:, 2 * query_width :] = d_key_value.astype(BF16)
     d_projected = d_scr[...]
     bias_ref[...] = jnp.sum(d_projected.astype(F32), axis=0, keepdims=True)
     total_scr[...] = dot(normed_ref[...], d_projected, 0, 0)
+    tokens = own_ref.shape[0]
+    hidden_scr[:tokens] = jnp.where(table[ROW] == 0, d_hidden_ref[...], d_hidden_near_ref[...])
+    hidden_scr[tokens:] = jnp.where(table[ROW] == 0, d_hidden_near_ref[...], d_hidden_ref[...])
+    out_scr[...] = dot(group_ref[...], hidden_scr[...], 0, 0)
     rows = sent_ref.shape[1]
+    width = total_scr.shape[1]
     side = table[BITS + bit]
     for out_ref, value in ((sent_ref, 1 - side), (kept_ref, side)):
         for index in range(count // 2):
             start = with_bit(index, bit, value) * rows
             if rows % 8 == 0:
                 start = pl.multiple_of(start, 8)
-            out_ref[index] = total_scr[pl.ds(start, rows)].astype(BF16)
-    tokens = own_ref.shape[0]
+            out_ref[index, :, :width] = total_scr[pl.ds(start, rows)].astype(BF16)
+            out_ref[index, :, width:] = out_scr[pl.ds(start, rows)].astype(BF16)
     for out_ref, half in ((own_ref, table[ROW]), (other_ref, 1 - table[ROW])):
         d_half = d_scr[pl.ds(pl.multiple_of(half * tokens, tokens), tokens)]
-        out_ref[...] = dot(d_half, weight_ref[...], 1, 1)
-
-
-def project_back(table, d_query, d_key_value, arrived, normed, weight, count, bit):
-    seq_len, query_width = d_query.shape
+        out_ref[...] = dot(d_half, weight_ref[...], 1, 1).astype(out_ref.dtype)
+
+
+def project_back(table, d_query, d_key_value, arrived_query, arrived, normed, weight, group, d_hidden, near, count, bit):
+    seq_len = d_query.shape[0]
     width, columns = weight.shape
     rows = width // count
-    return pl.pallas_call(
-        functools.partial(project_back_kernel, count, bit, query_width),
+    arrays = (d_query, d_key_value, arrived_query, arrived, normed, weight, group, d_hidden, near)
+    terms = (count // 2, rows, columns + d_hidden.shape[1])
+    return pl.pallas_call(
+        functools.partial(project_back_kernel, count, bit),
         grid_spec=pltpu.PrefetchScalarGridSpec(
             num_scalar_prefetch=1,
             grid=(1,),
-            in_specs=[
-                whole(array.shape) for array in (d_query, d_key_value, arrived, normed, weight)
+            in_specs=[whole(array.shape) for array in arrays],
+            out_specs=[
+                whole(terms), whole(terms), whole((seq_len // 2, width)), whole((seq_len // 2, width)),
+                whole((1, columns)),
             ],
-            out_specs=[
-                whole((count // 2, rows, columns)), whole((count // 2, rows, columns)),
-                whole((seq_len // 2, width)), whole((seq_len // 2, width)), whole((1, columns)),
+            scratch_shapes=[
+                pltpu.VMEM((seq_len, columns), BF16), pltpu.VMEM((width, columns), F32),
+                pltpu.VMEM((seq_len, d_hidden.shape[1]), BF16), pltpu.VMEM((width, d_hidden.shape[1]), F32),
             ],
-            scratch_shapes=[pltpu.VMEM((seq_len, columns), BF16), pltpu.VMEM((width, columns), F32)],
         ),
         out_shape=[
-            jax.ShapeDtypeStruct((count // 2, rows, columns), BF16),
-            jax.ShapeDtypeStruct((count // 2, rows, columns), BF16),
+            jax.ShapeDtypeStruct(terms, BF16),
+            jax.ShapeDtypeStruct(terms, BF16),
             jax.ShapeDtypeStruct((seq_len // 2, width), F32),
-            jax.ShapeDtypeStruct((seq_len // 2, width), F32),
+            jax.ShapeDtypeStruct((seq_len // 2, width), BF16),
             jax.ShapeDtypeStruct((1, columns), F32),
         ],
         compiler_params=params("arbitrary"),
         cost_estimate=cost(4 * seq_len * width * columns, 8 * seq_len * columns),
         name="project_back",
-    )(table, d_query, d_key_value, arrived, normed, weight)
+    )(table, *arrays)
 
 
 def swap(part, axis_name):
@@ -924,9 +993,7 @@
 
 def laid_out(parts, rank):
     low, high = rank % 2, rank // 2 % 2
-    return jnp.concatenate(
-        [in_order(high, parts[0], parts[2], 0), in_order(low, parts[1], parts[3], 0)], axis=0
-    )
+    return [in_order(high, parts[0], parts[2], 0), in_order(low, parts[1], parts[3], 0)]
 
 
 class Scatter:
@@ -953,13 +1020,10 @@
     def finish(self, line):
         while self.order:
             self.relay(line)
-        return self.kept[0].astype(F32) + self.arriving[0].astype(F32)
-
-
-def dp_sum(part):
-    for bit in range(lax.axis_size("dp").bit_length() - 1):
-        part = part + dp_swap(part, bit)
-    return part
+        total = self.kept.astype(F32) + line.step(self.arriving).astype(F32)
+        total = lax.optimization_barrier(total)
+        line.mark(total)
+        return total
 
 
 def shards(
@@ -989,7 +1053,7 @@
     own_units = down_block.shape[0] // 2
     segment = own_units // count
     step = max(16, 128 // count)
-    padded = pl.cdiv(segment, 2 * step) * 2 * step
+    padded = pl.cdiv(segment, 3 * step) * 3 * step
     feature_rows = half_width // count
     slot_rows = half_width // 8
     slots = quad_slots(rank)
@@ -1004,7 +1068,6 @@
 
     table = jnp.stack([row, col] + [(rank >> bit) & 1 for bit in range(bits)]).astype(jnp.int32)
     line = Line()
-    half_rows = padded // 2
     pair_first, line_first = [0, 1, 2], [1, 2, 0]
 
     def qkv_columns(side):
@@ -1029,7 +1092,6 @@
 
     near = swap(block_input, "row")
     far = swap(line.step(block_input), "col")
-    far_near = swap(far, "row")
 
     position_index = jnp.arange(seq_len, dtype=jnp.int32)
     doc_first = jnp.concatenate([jnp.ones((1,), jnp.bool_), segment_ids[1:] != segment_ids[:-1]])
@@ -1041,53 +1103,62 @@
     sine = jnp.concatenate([-sine, sine], axis=1)
     seg_col, seg_row = segment_ids[:, None], segment_ids[None, :]
 
+    low_slots, high_slots = jnp.arange(4), 4 + jnp.arange(4)
+    gate_up_own = unit_columns(
+        line.step(gate_up_block), col, low_slots, count, slot_rows, padded, (0, 1), low_slots, 8
+    )
+    line.mark(*gate_up_own)
     early_quad.first_round(line)
     gate_up_quad = Quad(swap(line.step(send), "col"), rank)
-    line.mark(*early_quad.sent, cosine, sine)
     early_far = early_quad.second_round(line)
+    down_own = unit_rows(line.step(down_block), col, jnp.arange(count), count, padded)
+    line.mark(*down_own)
+    down_own = [part.reshape(-1, half_width) for part in down_own]
+    far_halves = lax.optimization_barrier((far[: own_rows // 2], far[own_rows // 2 :]))
+    far_near = [swap(half, "row") for half in far_halves]
     gate_up_own = unit_columns(
-        line.step(gate_up_block), col, jnp.arange(8), count, slot_rows, padded
+        line.step(gate_up_block), col, high_slots, count, slot_rows, padded, (0, 1), high_slots, 8, gate_up_own
     )
     line.mark(*gate_up_own)
     gate_up_own = [part.reshape(half_width, -1) for part in gate_up_own]
+    out_near = swap(out_block, "row")
     stream, first_normed, first_scale, query, key, value = project(
         table, line.step(block_input), near, far, far_near, gains[:1], qkv_own, early_far,
         bias_own[None], cosine, sine,
     )
     line.mark(query)
+    gate_up_quad.first_round(line)
     attended = attend(line.step(query), key, value, seg_col, seg_row)
-    line.mark(attended)
-    attended_far = swap(attended, "col")
-    attended_near = swap(attended, "row")
-
-    gate_up_quad.first_round(line)
+    line.mark(*attended)
+    attended_far = [swap(part, "col") for part in attended]
+    attended_near = [swap(part, "row") for part in attended]
+    gate_up_far = [gate_up_quad.second_round(line)]
     out_far = lax.optimization_barrier(
         laid_out([line.step(part)[:, qkv_width:] for part in early_far], rank)
     )
-    line.mark(out_far)
-    out_near = swap(line.step(out_block), "row")
-    out_far_near = swap(out_far, "row")
+    line.mark(*out_far)
+    out_far_near = [swap(part, "row") for part in out_far]
     share = count // 8
     send_ranks = (slots[:, None] * share + jnp.arange(share)[None, :]).reshape(-1)
-    down_send = unit_rows(line.step(down_block), 1 - col, send_ranks, count, padded)
+    (down_send,) = unit_rows(line.step(down_block), 1 - col, send_ranks, count, padded, (0,))
     line.mark(down_send)
-    gate_up_far = [gate_up_quad.second_round(line)]
-    attended_far = line.step(attended_far)
-    line.mark(attended_far)
-    attended_far_near = swap(attended_far, "row")
-    grad_far = swap(line.step(output_grad), "col")
-    down_quad = Quad(
-        swap(line.step(down_send).reshape(2, share * half_rows, model_width), "col"), rank
-    )
-    hidden_one, second_normed, second_scale, attended_group = residual(
-        table, line.step(stream), attended, attended_far, attended_near, attended_far_near,
-        [out_block, out_far, out_near, out_far_near], gains[1:],
-    )
-    line.mark(second_normed)
     (send,) = unit_columns(
         line.step(gate_up_block), 1 - col, jnp.arange(8), count, slot_rows, padded, (1,)
     )
     line.mark(send)
+    attended_far = [line.step(part) for part in attended_far]
+    line.mark(*attended_far)
+    attended_far_near = [swap(part, "row") for part in attended_far]
+    down_quad = Quad(swap(line.step(down_send).reshape(2, -1, half_width), "col"), rank)
+    grad_far = swap(line.step(output_grad), "col")
+    hidden_one, second_normed, second_scale, attended_group = residual(
+        table, line.step(stream), (attended, attended_far, attended_near, attended_far_near),
+        out_block, out_near, out_far, out_far_near, gains[1:],
+    )
+    line.mark(second_normed)
+    gate_up_far[0] = [line.step(part) for part in gate_up_far[0]]
+    line.mark(*gate_up_far[0])
+    down_quad.first_round(line)
 
     act0, gate_factor0, up_factor0 = activate(
         table, line.step(second_normed), gate_up_own[0], gate_up_far[0]
@@ -1095,103 +1166,98 @@
     line.mark(act0)
     grad_far = line.step(grad_far)
     line.mark(grad_far)
+    down_far = [down_quad.second_round(line)]
     grad_near = swap(line.step(output_grad), "row")
     grad_far_near = swap(grad_far, "row")
     gate_up_far.append([swap(line.step(send).reshape(half_width, -1), "col")])
-    down_quad.first_round(line)
-    down_own = unit_rows(line.step(down_block), col, jnp.arange(count), count, padded)
-    line.mark(down_own)
-    down_own = down_own.reshape(count * half_rows, model_width)
     grad_full = join(table, line.step(output_grad), grad_near, grad_far, grad_far_near)
     line.mark(grad_full)
 
     def down_terms(act, order):
-        sent, kept = split_product(table, line.step(act), [grad_full], 768, 1, count, [order[0]])
+        sent, kept = split_product(
+            table, line.step(act), [(grad_full, 0, 2)], half_width, 1, count, [order[0]]
+        )
         line.mark(sent)
         return sent, kept
 
-    def gate_up_terms(d_gate, d_up, orders):
-        bits = [order[0] for order in orders]
+    def gate_up_terms(d_gate, d_up, order, merge):
+        tile = tile_of(d_gate.shape[1])
+        rights = [(part, 0, part.shape[1] // tile) for part in (d_gate, d_up)]
         terms = split_product(
-            table, line.step(second_normed), [d_gate, d_up], tile_of(d_gate.shape[1]), 2, count, bits
+            table, line.step(second_normed), rights, tile, 2, count, [order[0]] * 2, merge
         )
         line.mark(terms[0])
         return terms
 
-    down_far = down_quad.second_round(line)
-    sent, kept = down_terms(act0, pair_first)
-    down_far = [line.step(part) for part in down_far]
-    line.mark(*down_far)
-    down_sum0 = Scatter(table, sent, kept, pair_first, line)
+    terms = down_terms(act0, pair_first)
+    down_far[0] = [line.step(part) for part in down_far[0]]
+    line.mark(*down_far[0])
+    down_sum0 = Scatter(table, *terms, pair_first, line)
     d_gate0, d_up0 = activate_back(
-        table, line.step(grad_full), down_own, down_far, 0, gate_factor0, up_factor0
+        table, line.step(grad_full), down_own[0], down_far[0], gate_factor0, up_factor0
     )
     line.mark(d_gate0)
-    own_sent0, own_kept0, far_sent0, far_kept0 = gate_up_terms(d_gate0, d_up0, (pair_first, pair_first))
+    own_sent0, own_kept0, far_sent0, far_kept0 = gate_up_terms(d_gate0, d_up0, pair_first, False)
+    far_sum0 = Scatter(table, far_sent0, far_kept0, pair_first, line)
+    begin, width, full = halves_of(segment, padded)[1]
+    down_send = pick(line.step(down_block).reshape(count, 2, segment, half_width), 1 - col, 1)
+    down_send = jnp.pad(down_send[:, begin : begin + width], ((0, 0), (0, full - width), (0, 0)))
+    down_send = lax.optimization_barrier(down_send.reshape(-1, half_width))
+    line.mark(down_send)
+    down_far.append([swap(down_send, "col")])
     act1, gate_factor1, up_factor1 = activate(
         table, line.step(second_normed), gate_up_own[1], gate_up_far[1]
     )
     line.mark(act1)
     down_sum0.relay(line)
-    far_sum0 = Scatter(table, far_sent0, far_kept0, pair_first, line)
-    sent1, kept1 = down_terms(act1, pair_first)
     d_gate1, d_up1 = activate_back(
-        table, line.step(grad_full), down_own, down_far, 1, gate_factor1, up_factor1
+        table, line.step(grad_full), down_own[1], down_far[1], gate_factor1, up_factor1
     )
     line.mark(d_gate1)
+    d_second_own, *d_second_other = normed_grad(
+        table, [line.step(d_gate0), d_up0, d_gate1, d_up1], gate_up_own, gate_up_far
+    )
+    line.mark(*d_second_other)
+    d_second_near = [swap(part, "row") for part in d_second_other]
+    down_terms1 = down_terms(act1, pair_first)
     down_sum0.relay(line)
-    own_sent1, own_kept1, far_sent1, far_kept1 = gate_up_terms(d_gate1, d_up1, (line_first, pair_first))
+    d_second_chip, *d_second_low = chip_sum(line.step(d_second_own), d_second_near)
+    line.mark(*d_second_low)
+    d_second_far = [swap(part, "col") for part in d_second_low]
     far_sum0.relay(line)
     own_sum0 = Scatter(table, own_sent0, own_kept0, pair_first, line)
-    own_sum1 = Scatter(table, own_sent1, own_kept1, line_first, line)
-    d_second_own, d_second_other = normed_grad(
-        table, [line.step(d_gate0), d_up0, d_gate1, d_up1], gate_up_own, gate_up_far
-    )
-    line.mark(d_second_other)
-    far_sum0.relay(line)
-    d_second_near = swap(line.step(d_second_other), "row")
+    gate_up_terms1 = gate_up_terms(d_gate1, d_up1, pair_first, True)
     mlp_own, mlp_other = down(table, [line.step(act0), act1], down_own, down_far)
     line.mark(mlp_other)
+    far_sum0.relay(line)
+
+    d_hidden, *d_hidden_low, second_gain_part = norm_back(
+        table, line.step(d_second_chip), d_second_far, hidden_one, second_scale, grad_full, gains[1:]
+    )
+    line.mark(*d_hidden_low)
+    d_hidden_near = [swap(part, "row") for part in d_hidden_low]
+    down_sum0 = down_sum0.finish(line)[0]
     own_sum0.relay(line)
-    down_sum1 = Scatter(table, sent1, kept1, pair_first, line)
-    d_second_chip, d_second_low = chip_sum(line.step(d_second_own), d_second_near)
-    line.mark(d_second_low)
-    d_second_far = swap(d_second_low, "col")
-    own_sum1.relay(line)
-
-    d_hidden, d_hidden_low, second_gain_part = norm_back(
-        table, line.step(d_second_chip), d_second_far, hidden_one, second_scale, grad_full, gains[1:]
-    )
-    line.mark(d_hidden_low)
-    down_sum1.relay(line)
-    far_sum1 = Scatter(table, far_sent1, far_kept1, pair_first, line)
-    d_hidden_near = swap(line.step(d_hidden_low), "row")
+    gate_up_sum1 = Scatter(table, *gate_up_terms1, pair_first, line)
+
+    d_query, d_key_value = attend_back(
+        table, line.step(query), key, value, seg_col, seg_row, [*d_hidden_low, *d_hidden_near],
+        out_block, out_far, cosine, sine,
+    )
+    d_key_value_low = lax.optimization_barrier(d_key_value.astype(BF16))
+    line.mark(d_query, d_key_value_low)
+    arrived = swap(d_query, "col"), swap(d_key_value_low, "col")
+    far_sum0 = far_sum0.finish(line)[0]
+    sent, kept, d_first_own, d_first_other, bias_part = project_back(
+        table, line.step(d_query), d_key_value, *arrived, first_normed, qkv_block, attended_group,
+        d_hidden_low[0], d_hidden_near[0], count, 0,
+    )
+    line.mark(sent)
+    heads_sum = Scatter(table, sent, kept, pair_first, line)
+    d_first_near = swap(d_first_other, "row")
     own_sum0.relay(line)
-    d_hidden_full = in_order(row, d_hidden_low[:, :half_width], d_hidden_near[:, :half_width], 0)
-    sent_out, kept_out = split_product(
-        table, line.step(attended_group), [d_hidden_full], tile_of(half_width), 1, count, [0]
-    )
-    line.mark(sent_out)
-
-    d_query, d_key_value = attend_back(
-        table, line.step(query), key, value, seg_col, seg_row, d_hidden_low, d_hidden_near,
-        out_block, out_far, cosine, sine,
-    )
-    d_projected_sent = jnp.concatenate([d_query, d_key_value.astype(BF16)], axis=1)
-    d_projected_sent = lax.optimization_barrier(d_projected_sent)
-    line.mark(d_projected_sent)
-    arrived = swap(d_projected_sent, "col")
-    down_sum1.relay(line)
-    own_sum1.relay(line)
-    out_sum = Scatter(table, sent_out, kept_out, pair_first, line)
-    far_sum1.relay(line)
-    sent, kept, d_first_own, d_first_other, bias_part = project_back(
-        table, line.step(d_query), d_key_value, arrived, first_normed, qkv_block, count, 0
-    )
-    line.mark(sent)
-    qkv_sum = Scatter(table, sent, kept, pair_first, line)
-
-    d_first = line.step(d_first_own) + swap(line.step(d_first_other), "row")
+
+    d_first = line.step(d_first_own) + d_first_near.astype(F32)
     stream_own = block_input.astype(F32)
     first_scale_own = own_tokens(first_scale)[:, :1]
     first_gain_part = jnp.sum(d_first * stream_own * first_scale_own, axis=0)
@@ -1202,35 +1268,46 @@
         weighted - stream_own * (first_scale_own * first_scale_own) * (inner / model_width)
     )
 
+    gain_parts = jnp.concatenate([first_gain_part, second_gain_part[0]])
+    gain_parts = lax.optimization_barrier(gain_parts + swap(gain_parts, "row"))
+    line.mark(gain_parts)
+    small = line.step(jnp.concatenate([gain_parts, bias_part[0]]))
+
+    def dp_step(part, bit):
+        part = lax.optimization_barrier(part + line.step(dp_swap(part, bit)))
+        line.mark(part)
+        return part
+
+    gate_up_sum1.relay(line)
+    down_sum1 = Scatter(table, *down_terms1, pair_first, line)
     mlp_chip = mlp_own + swap(line.step(mlp_other), "row").astype(F32)
-    mlp_far = swap(mlp_chip[:, half_width:].astype(BF16), "col").astype(F32)
+    mlp_sent = lax.optimization_barrier(mlp_chip[:, half_width:].astype(BF16))
+    line.mark(mlp_sent)
+    mlp_far = swap(mlp_sent, "col").astype(F32)
     hidden_own = own_tokens(hidden_one)[:, :half_width]
     block_output = (hidden_own + (mlp_chip[:, :half_width] + mlp_far)).astype(BF16)
-
-    down_sum0 = down_sum0.finish(line)
-    far_sum0 = far_sum0.finish(line)
-    own_sum0 = own_sum0.finish(line)
     down_sum0_far = swap(line.step(down_sum0[:, half_width:].astype(BF16)), "col")
     far_sum0 = swap(line.step(far_sum0.astype(BF16)), "col")
-    far_sum1.relay(line)
-    out_sum.relay(line)
-    qkv_sum.relay(line)
-    own_sum1 = own_sum1.finish(line)
-    down_sum1 = down_sum1.finish(line)
-    out_sum.relay(line)
-    qkv_sum.relay(line)
-    far_sum1 = far_sum1.finish(line)
-    out_sum, qkv_sum = out_sum.finish(line), qkv_sum.finish(line)
-    down_sum1_far = swap(down_sum1[:, half_width:].astype(BF16), "col")
-    far_sum1 = swap(far_sum1.astype(BF16), "col")
-
-    gain_parts = jnp.concatenate([first_gain_part, second_gain_part[0]])
-    gain_parts = gain_parts + swap(gain_parts, "row")
-    small = dp_sum(jnp.concatenate([gain_parts, bias_part[0]]))
+    heads_sum.relay(line)
+    small = dp_step(small, 0)
+    own_sum0 = own_sum0.finish(line)[0]
+    gate_up_sum1.relay(line)
+    heads_sum.relay(line)
+    down_sum1.relay(line)
+    small = dp_step(small, 1)
+    own_sum1, far_sum1 = gate_up_sum1.finish(line)
+    far_sum1 = swap(line.step(far_sum1.astype(BF16)), "col")
+    down_sum1.relay(line)
+    heads_sum = heads_sum.finish(line)[0]
+    for bit in range(2, bits):
+        small = dp_step(small, bit)
+    qkv_sum, out_sum = heads_sum[:, : bias.shape[0]], heads_sum[:, bias.shape[0] :]
+    down_sum1 = down_sum1.finish(line)[0]
+    down_sum1_far = swap(line.step(down_sum1[:, half_width:].astype(BF16)), "col")
     bias_width = bias.shape[0] // count
     bias_grad = lax.dynamic_slice_in_dim(small[model_width:], rank * bias_width, bias_width, 0)
 
-    widths = [width for _, width in halves_of(segment, padded)]
+    widths = [width for _, width, _ in halves_of(segment, padded)]
     own_rows_sum = [
         part[:width, :half_width] for part, width in zip((down_sum0, down_sum1), widths)
     ]

time: 647 us -> 589 us (0.910)
  waiting for transfers between devices: 184 us -> 127 us
  Pallas kernels: 321 us -> 310 us
  local copies, waits for them, and re-layouts: 30.6 us -> 40.6 us
  starting transfers between devices: 59 us -> 67.9 us
    ppermute x39 -> x33, waiting for transfers between devices: 107 us -> 65.8 us  [dp_swap(): return lax.ppermute(part, 'dp', [(i, i ^ 1 << bit) for i in range(count)])]
    ppermute x29 -> x40, waiting for transfers between devices: 76.5 us -> 61.2 us  [swap(): return lax.ppermute(part, axis_name, [(0, 1), (1, 0)])]
    pallas_call x16 -> x12, Pallas kernels: 52.4 us -> 43.9 us  [relay(): pl.pallas_call(relay_kernel, grid_spec=pltpu.PrefetchScalarGridSpec(num_s...]
    ppermute x29 -> x40, starting transfers between devices: 19.7 us -> 26.4 us  [swap(): return lax.ppermute(part, axis_name, [(0, 1), (1, 0)])]
    pallas_call x5 -> x4, Pallas kernels: 55.4 us -> 49.8 us  [split_product(): pl.pallas_call(kernel, grid_spec=pltpu.PrefetchScalarGridSpec(num_scalar_...]
    unnamed x98 -> x94, local copies, waits for them, and re-layouts: 14.8 us -> 18 us
    ppermute x39 -> x33, starting transfers between devices: 39.3 us -> 41.5 us  [dp_swap(): return lax.ppermute(part, 'dp', [(i, i ^ 1 << bit) for i in range(count)])]
    pallas_call x3 -> x4, Pallas kernels: 25.7 us -> 27 us  [unit_columns(): pl.pallas_call(functools.partial(units_kernel, count, segment, padded, ha...]
  transfers between devices with their start and end apart: 68 -> 73, of which waited for: 22 -> 18; matrix products, arithmetic and copies ran while one was open for 8% -> 9% of each run, Pallas kernels for 49% -> 51%
where the time goes in v3:
time: 589 us; the launch traced here: 584 us
  Pallas kernels  310 us (53%)
  waiting for transfers between devices  127 us (22%)
  starting transfers between devices  67.9 us (12%)
  local copies, waits for them, and re-layouts  40.6 us (7%)
  other arithmetic  36.6 us (6%)
    ppermute x33, waiting for transfers between devices, dp_swap(): return lax.ppermute(part, 'dp', [(i, i ^ 1 << bit) for i in range(count)])  65.8 us
    ppermute x40, waiting for transfers between devices, swap(): return lax.ppermute(part, axis_name, [(0, 1), (1, 0)])  61.2 us
    pallas_call x4, Pallas kernels, split_product(): pl.pallas_call(kernel, grid_spec=pltpu.PrefetchScalarGridSpec(num_scalar_...  49.8 us
    pallas_call x12, Pallas kernels, relay(): pl.pallas_call(relay_kernel, grid_spec=pltpu.PrefetchScalarGridSpec(num_s...  43.9 us
    ppermute x33, starting transfers between devices, dp_swap(): return lax.ppermute(part, 'dp', [(i, i ^ 1 << bit) for i in range(count)])  41.5 us
    pallas_call x2, Pallas kernels, activate(): pl.pallas_call(functools.partial(activate_kernel, width // 2), grid_spec=...  31.7 us
    pallas_call x4, Pallas kernels, unit_columns(): pl.pallas_call(functools.partial(units_kernel, count, segment, padded, ha...  27 us
    ppermute x40, starting transfers between devices, swap(): return lax.ppermute(part, axis_name, [(0, 1), (1, 0)])  26.4 us
  transfers between devices with their start and end apart: 73, of which 18 were waited for; matrix products, arithmetic and copies ran while one was open for 9% of the time, Pallas kernels for 51%

profile of v3, /device:TPU:0, one launch (start us, length us, event | category | flops | bytes accessed | tf_op | source)
XLA Modules:
  0.0 583.6 jit_solution(569666223544679261)
XLA Ops:
  2.0 3.0 collective-permute-start.1
  15.8 4.0 unit_columns.4
  19.8 6.7 %unit_columns.5 = (bf16[8,96,3072]{2,1,0:T(8,128)(2,1)}, bf16[8,96,1536]{2,1,0:T(8,128)(2,1)}) custom-call(s32[9]{0:T(128)} %pad_add_fusion.2.table, bf16[768,8960]{1,0:T(8,128)(2,1)} %bitcast.73), custom_call_target="tpu_custom_call" | custom-call | flops 1 | bytes 1 | tf_op jit(solution)/shard_map/unit_columns/pallas_call | solution.py:103
  35.4 5.1 collective-permute-done.3
  42.9 8.4 %collective-permute-done.5.far_ref = bf16[512,768]{1,0:T(8,128)(2,1)S(1)} collective-permute-done((bf16[512,768]{1,0:T(8,128)(2,1)S(1)}, bf16[512,768]{1,0:T(8,128)(2,1)S(1)}, u32[]{:S(2)}, u32[]{:S(2)}) %collective-permute-start.5) | collective-permute-done | bytes 786464 | tf_op jit(solution)/shard_map/ppermute | solution.py:935
  53.4 7.0 %unit_rows.2 = (bf16[8,192,768]{2,1,0:T(8,128)(2,1)}, bf16[8,96,768]{2,1,0:T(8,128)(2,1)}) custom-call(s32[9]{0:T(128)} %get-tuple-element.447.table, bf16[8,2,280,768]{3,2,1,0:T(8,128)(2,1)} %bitcast.79), custom_call_target="tpu_custom_call" | custom-call | flops 1 | bytes 1 | tf_op jit(solution)/shard_map/unit_rows/pallas_call | solution.py:136
  60.4 6.7 %unit_columns.6 = (bf16[8,96,3072]{2,1,0:T(8,128)(2,1)}, bf16[8,96,1536]{2,1,0:T(8,128)(2,1)}) custom-call(s32[9]{0:T(128)} %get-tuple-element.446.table, bf16[768,8960]{1,0:T(8,128)(2,1)} %bitcast.74, bf16[8,96,3072]{2,1,0:T(8,128)(2,1)} %get-tuple-element.209.refs_0_, ...), custom_call_target="tpu_custom_call", output_to_operand_aliasing={{0}: (2, {}), {1}: (3, {})} | custom-call | flops 1 | bytes 1 | tf_op jit(solution)/shard_map/unit_columns/pallas_call | solution.py:103
  68.4 8.5 %project.1 = (bf16[1024,1536]{1,0:T(8,128)(2,1)}, bf16[1024,768]{1,0:T(8,128)(2,1)}, f32[1024,128]{1,0:T(8,128)}, bf16[1024,384]{1,0:T(8,128)(2,1)}, bf16[1024,1...) custom-call(s32[5]{0:T(128)} %stack.44.table, bf16[512,768]{1,0:T(8,128)(2,1)} %own_ref, ...), custom_call_target="tpu_custom_call" | custom-call | flops 1 | bytes 1 | tf_op jit(solution)/shard_map/project/pallas_call | solution.py:244
  82.6 10.4 %attend.1 = (bf16[1024,256]{1,0:T(8,128)(2,1)}, bf16[1024,128]{1,0:T(8,128)(2,1)}) custom-call(bf16[1024,384]{1,0:T(8,128)(2,1)} %get-tuple-element.341.query_ref, bf16[1024,128]{1,0:T(8,128)(2,1)} %get-tuple-element.235.key_ref, bf16[1024,128]{1,0:T(8,128)(2,1)} %get-tuple-element.236.value_ref, s32[1024,1]{1,0:T(8,128)} %copy.21.seg_col_ref, ...), custom_call_target="tpu_custom_call" | custom-call | flops 1 | bytes 1 | tf_op jit(solution)/shard_map/attend/pallas_call | solution.py:333
  95.3 2.5 collective-permute-done.12
  102.0 6.3 %collective-permute-done.11.refs_2_ = bf16[1024,256]{1,0:T(8,128)(2,1)} collective-permute-done((bf16[1024,256]{1,0:T(8,128)(2,1)}, bf16[1024,256]{1,0:T(8,128)(2,1)}, u32[]{:S(2)}, u32[]{:S(2)}) %collective-permute-start.11) | collective-permute-done | bytes 524320 | tf_op jit(solution)/shard_map/ppermute | solution.py:935
  108.3 2.6 unit_rows.3
  110.9 9.6 %unit_columns.7 = bf16[8,96,1536]{2,1,0:T(8,128)(2,1)} custom-call(s32[17]{0:T(128)} %pad_add_fusion.4.table, bf16[768,8960]{1,0:T(8,128)(2,1)} %bitcast.75), custom_call_target="tpu_custom_call" | custom-call | flops 1 | bytes 1 | tf_op jit(solution)/shard_map/unit_columns/pallas_call | solution.py:103
  127.3 13.3 %residual.1 = (f32[1024,1536]{1,0:T(8,128)}, bf16[1024,1536]{1,0:T(8,128)(2,1)}, f32[1024,128]{1,0:T(8,128)}, bf16[1024,768]{1,0:T(8,128)(2,1)}) custom-call(s32[5]{0:T(128)} %stack.44.table, bf16[1024,1536]{1,0:T(8,128)(2,1)} %get-tuple-element.253.stream_ref, bf16[1024,256]{1,0:T(8,128)(2,1)} %get-tuple-element.237.refs_0_, ...), custom_call_target="tpu_custom_call" | custom-call | flops 1 | bytes 1 | tf_op jit(solution)/shard_map/residual/pallas_call | solution.py:459
  144.2 19.5 %activate.2 = (bf16[1024,1536]{1,0:T(8,128)(2,1)}, bf16[1024,1536]{1,0:T(8,128)(2,1)}, bf16[1024,1536]{1,0:T(8,128)(2,1)}) custom-call(s32[5]{0:T(128)} %stack.44.table, bf16[1024,1536]{1,0:T(8,128)(2,1)} %get-tuple-element.318.normed_ref.left_ref, bf16[768,3072]{1,0:T(8,128)(2,1)} %bitcast.76, bf16[768,3072]{1,0:T(8,128)(2,1)} %bitcast.77, ...), custom_call_target="tpu_custom_call" | custom-call | flops 1 | bytes 1 | tf_op jit(solution)/shard_map/activate/pallas_call | solution.py:513
  169.0 5.6 join.1.refs_0_.grad_ref
  174.6 10.4 %split_product.4 = (bf16[4,192,1536]{2,1,0:T(8,128)(2,1)}, bf16[4,192,1536]{2,1,0:T(8,128)(2,1)}) custom-call(s32[5]{0:T(128)} %stack.44.table, bf16[1024,1536]{1,0:T(8,128)(2,1)} %get-tuple-element.320.left_ref.refs_0_, bf16[1024,1536]{1,0:T(8,128)(2,1)} %join.1.refs_0_.grad_ref), custom_call_target="tpu_custom_call" | custom-call | flops 1 | bytes 1 | tf_op jit(solution)/shard_map/split_product/pallas_call | solution.py:648
  186.5 13.2 %activate_back.2 = (bf16[1024,1536]{1,0:T(8,128)(2,1)}, bf16[1024,1536]{1,0:T(8,128)(2,1)}) custom-call(s32[5]{0:T(128)} %stack.44.table, bf16[1024,1536]{1,0:T(8,128)(2,1)} %join.1.refs_0_.grad_ref, bf16[1536,768]{1,0:T(8,128)(2,1)} %bitcast.85, bf16[384,768]{1,0:T(8,128)(2,1)} %copy-done.9, bf16[384,768]{1,0:T(8,128)(2,1)} %copy-done.8, ...), custom_call_target="tpu_custom_call" | custom-call | flops 1 | bytes 1 | tf_op jit(solution)/shard_map/activate_back/pallas_call | solution.py:548
  199.7 20.3 %split_product.5 = (bf16[4,96,3072]{2,1,0:T(8,128)(2,1)}, bf16[4,96,3072]{2,1,0:T(8,128)(2,1)}, bf16[4,96,3072]{2,1,0:T(8,128)(2,1)}, bf16[4,96,3072]{2,1,0:T(8,128)(2,1)}) custom-call(s32[5]{0:T(128)} %stack.44.table, bf16[1024,1536]{1,0:T(8,128)(2,1)} %get-tuple-element.318.normed_ref.left_ref, bf16[1024,1536]{1,0:T(8,128)(2,1)} %get-tuple-element.301.refs_0_, ...), custom_call_target="tpu_custom_call" | custom-call | flops 1 | bytes 1 | tf_op jit(solution)/shard_map/split_product/pallas_call | solution.py:648
  226.2 12.3 %activate.3 = (bf16[1024,768]{1,0:T(8,128)(2,1)}, bf16[1024,768]{1,0:T(8,128)(2,1)}, bf16[1024,768]{1,0:T(8,128)(2,1)}) custom-call(s32[5]{0:T(128)} %stack.44.table, bf16[1024,1536]{1,0:T(8,128)(2,1)} %get-tuple-element.318.normed_ref.left_ref, bf16[768,1536]{1,0:T(8,128)(2,1)} %bitcast.82, bf16[768,1536]{1,0:T(8,128)(2,1)} %bitcast.83, ...), custom_call_target="tpu_custom_call" | custom-call | flops 1 | bytes 1 | tf_op jit(solution)/shard_map/activate/pallas_call | solution.py:513
  239.5 4.2 relay.12
  244.1 6.6 %collective-permute-done.35.refs_0_.refs_8_ = bf16[768,768]{1,0:T(8,128)(2,1)S(1)} collective-permute-done((bf16[768,768]{1,0:T(8,128)(2,1)}, bf16[768,768]{1,0:T(8,128)(2,1)S(1)}, u32[]{:S(2)}, u32[]{:S(2)}) %collective-permute-start.35) | collective-permute-done | bytes 1179680 | tf_op jit(solution)/shard_map/ppermute | solution.py:935
  251.7 8.7 %activate_back.3 = (bf16[1024,768]{1,0:T(8,128)(2,1)}, bf16[1024,768]{1,0:T(8,128)(2,1)}) custom-call(s32[5]{0:T(128)} %stack.44.table, bf16[1024,1536]{1,0:T(8,128)(2,1)} %join.1.refs_0_.grad_ref, bf16[768,768]{1,0:T(8,128)(2,1)} %bitcast.89, bf16[768,768]{1,0:T(8,128)(2,1)} %copy-done.11, bf16[1024,768]{1,0:T(8,128)(2,1)} %get-tuple-element.298.refs_1_, ...), custom_call_target="tpu_custom_call" | custom-call | flops 1 | bytes 1 | tf_op jit(solution)/shard_map/activate_back/pallas_call | solution.py:548
  260.5 25.9 %normed_grad.1 = (f32[512,1536]{1,0:T(8,128)}, bf16[512,512]{1,0:T(8,128)(2,1)}, bf16[512,512]{1,0:T(8,128)(2,1)}, bf16[512,512]{1,0:T(8,128)(2,1)}) custom-call(s32[5]{0:T(128)} %stack.44.table, bf16[1024,1536]{1,0:T(8,128)(2,1)} %get-tuple-element.301.refs_0_, bf16[1024,1536]{1,0:T(8,128)(2,1)} %get-tuple-element.284.refs_1_, ...), custom_call_target="tpu_custom_call" | custom-call | flops 1 | bytes 1 | tf_op jit(solution)/shard_map/normed_grad/pallas_call | solution.py:759
  287.0 6.7 %split_product.6 = (bf16[4,96,1536]{2,1,0:T(8,128)(2,1)}, bf16[4,96,1536]{2,1,0:T(8,128)(2,1)}) custom-call(s32[5]{0:T(128)} %stack.44.table, bf16[1024,768]{1,0:T(8,128)(2,1)} %get-tuple-element.309.left_ref.refs_1_, bf16[1024,1536]{1,0:T(8,128)(2,1)} %join.1.refs_0_.grad_ref), custom_call_target="tpu_custom_call" | custom-call | flops 1 | bytes 1 | tf_op jit(solution)/shard_map/split_product/pallas_call | solution.py:648
  294.7 3.4 relay.13
  300.0 4.9 chip_sum.1
  305.0 4.2 relay.14
  313.2 2.6 collective-permute-start.41
  315.8 12.4 %split_product.7 = (bf16[8,96,1536]{2,1,0:T(8,128)(2,1)}, bf16[8,96,1536]{2,1,0:T(8,128)(2,1)}) custom-call(s32[5]{0:T(128)} %stack.44.table, bf16[1024,1536]{1,0:T(8,128)(2,1)} %get-tuple-element.318.normed_ref.left_ref, bf16[1024,768]{1,0:T(8,128)(2,1)} %get-tuple-element.300.refs_2_.refs_0_, bf16[1024,768]{1,0:T(8,128)(2,1)} %get-tuple-element.302.refs_3_.refs_1_), custom_call_target="tpu_custom_call" | custom-call | flops 1 | bytes 1 | tf_op jit(solution)/shard_map/split_product/pallas_call | solution.py:648
  328.2 14.6 %down.1 = (f32[512,1536]{1,0:T(8,128)}, bf16[512,1536]{1,0:T(8,128)(2,1)}) custom-call(s32[5]{0:T(128)} %stack.44.table, bf16[1024,1536]{1,0:T(8,128)(2,1)} %get-tuple-element.320.left_ref.refs_0_, bf16[1024,768]{1,0:T(8,128)(2,1)} %get-tuple-element.309.left_ref.refs_1_, bf16[1536,768]{1,0:T(8,128)(2,1)} %bitcast.86, bf16[768,768]{1,0:T(8,128)(2,1)} %bitcast.90, ...), custom_call_target="tpu_custom_call" | custom-call | flops 1 | bytes 1 | tf_op jit(solution)/shard_map/down/pallas_call | solution.py:596
  342.8 8.7 %collective-permute-done.42.arrived_sent_ref.arrived_ref = bf16[2,96,3072]{2,1,0:T(8,128)(2,1)S(1)} collective-permute-done((bf16[2,96,3072]{2,1,0:T(8,128)(2,1)}, bf16[2,96,3072]{2,1,0:T(8,128)(2,1)S(1)}, u32[]{:S(2)}, u32[]{:S(2)}) %collective-permute-start.42) | collective-permute-done | bytes 1179680 | tf_op jit(solution)/shard_map/ppermute | solution.py:940
  352.5 3.4 relay.15
  356.0 7.1 %norm_back.1 = (f32[512,768]{1,0:T(8,128)}, bf16[512,768]{1,0:T(8,128)(2,1)}, bf16[512,768]{1,0:T(8,128)(2,1)}, f32[1,768]{1,0:T(1,128)}) custom-call(s32[5]{0:T(128)} %stack.44.table, f32[512,1536]{1,0:T(8,128)} %get-tuple-element.333.chip_ref, bf16[512,768]{1,0:T(8,128)(2,1)} %collective-permute-done.43.far_own_ref, ...), custom_call_target="tpu_custom_call" | custom-call | flops 1 | bytes 1 | tf_op jit(solution)/shard_map/norm_back/pallas_call | solution.py:847
  364.4 2.4 convert_add_fusion.5
  368.2 4.2 relay.16
  374.8 19.3 %attend_back.1 = (bf16[1024,384]{1,0:T(8,128)(2,1)}, f32[1024,256]{1,0:T(8,128)}) custom-call(s32[5]{0:T(128)} %stack.44.table, bf16[1024,384]{1,0:T(8,128)(2,1)} %get-tuple-element.341.query_ref, bf16[1024,128]{1,0:T(8,128)(2,1)} %get-tuple-element.235.key_ref, bf16[1024,128]{1,0:T(8,128)(2,1)} %get-tuple-element.236.value_ref, ...), custom_call_target="tpu_custom_call" | custom-call | flops 1 | bytes 1 | tf_op jit(solution)/shard_map/attend_back/pallas_call | solution.py:397
  397.5 2.4 collective-permute-start.51
  401.9 22.6 %collective-permute-done.50.arrived_ref = bf16[1024,256]{1,0:T(8,128)(2,1)S(1)} collective-permute-done((bf16[1024,256]{1,0:T(8,128)(2,1)S(1)}, bf16[1024,256]{1,0:T(8,128)(2,1)S(1)}, u32[]{:S(2)}, u32[]{:S(2)}) %collective-permute-start.50) | collective-permute-done | bytes 524320 | tf_op jit(solution)/shard_map/ppermute | solution.py:935
  425.4 10.7 %project_back.1 = (bf16[4,96,1792]{2,1,0:T(8,128)(2,1)}, bf16[4,96,1792]{2,1,0:T(8,128)(2,1)}, f32[512,768]{1,0:T(8,128)}, bf16[512,768]{1,0:T(8,128)(2,1)}, f32[1,1024]{1,0:T(1,128)}) custom-call(s32[5]{0:T(128)} %stack.44.table, bf16[1024,384]{1,0:T(8,128)(2,1)} %get-tuple-element.347.query_ref, f32[1024,256]{1,0:T(8,128)} %get-tuple-element.345.key_value_ref, ...), custom_call_target="tpu_custom_call" | custom-call | flops 1 | bytes 1 | tf_op jit(solution)/shard_map/project_back/pallas_call | solution.py:906
  438.3 3.5 relay.17
  441.8 2.3 fusion.6
  447.0 5.3 relay.18
  462.4 2.8 convert_add_fusion
  466.2 19.2 %collective-permute-done.58.arrived_sent_ref.arrived_ref = bf16[4,96,1792]{2,1,0:T(8,128)(2,1)} collective-permute-done((bf16[4,96,1792]{2,1,0:T(8,128)(2,1)}, bf16[4,96,1792]{2,1,0:T(8,128)(2,1)}, u32[]{:S(2)}, u32[]{:S(2)}) %collective-permute-start.58) | collective-permute-done | bytes 1376288 | tf_op jit(solution)/shard_map/ppermute | solution.py:940
  485.9 3.3 relay.19
  489.3 2.4 collective-permute-start.61
  491.7 2.4 convert_add_fusion.3
  494.1 6.7 %collective-permute-done.62.arrived_sent_ref.arrived_ref = bf16[4,96,1536]{2,1,0:T(8,128)(2,1)} collective-permute-done((bf16[4,96,1536]{2,1,0:T(8,128)(2,1)}, bf16[4,96,1536]{2,1,0:T(8,128)(2,1)}, u32[]{:S(2)}, u32[]{:S(2)}) %collective-permute-start.62) | collective-permute-done | bytes 1179680 | tf_op jit(solution)/shard_map/ppermute | solution.py:940
  500.8 3.2 relay.20
  504.0 2.5 collective-permute-start.67
  506.5 2.5 collective-permute-start.59
  509.0 3.7 fusion.5
  514.0 10.6 %collective-permute-done.61.arrived_sent_ref.arrived_ref = bf16[2,96,1792]{2,1,0:T(8,128)(2,1)} collective-permute-done((bf16[2,96,1792]{2,1,0:T(8,128)(2,1)}, bf16[2,96,1792]{2,1,0:T(8,128)(2,1)}, u32[]{:S(2)}, u32[]{:S(2)}) %collective-permute-start.61) | collective-permute-done | bytes 688160 | tf_op jit(solution)/shard_map/ppermute | solution.py:940
  525.6 2.9 relay.21
  529.5 3.3 relay.22
  534.1 2.3 collective-permute-start.66
  538.2 2.9 fusion.8
  541.1 8.5 %collective-permute-done.68.far0_ref = bf16[96,3072]{1,0:T(8,128)(2,1)} collective-permute-done((bf16[96,3072]{1,0:T(8,128)(2,1)}, bf16[96,3072]{1,0:T(8,128)(2,1)}, u32[]{:S(2)}, u32[]{:S(2)}) %collective-permute-start.68) | collective-permute-done | bytes 589856 | tf_op jit(solution)/shard_map/ppermute | solution.py:935
  550.5 2.9 collective-permute-done.69.far1_ref
  553.3 5.6 spread_columns.1
  559.8 2.8 relay.23
  564.6 11.0 %collective-permute-done.70 = bf16[1,96,1536]{2,1,0:T(8,128)(2,1)S(1)} collective-permute-done((bf16[1,96,1536]{2,1,0:T(8,128)(2,1)}, bf16[1,96,1536]{2,1,0:T(8,128)(2,1)S(1)}, u32[]{:S(2)}, u32[]{:S(2)}) %collective-permute-start.70) | collective-permute-done | bytes 294944 | tf_op jit(solution)/shard_map/ppermute | solution.py:940
  578.0 2.9 collective-permute-done.72
  (308 shorter events, 115.9 us)
Async XLA Ops:
  2.0 13.8 %collective-permute-start.1 = (f32[2,768]{1,0:T(2,128)S(1)}, f32[2,768]{1,0:T(2,128)S(1)}, u32[]{:S(2)}, u32[]{:S(2)}) collective-permute-start(f32[2,768]{1,0:T(2,128)S(1)} %pad_maximum_fusion.18), channel_id=1, source_target_pairs={{0,1},{1,0},{2,3},{3,2},{4,5},{5,4},{6,7},{7,6},{8,9},{9,8},{10,11... | collective-permute-start | bytes 18440 | tf_op jit(solution)/shard_map/ppermute | solution.py:935
  5.1 47.2 %collective-permute-start.4 = (bf16[512,768]{1,0:T(8,128)(2,1)}, bf16[512,768]{1,0:T(8,128)(2,1)}, u32[]{:S(2)}, u32[]{:S(2)}) collective-permute-start(bf16[512,768]{1,0:T(8,128)(2,1)} %own_ref), channel_id=1, source_target_pairs={{0,2},{2,0},{1,3},{3,1},{4,6},{6,4},{5,7},{7,5},{8,10},{10,8},{9,1... | collective-permute-start | bytes 2359304 | tf_op jit(solution)/shard_map/ppermute | solution.py:935
  9.9 16.6 %collective-permute-start = (bf16[2,96,1408]{2,1,0:T(8,128)(2,1)}, bf16[2,96,1408]{2,1,0:T(8,128)(2,1)S(1)}, u32[]{:S(2)}, u32[]{:S(2)}) collective-permute-start(bf16[2,96,1408]{2,1,0:T(8,128)(2,1)} %pad_maximum_fusion.9), channel_id=1, source_target_pairs={{0,1},{1,0},{2,3},{3,2},{4,5},{5,4},{6,7},{7,6},{8,9},{9,8},{10,11... | collective-permute-start | bytes 1622024 | tf_op jit(solution)/shard_map/ppermute | solution.py:935
  26.5 8.8 %collective-permute-start.2 = (bf16[96,1408]{1,0:T(8,128)(2,1)S(1)}, bf16[96,1408]{1,0:T(8,128)(2,1)S(1)}, u32[]{:S(2)}, u32[]{:S(2)}) collective-permute-start(bf16[96,1408]{1,0:T(8,128)(2,1)S(1)} %get-tuple-element.212), channel_id=1, source_target_pairs={{0,4},{4,0},{8,12},{12,8},{16,20},{20,16},{24,28},{28,24},{1,5},{5... | collective-permute-start | bytes 811016 | tf_op jit(solution)/shard_map/ppermute | solution.py:940
  30.9 20.4 %collective-permute-start.5 = (bf16[512,768]{1,0:T(8,128)(2,1)S(1)}, bf16[512,768]{1,0:T(8,128)(2,1)S(1)}, u32[]{:S(2)}, u32[]{:S(2)}) collective-permute-start(bf16[512,768]{1,0:T(8,128)(2,1)S(1)} %copy-done.6), channel_id=1, source_target_pairs={{0,1},{1,0},{2,3},{3,2},{4,5},{5,4},{6,7},{7,6},{8,9},{9,8},{10,11... | collective-permute-start | bytes 2359304 | tf_op jit(solution)/shard_map/ppermute | solution.py:935
  32.5 8.1 %collective-permute-start.3 = (bf16[96,1408]{1,0:T(8,128)(2,1)S(1)}, bf16[96,1408]{1,0:T(8,128)(2,1)S(1)}, u32[]{:S(2)}, u32[]{:S(2)}) collective-permute-start(bf16[96,1408]{1,0:T(8,128)(2,1)S(1)} %get-tuple-element.213), channel_id=1, source_target_pairs={{0,8},{4,12},{8,0},{12,4},{16,24},{20,28},{24,16},{28,20},{1,9},{5... | collective-permute-start | bytes 811016 | tf_op jit(solution)/shard_map/ppermute | solution.py:940
  34.0 42.9 %collective-permute-start.10 = (bf16[2,96,3072]{2,1,0:T(8,128)(2,1)}, bf16[2,96,3072]{2,1,0:T(8,128)(2,1)}, u32[]{:S(2)}, u32[]{:S(2)}) collective-permute-start(bf16[2,96,3072]{2,1,0:T(8,128)(2,1)} %unit_columns.4), channel_id=1, source_target_pairs={{0,1},{1,0},{2,3},{3,2},{4,5},{5,4},{6,7},{7,6},{8,9},{9,8},{10,11... | collective-permute-start | bytes 3538952 | tf_op jit(solution)/shard_map/ppermute | solution.py:935
  40.7 26.5 %collective-permute-start.8 = (bf16[192,1408]{1,0:T(8,128)(2,1)S(1)}, bf16[192,1408]{1,0:T(8,128)(2,1)S(1)}, u32[]{:S(2)}, u32[]{:S(2)}) collective-permute-start(bf16[192,1408]{1,0:T(8,128)(2,1)S(1)} %get-tuple-element.243.part0_ref), channel_id=1, source_target_pairs={{0,8},{4,12},{8,0},{12,4},{16,24},{20,28},{24,16},{28,20},{1,9},{5... | collective-permute-start | bytes 1622024 | tf_op jit(solution)/shard_map/ppermute | solution.py:940
  42.3 24.9 %collective-permute-start.9 = (bf16[192,1408]{1,0:T(8,128)(2,1)S(1)}, bf16[192,1408]{1,0:T(8,128)(2,1)S(1)}, u32[]{:S(2)}, u32[]{:S(2)}) collective-permute-start(bf16[192,1408]{1,0:T(8,128)(2,1)S(1)} %get-tuple-element.245.part1_ref), channel_id=1, source_target_pairs={{0,4},{4,0},{8,12},{12,8},{16,20},{20,16},{24,28},{28,24},{1,5},{5... | collective-permute-start | bytes 1622024 | tf_op jit(solution)/shard_map/ppermute | solution.py:940
  52.3 14.9 %collective-permute-start.6 = (bf16[256,768]{1,0:T(8,128)(2,1)}, bf16[256,768]{1,0:T(8,128)(2,1)S(1)}, u32[]{:S(2)}, u32[]{:S(2)}) collective-permute-start(bf16[256,768]{1,0:T(8,128)(2,1)} %get-tuple-element.226), channel_id=1, source_target_pairs={{0,2},{2,0},{1,3},{3,1},{4,6},{6,4},{5,7},{7,5},{8,10},{10,8},{9,1... | collective-permute-start | bytes 1179656 | tf_op jit(solution)/shard_map/ppermute | solution.py:935
  52.3 14.9 %collective-permute-start.7 = (bf16[256,768]{1,0:T(8,128)(2,1)}, bf16[256,768]{1,0:T(8,128)(2,1)S(1)}, u32[]{:S(2)}, u32[]{:S(2)}) collective-permute-start(bf16[256,768]{1,0:T(8,128)(2,1)} %get-tuple-element.227), channel_id=1, source_target_pairs={{0,2},{2,0},{1,3},{3,1},{4,6},{6,4},{5,7},{7,5},{8,10},{10,8},{9,1... | collective-permute-start | bytes 1179656 | tf_op jit(solution)/shard_map/ppermute | solution.py:935
  78.2 16.7 %collective-permute-start.13 = (bf16[96,3072]{1,0:T(8,128)(2,1)S(1)}, bf16[96,3072]{1,0:T(8,128)(2,1)S(1)}, u32[]{:S(2)}, u32[]{:S(2)}) collective-permute-start(bf16[96,3072]{1,0:T(8,128)(2,1)S(1)} %get-tuple-element.233), channel_id=1, source_target_pairs={{0,8},{4,12},{8,0},{12,4},{16,24},{20,28},{24,16},{28,20},{1,9},{5... | collective-permute-start | bytes 1769480 | tf_op jit(solution)/shard_map/ppermute | solution.py:940
  79.8 20.6 %collective-permute-start.19 = (bf16[768,768]{1,0:T(8,128)(2,1)}, bf16[768,768]{1,0:T(8,128)(2,1)}, u32[]{:S(2)}, u32[]{:S(2)}) collective-permute-start(bf16[768,768]{1,0:T(8,128)(2,1)} %bitcast.26.refs_8_.weight_ref), channel_id=1, source_target_pairs={{0,2},{2,0},{1,3},{3,1},{4,6},{6,4},{5,7},{7,5},{8,10},{10,8},{9,1... | collective-permute-start | bytes 3538952 | tf_op jit(solution)/shard_map/ppermute | solution.py:935
  82.1 15.7 %collective-permute-start.12 = (bf16[96,3072]{1,0:T(8,128)(2,1)S(1)}, bf16[96,3072]{1,0:T(8,128)(2,1)S(1)}, u32[]{:S(2)}, u32[]{:S(2)}) collective-permute-start(bf16[96,3072]{1,0:T(8,128)(2,1)S(1)} %get-tuple-element.232), channel_id=1, source_target_pairs={{0,4},{4,0},{8,12},{12,8},{16,20},{20,16},{24,28},{28,24},{1,5},{5... | collective-permute-start | bytes 1769480 | tf_op jit(solution)/shard_map/ppermute | solution.py:940
  93.0 28.1 %collective-permute-start.15 = (bf16[1024,256]{1,0:T(8,128)(2,1)}, bf16[1024,256]{1,0:T(8,128)(2,1)}, u32[]{:S(2)}, u32[]{:S(2)}) collective-permute-start(bf16[1024,256]{1,0:T(8,128)(2,1)} %get-tuple-element.237.refs_0_), channel_id=1, source_target_pairs={{0,2},{2,0},{1,3},{3,1},{4,6},{6,4},{5,7},{7,5},{8,10},{10,8},{9,1... | collective-permute-start | bytes 1572872 | tf_op jit(solution)/shard_map/ppermute | solution.py:935
  93.2 15.1 %collective-permute-start.11 = (bf16[1024,256]{1,0:T(8,128)(2,1)}, bf16[1024,256]{1,0:T(8,128)(2,1)}, u32[]{:S(2)}, u32[]{:S(2)}) collective-permute-start(bf16[1024,256]{1,0:T(8,128)(2,1)} %get-tuple-element.237.refs_0_), channel_id=1, source_target_pairs={{0,1},{1,0},{2,3},{3,2},{4,5},{5,4},{6,7},{7,6},{8,9},{9,8},{10,11... | collective-permute-start | bytes 1572872 | tf_op jit(solution)/shard_map/ppermute | solution.py:935
  94.9 25.6 %collective-permute-start.14 = (bf16[1024,128]{1,0:T(8,128)(2,1)}, bf16[1024,128]{1,0:T(8,128)(2,1)}, u32[]{:S(2)}, u32[]{:S(2)}) collective-permute-start(bf16[1024,128]{1,0:T(8,128)(2,1)} %get-tuple-element.238.refs_1_), channel_id=1, source_target_pairs={{0,1},{1,0},{2,3},{3,2},{4,5},{5,4},{6,7},{7,6},{8,9},{9,8},{10,11... | collective-permute-start | bytes 786440 | tf_op jit(solution)/shard_map/ppermute | solution.py:935
  98.1 42.6 %collective-permute-start.23 = (bf16[192,3072]{1,0:T(8,128)(2,1)S(1)}, bf16[192,3072]{1,0:T(8,128)(2,1)S(1)}, u32[]{:S(2)}, u32[]{:S(2)}) collective-permute-start(bf16[192,3072]{1,0:T(8,128)(2,1)S(1)} %pad_maximum_fusion.1.refs_0_.refs_4_.refs_6_), channel_id=1, source_target_pairs={{0,8},{4,12},{8,0},{12,4},{16,24},{20,28},{24,16},{28,20},{1,9},{5... | collective-permute-start | bytes 3538952 | tf_op jit(solution)/shard_map/ppermute | solution.py:940
  100.5 40.2 %collective-permute-start.24 = (bf16[192,3072]{1,0:T(8,128)(2,1)S(1)}, bf16[192,3072]{1,0:T(8,128)(2,1)}, u32[]{:S(2)}, u32[]{:S(2)}) collective-permute-start(bf16[192,3072]{1,0:T(8,128)(2,1)S(1)} %pad_maximum_fusion.2.refs_1_.refs_5_.refs_7_), channel_id=1, source_target_pairs={{0,4},{4,0},{8,12},{12,8},{16,20},{20,16},{24,28},{28,24},{1,5},{5... | collective-permute-start | bytes 3538952 | tf_op jit(solution)/shard_map/ppermute | solution.py:940
  108.3 12.7 %collective-permute-start.16 = (bf16[1024,128]{1,0:T(8,128)(2,1)}, bf16[1024,128]{1,0:T(8,128)(2,1)}, u32[]{:S(2)}, u32[]{:S(2)}) collective-permute-start(bf16[1024,128]{1,0:T(8,128)(2,1)} %get-tuple-element.238.refs_1_), channel_id=1, source_target_pairs={{0,2},{2,0},{1,3},{3,1},{4,6},{6,4},{5,7},{7,5},{8,10},{10,8},{9,1... | collective-permute-start | bytes 786440 | tf_op jit(solution)/shard_map/ppermute | solution.py:935
  124.0 16.7 %collective-permute-start.22 = (bf16[2,192,768]{2,1,0:T(8,128)(2,1)}, bf16[2,192,768]{2,1,0:T(8,128)(2,1)}, u32[]{:S(2)}, u32[]{:S(2)}) collective-permute-start(bf16[2,192,768]{2,1,0:T(8,128)(2,1)} %unit_rows.3), channel_id=1, source_target_pairs={{0,1},{1,0},{2,3},{3,2},{4,5},{5,4},{6,7},{7,6},{8,9},{9,8},{10,11... | collective-permute-start | bytes 1769480 | tf_op jit(solution)/shard_map/ppermute | solution.py:935
  125.7 38.0 %collective-permute-start.26 = (bf16[512,768]{1,0:T(8,128)(2,1)}, bf16[512,768]{1,0:T(8,128)(2,1)}, u32[]{:S(2)}, u32[]{:S(2)}) collective-permute-start(bf16[512,768]{1,0:T(8,128)(2,1)} %own_ref.1), channel_id=1, source_target_pairs={{0,1},{1,0},{2,3},{3,2},{4,5},{5,4},{6,7},{7,6},{8,9},{9,8},{10,11... | collective-permute-start | bytes 2359304 | tf_op jit(solution)/shard_map/ppermute | solution.py:935
  142.2 21.6 %collective-permute-start.27 = (bf16[192,768]{1,0:T(8,128)(2,1)S(1)}, bf16[192,768]{1,0:T(8,128)(2,1)S(1)}, u32[]{:S(2)}, u32[]{:S(2)}) collective-permute-start(bf16[192,768]{1,0:T(8,128)(2,1)S(1)} %get-tuple-element.263), channel_id=1, source_target_pairs={{0,8},{4,12},{8,0},{12,4},{16,24},{20,28},{24,16},{28,20},{1,9},{5... | collective-permute-start | bytes 884744 | tf_op jit(solution)/shard_map/ppermute | solution.py:940
  142.7 21.2 %collective-permute-start.25 = (bf16[192,768]{1,0:T(8,128)(2,1)S(1)}, bf16[192,768]{1,0:T(8,128)(2,1)S(1)}, u32[]{:S(2)}, u32[]{:S(2)}) collective-permute-start(bf16[192,768]{1,0:T(8,128)(2,1)S(1)} %get-tuple-element.262), channel_id=1, source_target_pairs={{0,4},{4,0},{8,12},{12,8},{16,20},{20,16},{24,28},{28,24},{1,5},{5... | collective-permute-start | bytes 884744 | tf_op jit(solution)/shard_map/ppermute | solution.py:940
  165.7 19.3 %collective-permute-start.31 = (bf16[384,768]{1,0:T(8,128)(2,1)S(1)}, bf16[384,768]{1,0:T(8,128)(2,1)}, u32[]{:S(2)}, u32[]{:S(2)}) collective-permute-start(bf16[384,768]{1,0:T(8,128)(2,1)S(1)} %pad_maximum_fusion.8.refs_1_.refs_5_), channel_id=1, source_target_pairs={{0,4},{4,0},{8,12},{12,8},{16,20},{20,16},{24,28},{28,24},{1,5},{5... | collective-permute-start | bytes 1769480 | tf_op jit(solution)/shard_map/ppermute | solution.py:940
  166.2 18.8 %collective-permute-start.30 = (bf16[384,768]{1,0:T(8,128)(2,1)S(1)}, bf16[384,768]{1,0:T(8,128)(2,1)}, u32[]{:S(2)}, u32[]{:S(2)}) collective-permute-start(bf16[384,768]{1,0:T(8,128)(2,1)S(1)} %pad_maximum_fusion.7.refs_0_.refs_4_), channel_id=1, source_target_pairs={{0,8},{4,12},{8,0},{12,4},{16,24},{20,28},{24,16},{28,20},{1,9},{5... | collective-permute-start | bytes 1769480 | tf_op jit(solution)/shard_map/ppermute | solution.py:940
  167.8 57.0 %collective-permute-start.34 = (bf16[768,1536]{1,0:T(8,128)(2,1)}, bf16[768,1536]{1,0:T(8,128)(2,1)S(1)}, u32[]{:S(2)}, u32[]{:S(2)}) collective-permute-start(bf16[768,1536]{1,0:T(8,128)(2,1)} %bitcast.35), channel_id=1, source_target_pairs={{0,1},{1,0},{2,3},{3,2},{4,5},{5,4},{6,7},{7,6},{8,9},{9,8},{10,11... | collective-permute-start | bytes 7077896 | tf_op jit(solution)/shard_map/ppermute | solution.py:935
  185.0 54.6 %collective-permute-start.33 = (bf16[4,192,1536]{2,1,0:T(8,128)(2,1)}, bf16[4,192,1536]{2,1,0:T(8,128)(2,1)}, u32[]{:S(2)}, u32[]{:S(2)}) collective-permute-start(bf16[4,192,1536]{2,1,0:T(8,128)(2,1)} %get-tuple-element.290), channel_id=1, source_target_pairs={{0,4},{4,0},{8,12},{12,8},{16,20},{20,16},{24,28},{28,24},{1,5},{5... | collective-permute-start | bytes 7077896 | tf_op jit(solution)/shard_map/ppermute | solution.py:940
  220.0 85.0 %collective-permute-start.32 = (bf16[4,96,3072]{2,1,0:T(8,128)(2,1)}, bf16[4,96,3072]{2,1,0:T(8,128)(2,1)}, u32[]{:S(2)}, u32[]{:S(2)}) collective-permute-start(bf16[4,96,3072]{2,1,0:T(8,128)(2,1)} %get-tuple-element.288), channel_id=1, source_target_pairs={{0,4},{4,0},{8,12},{12,8},{16,20},{20,16},{24,28},{28,24},{1,5},{5... | collective-permute-start | bytes 7077896 | tf_op jit(solution)/shard_map/ppermute | solution.py:940
  224.0 26.7 %collective-permute-start.35 = (bf16[768,768]{1,0:T(8,128)(2,1)}, bf16[768,768]{1,0:T(8,128)(2,1)S(1)}, u32[]{:S(2)}, u32[]{:S(2)}) collective-permute-start(bf16[768,768]{1,0:T(8,128)(2,1)} %bitcast.33), channel_id=1, source_target_pairs={{0,1},{1,0},{2,3},{3,2},{4,5},{5,4},{6,7},{7,6},{8,9},{9,8},{10,11... | collective-permute-start | bytes 3538952 | tf_op jit(solution)/shard_map/ppermute | solution.py:935
  243.8 50.0 %collective-permute-start.36 = (bf16[2,192,1536]{2,1,0:T(8,128)(2,1)}, bf16[2,192,1536]{2,1,0:T(8,128)(2,1)S(1)}, u32[]{:S(2)}, u32[]{:S(2)}) collective-permute-start(bf16[2,192,1536]{2,1,0:T(8,128)(2,1)} %get-tuple-element.305), channel_id=1, source_target_pairs={{0,8},{4,12},{8,0},{12,4},{16,24},{20,28},{24,16},{28,20},{1,9},{5... | collective-permute-start | bytes 3538952 | tf_op jit(solution)/shard_map/ppermute | solution.py:940
  286.4 11.8 %collective-permute-start.37 = (bf16[512,512]{1,0:T(8,128)(2,1)}, bf16[512,512]{1,0:T(8,128)(2,1)S(1)}, u32[]{:S(2)}, u32[]{:S(2)}) collective-permute-start(bf16[512,512]{1,0:T(8,128)(2,1)} %get-tuple-element.306), channel_id=1, source_target_pairs={{0,2},{2,0},{1,3},{3,1},{4,6},{6,4},{5,7},{7,5},{8,10},{10,8},{9,1... | collective-permute-start | bytes 1572872 | tf_op jit(solution)/shard_map/ppermute | solution.py:935
  286.4 11.8 %collective-permute-start.38 = (bf16[512,512]{1,0:T(8,128)(2,1)}, bf16[512,512]{1,0:T(8,128)(2,1)S(1)}, u32[]{:S(2)}, u32[]{:S(2)}) collective-permute-start(bf16[512,512]{1,0:T(8,128)(2,1)} %get-tuple-element.307), channel_id=1, source_target_pairs={{0,2},{2,0},{1,3},{3,1},{4,6},{6,4},{5,7},{7,5},{8,10},{10,8},{9,1... | collective-permute-start | bytes 1572872 | tf_op jit(solution)/shard_map/ppermute | solution.py:935
  286.9 11.3 %collective-permute-start.39 = (bf16[512,512]{1,0:T(8,128)(2,1)}, bf16[512,512]{1,0:T(8,128)(2,1)S(1)}, u32[]{:S(2)}, u32[]{:S(2)}) collective-permute-start(bf16[512,512]{1,0:T(8,128)(2,1)} %get-tuple-element.308), channel_id=1, source_target_pairs={{0,2},{2,0},{1,3},{3,1},{4,6},{6,4},{5,7},{7,5},{8,10},{10,8},{9,1... | collective-permute-start | bytes 1572872 | tf_op jit(solution)/shard_map/ppermute | solution.py:935
  309.2 57.6 %collective-permute-start.40 = (bf16[4,96,3072]{2,1,0:T(8,128)(2,1)}, bf16[4,96,3072]{2,1,0:T(8,128)(2,1)S(1)}, u32[]{:S(2)}, u32[]{:S(2)}) collective-permute-start(bf16[4,96,3072]{2,1,0:T(8,128)(2,1)} %get-tuple-element.325), channel_id=1, source_target_pairs={{0,4},{4,0},{8,12},{12,8},{16,20},{20,16},{24,28},{28,24},{1,5},{5... | collective-permute-start | bytes 7077896 | tf_op jit(solution)/shard_map/ppermute | solution.py:940
  310.6 40.9 %collective-permute-start.42 = (bf16[2,96,3072]{2,1,0:T(8,128)(2,1)}, bf16[2,96,3072]{2,1,0:T(8,128)(2,1)S(1)}, u32[]{:S(2)}, u32[]{:S(2)}) collective-permute-start(bf16[2,96,3072]{2,1,0:T(8,128)(2,1)} %get-tuple-element.330), channel_id=1, source_target_pairs={{0,8},{4,12},{8,0},{12,4},{16,24},{20,28},{24,16},{28,20},{1,9},{5... | collective-permute-start | bytes 3538952 | tf_op jit(solution)/shard_map/ppermute | solution.py:940
  311.2 44.8 %collective-permute-start.43 = (bf16[512,768]{1,0:T(8,128)(2,1)}, bf16[512,768]{1,0:T(8,128)(2,1)}, u32[]{:S(2)}, u32[]{:S(2)}) collective-permute-start(bf16[512,768]{1,0:T(8,128)(2,1)} %get-tuple-element.314), channel_id=1, source_target_pairs={{0,1},{1,0},{2,3},{3,2},{4,5},{5,4},{6,7},{7,6},{8,9},{9,8},{10,11... | collective-permute-start | bytes 2359304 | tf_op jit(solution)/shard_map/ppermute | solution.py:935
  312.4 43.6 %collective-permute-start.44 = (bf16[512,768]{1,0:T(8,128)(2,1)}, bf16[512,768]{1,0:T(8,128)(2,1)}, u32[]{:S(2)}, u32[]{:S(2)}) collective-permute-start(bf16[512,768]{1,0:T(8,128)(2,1)} %get-tuple-element.315), channel_id=1, source_target_pairs={{0,1},{1,0},{2,3},{3,2},{4,5},{5,4},{6,7},{7,6},{8,9},{9,8},{10,11... | collective-permute-start | bytes 2359304 | tf_op jit(solution)/shard_map/ppermute | solution.py:935
  313.2 50.4 %collective-permute-start.41 = (bf16[1,192,1536]{2,1,0:T(8,128)(2,1)}, bf16[1,192,1536]{2,1,0:T(8,128)(2,1)}, u32[]{:S(2)}, u32[]{:S(2)}) collective-permute-start(bf16[1,192,1536]{2,1,0:T(8,128)(2,1)} %get-tuple-element.327), channel_id=1, source_target_pairs={{0,16},{4,20},{8,24},{12,28},{16,0},{20,4},{24,8},{28,12},{1,17},{... | collective-permute-start | bytes 1769480 | tf_op jit(solution)/shard_map/ppermute | solution.py:940
  363.1 10.8 %collective-permute-start.47 = (bf16[512,768]{1,0:T(8,128)(2,1)}, bf16[512,768]{1,0:T(8,128)(2,1)}, u32[]{:S(2)}, u32[]{:S(2)}) collective-permute-start(bf16[512,768]{1,0:T(8,128)(2,1)} %get-tuple-element.336.far_ref), channel_id=1, source_target_pairs={{0,2},{2,0},{1,3},{3,1},{4,6},{6,4},{5,7},{7,5},{8,10},{10,8},{9,1... | collective-permute-start | bytes 2359304 | tf_op jit(solution)/shard_map/ppermute | solution.py:935
  363.1 10.8 %collective-permute-start.46 = (bf16[512,768]{1,0:T(8,128)(2,1)}, bf16[512,768]{1,0:T(8,128)(2,1)S(1)}, u32[]{:S(2)}, u32[]{:S(2)}) collective-permute-start(bf16[512,768]{1,0:T(8,128)(2,1)} %get-tuple-element.335.own_ref.d_hidden_ref), channel_id=1, source_target_pairs={{0,2},{2,0},{1,3},{3,1},{4,6},{6,4},{5,7},{7,5},{8,10},{10,8},{9,1... | collective-permute-start | bytes 2359304 | tf_op jit(solution)/shard_map/ppermute | solution.py:935
  363.6 33.9 %collective-permute-start.48 = (bf16[1,96,3072]{2,1,0:T(8,128)(2,1)}, bf16[1,96,3072]{2,1,0:T(8,128)(2,1)}, u32[]{:S(2)}, u32[]{:S(2)}) collective-permute-start(bf16[1,96,3072]{2,1,0:T(8,128)(2,1)} %get-tuple-element.344), channel_id=1, source_target_pairs={{0,16},{4,20},{8,24},{12,28},{16,0},{20,4},{24,8},{28,12},{1,17},{... | collective-permute-start | bytes 1769480 | tf_op jit(solution)/shard_map/ppermute | solution.py:940
  372.4 73.1 %collective-permute-start.45 = (bf16[8,96,1536]{2,1,0:T(8,128)(2,1)}, bf16[8,96,1536]{2,1,0:T(8,128)(2,1)S(1)}, u32[]{:S(2)}, u32[]{:S(2)}) collective-permute-start(bf16[8,96,1536]{2,1,0:T(8,128)(2,1)} %get-tuple-element.340), channel_id=1, source_target_pairs={{0,4},{4,0},{8,12},{12,8},{16,20},{20,16},{24,28},{28,24},{1,5},{5... | collective-permute-start | bytes 7077896 | tf_op jit(solution)/shard_map/ppermute | solution.py:940
  394.1 30.5 %collective-permute-start.49 = (bf16[1024,384]{1,0:T(8,128)(2,1)}, bf16[1024,384]{1,0:T(8,128)(2,1)}, u32[]{:S(2)}, u32[]{:S(2)}) collective-permute-start(bf16[1024,384]{1,0:T(8,128)(2,1)} %get-tuple-element.347.query_ref), channel_id=1, source_target_pairs={{0,1},{1,0},{2,3},{3,2},{4,5},{5,4},{6,7},{7,6},{8,9},{9,8},{10,11... | collective-permute-start | bytes 2359304 | tf_op jit(solution)/shard_map/ppermute | solution.py:935
  396.6 27.9 %collective-permute-start.50 = (bf16[1024,256]{1,0:T(8,128)(2,1)S(1)}, bf16[1024,256]{1,0:T(8,128)(2,1)S(1)}, u32[]{:S(2)}, u32[]{:S(2)}) collective-permute-start(bf16[1024,256]{1,0:T(8,128)(2,1)S(1)} %convert_element_type.82), channel_id=1, source_target_pairs={{0,1},{1,0},{2,3},{3,2},{4,5},{5,4},{6,7},{7,6},{8,9},{9,8},{10,11... | collective-permute-start | bytes 1572872 | tf_op jit(solution)/shard_map/ppermute | solution.py:935
  397.5 39.7 %collective-permute-start.51 = (bf16[2,96,3072]{2,1,0:T(8,128)(2,1)}, bf16[2,96,3072]{2,1,0:T(8,128)(2,1)S(1)}, u32[]{:S(2)}, u32[]{:S(2)}) collective-permute-start(bf16[2,96,3072]{2,1,0:T(8,128)(2,1)} %get-tuple-element.352), channel_id=1, source_target_pairs={{0,8},{4,12},{8,0},{12,4},{16,24},{20,28},{24,16},{28,20},{1,9},{5... | collective-permute-start | bytes 3538952 | tf_op jit(solution)/shard_map/ppermute | solution.py:940
  452.3 8.6 %collective-permute-start.54 = (bf16[512,1536]{1,0:T(8,128)(2,1)}, bf16[512,1536]{1,0:T(8,128)(2,1)S(1)}, u32[]{:S(2)}, u32[]{:S(2)}) collective-permute-start(bf16[512,1536]{1,0:T(8,128)(2,1)} %get-tuple-element.362), channel_id=1, source_target_pairs={{0,2},{2,0},{1,3},{3,1},{4,6},{6,4},{5,7},{7,5},{8,10},{10,8},{9,1... | collective-permute-start | bytes 4718600 | tf_op jit(solution)/shard_map/ppermute | solution.py:935
  452.7 32.7 %collective-permute-start.58 = (bf16[4,96,1792]{2,1,0:T(8,128)(2,1)}, bf16[4,96,1792]{2,1,0:T(8,128)(2,1)}, u32[]{:S(2)}, u32[]{:S(2)}) collective-permute-start(bf16[4,96,1792]{2,1,0:T(8,128)(2,1)} %get-tuple-element.367), channel_id=1, source_target_pairs={{0,4},{4,0},{8,12},{12,8},{16,20},{20,16},{24,28},{28,24},{1,5},{5... | collective-permute-start | bytes 4128776 | tf_op jit(solution)/shard_map/ppermute | solution.py:940
  457.0 32.3 %collective-permute-start.63 = (bf16[1,96,3072]{2,1,0:T(8,128)(2,1)}, bf16[1,96,3072]{2,1,0:T(8,128)(2,1)}, u32[]{:S(2)}, u32[]{:S(2)}) collective-permute-start(bf16[1,96,3072]{2,1,0:T(8,128)(2,1)} %get-tuple-element.378), channel_id=1, source_target_pairs={{0,16},{4,20},{8,24},{12,28},{16,0},{20,4},{24,8},{28,12},{1,17},{... | collective-permute-start | bytes 1769480 | tf_op jit(solution)/shard_map/ppermute | solution.py:940
  459.2 47.3 %collective-permute-start.56 = (f32[512]{0:T(512)S(1)}, f32[512]{0:T(512)S(1)}, u32[]{:S(2)}, u32[]{:S(2)}) collective-permute-start(f32[512]{0:T(512)S(1)} %get-tuple-element.405), channel_id=1, source_target_pairs={{0,1},{1,0},{2,3},{3,2},{4,5},{5,4},{6,7},{7,6},{8,9},{9,8},{10,11... | collective-permute-start | bytes 6152 | tf_op jit(solution)/shard_map/ppermute | solution.py:935
  460.0 29.3 %collective-permute-start.57 = (f32[2560]{0:T(1024)S(1)}, f32[2560]{0:T(1024)S(1)}, u32[]{:S(2)}, u32[]{:S(2)}) collective-permute-start(f32[2560]{0:T(1024)S(1)} %pad_maximum_fusion.16), channel_id=1, source_target_pairs={{0,4},{4,0},{8,12},{12,8},{16,20},{20,16},{24,28},{28,24},{1,5},{5... | collective-permute-start | bytes 30728 | tf_op jit(solution)/shard_map/ppermute | solution.py:940
  460.9 39.9 %collective-permute-start.62 = (bf16[4,96,1536]{2,1,0:T(8,128)(2,1)}, bf16[4,96,1536]{2,1,0:T(8,128)(2,1)}, u32[]{:S(2)}, u32[]{:S(2)}) collective-permute-start(bf16[4,96,1536]{2,1,0:T(8,128)(2,1)} %get-tuple-element.376), channel_id=1, source_target_pairs={{0,8},{4,12},{8,0},{12,4},{16,24},{20,28},{24,16},{28,20},{1,9},{5... | collective-permute-start | bytes 3538952 | tf_op jit(solution)/shard_map/ppermute | solution.py:940
  485.4 43.1 %collective-permute-start.60 = (bf16[4,96,1536]{2,1,0:T(8,128)(2,1)}, bf16[4,96,1536]{2,1,0:T(8,128)(2,1)}, u32[]{:S(2)}, u32[]{:S(2)}) collective-permute-start(bf16[4,96,1536]{2,1,0:T(8,128)(2,1)} %get-tuple-element.372), channel_id=1, source_target_pairs={{0,4},{4,0},{8,12},{12,8},{16,20},{20,16},{24,28},{28,24},{1,5},{5... | collective-permute-start | bytes 3538952 | tf_op jit(solution)/shard_map/ppermute | solution.py:940
  489.3 35.3 %collective-permute-start.61 = (bf16[2,96,1792]{2,1,0:T(8,128)(2,1)}, bf16[2,96,1792]{2,1,0:T(8,128)(2,1)}, u32[]{:S(2)}, u32[]{:S(2)}) collective-permute-start(bf16[2,96,1792]{2,1,0:T(8,128)(2,1)} %get-tuple-element.374), channel_id=1, source_target_pairs={{0,8},{4,12},{8,0},{12,4},{16,24},{20,28},{24,16},{28,20},{1,9},{5... | collective-permute-start | bytes 2064392 | tf_op jit(solution)/shard_map/ppermute | solution.py:940
  504.0 28.8 %collective-permute-start.67 = (bf16[2,96,1536]{2,1,0:T(8,128)(2,1)}, bf16[2,96,1536]{2,1,0:T(8,128)(2,1)}, u32[]{:S(2)}, u32[]{:S(2)}) collective-permute-start(bf16[2,96,1536]{2,1,0:T(8,128)(2,1)} %get-tuple-element.392), channel_id=1, source_target_pairs={{0,16},{4,20},{8,24},{12,28},{16,0},{20,4},{24,8},{28,12},{1,17},{... | collective-permute-start | bytes 1769480 | tf_op jit(solution)/shard_map/ppermute | solution.py:940
  506.5 26.3 %collective-permute-start.59 = (f32[2560]{0:T(1024)S(1)}, f32[2560]{0:T(1024)S(1)}, u32[]{:S(2)}, u32[]{:S(2)}) collective-permute-start(f32[2560]{0:T(1024)S(1)} %add.128), channel_id=1, source_target_pairs={{0,8},{4,12},{8,0},{12,4},{16,24},{20,28},{24,16},{28,20},{1,9},{5... | collective-permute-start | bytes 30728 | tf_op jit(solution)/shard_map/ppermute | solution.py:940
  512.7 24.6 %collective-permute-start.55 = (bf16[512,768]{1,0:T(8,128)(2,1)}, bf16[512,768]{1,0:T(8,128)(2,1)}, u32[]{:S(2)}, u32[]{:S(2)}) collective-permute-start(bf16[512,768]{1,0:T(8,128)(2,1)} %slice.196), channel_id=1, source_target_pairs={{0,1},{1,0},{2,3},{3,2},{4,5},{5,4},{6,7},{7,6},{8,9},{9,8},{10,11... | collective-permute-start | bytes 2359304 | tf_op jit(solution)/shard_map/ppermute | solution.py:935
  524.6 56.4 %collective-permute-start.71 = (bf16[192,768]{1,0:T(8,128)(2,1)}, bf16[192,768]{1,0:T(8,128)(2,1)}, u32[]{:S(2)}, u32[]{:S(2)}) collective-permute-start(bf16[192,768]{1,0:T(8,128)(2,1)} %slice.197), channel_id=1, source_target_pairs={{0,1},{1,0},{2,3},{3,2},{4,5},{5,4},{6,7},{7,6},{8,9},{9,8},{10,11... | collective-permute-start | bytes 884744 | tf_op jit(solution)/shard_map/ppermute | solution.py:935
  528.4 21.1 %collective-permute-start.68 = (bf16[96,3072]{1,0:T(8,128)(2,1)}, bf16[96,3072]{1,0:T(8,128)(2,1)}, u32[]{:S(2)}, u32[]{:S(2)}) collective-permute-start(bf16[96,3072]{1,0:T(8,128)(2,1)} %bitcast.71), channel_id=1, source_target_pairs={{0,1},{1,0},{2,3},{3,2},{4,5},{5,4},{6,7},{7,6},{8,9},{9,8},{10,11... | collective-permute-start | bytes 1769480 | tf_op jit(solution)/shard_map/ppermute | solution.py:935
  534.1 28.5 %collective-permute-start.65 = (bf16[1,96,1792]{2,1,0:T(8,128)(2,1)}, bf16[1,96,1792]{2,1,0:T(8,128)(2,1)S(1)}, u32[]{:S(2)}, u32[]{:S(2)}) collective-permute-start(bf16[1,96,1792]{2,1,0:T(8,128)(2,1)} %get-tuple-element.388), channel_id=1, source_target_pairs={{0,16},{4,20},{8,24},{12,28},{16,0},{20,4},{24,8},{28,12},{1,17},{... | collective-permute-start | bytes 1032200 | tf_op jit(solution)/shard_map/ppermute | solution.py:940
  534.1 24.8 %collective-permute-start.66 = (bf16[2,96,1536]{2,1,0:T(8,128)(2,1)}, bf16[2,96,1536]{2,1,0:T(8,128)(2,1)S(1)}, u32[]{:S(2)}, u32[]{:S(2)}) collective-permute-start(bf16[2,96,1536]{2,1,0:T(8,128)(2,1)} %get-tuple-element.390), channel_id=1, source_target_pairs={{0,8},{4,12},{8,0},{12,4},{16,24},{20,28},{24,16},{28,20},{1,9},{5... | collective-permute-start | bytes 1769480 | tf_op jit(solution)/shard_map/ppermute | solution.py:940
  537.3 16.0 %collective-permute-start.69 = (bf16[96,1536]{1,0:T(8,128)(2,1)S(1)}, bf16[96,1536]{1,0:T(8,128)(2,1)}, u32[]{:S(2)}, u32[]{:S(2)}) collective-permute-start(bf16[96,1536]{1,0:T(8,128)(2,1)S(1)} %fusion.9), channel_id=1, source_target_pairs={{0,1},{1,0},{2,3},{3,2},{4,5},{5,4},{6,7},{7,6},{8,9},{9,8},{10,11... | collective-permute-start | bytes 884744 | tf_op jit(solution)/shard_map/ppermute | solution.py:935
  549.6 14.2 %collective-permute-start.64 = (f32[2560]{0:T(1024)S(1)}, f32[2560]{0:T(1024)S(1)}, u32[]{:S(2)}, u32[]{:S(2)}) collective-permute-start(f32[2560]{0:T(1024)S(1)} %add.130), channel_id=1, source_target_pairs={{0,16},{4,20},{8,24},{12,28},{16,0},{20,4},{24,8},{28,12},{1,17},{... | collective-permute-start | bytes 30728 | tf_op jit(solution)/shard_map/ppermute | solution.py:940
  562.6 13.0 %collective-permute-start.70 = (bf16[1,96,1536]{2,1,0:T(8,128)(2,1)}, bf16[1,96,1536]{2,1,0:T(8,128)(2,1)S(1)}, u32[]{:S(2)}, u32[]{:S(2)}) collective-permute-start(bf16[1,96,1536]{2,1,0:T(8,128)(2,1)} %get-tuple-element.401), channel_id=1, source_target_pairs={{0,16},{4,20},{8,24},{12,28},{16,0},{20,4},{24,8},{28,12},{1,17},{... | collective-permute-start | bytes 884744 | tf_op jit(solution)/shard_map/ppermute | solution.py:940
  (57 other events, 243.1 us)

commit v4 on v3

--- a/solution.py
+++ b/solution.py
@@ -66,17 +66,17 @@
     return ((0, first, first), (first, segment - first, padded - first))
 
 
-def units_kernel(count, segment, padded, halves, table, block_ref, *refs):
+def units_kernel(count, segment, padded, outs, table, block_ref, *refs):
     rows = block_ref.shape[0]
-    out_refs = refs[-len(halves) :]
+    out_refs = refs[-len(outs) :]
 
     def write(side):
-        for out_ref, half in zip(out_refs, halves):
+        for out_ref, (other, half) in zip(out_refs, outs):
             begin, width, full = halves_of(segment, padded)[half]
             parts = []
             for kind in range(2):
                 for k in range(count):
-                    start = ((kind * count + k) * 2 + side) * segment + begin
+                    start = ((kind * count + k) * 2 + (side ^ other)) * segment + begin
                     parts.append(block_ref[:, start : start + width])
                     if width < full:
                         parts.append(jnp.zeros((rows, full - width), block_ref.dtype))
@@ -91,17 +91,17 @@
         write(1)
 
 
-def unit_columns(block, side, slots, count, rows, padded, halves=(0, 1), places=None, depth=None, begun=None):
+def unit_columns(block, side, slots, count, rows, padded, outs, places=None, depth=None, begun=None):
     columns = block.shape[1]
     segment = columns // (4 * count)
-    units = [2 * count * halves_of(segment, padded)[half][2] for half in halves]
+    units = [2 * count * halves_of(segment, padded)[half][2] for _, half in outs]
     steps = slots.shape[0]
     depth = steps if depth is None else depth
     places = jnp.arange(steps) if places is None else places
     begun = [] if begun is None else begun
     table = jnp.concatenate([side.reshape(1), slots, places]).astype(jnp.int32)
     return pl.pallas_call(
-        functools.partial(units_kernel, count, segment, padded, halves),
+        functools.partial(units_kernel, count, segment, padded, outs),
         grid_spec=pltpu.PrefetchScalarGridSpec(
             num_scalar_prefetch=1,
             grid=(steps,),
@@ -307,7 +307,7 @@
     return exponent / jnp.sum(exponent, axis=1, keepdims=True)
 
 
-def attend_kernel(block, query_ref, key_ref, value_ref, seg_col_ref, seg_row_ref, out_ref, last_ref):
+def attend_kernel(block, query_ref, key_ref, value_ref, seg_col_ref, seg_row_ref, all_ref, out_ref, last_ref):
     last = pl.program_id(0) == pl.num_programs(0) - 1
     for start in range(0, query_ref.shape[0], block):
         stop = start + block
@@ -315,6 +315,7 @@
             query_ref[start:stop], key_ref[:stop], seg_col_ref[start:stop], seg_row_ref[:, :stop], start, stop
         )
         out = dot(probs.astype(BF16), value_ref[:stop], 1, 0).astype(BF16)
+        all_ref[start:stop] = out
 
         @pl.when(last)
         def _():
@@ -334,28 +335,30 @@
         functools.partial(attend_kernel, 256),
         grid=(width // HEAD_DIM,),
         in_specs=[head, shared, shared, whole((seq_len, 1)), whole((1, seq_len))],
-        out_specs=[pl.BlockSpec((seq_len, HEAD_DIM), lambda h: (0, jnp.minimum(h, heads - 2))), shared],
+        out_specs=[head, pl.BlockSpec((seq_len, HEAD_DIM), lambda h: (0, jnp.minimum(h, heads - 2))), shared],
         out_shape=[
+            jax.ShapeDtypeStruct((seq_len, width), BF16),
             jax.ShapeDtypeStruct((seq_len, width - HEAD_DIM), BF16),
             jax.ShapeDtypeStruct((seq_len, HEAD_DIM), BF16),
         ],
         compiler_params=params("arbitrary"),
-        cost_estimate=cost(6 * seq_len * seq_len * width, 8 * seq_len * width),
+        cost_estimate=cost(12 * seq_len * seq_len * width, 8 * seq_len * width),
         name="attend",
     )(query, key, value, seg_col, seg_row)
 
 
 def attend_back_kernel(
-    block, table, query_ref, key_ref, value_ref, seg_col_ref, seg_row_ref, own_ref, far_ref, near_ref, far_near_ref,
-    weight_ref, far_top_ref, far_bottom_ref, cosine_ref, sine_ref, sent_ref, key_value_ref,
+    block, begun, ends, table, query_ref, key_ref, value_ref, seg_col_ref, seg_row_ref, own_ref, far_ref, near_ref, far_near_ref,
+    weight_ref, far_top_ref, far_bottom_ref, cosine_ref, sine_ref, *refs
 ):
+    sent_ref, key_value_ref = refs[-2:]
     scaling = HEAD_DIM ** (-0.5)
     own_rows = own_ref.shape[0]
     far_weight = jnp.where(table[COL] == 0, far_top_ref[...], far_bottom_ref[...])
 
     @pl.when(pl.program_id(0) == 0)
     def _():
-        key_value_ref[...] = jnp.zeros_like(key_value_ref)
+        key_value_ref[...] = refs[0][...] if begun else jnp.zeros_like(key_value_ref)
 
     for start in range(0, query_ref.shape[0], block):
         stop = start + block
@@ -379,47 +382,55 @@
         key_value_ref[:stop, :HEAD_DIM] += dot(d_scores, query, 0, 0) * scaling
         key_value_ref[:stop, HEAD_DIM:] += dot(probs.astype(BF16), grad, 0, 0)
 
-    @pl.when(pl.program_id(0) == pl.num_programs(0) - 1)
-    def _():
-        d_key = key_value_ref[:, :HEAD_DIM]
-        turned = pltpu.roll(d_key * sine_ref[...], HEAD_DIM // 2, 1)
-        key_value_ref[:, :HEAD_DIM] = d_key * cosine_ref[...] + turned
-
-
-def attend_back(table, query, key, value, seg_col, seg_row, d_hidden, weight, far_weights, cosine, sine):
+    if ends:
+
+        @pl.when(pl.program_id(0) == pl.num_programs(0) - 1)
+        def _():
+            d_key = key_value_ref[:, :HEAD_DIM]
+            turned = pltpu.roll(d_key * sine_ref[...], HEAD_DIM // 2, 1)
+            key_value_ref[:, :HEAD_DIM] = d_key * cosine_ref[...] + turned
+
+
+def attend_back(
+    table, query, key, value, seg_col, seg_row, d_hidden, weight, far_weights, cosine, sine, first, count, begun=None
+):
     seq_len, width = query.shape
     features = weight.shape[1]
     heads = width // HEAD_DIM
-    head = pl.BlockSpec((seq_len, HEAD_DIM), lambda h, t: (0, h))
-    rows = pl.BlockSpec((HEAD_DIM, features), lambda h, t: (heads * t[COL] + h, 0))
-    far_rows = pl.BlockSpec((HEAD_DIM, features), lambda h, t: (h, 0))
+    head = pl.BlockSpec((seq_len, HEAD_DIM), lambda h, t: (0, first + h))
+    rows = pl.BlockSpec((HEAD_DIM, features), lambda h, t: (heads * t[COL] + first + h, 0))
+    far_rows = pl.BlockSpec((HEAD_DIM, features), lambda h, t: (first + h, 0))
     shared = whole((seq_len, HEAD_DIM))
-    return pl.pallas_call(
-        functools.partial(attend_back_kernel, 256),
-        grid_spec=pltpu.PrefetchScalarGridSpec(
-            num_scalar_prefetch=1,
-            grid=(heads,),
+    key_value = whole((seq_len, 2 * HEAD_DIM))
+    more = [] if begun is None else [begun]
+    return pl.pallas_call(
+        functools.partial(attend_back_kernel, 256, begun is not None, first + count == heads),
+        grid_spec=pltpu.PrefetchScalarGridSpec(
+            num_scalar_prefetch=1,
+            grid=(count,),
             in_specs=[
                 head, shared, shared, whole((seq_len, 1)), whole((1, seq_len)),
                 *[whole(part.shape) for part in d_hidden], rows, far_rows, far_rows, shared, shared,
+                *[key_value] * len(more),
             ],
-            out_specs=[head, whole((seq_len, 2 * HEAD_DIM))],
+            out_specs=[pl.BlockSpec((seq_len, HEAD_DIM), lambda h, t: (0, h)), key_value],
         ),
         out_shape=[
-            jax.ShapeDtypeStruct(query.shape, BF16),
+            jax.ShapeDtypeStruct((seq_len, count * HEAD_DIM), BF16),
             jax.ShapeDtypeStruct((seq_len, 2 * HEAD_DIM), F32),
         ],
         compiler_params=params("arbitrary"),
-        cost_estimate=cost(12 * seq_len * seq_len * width, 12 * seq_len * width),
+        cost_estimate=cost(24 * seq_len * seq_len * count * HEAD_DIM, 12 * seq_len * width),
         name="attend_back",
-    )(table, query, key, value, seg_col, seg_row, *d_hidden, weight, *far_weights, cosine, sine)
+    )(table, query, key, value, seg_col, seg_row, *d_hidden, weight, *far_weights, cosine, sine, *more)
 
 
 def residual_kernel(table, stream_ref, *refs):
-    pieces, weights, (gain_ref, hidden_ref, normed_ref, scale_ref, group_ref) = refs[:8], refs[8:14], refs[14:]
+    pieces, weights, (gain_ref, hidden_ref, normed_ref, scale_ref, group_ref) = refs[:6], refs[6:12], refs[12:]
     first = table[COL] == 0
-    own, far, near, near_far = (
-        jnp.concatenate([pieces[2 * index][...], pieces[2 * index + 1][...]], axis=1) for index in range(4)
+    own, near = pieces[0][...], pieces[1][...]
+    far, near_far = (
+        jnp.concatenate([pieces[index][...], pieces[index + 1][...]], axis=1) for index in (2, 4)
     )
     part = own.shape[1]
     group = [jnp.where(first, own, far), jnp.where(first, far, own)]
@@ -448,8 +459,8 @@
 
 def residual(table, stream, attended, own_weight, near_weight, far_weights, near_far_weights, gain):
     seq_len, width = stream.shape
-    pieces = [piece for pair in attended for piece in pair]
-    part = attended[0][0].shape[1] + attended[0][1].shape[1]
+    pieces = attended
+    part = attended[0].shape[1]
     weights = [own_weight, near_weight, *far_weights, *near_far_weights]
     block = min(256, seq_len)
 
@@ -566,26 +577,26 @@
 def down_kernel(counts, table, *refs):
     halves = len(counts)
     act_refs, own_refs, refs = refs[:halves], refs[halves : 2 * halves], refs[2 * halves :]
-    own_out_ref, other_out_ref, total_scr = refs[-3:]
+    own_out_ref, *other_refs, total_scr = refs[-4:]
     part_refs = []
     for parts in counts:
         part_refs.append(refs[:parts])
         refs = refs[parts:]
 
-    def write(weights):
+    def write(weights, other_ref):
         total_scr[...] = sum(dot(act_ref[...], weight, 1, 0) for act_ref, weight in zip(act_refs, weights))
         rows = own_out_ref.shape[0]
         own_out_ref[...] = total_scr[pl.ds(pl.multiple_of(table[ROW] * rows, rows), rows)]
         other = pl.multiple_of((1 - table[ROW]) * rows, rows)
-        other_out_ref[...] = total_scr[pl.ds(other, rows)].astype(BF16)
+        other_ref[...] = total_scr[pl.ds(other, rows)].astype(BF16)
 
     @pl.when(pl.program_id(0) == 0)
     def _():
-        write([own_ref[...] for own_ref in own_refs])
+        write([own_ref[...] for own_ref in own_refs], other_refs[0])
 
     @pl.when(pl.program_id(0) == 1)
     def _():
-        write([ordered(table, parts) for parts in part_refs])
+        write([ordered(table, parts) for parts in part_refs], other_refs[1])
 
 
 def down(table, acts, own, far_parts):
@@ -599,12 +610,13 @@
             num_scalar_prefetch=1,
             grid=(2,),
             in_specs=[whole(array.shape) for array in arrays],
-            out_specs=[pl.BlockSpec((seq_len // 2, features), lambda j, t: (0, j))] * 2,
+            out_specs=[pl.BlockSpec((seq_len // 2, features), lambda j, t: (0, j))]
+            + [whole((seq_len // 2, features))] * 2,
             scratch_shapes=[pltpu.VMEM((seq_len, features), F32)],
         ),
         out_shape=[
             jax.ShapeDtypeStruct((seq_len // 2, 2 * features), F32),
-            jax.ShapeDtypeStruct((seq_len // 2, 2 * features), BF16),
+            *[jax.ShapeDtypeStruct((seq_len // 2, features), BF16)] * 2,
         ],
         compiler_params=params("arbitrary"),
         cost_estimate=cost(4 * seq_len * units * features, 8 * seq_len * features + 8 * units * (seq_len + features)),
@@ -701,8 +713,7 @@
     for parts in counts:
         part_refs.append(refs[:parts])
         refs = refs[parts:]
-    own_out_ref, other_refs, far_scrs, total_scr = refs[0], refs[1:4], refs[4:-1], refs[-1]
-    share = 2 * steps // 3
+    own_out_ref, other_refs, far_scrs, total_scr = refs[0], refs[1:3], refs[3:-1], refs[-1]
 
     @pl.when(pl.program_id(0) == 0)
     def _():
@@ -724,7 +735,7 @@
         other = pl.multiple_of((1 - table[ROW]) * rows, rows)
         for index, other_ref in enumerate(other_refs):
 
-            @pl.when(pl.program_id(0) // share == index)
+            @pl.when(pl.program_id(0) // steps == index)
             def _():
                 other_ref[...] = total_scr[pl.ds(other, rows)].astype(BF16)
 
@@ -746,11 +757,10 @@
     steps = features // tile
     halves = len(own)
     parts = [piece for half in far_parts for piece in half]
-    share = 2 * steps // 3
-
-    def third(index):
+
+    def side(index):
         return pl.BlockSpec(
-            (seq_len // 2, tile), lambda j, t: (0, jnp.clip(j - share * index, 0, share - 1))
+            (seq_len // 2, tile), lambda j, t: (0, jnp.clip(j - steps * index, 0, steps - 1))
         )
 
     own_specs = [
@@ -765,13 +775,13 @@
             + own_specs
             + [whole(piece.shape) for piece in parts],
             out_specs=[pl.BlockSpec((seq_len // 2, tile), lambda j, t: (0, j))]
-            + [third(index) for index in range(3)],
+            + [side(index) for index in range(2)],
             scratch_shapes=[pltpu.VMEM((features, 2 * wide), BF16) for wide in units]
             + [pltpu.VMEM((seq_len, tile), F32)],
         ),
         out_shape=[
             jax.ShapeDtypeStruct((seq_len // 2, 2 * features), F32),
-            *[jax.ShapeDtypeStruct((seq_len // 2, 2 * features // 3), BF16)] * 3,
+            *[jax.ShapeDtypeStruct((seq_len // 2, features), BF16)] * 2,
         ],
         compiler_params=params("arbitrary"),
         cost_estimate=cost(
@@ -865,15 +875,15 @@
 
 
 def project_back_kernel(
-    count, bit, table, query_ref, key_value_ref, arrived_query_ref, arrived_ref, normed_ref, weight_ref, group_ref,
+    count, bit, table, query_ref, key_value_ref, arrived_ref, normed_ref, weight_ref, group_ref,
     d_hidden_ref, d_hidden_near_ref, sent_ref, kept_ref, own_ref, other_ref, bias_ref, d_scr, total_scr, hidden_scr, out_scr,
 ):
     first = table[COL] == 0
     query_width = query_ref.shape[1]
-    own, far = query_ref[...], arrived_query_ref[...]
+    own, far = query_ref[...], arrived_ref[:, :query_width]
     d_scr[:, :query_width] = jnp.where(first, own, far)
     d_scr[:, query_width : 2 * query_width] = jnp.where(first, far, own)
-    d_key_value = key_value_ref[...] + arrived_ref[...].astype(F32)
+    d_key_value = key_value_ref[...] + arrived_ref[:, query_width:].astype(F32)
     d_scr[:, 2 * query_width :] = d_key_value.astype(BF16)
     d_projected = d_scr[...]
     bias_ref[...] = jnp.sum(d_projected.astype(F32), axis=0, keepdims=True)
@@ -897,11 +907,11 @@
         out_ref[...] = dot(d_half, weight_ref[...], 1, 1).astype(out_ref.dtype)
 
 
-def project_back(table, d_query, d_key_value, arrived_query, arrived, normed, weight, group, d_hidden, near, count, bit):
+def project_back(table, d_query, d_key_value, arrived, normed, weight, group, d_hidden, near, count, bit):
     seq_len = d_query.shape[0]
     width, columns = weight.shape
     rows = width // count
-    arrays = (d_query, d_key_value, arrived_query, arrived, normed, weight, group, d_hidden, near)
+    arrays = (d_query, d_key_value, arrived, normed, weight, group, d_hidden, near)
     terms = (count // 2, rows, columns + d_hidden.shape[1])
     return pl.pallas_call(
         functools.partial(project_back_kernel, count, bit),
@@ -976,8 +986,11 @@
         self.low, self.high = rank % 2, rank // 2 % 2
 
     def first_round(self, line):
-        part = line.step(self.part)
-        self.sent = lax.optimization_barrier((part[0], part[1]))
+        if isinstance(self.part, list):
+            self.sent = [line.step(slot) for slot in self.part]
+        else:
+            part = line.step(self.part)
+            self.sent = lax.optimization_barrier([part[0], part[1]])
         line.mark(*self.sent)
         self.arriving = dp_swap(self.sent[0], 0), dp_swap(self.sent[1], 1)
 
@@ -1064,11 +1077,14 @@
 
     def slot_pair(array):
         parts = array.reshape((8, array.shape[0] // 8) + array.shape[1:])
-        return jnp.stack([pick(parts, slots[0], 0), pick(parts, slots[1], 0)])
+        return [pick(parts, slot, 0) for slot in slots]
+
+    def swap_pair(pair):
+        return [swap(slot, "col") for slot in pair]
 
     table = jnp.stack([row, col] + [(rank >> bit) & 1 for bit in range(bits)]).astype(jnp.int32)
     line = Line()
-    pair_first, line_first = [0, 1, 2], [1, 2, 0]
+    pair_first, line_first = [0, 1, 2], [1, 0, 2]
 
     def qkv_columns(side):
         heads = lax.dynamic_slice_in_dim(qkv_block, side * query_width, query_width, 1)
@@ -1077,7 +1093,8 @@
     gains = jnp.stack([first_gain, second_gain])
     gains = jnp.concatenate([gains, swap(gains, "col")], axis=1)
     early_send = slot_pair(jnp.concatenate([qkv_columns(1 - col), out_block], axis=1))
-    early_quad = Quad(swap(early_send, "col"), rank)
+    early_send = lax.optimization_barrier(early_send)
+    early_quad = Quad(swap_pair(early_send), rank)
     qkv_own = qkv_columns(col)
     qkv_width = qkv_own.shape[1]
     bias = qkv_bias[0]
@@ -1086,12 +1103,13 @@
     )
 
     (send,) = unit_columns(
-        after(gate_up_block, early_send, gains), 1 - col, slots, count, slot_rows, padded, (0,)
+        after(gate_up_block, *early_send, gains), 1 - col, slots, count, slot_rows, padded, ((0, 0),)
     )
     line.mark(send)
 
     near = swap(block_input, "row")
-    far = swap(line.step(block_input), "col")
+    out_near = swap(out_block, "row")
+    far = swap(after(block_input, *early_send), "col")
 
     position_index = jnp.arange(seq_len, dtype=jnp.int32)
     doc_first = jnp.concatenate([jnp.ones((1,), jnp.bool_), segment_ids[1:] != segment_ids[:-1]])
@@ -1104,34 +1122,33 @@
     seg_col, seg_row = segment_ids[:, None], segment_ids[None, :]
 
     low_slots, high_slots = jnp.arange(4), 4 + jnp.arange(4)
-    gate_up_own = unit_columns(
-        line.step(gate_up_block), col, low_slots, count, slot_rows, padded, (0, 1), low_slots, 8
-    )
-    line.mark(*gate_up_own)
     early_quad.first_round(line)
     gate_up_quad = Quad(swap(line.step(send), "col"), rank)
+    outs = ((0, 0), (0, 1), (1, 1))
+    gate_up_own = unit_columns(
+        line.step(gate_up_block), col, low_slots, count, slot_rows, padded, outs, low_slots, 8
+    )
+    line.mark(*gate_up_own)
     early_far = early_quad.second_round(line)
-    down_own = unit_rows(line.step(down_block), col, jnp.arange(count), count, padded)
-    line.mark(*down_own)
-    down_own = [part.reshape(-1, half_width) for part in down_own]
     far_halves = lax.optimization_barrier((far[: own_rows // 2], far[own_rows // 2 :]))
     far_near = [swap(half, "row") for half in far_halves]
     gate_up_own = unit_columns(
-        line.step(gate_up_block), col, high_slots, count, slot_rows, padded, (0, 1), high_slots, 8, gate_up_own
+        line.step(gate_up_block), col, high_slots, count, slot_rows, padded, outs, high_slots, 8, gate_up_own
     )
     line.mark(*gate_up_own)
-    gate_up_own = [part.reshape(half_width, -1) for part in gate_up_own]
-    out_near = swap(out_block, "row")
+    *gate_up_own, send = [part.reshape(half_width, -1) for part in gate_up_own]
+    out_near = line.step(out_near)
+    line.mark(out_near)
     stream, first_normed, first_scale, query, key, value = project(
         table, line.step(block_input), near, far, far_near, gains[:1], qkv_own, early_far,
         bias_own[None], cosine, sine,
     )
     line.mark(query)
     gate_up_quad.first_round(line)
-    attended = attend(line.step(query), key, value, seg_col, seg_row)
-    line.mark(*attended)
-    attended_far = [swap(part, "col") for part in attended]
-    attended_near = [swap(part, "row") for part in attended]
+    attended, *attended_parts = attend(line.step(query), key, value, seg_col, seg_row)
+    line.mark(attended)
+    attended_far = [swap(part, "col") for part in attended_parts]
+    attended_near = swap(attended, "row")
     gate_up_far = [gate_up_quad.second_round(line)]
     out_far = lax.optimization_barrier(
         laid_out([line.step(part)[:, qkv_width:] for part in early_far], rank)
@@ -1142,17 +1159,16 @@
     send_ranks = (slots[:, None] * share + jnp.arange(share)[None, :]).reshape(-1)
     (down_send,) = unit_rows(line.step(down_block), 1 - col, send_ranks, count, padded, (0,))
     line.mark(down_send)
-    (send,) = unit_columns(
-        line.step(gate_up_block), 1 - col, jnp.arange(8), count, slot_rows, padded, (1,)
-    )
-    line.mark(send)
+    down_own = unit_rows(line.step(down_block), col, jnp.arange(count), count, padded)
+    line.mark(*down_own)
+    down_own = [part.reshape(-1, half_width) for part in down_own]
     attended_far = [line.step(part) for part in attended_far]
     line.mark(*attended_far)
     attended_far_near = [swap(part, "row") for part in attended_far]
     down_quad = Quad(swap(line.step(down_send).reshape(2, -1, half_width), "col"), rank)
     grad_far = swap(line.step(output_grad), "col")
     hidden_one, second_normed, second_scale, attended_group = residual(
-        table, line.step(stream), (attended, attended_far, attended_near, attended_far_near),
+        table, line.step(stream), [attended, attended_near, *attended_far, *attended_far_near],
         out_block, out_near, out_far, out_far_near, gains[1:],
     )
     line.mark(second_normed)
@@ -1169,7 +1185,7 @@
     down_far = [down_quad.second_round(line)]
     grad_near = swap(line.step(output_grad), "row")
     grad_far_near = swap(grad_far, "row")
-    gate_up_far.append([swap(line.step(send).reshape(half_width, -1), "col")])
+    gate_up_far.append([swap(line.step(send), "col")])
     grad_full = join(table, line.step(output_grad), grad_near, grad_far, grad_far_near)
     line.mark(grad_full)
 
@@ -1193,23 +1209,26 @@
     down_far[0] = [line.step(part) for part in down_far[0]]
     line.mark(*down_far[0])
     down_sum0 = Scatter(table, *terms, pair_first, line)
-    d_gate0, d_up0 = activate_back(
-        table, line.step(grad_full), down_own[0], down_far[0], gate_factor0, up_factor0
-    )
-    line.mark(d_gate0)
-    own_sent0, own_kept0, far_sent0, far_kept0 = gate_up_terms(d_gate0, d_up0, pair_first, False)
-    far_sum0 = Scatter(table, far_sent0, far_kept0, pair_first, line)
     begin, width, full = halves_of(segment, padded)[1]
     down_send = pick(line.step(down_block).reshape(count, 2, segment, half_width), 1 - col, 1)
     down_send = jnp.pad(down_send[:, begin : begin + width], ((0, 0), (0, full - width), (0, 0)))
     down_send = lax.optimization_barrier(down_send.reshape(-1, half_width))
     line.mark(down_send)
     down_far.append([swap(down_send, "col")])
+    d_gate0, d_up0 = activate_back(
+        table, line.step(grad_full), down_own[0], down_far[0], gate_factor0, up_factor0
+    )
+    line.mark(d_gate0)
+    own_sent0, own_kept0, far_sent0, far_kept0 = gate_up_terms(d_gate0, d_up0, pair_first, False)
+    far_sum0 = Scatter(table, far_sent0, far_kept0, pair_first, line)
     act1, gate_factor1, up_factor1 = activate(
         table, line.step(second_normed), gate_up_own[1], gate_up_far[1]
     )
     line.mark(act1)
+    down_far[1] = [line.step(down_far[1][0])]
+    line.mark(*down_far[1])
     down_sum0.relay(line)
+    own_sum0 = Scatter(table, own_sent0, own_kept0, pair_first, line)
     d_gate1, d_up1 = activate_back(
         table, line.step(grad_full), down_own[1], down_far[1], gate_factor1, up_factor1
     )
@@ -1221,41 +1240,47 @@
     d_second_near = [swap(part, "row") for part in d_second_other]
     down_terms1 = down_terms(act1, pair_first)
     down_sum0.relay(line)
+    far_sum0.relay(line)
     d_second_chip, *d_second_low = chip_sum(line.step(d_second_own), d_second_near)
     line.mark(*d_second_low)
     d_second_far = [swap(part, "col") for part in d_second_low]
-    far_sum0.relay(line)
-    own_sum0 = Scatter(table, own_sent0, own_kept0, pair_first, line)
     gate_up_terms1 = gate_up_terms(d_gate1, d_up1, pair_first, True)
-    mlp_own, mlp_other = down(table, [line.step(act0), act1], down_own, down_far)
+    mlp_own, mlp_other, mlp_other_far = down(table, [line.step(act0), act1], down_own, down_far)
     line.mark(mlp_other)
     far_sum0.relay(line)
+    own_sum0.relay(line)
+    down_sum0 = down_sum0.finish(line)[0]
+    down_sum1 = Scatter(table, *down_terms1, pair_first, line)
+    mlp_near = swap(line.step(mlp_other_far), "row")
 
     d_hidden, *d_hidden_low, second_gain_part = norm_back(
         table, line.step(d_second_chip), d_second_far, hidden_one, second_scale, grad_full, gains[1:]
     )
     line.mark(*d_hidden_low)
     d_hidden_near = [swap(part, "row") for part in d_hidden_low]
-    down_sum0 = down_sum0.finish(line)[0]
-    own_sum0.relay(line)
+    mlp_sent = mlp_own[:, half_width:] + line.step(mlp_near).astype(F32)
+    mlp_sent = lax.optimization_barrier(mlp_sent.astype(BF16))
+    line.mark(mlp_sent)
+
+    attend_inputs = [key, value, seg_col, seg_row, [*d_hidden_low, *d_hidden_near], out_block, out_far, cosine, sine]
+    d_query, d_key_value = attend_back(table, line.step(query), *attend_inputs, 0, HEADS // 4)
+    d_projected_sent = jnp.concatenate([d_query, d_key_value.astype(BF16)], axis=1)
+    d_projected_sent = lax.optimization_barrier(d_projected_sent)
+    line.mark(d_projected_sent)
+    arrived = swap(d_projected_sent, "col")
+    down_sum1.relay(line)
     gate_up_sum1 = Scatter(table, *gate_up_terms1, pair_first, line)
-
-    d_query, d_key_value = attend_back(
-        table, line.step(query), key, value, seg_col, seg_row, [*d_hidden_low, *d_hidden_near],
-        out_block, out_far, cosine, sine,
-    )
-    d_key_value_low = lax.optimization_barrier(d_key_value.astype(BF16))
-    line.mark(d_query, d_key_value_low)
-    arrived = swap(d_query, "col"), swap(d_key_value_low, "col")
-    far_sum0 = far_sum0.finish(line)[0]
     sent, kept, d_first_own, d_first_other, bias_part = project_back(
-        table, line.step(d_query), d_key_value, *arrived, first_normed, qkv_block, attended_group,
+        table, line.step(d_query), d_key_value, arrived, first_normed, qkv_block, attended_group,
         d_hidden_low[0], d_hidden_near[0], count, 0,
     )
     line.mark(sent)
     heads_sum = Scatter(table, sent, kept, pair_first, line)
     d_first_near = swap(d_first_other, "row")
     own_sum0.relay(line)
+    down_sum1.relay(line)
+    far_sum0 = far_sum0.finish(line)[0]
+    gate_up_sum1.relay(line)
 
     d_first = line.step(d_first_own) + d_first_near.astype(F32)
     stream_own = block_input.astype(F32)
@@ -1268,7 +1293,7 @@
         weighted - stream_own * (first_scale_own * first_scale_own) * (inner / model_width)
     )
 
-    gain_parts = jnp.concatenate([first_gain_part, second_gain_part[0]])
+    gain_parts = line.step(jnp.concatenate([first_gain_part, second_gain_part[0]]))
     gain_parts = lax.optimization_barrier(gain_parts + swap(gain_parts, "row"))
     line.mark(gain_parts)
     small = line.step(jnp.concatenate([gain_parts, bias_part[0]]))
@@ -1278,32 +1303,27 @@
         line.mark(part)
         return part
 
+    heads_sum.relay(line)
+    far_sum0 = swap(line.step(far_sum0.astype(BF16)), "col")
+    down_sum0_far = swap(line.step(down_sum0[:, half_width:].astype(BF16)), "col")
+    own_sum0 = own_sum0.finish(line)[0]
+    down_sum1 = down_sum1.finish(line)[0]
+    mlp_far = swap(line.step(mlp_sent), "col")
+    down_sum1_far = swap(line.step(down_sum1[:, half_width:].astype(BF16)), "col")
     gate_up_sum1.relay(line)
-    down_sum1 = Scatter(table, *down_terms1, pair_first, line)
-    mlp_chip = mlp_own + swap(line.step(mlp_other), "row").astype(F32)
-    mlp_sent = lax.optimization_barrier(mlp_chip[:, half_width:].astype(BF16))
-    line.mark(mlp_sent)
-    mlp_far = swap(mlp_sent, "col").astype(F32)
+    small = dp_step(small, 0)
+    heads_sum.relay(line)
     hidden_own = own_tokens(hidden_one)[:, :half_width]
-    block_output = (hidden_own + (mlp_chip[:, :half_width] + mlp_far)).astype(BF16)
-    down_sum0_far = swap(line.step(down_sum0[:, half_width:].astype(BF16)), "col")
-    far_sum0 = swap(line.step(far_sum0.astype(BF16)), "col")
-    heads_sum.relay(line)
-    small = dp_step(small, 0)
-    own_sum0 = own_sum0.finish(line)[0]
-    gate_up_sum1.relay(line)
-    heads_sum.relay(line)
-    down_sum1.relay(line)
+    mlp_near = swap(line.step(mlp_other), "row")
+    mlp_chip = mlp_own[:, :half_width] + mlp_near.astype(F32)
+    block_output = (hidden_own + (mlp_chip + line.step(mlp_far).astype(F32))).astype(BF16)
     small = dp_step(small, 1)
     own_sum1, far_sum1 = gate_up_sum1.finish(line)
     far_sum1 = swap(line.step(far_sum1.astype(BF16)), "col")
-    down_sum1.relay(line)
-    heads_sum = heads_sum.finish(line)[0]
     for bit in range(2, bits):
         small = dp_step(small, bit)
+    heads_sum = heads_sum.finish(line)[0]
     qkv_sum, out_sum = heads_sum[:, : bias.shape[0]], heads_sum[:, bias.shape[0] :]
-    down_sum1 = down_sum1.finish(line)[0]
-    down_sum1_far = swap(line.step(down_sum1[:, half_width:].astype(BF16)), "col")
     bias_width = bias.shape[0] // count
     bias_grad = lax.dynamic_slice_in_dim(small[model_width:], rank * bias_width, bias_width, 0)
 

time: 589 us -> 563 us (0.956)
  waiting for transfers between devices: 127 us -> 110 us
  Pallas kernels: 310 us -> 302 us
    ppermute x40 -> x39, waiting for transfers between devices: 61.2 us -> 50.2 us  [swap(): return lax.ppermute(part, axis_name, [(0, 1), (1, 0)])]
    pallas_call x5 -> x4, Pallas kernels: 46.3 us -> 37.9 us  [the longest x1 19.3 us: attend_back(): pl.pallas_call(functools.partial(attend_back_kernel, 256, begun is not No...]
    unnamed x94 -> x114, local copies, waits for them, and re-layouts: 18 us -> 13.6 us
    ppermute x40 -> x39, starting transfers between devices: 26.4 us -> 24.7 us  [swap(): return lax.ppermute(part, axis_name, [(0, 1), (1, 0)])]
  transfers between devices with their start and end apart: 73 -> 72, of which waited for: 18 -> 21; matrix products, arithmetic and copies ran while one was open for 9% -> 10% of each run, Pallas kernels for 51% -> 53%
where the time goes in v4:
time: 563 us; the launch traced here: 553 us
  Pallas kernels  302 us (54%)
  waiting for transfers between devices  110 us (20%)
  starting transfers between devices  66.1 us (12%)
  local copies, waits for them, and re-layouts  37.4 us (7%)
  other arithmetic  35.5 us (6%)
    ppermute x33, waiting for transfers between devices, dp_swap(): return lax.ppermute(part, 'dp', [(i, i ^ 1 << bit) for i in range(count)])  60 us
    ppermute x39, waiting for transfers between devices, swap(): return lax.ppermute(part, axis_name, [(0, 1), (1, 0)])  50.2 us
    pallas_call x4, Pallas kernels, split_product(): pl.pallas_call(kernel, grid_spec=pltpu.PrefetchScalarGridSpec(num_scalar_...  50.1 us
    pallas_call x12, Pallas kernels, relay(): pl.pallas_call(relay_kernel, grid_spec=pltpu.PrefetchScalarGridSpec(num_s...  44.4 us
    ppermute x33, starting transfers between devices, dp_swap(): return lax.ppermute(part, 'dp', [(i, i ^ 1 << bit) for i in range(count)])  41.3 us
    pallas_call x2, Pallas kernels, activate(): pl.pallas_call(functools.partial(activate_kernel, width // 2), grid_spec=...  31.3 us
    pallas_call x1, Pallas kernels, normed_grad(): pl.pallas_call(functools.partial(normed_grad_kernel, halves, steps, tile,...  25.6 us
    ppermute x39, starting transfers between devices, swap(): return lax.ppermute(part, axis_name, [(0, 1), (1, 0)])  24.7 us
  transfers between devices with their start and end apart: 72, of which 21 were waited for; matrix products, arithmetic and copies ran while one was open for 10% of the time, Pallas kernels for 53%

profile of v4, /device:TPU:0, one launch (start us, length us, event | category | flops | bytes accessed | tf_op | source)
XLA Modules:
  0.0 552.6 jit_solution(13367950437845568127)
XLA Ops:
  2.0 3.0 collective-permute-start.2
  9.2 1.9 collective-permute-start.4
  11.9 3.1 fusion.9
  17.5 3.8 unit_columns.3
  21.4 3.0 collective-permute-done.4
  29.8 7.4 %unit_columns.4 = (bf16[8,96,3072]{2,1,0:T(8,128)(2,1)}, bf16[8,96,1536]{2,1,0:T(8,128)(2,1)}, bf16[8,96,1536]{2,1,0:T(8,128)(2,1)}) custom-call(s32[9]{0:T(128)} %get-tuple-element.465.table, bf16[768,8960]{1,0:T(8,128)(2,1)} %bitcast.73), custom_call_target="tpu_custom_call" | custom-call | flops 1 | bytes 1 | tf_op jit(solution)/shard_map/unit_columns/pallas_call | solution.py:103
  44.7 7.4 %unit_columns.5 = (bf16[8,96,3072]{2,1,0:T(8,128)(2,1)}, bf16[8,96,1536]{2,1,0:T(8,128)(2,1)}, bf16[8,96,1536]{2,1,0:T(8,128)(2,1)}) custom-call(s32[9]{0:T(128)} %get-tuple-element.464.table, bf16[768,8960]{1,0:T(8,128)(2,1)} %bitcast.74, ...), custom_call_target="tpu_custom_call", output_to_operand_aliasing={{0}: (2, {}), {1}: (3, {}), {2}: (4, {})} | custom-call | flops 1 | bytes 1 | tf_op jit(solution)/shard_map/unit_columns/pallas_call | solution.py:103
  54.5 8.5 %project.1 = (bf16[1024,1536]{1,0:T(8,128)(2,1)}, bf16[1024,768]{1,0:T(8,128)(2,1)}, f32[1024,128]{1,0:T(8,128)}, bf16[1024,384]{1,0:T(8,128)(2,1)}, bf16[1024,1...) custom-call(s32[5]{0:T(128)} %stack.39.table, bf16[512,768]{1,0:T(8,128)(2,1)} %own_ref, ...), custom_call_target="tpu_custom_call" | custom-call | flops 1 | bytes 1 | tf_op jit(solution)/shard_map/project/pallas_call | solution.py:244
  63.0 2.5 collective-permute-done.12
  72.2 10.5 %attend.1 = (bf16[1024,384]{1,0:T(8,128)(2,1)}, bf16[1024,256]{1,0:T(8,128)(2,1)}, bf16[1024,128]{1,0:T(8,128)(2,1)}) custom-call(bf16[1024,384]{1,0:T(8,128)(2,1)} %get-tuple-element.356.query_ref, bf16[1024,128]{1,0:T(8,128)(2,1)} %get-tuple-element.246.key_ref, bf16[1024,128]{1,0:T(8,128)(2,1)} %get-tuple-element.247.value_ref, ...), custom_call_target="tpu_custom_call" | custom-call | flops 1 | bytes 1 | tf_op jit(solution)/shard_map/attend/pallas_call | solution.py:334
  88.5 2.5 unit_rows.2
  91.0 7.0 %unit_rows.3 = (bf16[8,192,768]{2,1,0:T(8,128)(2,1)}, bf16[8,96,768]{2,1,0:T(8,128)(2,1)}) custom-call(s32[9]{0:T(128)} %pad_add_fusion.3.table, bf16[8,2,280,768]{3,2,1,0:T(8,128)(2,1)} %bitcast.79), custom_call_target="tpu_custom_call" | custom-call | flops 1 | bytes 1 | tf_op jit(solution)/shard_map/unit_rows/pallas_call | solution.py:136
  98.0 3.1 collective-permute-done.13.refs_2_
  101.7 2.0 collective-permute-done.19.refs_5_
  107.0 13.3 %residual.1 = (f32[1024,1536]{1,0:T(8,128)}, bf16[1024,1536]{1,0:T(8,128)(2,1)}, f32[1024,128]{1,0:T(8,128)}, bf16[1024,768]{1,0:T(8,128)(2,1)}) custom-call(s32[5]{0:T(128)} %stack.39.table, bf16[1024,1536]{1,0:T(8,128)(2,1)} %get-tuple-element.267.stream_ref, bf16[1024,384]{1,0:T(8,128)(2,1)} %get-tuple-element.249.refs_0_, ...), custom_call_target="tpu_custom_call" | custom-call | flops 1 | bytes 1 | tf_op jit(solution)/shard_map/residual/pallas_call | solution.py:470
  122.9 19.3 %activate.2 = (bf16[1024,1536]{1,0:T(8,128)(2,1)}, bf16[1024,1536]{1,0:T(8,128)(2,1)}, bf16[1024,1536]{1,0:T(8,128)(2,1)}) custom-call(s32[5]{0:T(128)} %stack.39.table, bf16[1024,1536]{1,0:T(8,128)(2,1)} %get-tuple-element.332.normed_ref.left_ref, bf16[768,3072]{1,0:T(8,128)(2,1)} %bitcast.75, bf16[768,3072]{1,0:T(8,128)(2,1)} %bitcast.76, ...), custom_call_target="tpu_custom_call" | custom-call | flops 1 | bytes 1 | tf_op jit(solution)/shard_map/activate/pallas_call | solution.py:524
  148.1 5.6 %join.1.refs_0_.grad_ref = bf16[1024,1536]{1,0:T(8,128)(2,1)} custom-call(s32[5]{0:T(128)} %stack.39.table, bf16[512,768]{1,0:T(8,128)(2,1)} %own_ref.1, bf16[512,768]{1,0:T(8,128)(2,1)} %collective-permute-done.28.near_ref, bf16[512,768]{1,0:T(8,128)(2,1)} %collective-permute-done.26.far_ref, bf16[512,768]{1,0:T(8,128)(2,1)} %collective-permute-done.29.far_near_ref), custom_call_target="tpu_custom_call" | custom-call | flops 1 | bytes 1 | tf_op jit(solution)/shard_map/join/pallas_call | solution.py:284
  153.7 10.4 %split_product.4 = (bf16[4,192,1536]{2,1,0:T(8,128)(2,1)}, bf16[4,192,1536]{2,1,0:T(8,128)(2,1)}) custom-call(s32[5]{0:T(128)} %stack.39.table, bf16[1024,1536]{1,0:T(8,128)(2,1)} %get-tuple-element.334.left_ref.refs_0_, bf16[1024,1536]{1,0:T(8,128)(2,1)} %join.1.refs_0_.grad_ref), custom_call_target="tpu_custom_call" | custom-call | flops 1 | bytes 1 | tf_op jit(solution)/shard_map/split_product/pallas_call | solution.py:660
  164.7 2.2 dynamic-slice_bitcast_fusion
  169.3 13.2 %activate_back.2 = (bf16[1024,1536]{1,0:T(8,128)(2,1)}, bf16[1024,1536]{1,0:T(8,128)(2,1)}) custom-call(s32[5]{0:T(128)} %stack.39.table, bf16[1024,1536]{1,0:T(8,128)(2,1)} %join.1.refs_0_.grad_ref, bf16[1536,768]{1,0:T(8,128)(2,1)} %bitcast.88, bf16[384,768]{1,0:T(8,128)(2,1)} %copy-done.11, bf16[384,768]{1,0:T(8,128)(2,1)} %copy-done.10, ...), custom_call_target="tpu_custom_call" | custom-call | flops 1 | bytes 1 | tf_op jit(solution)/shard_map/activate_back/pallas_call | solution.py:559
  182.5 20.7 %split_product.5 = (bf16[4,96,3072]{2,1,0:T(8,128)(2,1)}, bf16[4,96,3072]{2,1,0:T(8,128)(2,1)}, bf16[4,96,3072]{2,1,0:T(8,128)(2,1)}, bf16[4,96,3072]{2,1,0:T(8,128)(2,1)}) custom-call(s32[5]{0:T(128)} %stack.39.table, bf16[1024,1536]{1,0:T(8,128)(2,1)} %get-tuple-element.332.normed_ref.left_ref, bf16[1024,1536]{1,0:T(8,128)(2,1)} %get-tuple-element.313.refs_0_, ...), custom_call_target="tpu_custom_call" | custom-call | flops 1 | bytes 1 | tf_op jit(solution)/shard_map/split_product/pallas_call | solution.py:660
  206.0 12.0 %activate.3 = (bf16[1024,768]{1,0:T(8,128)(2,1)}, bf16[1024,768]{1,0:T(8,128)(2,1)}, bf16[1024,768]{1,0:T(8,128)(2,1)}) custom-call(s32[5]{0:T(128)} %stack.39.table, bf16[1024,1536]{1,0:T(8,128)(2,1)} %get-tuple-element.332.normed_ref.left_ref, bf16[768,1536]{1,0:T(8,128)(2,1)} %bitcast.81, bf16[768,1536]{1,0:T(8,128)(2,1)} %bitcast.82, ...), custom_call_target="tpu_custom_call" | custom-call | flops 1 | bytes 1 | tf_op jit(solution)/shard_map/activate/pallas_call | solution.py:524
  218.0 7.3 %collective-permute-done.33.refs_0_.refs_8_ = bf16[768,768]{1,0:T(8,128)(2,1)S(1)} collective-permute-done((bf16[768,768]{1,0:T(8,128)(2,1)}, bf16[768,768]{1,0:T(8,128)(2,1)S(1)}, u32[]{:S(2)}, u32[]{:S(2)}) %collective-permute-start.33) | collective-permute-done | bytes 1179680 | tf_op jit(solution)/shard_map/ppermute | solution.py:945
  225.3 4.2 relay.12
  230.6 8.8 %activate_back.3 = (bf16[1024,768]{1,0:T(8,128)(2,1)}, bf16[1024,768]{1,0:T(8,128)(2,1)}) custom-call(s32[5]{0:T(128)} %stack.39.table, bf16[1024,1536]{1,0:T(8,128)(2,1)} %join.1.refs_0_.grad_ref, bf16[768,768]{1,0:T(8,128)(2,1)} %bitcast.92, bf16[768,768]{1,0:T(8,128)(2,1)} %copy-done.13, bf16[1024,768]{1,0:T(8,128)(2,1)} %get-tuple-element.310.refs_1_, ...), custom_call_target="tpu_custom_call" | custom-call | flops 1 | bytes 1 | tf_op jit(solution)/shard_map/activate_back/pallas_call | solution.py:559
  239.3 25.6 %normed_grad.1 = (f32[512,1536]{1,0:T(8,128)}, bf16[512,768]{1,0:T(8,128)(2,1)}, bf16[512,768]{1,0:T(8,128)(2,1)}) custom-call(s32[5]{0:T(128)} %stack.39.table, bf16[1024,1536]{1,0:T(8,128)(2,1)} %get-tuple-element.313.refs_0_, bf16[1024,1536]{1,0:T(8,128)(2,1)} %get-tuple-element.301.refs_1_, bf16[1024,768]{1,0:T(8,128)(2,1)} %get-tuple-element.312.refs_2_.refs_0_, ...), custom_call_target="tpu_custom_call" | custom-call | flops 1 | bytes 1 | tf_op jit(solution)/shard_map/normed_grad/pallas_call | solution.py:769
  264.9 6.8 %split_product.6 = (bf16[4,96,1536]{2,1,0:T(8,128)(2,1)}, bf16[4,96,1536]{2,1,0:T(8,128)(2,1)}) custom-call(s32[5]{0:T(128)} %stack.39.table, bf16[1024,768]{1,0:T(8,128)(2,1)} %get-tuple-element.323.left_ref.refs_1_, bf16[1024,1536]{1,0:T(8,128)(2,1)} %join.1.refs_0_.grad_ref), custom_call_target="tpu_custom_call" | custom-call | flops 1 | bytes 1 | tf_op jit(solution)/shard_map/split_product/pallas_call | solution.py:660
  272.8 3.4 relay.13
  276.2 4.4 relay.14
  282.7 2.6 collective-permute-start.39
  286.0 5.0 chip_sum.1
  293.0 12.2 %split_product.7 = (bf16[8,96,1536]{2,1,0:T(8,128)(2,1)}, bf16[8,96,1536]{2,1,0:T(8,128)(2,1)}) custom-call(s32[5]{0:T(128)} %stack.39.table, bf16[1024,1536]{1,0:T(8,128)(2,1)} %get-tuple-element.332.normed_ref.left_ref, bf16[1024,768]{1,0:T(8,128)(2,1)} %get-tuple-element.312.refs_2_.refs_0_, bf16[1024,768]{1,0:T(8,128)(2,1)} %get-tuple-element.314.refs_3_.refs_1_), custom_call_target="tpu_custom_call" | custom-call | flops 1 | bytes 1 | tf_op jit(solution)/shard_map/split_product/pallas_call | solution.py:660
  305.2 14.8 %down.1 = (f32[512,1536]{1,0:T(8,128)}, bf16[512,768]{1,0:T(8,128)(2,1)}, bf16[512,768]{1,0:T(8,128)(2,1)}) custom-call(s32[5]{0:T(128)} %stack.39.table, bf16[1024,1536]{1,0:T(8,128)(2,1)} %get-tuple-element.334.left_ref.refs_0_, bf16[1024,768]{1,0:T(8,128)(2,1)} %get-tuple-element.323.left_ref.refs_1_, bf16[1536,768]{1,0:T(8,128)(2,1)} %bitcast.89, ...), custom_call_target="tpu_custom_call" | custom-call | flops 1 | bytes 1 | tf_op jit(solution)/shard_map/down/pallas_call | solution.py:607
  321.0 3.4 relay.15
  325.9 4.3 relay.16
  332.9 7.1 %norm_back.1 = (f32[512,768]{1,0:T(8,128)}, bf16[512,768]{1,0:T(8,128)(2,1)}, bf16[512,768]{1,0:T(8,128)(2,1)}, f32[1,768]{1,0:T(1,128)}) custom-call(s32[5]{0:T(128)} %stack.39.table, f32[512,1536]{1,0:T(8,128)} %get-tuple-element.351.chip_ref, bf16[512,768]{1,0:T(8,128)(2,1)} %collective-permute-done.43.far_own_ref, ...), custom_call_target="tpu_custom_call" | custom-call | flops 1 | bytes 1 | tf_op jit(solution)/shard_map/norm_back/pallas_call | solution.py:857
  340.5 2.5 add_convert_fusion
  344.8 19.3 %attend_back.1 = (bf16[1024,384]{1,0:T(8,128)(2,1)}, f32[1024,256]{1,0:T(8,128)}) custom-call(s32[5]{0:T(128)} %stack.39.table, bf16[1024,384]{1,0:T(8,128)(2,1)} %get-tuple-element.356.query_ref, bf16[1024,128]{1,0:T(8,128)(2,1)} %get-tuple-element.246.key_ref, bf16[1024,128]{1,0:T(8,128)(2,1)} %get-tuple-element.247.value_ref, ...), custom_call_target="tpu_custom_call" | custom-call | flops 1 | bytes 1 | tf_op jit(solution)/shard_map/attend_back/pallas_call | solution.py:406
  367.7 3.2 relay.17
  374.3 2.6 collective-permute-start.51
  376.9 25.5 %collective-permute-done.48.arrived_ref = bf16[1024,640]{1,0:T(8,128)(2,1)} collective-permute-done((bf16[1024,640]{1,0:T(8,128)(2,1)}, bf16[1024,640]{1,0:T(8,128)(2,1)}, u32[]{:S(2)}, u32[]{:S(2)}) %collective-permute-start.48) | collective-permute-done | bytes 1310752 | tf_op jit(solution)/shard_map/ppermute | solution.py:945
  402.4 10.6 %project_back.1 = (bf16[4,96,1792]{2,1,0:T(8,128)(2,1)}, bf16[4,96,1792]{2,1,0:T(8,128)(2,1)}, f32[512,768]{1,0:T(8,128)}, bf16[512,768]{1,0:T(8,128)(2,1)}, f32[1,1024]{1,0:T(1,128)}) custom-call(s32[5]{0:T(128)} %stack.39.table, bf16[1024,384]{1,0:T(8,128)(2,1)} %get-tuple-element.363.query_ref, f32[1024,256]{1,0:T(8,128)} %get-tuple-element.360.key_value_ref, ...), custom_call_target="tpu_custom_call" | custom-call | flops 1 | bytes 1 | tf_op jit(solution)/shard_map/project_back/pallas_call | solution.py:916
  418.5 1.9 slice.153
  420.4 3.5 relay.18
  425.4 2.8 relay.19
  428.2 2.0 convert_add_fusion.3
  434.6 5.3 relay.20
  440.0 2.3 fusion.6
  443.5 2.4 collective-permute-done.63
  446.7 7.4 %collective-permute-done.49.arrived_sent_ref.arrived_ref = bf16[4,96,1792]{2,1,0:T(8,128)(2,1)} collective-permute-done((bf16[4,96,1792]{2,1,0:T(8,128)(2,1)}, bf16[4,96,1792]{2,1,0:T(8,128)(2,1)}, u32[]{:S(2)}, u32[]{:S(2)}) %collective-permute-start.49) | collective-permute-done | bytes 1376288 | tf_op jit(solution)/shard_map/ppermute | solution.py:950
  454.1 3.5 relay.21
  457.5 13.3 %collective-permute-done.60 = bf16[1,96,3072]{2,1,0:T(8,128)(2,1)} collective-permute-done((bf16[1,96,3072]{2,1,0:T(8,128)(2,1)}, bf16[1,96,3072]{2,1,0:T(8,128)(2,1)}, u32[]{:S(2)}, u32[]{:S(2)}) %collective-permute-start.60) | collective-permute-done | bytes 589856 | tf_op jit(solution)/shard_map/ppermute | solution.py:950
  470.9 2.2 convert_add_fusion.2
  476.5 17.0 %collective-permute-done.58.arrived_sent_ref.arrived_ref = bf16[4,96,1536]{2,1,0:T(8,128)(2,1)S(1)} collective-permute-done((bf16[4,96,1536]{2,1,0:T(8,128)(2,1)}, bf16[4,96,1536]{2,1,0:T(8,128)(2,1)S(1)}, u32[]{:S(2)}, u32[]{:S(2)}) %collective-permute-start.58) | collective-permute-done | bytes 1179680 | tf_op jit(solution)/shard_map/ppermute | solution.py:950
  494.5 3.3 relay.22
  499.4 3.3 fusion.5
  507.5 2.4 collective-permute-start.64
  511.2 3.0 relay.23
  514.3 2.9 collective-permute-start.65
  517.2 12.8 %collective-permute-done.66 = bf16[2,96,1536]{2,1,0:T(8,128)(2,1)} collective-permute-done((bf16[2,96,1536]{2,1,0:T(8,128)(2,1)}, bf16[2,96,1536]{2,1,0:T(8,128)(2,1)}, u32[]{:S(2)}, u32[]{:S(2)}) %collective-permute-start.66) | collective-permute-done | bytes 589856 | tf_op jit(solution)/shard_map/ppermute | solution.py:950
  531.3 5.2 collective-permute-done.65
  540.7 3.0 fusion.7
  543.7 2.1 collective-permute-done.69.far1_ref
  546.5 5.6 %spread_columns.1 = f32[96,8960]{1,0:T(8,128)} custom-call(s32[5]{0:T(128)} %stack.39.table, f32[96,3072]{1,0:T(8,128)} %bitcast.94, f32[96,1536]{1,0:T(8,128)} %slice_bitcast_fusion.own1_ref, bf16[96,3072]{1,0:T(8,128)(2,1)} %copy-done.37, bf16[96,1536]{1,0:T(8,128)(2,1)} %copy-done.49), custom_call_target="tpu_custom_call" | custom-call | flops 1 | bytes 1 | tf_op jit(solution)/shard_map/spread_columns/pallas_call | solution.py:178
  (322 shorter events, 107.5 us)
Async XLA Ops:
  2.0 15.4 %collective-permute-start.2 = (f32[2,768]{1,0:T(2,128)S(1)}, f32[2,768]{1,0:T(2,128)S(1)}, u32[]{:S(2)}, u32[]{:S(2)}) collective-permute-start(f32[2,768]{1,0:T(2,128)S(1)} %pad_maximum_fusion.18), channel_id=1, source_target_pairs={{0,1},{1,0},{2,3},{3,2},{4,5},{5,4},{6,7},{7,6},{8,9},{9,8},{10,11... | collective-permute-start | bytes 18440 | tf_op jit(solution)/shard_map/ppermute | solution.py:945
  5.1 38.5 %collective-permute-start.6 = (bf16[512,768]{1,0:T(8,128)(2,1)}, bf16[512,768]{1,0:T(8,128)(2,1)}, u32[]{:S(2)}, u32[]{:S(2)}) collective-permute-start(bf16[512,768]{1,0:T(8,128)(2,1)} %own_ref), channel_id=1, source_target_pairs={{0,2},{2,0},{1,3},{3,1},{4,6},{6,4},{5,7},{7,5},{8,10},{10,8},{9,1... | collective-permute-start | bytes 2359304 | tf_op jit(solution)/shard_map/ppermute | solution.py:945
  5.1 38.5 %collective-permute-start = (bf16[768,768]{1,0:T(8,128)(2,1)}, bf16[768,768]{1,0:T(8,128)(2,1)}, u32[]{:S(2)}, u32[]{:S(2)}) collective-permute-start(bf16[768,768]{1,0:T(8,128)(2,1)} %bitcast.84), channel_id=1, source_target_pairs={{0,2},{2,0},{1,3},{3,1},{4,6},{6,4},{5,7},{7,5},{8,10},{10,8},{9,1... | collective-permute-start | bytes 3538952 | tf_op jit(solution)/shard_map/ppermute | solution.py:945
  9.1 15.3 %collective-permute-start.1 = (bf16[96,1408]{1,0:T(8,128)(2,1)S(1)}, bf16[96,1408]{1,0:T(8,128)(2,1)}, u32[]{:S(2)}, u32[]{:S(2)}) collective-permute-start(bf16[96,1408]{1,0:T(8,128)(2,1)S(1)} %get-tuple-element.217), channel_id=1, source_target_pairs={{0,1},{1,0},{2,3},{3,2},{4,5},{5,4},{6,7},{7,6},{8,9},{9,8},{10,11... | collective-permute-start | bytes 811016 | tf_op jit(solution)/shard_map/ppermute | solution.py:945
  9.2 15.2 %collective-permute-start.4 = (bf16[96,1408]{1,0:T(8,128)(2,1)}, bf16[96,1408]{1,0:T(8,128)(2,1)}, u32[]{:S(2)}, u32[]{:S(2)}) collective-permute-start(bf16[96,1408]{1,0:T(8,128)(2,1)} %get-tuple-element.218), channel_id=1, source_target_pairs={{0,1},{1,0},{2,3},{3,2},{4,5},{5,4},{6,7},{7,6},{8,9},{9,8},{10,11... | collective-permute-start | bytes 811016 | tf_op jit(solution)/shard_map/ppermute | solution.py:945
  17.5 23.6 %collective-permute-start.7 = (bf16[512,768]{1,0:T(8,128)(2,1)S(1)}, bf16[512,768]{1,0:T(8,128)(2,1)S(1)}, u32[]{:S(2)}, u32[]{:S(2)}) collective-permute-start(bf16[512,768]{1,0:T(8,128)(2,1)S(1)} %copy-done.7), channel_id=1, source_target_pairs={{0,1},{1,0},{2,3},{3,2},{4,5},{5,4},{6,7},{7,6},{8,9},{9,8},{10,11... | collective-permute-start | bytes 2359304 | tf_op jit(solution)/shard_map/ppermute | solution.py:945
  24.4 13.5 %collective-permute-start.3 = (bf16[96,1408]{1,0:T(8,128)(2,1)}, bf16[96,1408]{1,0:T(8,128)(2,1)S(1)}, u32[]{:S(2)}, u32[]{:S(2)}) collective-permute-start(bf16[96,1408]{1,0:T(8,128)(2,1)} %collective-permute-done.1), channel_id=1, source_target_pairs={{0,4},{4,0},{8,12},{12,8},{16,20},{20,16},{24,28},{28,24},{1,5},{5... | collective-permute-start | bytes 811016 | tf_op jit(solution)/shard_map/ppermute | solution.py:950
  25.9 11.3 %collective-permute-start.5 = (bf16[96,1408]{1,0:T(8,128)(2,1)}, bf16[96,1408]{1,0:T(8,128)(2,1)S(1)}, u32[]{:S(2)}, u32[]{:S(2)}) collective-permute-start(bf16[96,1408]{1,0:T(8,128)(2,1)} %collective-permute-done.4), channel_id=1, source_target_pairs={{0,8},{4,12},{8,0},{12,4},{16,24},{20,28},{24,16},{28,20},{1,9},{5... | collective-permute-start | bytes 811016 | tf_op jit(solution)/shard_map/ppermute | solution.py:950
  37.2 28.3 %collective-permute-start.12 = (bf16[2,96,3072]{2,1,0:T(8,128)(2,1)}, bf16[2,96,3072]{2,1,0:T(8,128)(2,1)}, u32[]{:S(2)}, u32[]{:S(2)}) collective-permute-start(bf16[2,96,3072]{2,1,0:T(8,128)(2,1)} %unit_columns.3), channel_id=1, source_target_pairs={{0,1},{1,0},{2,3},{3,2},{4,5},{5,4},{6,7},{7,6},{8,9},{9,8},{10,11... | collective-permute-start | bytes 3538952 | tf_op jit(solution)/shard_map/ppermute | solution.py:945
  40.0 12.2 %collective-permute-start.10 = (bf16[192,1408]{1,0:T(8,128)(2,1)S(1)}, bf16[192,1408]{1,0:T(8,128)(2,1)S(1)}, u32[]{:S(2)}, u32[]{:S(2)}) collective-permute-start(bf16[192,1408]{1,0:T(8,128)(2,1)S(1)} %pad_maximum_fusion.10.part0_ref), channel_id=1, source_target_pairs={{0,8},{4,12},{8,0},{12,4},{16,24},{20,28},{24,16},{28,20},{1,9},{5... | collective-permute-start | bytes 1622024 | tf_op jit(solution)/shard_map/ppermute | solution.py:950
  41.1 12.4 %collective-permute-start.11 = (bf16[192,1408]{1,0:T(8,128)(2,1)S(1)}, bf16[192,1408]{1,0:T(8,128)(2,1)S(1)}, u32[]{:S(2)}, u32[]{:S(2)}) collective-permute-start(bf16[192,1408]{1,0:T(8,128)(2,1)S(1)} %pad_maximum_fusion.11.part1_ref), channel_id=1, source_target_pairs={{0,4},{4,0},{8,12},{12,8},{16,20},{20,16},{24,28},{28,24},{1,5},{5... | collective-permute-start | bytes 1622024 | tf_op jit(solution)/shard_map/ppermute | solution.py:950
  43.6 9.9 %collective-permute-start.8 = (bf16[256,768]{1,0:T(8,128)(2,1)}, bf16[256,768]{1,0:T(8,128)(2,1)S(1)}, u32[]{:S(2)}, u32[]{:S(2)}) collective-permute-start(bf16[256,768]{1,0:T(8,128)(2,1)} %get-tuple-element.237), channel_id=1, source_target_pairs={{0,2},{2,0},{1,3},{3,1},{4,6},{6,4},{5,7},{7,5},{8,10},{10,8},{9,1... | collective-permute-start | bytes 1179656 | tf_op jit(solution)/shard_map/ppermute | solution.py:945
  43.6 9.9 %collective-permute-start.9 = (bf16[256,768]{1,0:T(8,128)(2,1)}, bf16[256,768]{1,0:T(8,128)(2,1)S(1)}, u32[]{:S(2)}, u32[]{:S(2)}) collective-permute-start(bf16[256,768]{1,0:T(8,128)(2,1)} %get-tuple-element.238), channel_id=1, source_target_pairs={{0,2},{2,0},{1,3},{3,1},{4,6},{6,4},{5,7},{7,5},{8,10},{10,8},{9,1... | collective-permute-start | bytes 1179656 | tf_op jit(solution)/shard_map/ppermute | solution.py:945
  66.8 17.9 %collective-permute-start.15 = (bf16[96,3072]{1,0:T(8,128)(2,1)S(1)}, bf16[96,3072]{1,0:T(8,128)(2,1)S(1)}, u32[]{:S(2)}, u32[]{:S(2)}) collective-permute-start(bf16[96,3072]{1,0:T(8,128)(2,1)S(1)} %get-tuple-element.244), channel_id=1, source_target_pairs={{0,8},{4,12},{8,0},{12,4},{16,24},{20,28},{24,16},{28,20},{1,9},{5... | collective-permute-start | bytes 1769480 | tf_op jit(solution)/shard_map/ppermute | solution.py:950
  70.7 14.1 %collective-permute-start.14 = (bf16[96,3072]{1,0:T(8,128)(2,1)S(1)}, bf16[96,3072]{1,0:T(8,128)(2,1)S(1)}, u32[]{:S(2)}, u32[]{:S(2)}) collective-permute-start(bf16[96,3072]{1,0:T(8,128)(2,1)S(1)} %get-tuple-element.243), channel_id=1, source_target_pairs={{0,4},{4,0},{8,12},{12,8},{16,20},{20,16},{24,28},{28,24},{1,5},{5... | collective-permute-start | bytes 1769480 | tf_op jit(solution)/shard_map/ppermute | solution.py:950
  82.7 18.4 %collective-permute-start.16 = (bf16[1024,128]{1,0:T(8,128)(2,1)}, bf16[1024,128]{1,0:T(8,128)(2,1)}, u32[]{:S(2)}, u32[]{:S(2)}) collective-permute-start(bf16[1024,128]{1,0:T(8,128)(2,1)} %get-tuple-element.265), channel_id=1, source_target_pairs={{0,1},{1,0},{2,3},{3,2},{4,5},{5,4},{6,7},{7,6},{8,9},{9,8},{10,11... | collective-permute-start | bytes 786440 | tf_op jit(solution)/shard_map/ppermute | solution.py:945
  83.3 17.8 %collective-permute-start.13 = (bf16[1024,256]{1,0:T(8,128)(2,1)}, bf16[1024,256]{1,0:T(8,128)(2,1)}, u32[]{:S(2)}, u32[]{:S(2)}) collective-permute-start(bf16[1024,256]{1,0:T(8,128)(2,1)} %get-tuple-element.248), channel_id=1, source_target_pairs={{0,1},{1,0},{2,3},{3,2},{4,5},{5,4},{6,7},{7,6},{8,9},{9,8},{10,11... | collective-permute-start | bytes 1572872 | tf_op jit(solution)/shard_map/ppermute | solution.py:945
  84.8 16.8 %collective-permute-start.17 = (bf16[1024,384]{1,0:T(8,128)(2,1)}, bf16[1024,384]{1,0:T(8,128)(2,1)}, u32[]{:S(2)}, u32[]{:S(2)}) collective-permute-start(bf16[1024,384]{1,0:T(8,128)(2,1)} %get-tuple-element.249.refs_0_), channel_id=1, source_target_pairs={{0,2},{2,0},{1,3},{3,1},{4,6},{6,4},{5,7},{7,5},{8,10},{10,8},{9,1... | collective-permute-start | bytes 2359304 | tf_op jit(solution)/shard_map/ppermute | solution.py:945
  85.2 35.1 %collective-permute-start.23 = (bf16[192,3072]{1,0:T(8,128)(2,1)S(1)}, bf16[192,3072]{1,0:T(8,128)(2,1)S(1)}, u32[]{:S(2)}, u32[]{:S(2)}) collective-permute-start(bf16[192,3072]{1,0:T(8,128)(2,1)S(1)} %pad_maximum_fusion.2.refs_0_.refs_4_.refs_6_), channel_id=1, source_target_pairs={{0,8},{4,12},{8,0},{12,4},{16,24},{20,28},{24,16},{28,20},{1,9},{5... | collective-permute-start | bytes 3538952 | tf_op jit(solution)/shard_map/ppermute | solution.py:950
  85.7 34.5 %collective-permute-start.24 = (bf16[192,3072]{1,0:T(8,128)(2,1)S(1)}, bf16[192,3072]{1,0:T(8,128)(2,1)}, u32[]{:S(2)}, u32[]{:S(2)}) collective-permute-start(bf16[192,3072]{1,0:T(8,128)(2,1)S(1)} %pad_maximum_fusion.3.refs_1_.refs_5_.refs_7_), channel_id=1, source_target_pairs={{0,4},{4,0},{8,12},{12,8},{16,20},{20,16},{24,28},{28,24},{1,5},{5... | collective-permute-start | bytes 3538952 | tf_op jit(solution)/shard_map/ppermute | solution.py:950
  104.1 16.5 %collective-permute-start.22 = (bf16[2,192,768]{2,1,0:T(8,128)(2,1)}, bf16[2,192,768]{2,1,0:T(8,128)(2,1)}, u32[]{:S(2)}, u32[]{:S(2)}) collective-permute-start(bf16[2,192,768]{2,1,0:T(8,128)(2,1)} %unit_rows.2), channel_id=1, source_target_pairs={{0,1},{1,0},{2,3},{3,2},{4,5},{5,4},{6,7},{7,6},{8,9},{9,8},{10,11... | collective-permute-start | bytes 1769480 | tf_op jit(solution)/shard_map/ppermute | solution.py:945
  104.6 37.5 %collective-permute-start.26 = (bf16[512,768]{1,0:T(8,128)(2,1)}, bf16[512,768]{1,0:T(8,128)(2,1)}, u32[]{:S(2)}, u32[]{:S(2)}) collective-permute-start(bf16[512,768]{1,0:T(8,128)(2,1)} %own_ref.1), channel_id=1, source_target_pairs={{0,1},{1,0},{2,3},{3,2},{4,5},{5,4},{6,7},{7,6},{8,9},{9,8},{10,11... | collective-permute-start | bytes 2359304 | tf_op jit(solution)/shard_map/ppermute | solution.py:945
  121.8 20.4 %collective-permute-start.27 = (bf16[192,768]{1,0:T(8,128)(2,1)S(1)}, bf16[192,768]{1,0:T(8,128)(2,1)S(1)}, u32[]{:S(2)}, u32[]{:S(2)}) collective-permute-start(bf16[192,768]{1,0:T(8,128)(2,1)S(1)} %get-tuple-element.277), channel_id=1, source_target_pairs={{0,8},{4,12},{8,0},{12,4},{16,24},{20,28},{24,16},{28,20},{1,9},{5... | collective-permute-start | bytes 884744 | tf_op jit(solution)/shard_map/ppermute | solution.py:950
  122.4 20.0 %collective-permute-start.25 = (bf16[192,768]{1,0:T(8,128)(2,1)S(1)}, bf16[192,768]{1,0:T(8,128)(2,1)S(1)}, u32[]{:S(2)}, u32[]{:S(2)}) collective-permute-start(bf16[192,768]{1,0:T(8,128)(2,1)S(1)} %get-tuple-element.276), channel_id=1, source_target_pairs={{0,4},{4,0},{8,12},{12,8},{16,20},{20,16},{24,28},{28,24},{1,5},{5... | collective-permute-start | bytes 884744 | tf_op jit(solution)/shard_map/ppermute | solution.py:950
  142.2 5.9 %collective-permute-start.29 = (bf16[512,768]{1,0:T(8,128)(2,1)}, bf16[512,768]{1,0:T(8,128)(2,1)}, u32[]{:S(2)}, u32[]{:S(2)}) collective-permute-start(bf16[512,768]{1,0:T(8,128)(2,1)} %collective-permute-done.26.far_ref), channel_id=1, source_target_pairs={{0,2},{2,0},{1,3},{3,1},{4,6},{6,4},{5,7},{7,5},{8,10},{10,8},{9,1... | collective-permute-start | bytes 2359304 | tf_op jit(solution)/shard_map/ppermute | solution.py:945
  143.7 4.4 collective-permute-start.28
  144.2 19.9 %collective-permute-start.31 = (bf16[384,768]{1,0:T(8,128)(2,1)S(1)}, bf16[384,768]{1,0:T(8,128)(2,1)}, u32[]{:S(2)}, u32[]{:S(2)}) collective-permute-start(bf16[384,768]{1,0:T(8,128)(2,1)S(1)} %pad_maximum_fusion.9.refs_1_.refs_5_), channel_id=1, source_target_pairs={{0,4},{4,0},{8,12},{12,8},{16,20},{20,16},{24,28},{28,24},{1,5},{5... | collective-permute-start | bytes 1769480 | tf_op jit(solution)/shard_map/ppermute | solution.py:950
  145.7 18.4 %collective-permute-start.30 = (bf16[384,768]{1,0:T(8,128)(2,1)S(1)}, bf16[384,768]{1,0:T(8,128)(2,1)}, u32[]{:S(2)}, u32[]{:S(2)}) collective-permute-start(bf16[384,768]{1,0:T(8,128)(2,1)S(1)} %pad_maximum_fusion.8.refs_0_.refs_4_), channel_id=1, source_target_pairs={{0,8},{4,12},{8,0},{12,4},{16,24},{20,28},{24,16},{28,20},{1,9},{5... | collective-permute-start | bytes 1769480 | tf_op jit(solution)/shard_map/ppermute | solution.py:950
  147.2 57.4 %collective-permute-start.34 = (bf16[768,1536]{1,0:T(8,128)(2,1)}, bf16[768,1536]{1,0:T(8,128)(2,1)S(1)}, u32[]{:S(2)}, u32[]{:S(2)}) collective-permute-start(bf16[768,1536]{1,0:T(8,128)(2,1)} %bitcast.35), channel_id=1, source_target_pairs={{0,1},{1,0},{2,3},{3,2},{4,5},{5,4},{6,7},{7,6},{8,9},{9,8},{10,11... | collective-permute-start | bytes 7077896 | tf_op jit(solution)/shard_map/ppermute | solution.py:945
  164.1 61.3 %collective-permute-start.32 = (bf16[4,192,1536]{2,1,0:T(8,128)(2,1)}, bf16[4,192,1536]{2,1,0:T(8,128)(2,1)}, u32[]{:S(2)}, u32[]{:S(2)}) collective-permute-start(bf16[4,192,1536]{2,1,0:T(8,128)(2,1)} %get-tuple-element.299), channel_id=1, source_target_pairs={{0,4},{4,0},{8,12},{12,8},{16,20},{20,16},{24,28},{28,24},{1,5},{5... | collective-permute-start | bytes 7077896 | tf_op jit(solution)/shard_map/ppermute | solution.py:950
  168.1 57.3 %collective-permute-start.33 = (bf16[768,768]{1,0:T(8,128)(2,1)}, bf16[768,768]{1,0:T(8,128)(2,1)S(1)}, u32[]{:S(2)}, u32[]{:S(2)}) collective-permute-start(bf16[768,768]{1,0:T(8,128)(2,1)} %bitcast.32), channel_id=1, source_target_pairs={{0,1},{1,0},{2,3},{3,2},{4,5},{5,4},{6,7},{7,6},{8,9},{9,8},{10,11... | collective-permute-start | bytes 3538952 | tf_op jit(solution)/shard_map/ppermute | solution.py:945
  203.2 73.0 %collective-permute-start.35 = (bf16[4,96,3072]{2,1,0:T(8,128)(2,1)}, bf16[4,96,3072]{2,1,0:T(8,128)(2,1)}, u32[]{:S(2)}, u32[]{:S(2)}) collective-permute-start(bf16[4,96,3072]{2,1,0:T(8,128)(2,1)} %get-tuple-element.318), channel_id=1, source_target_pairs={{0,4},{4,0},{8,12},{12,8},{16,20},{20,16},{24,28},{28,24},{1,5},{5... | collective-permute-start | bytes 7077896 | tf_op jit(solution)/shard_map/ppermute | solution.py:950
  229.6 42.1 %collective-permute-start.36 = (bf16[2,192,1536]{2,1,0:T(8,128)(2,1)}, bf16[2,192,1536]{2,1,0:T(8,128)(2,1)S(1)}, u32[]{:S(2)}, u32[]{:S(2)}) collective-permute-start(bf16[2,192,1536]{2,1,0:T(8,128)(2,1)} %get-tuple-element.320), channel_id=1, source_target_pairs={{0,8},{4,12},{8,0},{12,4},{16,24},{20,28},{24,16},{28,20},{1,9},{5... | collective-permute-start | bytes 3538952 | tf_op jit(solution)/shard_map/ppermute | solution.py:950
  230.1 94.4 %collective-permute-start.40 = (bf16[4,96,3072]{2,1,0:T(8,128)(2,1)}, bf16[4,96,3072]{2,1,0:T(8,128)(2,1)S(1)}, u32[]{:S(2)}, u32[]{:S(2)}) collective-permute-start(bf16[4,96,3072]{2,1,0:T(8,128)(2,1)} %get-tuple-element.341), channel_id=1, source_target_pairs={{0,4},{4,0},{8,12},{12,8},{16,20},{20,16},{24,28},{28,24},{1,5},{5... | collective-permute-start | bytes 7077896 | tf_op jit(solution)/shard_map/ppermute | solution.py:950
  280.6 39.4 %collective-permute-start.41 = (bf16[2,96,3072]{2,1,0:T(8,128)(2,1)}, bf16[2,96,3072]{2,1,0:T(8,128)(2,1)S(1)}, u32[]{:S(2)}, u32[]{:S(2)}) collective-permute-start(bf16[2,96,3072]{2,1,0:T(8,128)(2,1)} %get-tuple-element.343), channel_id=1, source_target_pairs={{0,8},{4,12},{8,0},{12,4},{16,24},{20,28},{24,16},{28,20},{1,9},{5... | collective-permute-start | bytes 3538952 | tf_op jit(solution)/shard_map/ppermute | solution.py:950
  282.2 3.7 collective-permute-start.38
  282.7 47.4 %collective-permute-start.39 = (bf16[1,192,1536]{2,1,0:T(8,128)(2,1)}, bf16[1,192,1536]{2,1,0:T(8,128)(2,1)S(1)}, u32[]{:S(2)}, u32[]{:S(2)}) collective-permute-start(bf16[1,192,1536]{2,1,0:T(8,128)(2,1)} %get-tuple-element.339), channel_id=1, source_target_pairs={{0,16},{4,20},{8,24},{12,28},{16,0},{20,4},{24,8},{28,12},{1,17},{... | collective-permute-start | bytes 1769480 | tf_op jit(solution)/shard_map/ppermute | solution.py:950
  290.9 41.9 %collective-permute-start.43 = (bf16[512,768]{1,0:T(8,128)(2,1)}, bf16[512,768]{1,0:T(8,128)(2,1)}, u32[]{:S(2)}, u32[]{:S(2)}) collective-permute-start(bf16[512,768]{1,0:T(8,128)(2,1)} %get-tuple-element.330), channel_id=1, source_target_pairs={{0,1},{1,0},{2,3},{3,2},{4,5},{5,4},{6,7},{7,6},{8,9},{9,8},{10,11... | collective-permute-start | bytes 2359304 | tf_op jit(solution)/shard_map/ppermute | solution.py:945
  291.8 41.1 %collective-permute-start.44 = (bf16[512,768]{1,0:T(8,128)(2,1)}, bf16[512,768]{1,0:T(8,128)(2,1)}, u32[]{:S(2)}, u32[]{:S(2)}) collective-permute-start(bf16[512,768]{1,0:T(8,128)(2,1)} %get-tuple-element.331), channel_id=1, source_target_pairs={{0,1},{1,0},{2,3},{3,2},{4,5},{5,4},{6,7},{7,6},{8,9},{9,8},{10,11... | collective-permute-start | bytes 2359304 | tf_op jit(solution)/shard_map/ppermute | solution.py:945
  331.4 9.1 %collective-permute-start.42 = (bf16[512,768]{1,0:T(8,128)(2,1)}, bf16[512,768]{1,0:T(8,128)(2,1)S(1)}, u32[]{:S(2)}, u32[]{:S(2)}) collective-permute-start(bf16[512,768]{1,0:T(8,128)(2,1)} %get-tuple-element.349), channel_id=1, source_target_pairs={{0,2},{2,0},{1,3},{3,1},{4,6},{6,4},{5,7},{7,5},{8,10},{10,8},{9,1... | collective-permute-start | bytes 2359304 | tf_op jit(solution)/shard_map/ppermute | solution.py:945
  331.4 35.3 %collective-permute-start.47 = (bf16[4,96,1536]{2,1,0:T(8,128)(2,1)}, bf16[4,96,1536]{2,1,0:T(8,128)(2,1)S(1)}, u32[]{:S(2)}, u32[]{:S(2)}) collective-permute-start(bf16[4,96,1536]{2,1,0:T(8,128)(2,1)} %get-tuple-element.359), channel_id=1, source_target_pairs={{0,4},{4,0},{8,12},{12,8},{16,20},{20,16},{24,28},{28,24},{1,5},{5... | collective-permute-start | bytes 3538952 | tf_op jit(solution)/shard_map/ppermute | solution.py:950
  370.9 62.3 %collective-permute-start.50 = (bf16[8,96,1536]{2,1,0:T(8,128)(2,1)}, bf16[8,96,1536]{2,1,0:T(8,128)(2,1)S(1)}, u32[]{:S(2)}, u32[]{:S(2)}) collective-permute-start(bf16[8,96,1536]{2,1,0:T(8,128)(2,1)} %get-tuple-element.371), channel_id=1, source_target_pairs={{0,4},{4,0},{8,12},{12,8},{16,20},{20,16},{24,28},{28,24},{1,5},{5... | collective-permute-start | bytes 7077896 | tf_op jit(solution)/shard_map/ppermute | solution.py:950
  371.4 30.9 %collective-permute-start.48 = (bf16[1024,640]{1,0:T(8,128)(2,1)}, bf16[1024,640]{1,0:T(8,128)(2,1)}, u32[]{:S(2)}, u32[]{:S(2)}) collective-permute-start(bf16[1024,640]{1,0:T(8,128)(2,1)} %pad_maximum_fusion.1), channel_id=1, source_target_pairs={{0,1},{1,0},{2,3},{3,2},{4,5},{5,4},{6,7},{7,6},{8,9},{9,8},{10,11... | collective-permute-start | bytes 3932168 | tf_op jit(solution)/shard_map/ppermute | solution.py:945
  372.3 41.7 %collective-permute-start.53 = (bf16[2,96,3072]{2,1,0:T(8,128)(2,1)}, bf16[2,96,3072]{2,1,0:T(8,128)(2,1)S(1)}, u32[]{:S(2)}, u32[]{:S(2)}) collective-permute-start(bf16[2,96,3072]{2,1,0:T(8,128)(2,1)} %get-tuple-element.377), channel_id=1, source_target_pairs={{0,8},{4,12},{8,0},{12,4},{16,24},{20,28},{24,16},{28,20},{1,9},{5... | collective-permute-start | bytes 3538952 | tf_op jit(solution)/shard_map/ppermute | solution.py:950
  372.7 52.7 %collective-permute-start.52 = (bf16[2,96,1536]{2,1,0:T(8,128)(2,1)}, bf16[2,96,1536]{2,1,0:T(8,128)(2,1)}, u32[]{:S(2)}, u32[]{:S(2)}) collective-permute-start(bf16[2,96,1536]{2,1,0:T(8,128)(2,1)} %get-tuple-element.375), channel_id=1, source_target_pairs={{0,8},{4,12},{8,0},{12,4},{16,24},{20,28},{24,16},{28,20},{1,9},{5... | collective-permute-start | bytes 1769480 | tf_op jit(solution)/shard_map/ppermute | solution.py:950
  374.3 53.9 %collective-permute-start.51 = (bf16[1,96,3072]{2,1,0:T(8,128)(2,1)}, bf16[1,96,3072]{2,1,0:T(8,128)(2,1)}, u32[]{:S(2)}, u32[]{:S(2)}) collective-permute-start(bf16[1,96,3072]{2,1,0:T(8,128)(2,1)} %get-tuple-element.373), channel_id=1, source_target_pairs={{0,16},{4,20},{8,24},{12,28},{16,0},{20,4},{24,8},{28,12},{1,17},{... | collective-permute-start | bytes 1769480 | tf_op jit(solution)/shard_map/ppermute | solution.py:950
  413.0 27.0 %collective-permute-start.54 = (bf16[512,768]{1,0:T(8,128)(2,1)}, bf16[512,768]{1,0:T(8,128)(2,1)}, u32[]{:S(2)}, u32[]{:S(2)}) collective-permute-start(bf16[512,768]{1,0:T(8,128)(2,1)} %get-tuple-element.386), channel_id=1, source_target_pairs={{0,2},{2,0},{1,3},{3,1},{4,6},{6,4},{5,7},{7,5},{8,10},{10,8},{9,1... | collective-permute-start | bytes 2359304 | tf_op jit(solution)/shard_map/ppermute | solution.py:945
  414.0 40.1 %collective-permute-start.49 = (bf16[4,96,1792]{2,1,0:T(8,128)(2,1)}, bf16[4,96,1792]{2,1,0:T(8,128)(2,1)}, u32[]{:S(2)}, u32[]{:S(2)}) collective-permute-start(bf16[4,96,1792]{2,1,0:T(8,128)(2,1)} %get-tuple-element.368), channel_id=1, source_target_pairs={{0,4},{4,0},{8,12},{12,8},{16,20},{20,16},{24,28},{28,24},{1,5},{5... | collective-permute-start | bytes 4128776 | tf_op jit(solution)/shard_map/ppermute | solution.py:950
  430.2 42.9 %collective-permute-start.59 = (bf16[1,96,1536]{2,1,0:T(8,128)(2,1)}, bf16[1,96,1536]{2,1,0:T(8,128)(2,1)S(1)}, u32[]{:S(2)}, u32[]{:S(2)}) collective-permute-start(bf16[1,96,1536]{2,1,0:T(8,128)(2,1)} %get-tuple-element.399), channel_id=1, source_target_pairs={{0,16},{4,20},{8,24},{12,28},{16,0},{20,4},{24,8},{28,12},{1,17},{... | collective-permute-start | bytes 884744 | tf_op jit(solution)/shard_map/ppermute | solution.py:950
  431.4 39.5 %collective-permute-start.60 = (bf16[1,96,3072]{2,1,0:T(8,128)(2,1)}, bf16[1,96,3072]{2,1,0:T(8,128)(2,1)}, u32[]{:S(2)}, u32[]{:S(2)}) collective-permute-start(bf16[1,96,3072]{2,1,0:T(8,128)(2,1)} %get-tuple-element.401), channel_id=1, source_target_pairs={{0,16},{4,20},{8,24},{12,28},{16,0},{20,4},{24,8},{28,12},{1,17},{... | collective-permute-start | bytes 1769480 | tf_op jit(solution)/shard_map/ppermute | solution.py:950
  442.2 3.6 collective-permute-start.63
  445.9 47.6 %collective-permute-start.58 = (bf16[4,96,1536]{2,1,0:T(8,128)(2,1)}, bf16[4,96,1536]{2,1,0:T(8,128)(2,1)S(1)}, u32[]{:S(2)}, u32[]{:S(2)}) collective-permute-start(bf16[4,96,1536]{2,1,0:T(8,128)(2,1)} %get-tuple-element.397), channel_id=1, source_target_pairs={{0,8},{4,12},{8,0},{12,4},{16,24},{20,28},{24,16},{28,20},{1,9},{5... | collective-permute-start | bytes 3538952 | tf_op jit(solution)/shard_map/ppermute | solution.py:950
  473.2 30.5 %collective-permute-start.71 = (bf16[96,768]{1,0:T(8,128)(2,1)S(1)}, bf16[96,768]{1,0:T(8,128)(2,1)}, u32[]{:S(2)}, u32[]{:S(2)}) collective-permute-start(bf16[96,768]{1,0:T(8,128)(2,1)S(1)} %slice.180), channel_id=1, source_target_pairs={{0,1},{1,0},{2,3},{3,2},{4,5},{5,4},{6,7},{7,6},{8,9},{9,8},{10,11... | collective-permute-start | bytes 442376 | tf_op jit(solution)/shard_map/ppermute | solution.py:945
  474.5 31.2 %collective-permute-start.70 = (bf16[192,768]{1,0:T(8,128)(2,1)}, bf16[192,768]{1,0:T(8,128)(2,1)S(1)}, u32[]{:S(2)}, u32[]{:S(2)}) collective-permute-start(bf16[192,768]{1,0:T(8,128)(2,1)} %slice.179), channel_id=1, source_target_pairs={{0,1},{1,0},{2,3},{3,2},{4,5},{5,4},{6,7},{7,6},{8,9},{9,8},{10,11... | collective-permute-start | bytes 884744 | tf_op jit(solution)/shard_map/ppermute | solution.py:945
  475.3 35.8 %collective-permute-start.56 = (bf16[2,96,1792]{2,1,0:T(8,128)(2,1)}, bf16[2,96,1792]{2,1,0:T(8,128)(2,1)}, u32[]{:S(2)}, u32[]{:S(2)}) collective-permute-start(bf16[2,96,1792]{2,1,0:T(8,128)(2,1)} %get-tuple-element.393), channel_id=1, source_target_pairs={{0,8},{4,12},{8,0},{12,4},{16,24},{20,28},{24,16},{28,20},{1,9},{5... | collective-permute-start | bytes 2064392 | tf_op jit(solution)/shard_map/ppermute | solution.py:950
  475.3 38.9 %collective-permute-start.62 = (bf16[512,768]{1,0:T(8,128)(2,1)}, bf16[512,768]{1,0:T(8,128)(2,1)}, u32[]{:S(2)}, u32[]{:S(2)}) collective-permute-start(bf16[512,768]{1,0:T(8,128)(2,1)} %add_convert_fusion), channel_id=1, source_target_pairs={{0,1},{1,0},{2,3},{3,2},{4,5},{5,4},{6,7},{7,6},{8,9},{9,8},{10,11... | collective-permute-start | bytes 2359304 | tf_op jit(solution)/shard_map/ppermute | solution.py:945
  497.8 32.2 %collective-permute-start.66 = (bf16[2,96,1536]{2,1,0:T(8,128)(2,1)}, bf16[2,96,1536]{2,1,0:T(8,128)(2,1)}, u32[]{:S(2)}, u32[]{:S(2)}) collective-permute-start(bf16[2,96,1536]{2,1,0:T(8,128)(2,1)} %get-tuple-element.415), channel_id=1, source_target_pairs={{0,16},{4,20},{8,24},{12,28},{16,0},{20,4},{24,8},{28,12},{1,17},{... | collective-permute-start | bytes 1769480 | tf_op jit(solution)/shard_map/ppermute | solution.py:950
  503.7 3.8 collective-permute-start.57
  505.7 37.9 %collective-permute-start.68 = (bf16[96,3072]{1,0:T(8,128)(2,1)S(1)}, bf16[96,3072]{1,0:T(8,128)(2,1)S(1)}, u32[]{:S(2)}, u32[]{:S(2)}) collective-permute-start(bf16[96,3072]{1,0:T(8,128)(2,1)S(1)} %bitcast.104), channel_id=1, source_target_pairs={{0,1},{1,0},{2,3},{3,2},{4,5},{5,4},{6,7},{7,6},{8,9},{9,8},{10,11... | collective-permute-start | bytes 1769480 | tf_op jit(solution)/shard_map/ppermute | solution.py:945
  507.5 6.8 %collective-permute-start.64 = (f32[2560]{0:T(1024)S(1)}, f32[2560]{0:T(1024)S(1)}, u32[]{:S(2)}, u32[]{:S(2)}) collective-permute-start(f32[2560]{0:T(1024)S(1)} %add.129), channel_id=1, source_target_pairs={{0,8},{4,12},{8,0},{12,4},{16,24},{20,28},{24,16},{28,20},{1,9},{5... | collective-permute-start | bytes 30728 | tf_op jit(solution)/shard_map/ppermute | solution.py:950
  514.2 22.9 %collective-permute-start.67 = (bf16[1,96,1792]{2,1,0:T(8,128)(2,1)}, bf16[1,96,1792]{2,1,0:T(8,128)(2,1)S(1)}, u32[]{:S(2)}, u32[]{:S(2)}) collective-permute-start(bf16[1,96,1792]{2,1,0:T(8,128)(2,1)} %get-tuple-element.419), channel_id=1, source_target_pairs={{0,16},{4,20},{8,24},{12,28},{16,0},{20,4},{24,8},{28,12},{1,17},{... | collective-permute-start | bytes 1032200 | tf_op jit(solution)/shard_map/ppermute | solution.py:950
  514.2 26.4 %collective-permute-start.61 = (bf16[512,768]{1,0:T(8,128)(2,1)S(1)}, bf16[512,768]{1,0:T(8,128)(2,1)S(1)}, u32[]{:S(2)}, u32[]{:S(2)}) collective-permute-start(bf16[512,768]{1,0:T(8,128)(2,1)S(1)} %copy-done.56), channel_id=1, source_target_pairs={{0,2},{2,0},{1,3},{3,1},{4,6},{6,4},{5,7},{7,5},{8,10},{10,8},{9,1... | collective-permute-start | bytes 2359304 | tf_op jit(solution)/shard_map/ppermute | solution.py:945
  514.3 22.1 %collective-permute-start.65 = (f32[2560]{0:T(1024)S(1)}, f32[2560]{0:T(1024)S(1)}, u32[]{:S(2)}, u32[]{:S(2)}) collective-permute-start(f32[2560]{0:T(1024)S(1)} %add.135), channel_id=1, source_target_pairs={{0,16},{4,20},{8,24},{12,28},{16,0},{20,4},{24,8},{28,12},{1,17},{... | collective-permute-start | bytes 30728 | tf_op jit(solution)/shard_map/ppermute | solution.py:950
  537.9 7.9 %collective-permute-start.69 = (bf16[96,1536]{1,0:T(8,128)(2,1)S(1)}, bf16[96,1536]{1,0:T(8,128)(2,1)S(1)}, u32[]{:S(2)}, u32[]{:S(2)}) collective-permute-start(bf16[96,1536]{1,0:T(8,128)(2,1)S(1)} %fusion.8), channel_id=1, source_target_pairs={{0,1},{1,0},{2,3},{3,2},{4,5},{5,4},{6,7},{7,6},{8,9},{9,8},{10,11... | collective-permute-start | bytes 884744 | tf_op jit(solution)/shard_map/ppermute | solution.py:945
  (66 other events, 334.1 us)

commit v5 on v4

--- a/solution.py
+++ b/solution.py
@@ -348,17 +348,19 @@
 
 
 def attend_back_kernel(
-    block, begun, ends, table, query_ref, key_ref, value_ref, seg_col_ref, seg_row_ref, own_ref, far_ref, near_ref, far_near_ref,
+    block, table, query_ref, key_ref, value_ref, seg_col_ref, seg_row_ref, own_ref, far_ref, near_ref, far_near_ref,
     weight_ref, far_top_ref, far_bottom_ref, cosine_ref, sine_ref, *refs
 ):
-    sent_ref, key_value_ref = refs[-2:]
+    sent_ref, key_value_ref = refs
+    head = pl.ds(pl.multiple_of(pl.program_id(0) * HEAD_DIM, HEAD_DIM), HEAD_DIM)
+    width = sent_ref.shape[1] - 2 * HEAD_DIM
     scaling = HEAD_DIM ** (-0.5)
     own_rows = own_ref.shape[0]
     far_weight = jnp.where(table[COL] == 0, far_top_ref[...], far_bottom_ref[...])
 
     @pl.when(pl.program_id(0) == 0)
     def _():
-        key_value_ref[...] = refs[0][...] if begun else jnp.zeros_like(key_value_ref)
+        key_value_ref[...] = jnp.zeros_like(key_value_ref)
 
     for start in range(0, query_ref.shape[0], block):
         stop = start + block
@@ -378,51 +380,46 @@
         d_scores = d_scores.astype(BF16)
         d_query = dot(d_scores, key, 1, 0) * scaling
         turned = pltpu.roll(d_query * sine_ref[start:stop], HEAD_DIM // 2, 1)
-        sent_ref[start:stop] = (d_query * cosine_ref[start:stop] + turned).astype(BF16)
+        sent_ref[start:stop, head] = (d_query * cosine_ref[start:stop] + turned).astype(BF16)
         key_value_ref[:stop, :HEAD_DIM] += dot(d_scores, query, 0, 0) * scaling
         key_value_ref[:stop, HEAD_DIM:] += dot(probs.astype(BF16), grad, 0, 0)
 
-    if ends:
-
-        @pl.when(pl.program_id(0) == pl.num_programs(0) - 1)
-        def _():
-            d_key = key_value_ref[:, :HEAD_DIM]
-            turned = pltpu.roll(d_key * sine_ref[...], HEAD_DIM // 2, 1)
-            key_value_ref[:, :HEAD_DIM] = d_key * cosine_ref[...] + turned
-
-
-def attend_back(
-    table, query, key, value, seg_col, seg_row, d_hidden, weight, far_weights, cosine, sine, first, count, begun=None
-):
+    @pl.when(pl.program_id(0) == pl.num_programs(0) - 1)
+    def _():
+        d_key = key_value_ref[:, :HEAD_DIM]
+        turned = pltpu.roll(d_key * sine_ref[...], HEAD_DIM // 2, 1)
+        key_value_ref[:, :HEAD_DIM] = d_key * cosine_ref[...] + turned
+        sent_ref[:, width:] = key_value_ref[...].astype(BF16)
+
+
+def attend_back(table, query, key, value, seg_col, seg_row, d_hidden, weight, far_weights, cosine, sine):
     seq_len, width = query.shape
     features = weight.shape[1]
     heads = width // HEAD_DIM
-    head = pl.BlockSpec((seq_len, HEAD_DIM), lambda h, t: (0, first + h))
-    rows = pl.BlockSpec((HEAD_DIM, features), lambda h, t: (heads * t[COL] + first + h, 0))
-    far_rows = pl.BlockSpec((HEAD_DIM, features), lambda h, t: (first + h, 0))
+    head = pl.BlockSpec((seq_len, HEAD_DIM), lambda h, t: (0, h))
+    rows = pl.BlockSpec((HEAD_DIM, features), lambda h, t: (heads * t[COL] + h, 0))
+    far_rows = pl.BlockSpec((HEAD_DIM, features), lambda h, t: (h, 0))
     shared = whole((seq_len, HEAD_DIM))
     key_value = whole((seq_len, 2 * HEAD_DIM))
-    more = [] if begun is None else [begun]
-    return pl.pallas_call(
-        functools.partial(attend_back_kernel, 256, begun is not None, first + count == heads),
-        grid_spec=pltpu.PrefetchScalarGridSpec(
-            num_scalar_prefetch=1,
-            grid=(count,),
+    return pl.pallas_call(
+        functools.partial(attend_back_kernel, 256),
+        grid_spec=pltpu.PrefetchScalarGridSpec(
+            num_scalar_prefetch=1,
+            grid=(heads,),
             in_specs=[
                 head, shared, shared, whole((seq_len, 1)), whole((1, seq_len)),
                 *[whole(part.shape) for part in d_hidden], rows, far_rows, far_rows, shared, shared,
-                *[key_value] * len(more),
             ],
-            out_specs=[pl.BlockSpec((seq_len, HEAD_DIM), lambda h, t: (0, h)), key_value],
+            out_specs=[whole((seq_len, width + 2 * HEAD_DIM)), key_value],
         ),
         out_shape=[
-            jax.ShapeDtypeStruct((seq_len, count * HEAD_DIM), BF16),
+            jax.ShapeDtypeStruct((seq_len, width + 2 * HEAD_DIM), BF16),
             jax.ShapeDtypeStruct((seq_len, 2 * HEAD_DIM), F32),
         ],
         compiler_params=params("arbitrary"),
-        cost_estimate=cost(24 * seq_len * seq_len * count * HEAD_DIM, 12 * seq_len * width),
+        cost_estimate=cost(24 * seq_len * seq_len * width, 12 * seq_len * width),
         name="attend_back",
-    )(table, query, key, value, seg_col, seg_row, *d_hidden, weight, *far_weights, cosine, sine, *more)
+    )(table, query, key, value, seg_col, seg_row, *d_hidden, weight, *far_weights, cosine, sine)
 
 
 def residual_kernel(table, stream_ref, *refs):
@@ -503,8 +500,8 @@
     up_factor_ref[...] = silu.astype(BF16)
 
 
-def tile_of(units):
-    return next(t for t in (384, 256, 128, units) if units % t == 0)
+def tile_of(units, most=384):
+    return next(t for t in (768, 512, 384, 256, 128, units) if units % t == 0 and (t <= most or t == units))
 
 
 def activate(table, normed, own, far_parts):
@@ -879,8 +876,8 @@
     d_hidden_ref, d_hidden_near_ref, sent_ref, kept_ref, own_ref, other_ref, bias_ref, d_scr, total_scr, hidden_scr, out_scr,
 ):
     first = table[COL] == 0
-    query_width = query_ref.shape[1]
-    own, far = query_ref[...], arrived_ref[:, :query_width]
+    query_width = query_ref.shape[1] - 2 * HEAD_DIM
+    own, far = query_ref[:, :query_width], arrived_ref[:, :query_width]
     d_scr[:, :query_width] = jnp.where(first, own, far)
     d_scr[:, query_width : 2 * query_width] = jnp.where(first, far, own)
     d_key_value = key_value_ref[...] + arrived_ref[:, query_width:].astype(F32)
@@ -1197,7 +1194,7 @@
         return sent, kept
 
     def gate_up_terms(d_gate, d_up, order, merge):
-        tile = tile_of(d_gate.shape[1])
+        tile = tile_of(d_gate.shape[1], 768)
         rights = [(part, 0, part.shape[1] // tile) for part in (d_gate, d_up)]
         terms = split_product(
             table, line.step(second_normed), rights, tile, 2, count, [order[0]] * 2, merge
@@ -1262,16 +1259,16 @@
     mlp_sent = lax.optimization_barrier(mlp_sent.astype(BF16))
     line.mark(mlp_sent)
 
-    attend_inputs = [key, value, seg_col, seg_row, [*d_hidden_low, *d_hidden_near], out_block, out_far, cosine, sine]
-    d_query, d_key_value = attend_back(table, line.step(query), *attend_inputs, 0, HEADS // 4)
-    d_projected_sent = jnp.concatenate([d_query, d_key_value.astype(BF16)], axis=1)
-    d_projected_sent = lax.optimization_barrier(d_projected_sent)
+    d_projected_sent, d_key_value = attend_back(
+        table, line.step(query), key, value, seg_col, seg_row, [*d_hidden_low, *d_hidden_near], out_block, out_far,
+        cosine, sine,
+    )
     line.mark(d_projected_sent)
     arrived = swap(d_projected_sent, "col")
     down_sum1.relay(line)
     gate_up_sum1 = Scatter(table, *gate_up_terms1, pair_first, line)
     sent, kept, d_first_own, d_first_other, bias_part = project_back(
-        table, line.step(d_query), d_key_value, arrived, first_normed, qkv_block, attended_group,
+        table, line.step(d_projected_sent), d_key_value, arrived, first_normed, qkv_block, attended_group,
         d_hidden_low[0], d_hidden_near[0], count, 0,
     )
     line.mark(sent)
@@ -1320,6 +1317,8 @@
     small = dp_step(small, 1)
     own_sum1, far_sum1 = gate_up_sum1.finish(line)
     far_sum1 = swap(line.step(far_sum1.astype(BF16)), "col")
+    far_sum1 = line.step(far_sum1)
+    line.mark(far_sum1)
     for bit in range(2, bits):
         small = dp_step(small, bit)
     heads_sum = heads_sum.finish(line)[0]

time: 563 us -> 556 us (0.988)
  Pallas kernels: 302 us -> 296 us
    ppermute x33, waiting for transfers between devices: 60 us -> 53.5 us  [dp_swap(): return lax.ppermute(part, 'dp', [(i, i ^ 1 << bit) for i in range(count)])]
    unnamed x114 -> x112, local copies, waits for them, and re-layouts: 13.6 us -> 13.6 us
where the time goes in v5:
time: 556 us; the launch traced here: 546 us
  Pallas kernels  296 us (53%)
  waiting for transfers between devices  109 us (20%)
  starting transfers between devices  68 us (12%)
  local copies, waits for them, and re-layouts  37.5 us (7%)
  other arithmetic  33.1 us (6%)
    ppermute x39, waiting for transfers between devices, swap(): return lax.ppermute(part, axis_name, [(0, 1), (1, 0)])  55.5 us
    ppermute x33, waiting for transfers between devices, dp_swap(): return lax.ppermute(part, 'dp', [(i, i ^ 1 << bit) for i in range(count)])  53.5 us
    pallas_call x4, Pallas kernels, split_product(): pl.pallas_call(kernel, grid_spec=pltpu.PrefetchScalarGridSpec(num_scalar_...  45.3 us
    pallas_call x12, Pallas kernels, relay(): pl.pallas_call(relay_kernel, grid_spec=pltpu.PrefetchScalarGridSpec(num_s...  44.2 us
    ppermute x33, starting transfers between devices, dp_swap(): return lax.ppermute(part, 'dp', [(i, i ^ 1 << bit) for i in range(count)])  43.2 us
    pallas_call x2, Pallas kernels, activate(): pl.pallas_call(functools.partial(activate_kernel, width // 2), grid_spec=...  30.4 us
    pallas_call x1, Pallas kernels, normed_grad(): pl.pallas_call(functools.partial(normed_grad_kernel, halves, steps, tile,...  25.8 us
    ppermute x39, starting transfers between devices, swap(): return lax.ppermute(part, axis_name, [(0, 1), (1, 0)])  24.8 us
  transfers between devices with their start and end apart: 72, of which 21 were waited for; matrix products, arithmetic and copies ran while one was open for 10% of the time, Pallas kernels for 53%

profile of v5, /device:TPU:0, one launch (start us, length us, event | category | flops | bytes accessed | tf_op | source)
XLA Modules:
  0.0 545.7 jit_solution(10730721476668892243)
XLA Ops:
  2.0 3.0 collective-permute-start.2
  9.2 1.9 collective-permute-start.4
  11.9 3.1 fusion.9
  17.5 3.8 unit_columns.3
  21.3 3.1 collective-permute-done.4
  29.8 7.4 %unit_columns.4 = (bf16[8,96,3072]{2,1,0:T(8,128)(2,1)}, bf16[8,96,1536]{2,1,0:T(8,128)(2,1)}, bf16[8,96,1536]{2,1,0:T(8,128)(2,1)}) custom-call(s32[9]{0:T(128)} %get-tuple-element.467.table, bf16[768,8960]{1,0:T(8,128)(2,1)} %bitcast.73), custom_call_target="tpu_custom_call" | custom-call | flops 1 | bytes 1 | tf_op jit(solution)/shard_map/unit_columns/pallas_call | solution.py:103
  44.7 7.4 %unit_columns.5 = (bf16[8,96,3072]{2,1,0:T(8,128)(2,1)}, bf16[8,96,1536]{2,1,0:T(8,128)(2,1)}, bf16[8,96,1536]{2,1,0:T(8,128)(2,1)}) custom-call(s32[9]{0:T(128)} %get-tuple-element.466.table, bf16[768,8960]{1,0:T(8,128)(2,1)} %bitcast.74, ...), custom_call_target="tpu_custom_call", output_to_operand_aliasing={{0}: (2, {}), {1}: (3, {}), {2}: (4, {})} | custom-call | flops 1 | bytes 1 | tf_op jit(solution)/shard_map/unit_columns/pallas_call | solution.py:103
  54.5 8.5 %project.1 = (bf16[1024,1536]{1,0:T(8,128)(2,1)}, bf16[1024,768]{1,0:T(8,128)(2,1)}, f32[1024,128]{1,0:T(8,128)}, bf16[1024,384]{1,0:T(8,128)(2,1)}, bf16[1024,1...) custom-call(s32[5]{0:T(128)} %stack.39.table, bf16[512,768]{1,0:T(8,128)(2,1)} %own_ref, ...), custom_call_target="tpu_custom_call" | custom-call | flops 1 | bytes 1 | tf_op jit(solution)/shard_map/project/pallas_call | solution.py:244
  63.0 2.5 collective-permute-done.12
  72.2 10.5 %attend.1 = (bf16[1024,384]{1,0:T(8,128)(2,1)}, bf16[1024,256]{1,0:T(8,128)(2,1)}, bf16[1024,128]{1,0:T(8,128)(2,1)}) custom-call(bf16[1024,384]{1,0:T(8,128)(2,1)} %get-tuple-element.357.query_ref, bf16[1024,128]{1,0:T(8,128)(2,1)} %get-tuple-element.247.key_ref, bf16[1024,128]{1,0:T(8,128)(2,1)} %get-tuple-element.248.value_ref, ...), custom_call_target="tpu_custom_call" | custom-call | flops 1 | bytes 1 | tf_op jit(solution)/shard_map/attend/pallas_call | solution.py:334
  88.5 2.5 unit_rows.2
  91.0 7.0 %unit_rows.3 = (bf16[8,192,768]{2,1,0:T(8,128)(2,1)}, bf16[8,96,768]{2,1,0:T(8,128)(2,1)}) custom-call(s32[9]{0:T(128)} %pad_add_fusion.3.table, bf16[8,2,280,768]{3,2,1,0:T(8,128)(2,1)} %bitcast.79), custom_call_target="tpu_custom_call" | custom-call | flops 1 | bytes 1 | tf_op jit(solution)/shard_map/unit_rows/pallas_call | solution.py:136
  98.0 3.1 collective-permute-done.13.refs_2_
  101.7 2.0 collective-permute-done.19.refs_5_
  107.0 13.3 %residual.1 = (f32[1024,1536]{1,0:T(8,128)}, bf16[1024,1536]{1,0:T(8,128)(2,1)}, f32[1024,128]{1,0:T(8,128)}, bf16[1024,768]{1,0:T(8,128)(2,1)}) custom-call(s32[5]{0:T(128)} %stack.39.table, bf16[1024,1536]{1,0:T(8,128)(2,1)} %get-tuple-element.268.stream_ref, bf16[1024,384]{1,0:T(8,128)(2,1)} %get-tuple-element.250.refs_0_, ...), custom_call_target="tpu_custom_call" | custom-call | flops 1 | bytes 1 | tf_op jit(solution)/shard_map/residual/pallas_call | solution.py:467
  122.9 19.3 %activate.2 = (bf16[1024,1536]{1,0:T(8,128)(2,1)}, bf16[1024,1536]{1,0:T(8,128)(2,1)}, bf16[1024,1536]{1,0:T(8,128)(2,1)}) custom-call(s32[5]{0:T(128)} %stack.39.table, bf16[1024,1536]{1,0:T(8,128)(2,1)} %get-tuple-element.333.normed_ref.left_ref, bf16[768,3072]{1,0:T(8,128)(2,1)} %bitcast.75, bf16[768,3072]{1,0:T(8,128)(2,1)} %bitcast.76, ...), custom_call_target="tpu_custom_call" | custom-call | flops 1 | bytes 1 | tf_op jit(solution)/shard_map/activate/pallas_call | solution.py:521
  148.0 5.6 %join.1.refs_0_.grad_ref = bf16[1024,1536]{1,0:T(8,128)(2,1)} custom-call(s32[5]{0:T(128)} %stack.39.table, bf16[512,768]{1,0:T(8,128)(2,1)} %own_ref.1, bf16[512,768]{1,0:T(8,128)(2,1)} %collective-permute-done.28.near_ref, bf16[512,768]{1,0:T(8,128)(2,1)} %collective-permute-done.26.far_ref, bf16[512,768]{1,0:T(8,128)(2,1)} %collective-permute-done.29.far_near_ref), custom_call_target="tpu_custom_call" | custom-call | flops 1 | bytes 1 | tf_op jit(solution)/shard_map/join/pallas_call | solution.py:284
  153.7 10.4 %split_product.4 = (bf16[4,192,1536]{2,1,0:T(8,128)(2,1)}, bf16[4,192,1536]{2,1,0:T(8,128)(2,1)}) custom-call(s32[5]{0:T(128)} %stack.39.table, bf16[1024,1536]{1,0:T(8,128)(2,1)} %get-tuple-element.335.left_ref.refs_0_, bf16[1024,1536]{1,0:T(8,128)(2,1)} %join.1.refs_0_.grad_ref), custom_call_target="tpu_custom_call" | custom-call | flops 1 | bytes 1 | tf_op jit(solution)/shard_map/split_product/pallas_call | solution.py:657
  164.7 2.2 dynamic-slice_bitcast_fusion
  169.2 13.2 %activate_back.2 = (bf16[1024,1536]{1,0:T(8,128)(2,1)}, bf16[1024,1536]{1,0:T(8,128)(2,1)}) custom-call(s32[5]{0:T(128)} %stack.39.table, bf16[1024,1536]{1,0:T(8,128)(2,1)} %join.1.refs_0_.grad_ref, bf16[1536,768]{1,0:T(8,128)(2,1)} %bitcast.88, bf16[384,768]{1,0:T(8,128)(2,1)} %copy-done.11, bf16[384,768]{1,0:T(8,128)(2,1)} %copy-done.10, ...), custom_call_target="tpu_custom_call" | custom-call | flops 1 | bytes 1 | tf_op jit(solution)/shard_map/activate_back/pallas_call | solution.py:556
  182.4 17.2 %split_product.5 = (bf16[4,96,3072]{2,1,0:T(8,128)(2,1)}, bf16[4,96,3072]{2,1,0:T(8,128)(2,1)}, bf16[4,96,3072]{2,1,0:T(8,128)(2,1)}, bf16[4,96,3072]{2,1,0:T(8,128)(2,1)}) custom-call(s32[5]{0:T(128)} %stack.39.table, bf16[1024,1536]{1,0:T(8,128)(2,1)} %get-tuple-element.333.normed_ref.left_ref, bf16[1024,1536]{1,0:T(8,128)(2,1)} %get-tuple-element.314.refs_0_, ...), custom_call_target="tpu_custom_call" | custom-call | flops 1 | bytes 1 | tf_op jit(solution)/shard_map/split_product/pallas_call | solution.py:657
  203.0 11.2 %activate.3 = (bf16[1024,768]{1,0:T(8,128)(2,1)}, bf16[1024,768]{1,0:T(8,128)(2,1)}, bf16[1024,768]{1,0:T(8,128)(2,1)}) custom-call(s32[5]{0:T(128)} %stack.39.table, bf16[1024,1536]{1,0:T(8,128)(2,1)} %get-tuple-element.333.normed_ref.left_ref, bf16[768,1536]{1,0:T(8,128)(2,1)} %bitcast.81, bf16[768,1536]{1,0:T(8,128)(2,1)} %bitcast.82, ...), custom_call_target="tpu_custom_call" | custom-call | flops 1 | bytes 1 | tf_op jit(solution)/shard_map/activate/pallas_call | solution.py:521
  214.2 11.1 %collective-permute-done.33.refs_0_.refs_8_ = bf16[768,768]{1,0:T(8,128)(2,1)S(1)} collective-permute-done((bf16[768,768]{1,0:T(8,128)(2,1)}, bf16[768,768]{1,0:T(8,128)(2,1)S(1)}, u32[]{:S(2)}, u32[]{:S(2)}) %collective-permute-start.33) | collective-permute-done | bytes 1179680 | tf_op jit(solution)/shard_map/ppermute | solution.py:942
  225.3 4.3 relay.12
  230.6 8.5 %activate_back.3 = (bf16[1024,768]{1,0:T(8,128)(2,1)}, bf16[1024,768]{1,0:T(8,128)(2,1)}) custom-call(s32[5]{0:T(128)} %stack.39.table, bf16[1024,1536]{1,0:T(8,128)(2,1)} %join.1.refs_0_.grad_ref, bf16[768,768]{1,0:T(8,128)(2,1)} %bitcast.92, bf16[768,768]{1,0:T(8,128)(2,1)} %copy-done.13, bf16[1024,768]{1,0:T(8,128)(2,1)} %get-tuple-element.311.refs_1_, ...), custom_call_target="tpu_custom_call" | custom-call | flops 1 | bytes 1 | tf_op jit(solution)/shard_map/activate_back/pallas_call | solution.py:556
  239.1 25.8 %normed_grad.1 = (f32[512,1536]{1,0:T(8,128)}, bf16[512,768]{1,0:T(8,128)(2,1)}, bf16[512,768]{1,0:T(8,128)(2,1)}) custom-call(s32[5]{0:T(128)} %stack.39.table, bf16[1024,1536]{1,0:T(8,128)(2,1)} %get-tuple-element.314.refs_0_, bf16[1024,1536]{1,0:T(8,128)(2,1)} %get-tuple-element.302.refs_1_, bf16[1024,768]{1,0:T(8,128)(2,1)} %get-tuple-element.313.refs_2_.refs_0_, ...), custom_call_target="tpu_custom_call" | custom-call | flops 1 | bytes 1 | tf_op jit(solution)/shard_map/normed_grad/pallas_call | solution.py:766
  264.9 6.8 %split_product.6 = (bf16[4,96,1536]{2,1,0:T(8,128)(2,1)}, bf16[4,96,1536]{2,1,0:T(8,128)(2,1)}) custom-call(s32[5]{0:T(128)} %stack.39.table, bf16[1024,768]{1,0:T(8,128)(2,1)} %get-tuple-element.324.left_ref.refs_1_, bf16[1024,1536]{1,0:T(8,128)(2,1)} %join.1.refs_0_.grad_ref), custom_call_target="tpu_custom_call" | custom-call | flops 1 | bytes 1 | tf_op jit(solution)/shard_map/split_product/pallas_call | solution.py:657
  272.8 3.4 relay.13
  276.2 4.2 relay.14
  282.6 2.6 collective-permute-start.39
  285.8 5.0 chip_sum.1
  292.8 10.9 %split_product.7 = (bf16[8,96,1536]{2,1,0:T(8,128)(2,1)}, bf16[8,96,1536]{2,1,0:T(8,128)(2,1)}) custom-call(s32[5]{0:T(128)} %stack.39.table, bf16[1024,1536]{1,0:T(8,128)(2,1)} %get-tuple-element.333.normed_ref.left_ref, bf16[1024,768]{1,0:T(8,128)(2,1)} %get-tuple-element.313.refs_2_.refs_0_, bf16[1024,768]{1,0:T(8,128)(2,1)} %get-tuple-element.315.refs_3_.refs_1_), custom_call_target="tpu_custom_call" | custom-call | flops 1 | bytes 1 | tf_op jit(solution)/shard_map/split_product/pallas_call | solution.py:657
  303.7 15.0 %down.1 = (f32[512,1536]{1,0:T(8,128)}, bf16[512,768]{1,0:T(8,128)(2,1)}, bf16[512,768]{1,0:T(8,128)(2,1)}) custom-call(s32[5]{0:T(128)} %stack.39.table, bf16[1024,1536]{1,0:T(8,128)(2,1)} %get-tuple-element.335.left_ref.refs_0_, bf16[1024,768]{1,0:T(8,128)(2,1)} %get-tuple-element.324.left_ref.refs_1_, bf16[1536,768]{1,0:T(8,128)(2,1)} %bitcast.89, ...), custom_call_target="tpu_custom_call" | custom-call | flops 1 | bytes 1 | tf_op jit(solution)/shard_map/down/pallas_call | solution.py:604
  320.3 3.4 relay.15
  325.1 4.3 relay.16
  332.2 7.1 %norm_back.1 = (f32[512,768]{1,0:T(8,128)}, bf16[512,768]{1,0:T(8,128)(2,1)}, bf16[512,768]{1,0:T(8,128)(2,1)}, f32[1,768]{1,0:T(1,128)}) custom-call(s32[5]{0:T(128)} %stack.39.table, f32[512,1536]{1,0:T(8,128)} %get-tuple-element.352.chip_ref, bf16[512,768]{1,0:T(8,128)(2,1)} %collective-permute-done.43.far_own_ref, ...), custom_call_target="tpu_custom_call" | custom-call | flops 1 | bytes 1 | tf_op jit(solution)/shard_map/norm_back/pallas_call | solution.py:854
  339.9 2.5 add_convert_fusion
  344.2 19.4 %attend_back.1 = (bf16[1024,640]{1,0:T(8,128)(2,1)}, f32[1024,256]{1,0:T(8,128)}) custom-call(s32[5]{0:T(128)} %stack.39.table, bf16[1024,384]{1,0:T(8,128)(2,1)} %get-tuple-element.357.query_ref, bf16[1024,128]{1,0:T(8,128)(2,1)} %get-tuple-element.247.key_ref, bf16[1024,128]{1,0:T(8,128)(2,1)} %get-tuple-element.248.value_ref, ...), custom_call_target="tpu_custom_call" | custom-call | flops 1 | bytes 1 | tf_op jit(solution)/shard_map/attend_back/pallas_call | solution.py:404
  364.6 3.4 relay.17
  369.4 2.0 collective-permute-start.52
  371.4 2.2 collective-permute-start.51
  373.6 26.1 %collective-permute-done.48.arrived_ref = bf16[1024,640]{1,0:T(8,128)(2,1)} collective-permute-done((bf16[1024,640]{1,0:T(8,128)(2,1)}, bf16[1024,640]{1,0:T(8,128)(2,1)}, u32[]{:S(2)}, u32[]{:S(2)}) %collective-permute-start.48) | collective-permute-done | bytes 1310752 | tf_op jit(solution)/shard_map/ppermute | solution.py:942
  399.7 10.7 %project_back.1 = (bf16[4,96,1792]{2,1,0:T(8,128)(2,1)}, bf16[4,96,1792]{2,1,0:T(8,128)(2,1)}, f32[512,768]{1,0:T(8,128)}, bf16[512,768]{1,0:T(8,128)(2,1)}, f32[1,1024]{1,0:T(1,128)}) custom-call(s32[5]{0:T(128)} %stack.39.table, bf16[1024,640]{1,0:T(8,128)(2,1)} %get-tuple-element.363.query_ref, f32[1024,256]{1,0:T(8,128)} %get-tuple-element.364.key_value_ref, ...), custom_call_target="tpu_custom_call" | custom-call | flops 1 | bytes 1 | tf_op jit(solution)/shard_map/project_back/pallas_call | solution.py:913
  417.5 3.5 relay.18
  422.7 2.8 relay.19
  425.5 2.1 convert_add_fusion.3
  431.9 5.1 relay.20
  437.0 2.3 fusion.6
  440.6 2.4 collective-permute-done.63
  444.3 7.2 %collective-permute-done.49.arrived_sent_ref.arrived_ref = bf16[4,96,1792]{2,1,0:T(8,128)(2,1)} collective-permute-done((bf16[4,96,1792]{2,1,0:T(8,128)(2,1)}, bf16[4,96,1792]{2,1,0:T(8,128)(2,1)}, u32[]{:S(2)}, u32[]{:S(2)}) %collective-permute-start.49) | collective-permute-done | bytes 1376288 | tf_op jit(solution)/shard_map/ppermute | solution.py:947
  451.5 3.5 relay.21
  454.9 13.5 %collective-permute-done.60 = bf16[1,96,3072]{2,1,0:T(8,128)(2,1)} collective-permute-done((bf16[1,96,3072]{2,1,0:T(8,128)(2,1)}, bf16[1,96,3072]{2,1,0:T(8,128)(2,1)}, u32[]{:S(2)}, u32[]{:S(2)}) %collective-permute-start.60) | collective-permute-done | bytes 589856 | tf_op jit(solution)/shard_map/ppermute | solution.py:947
  468.4 2.2 convert_add_fusion.2
  474.1 15.9 %collective-permute-done.58.arrived_sent_ref.arrived_ref = bf16[4,96,1536]{2,1,0:T(8,128)(2,1)S(1)} collective-permute-done((bf16[4,96,1536]{2,1,0:T(8,128)(2,1)}, bf16[4,96,1536]{2,1,0:T(8,128)(2,1)S(1)}, u32[]{:S(2)}, u32[]{:S(2)}) %collective-permute-start.58) | collective-permute-done | bytes 1179680 | tf_op jit(solution)/shard_map/ppermute | solution.py:947
  491.0 3.3 relay.22
  494.3 2.6 collective-permute-start.66
  496.9 3.3 fusion.5
  505.2 2.4 collective-permute-start.64
  508.9 3.0 relay.23
  512.0 2.9 collective-permute-start.65
  514.9 12.8 %collective-permute-done.66 = bf16[2,96,1536]{2,1,0:T(8,128)(2,1)} collective-permute-done((bf16[2,96,1536]{2,1,0:T(8,128)(2,1)}, bf16[2,96,1536]{2,1,0:T(8,128)(2,1)}, u32[]{:S(2)}, u32[]{:S(2)}) %collective-permute-start.66) | collective-permute-done | bytes 589856 | tf_op jit(solution)/shard_map/ppermute | solution.py:947
  530.6 3.0 fusion.7
  533.7 2.3 collective-permute-done.67.far1_ref
  539.7 5.6 %spread_columns.1 = f32[96,8960]{1,0:T(8,128)} custom-call(s32[5]{0:T(128)} %stack.39.table, f32[96,3072]{1,0:T(8,128)} %bitcast.94, f32[96,1536]{1,0:T(8,128)} %slice_bitcast_fusion.own1_ref, bf16[96,3072]{1,0:T(8,128)(2,1)} %copy-done.36, bf16[96,1536]{1,0:T(8,128)(2,1)} %copy-done.48), custom_call_target="tpu_custom_call" | custom-call | flops 1 | bytes 1 | tf_op jit(solution)/shard_map/spread_columns/pallas_call | solution.py:178
  (318 shorter events, 105.1 us)
Async XLA Ops:
  2.0 15.4 %collective-permute-start.2 = (f32[2,768]{1,0:T(2,128)S(1)}, f32[2,768]{1,0:T(2,128)S(1)}, u32[]{:S(2)}, u32[]{:S(2)}) collective-permute-start(f32[2,768]{1,0:T(2,128)S(1)} %pad_maximum_fusion.17), channel_id=1, source_target_pairs={{0,1},{1,0},{2,3},{3,2},{4,5},{5,4},{6,7},{7,6},{8,9},{9,8},{10,11... | collective-permute-start | bytes 18440 | tf_op jit(solution)/shard_map/ppermute | solution.py:942
  5.1 38.5 %collective-permute-start.6 = (bf16[512,768]{1,0:T(8,128)(2,1)}, bf16[512,768]{1,0:T(8,128)(2,1)}, u32[]{:S(2)}, u32[]{:S(2)}) collective-permute-start(bf16[512,768]{1,0:T(8,128)(2,1)} %own_ref), channel_id=1, source_target_pairs={{0,2},{2,0},{1,3},{3,1},{4,6},{6,4},{5,7},{7,5},{8,10},{10,8},{9,1... | collective-permute-start | bytes 2359304 | tf_op jit(solution)/shard_map/ppermute | solution.py:942
  5.1 38.5 %collective-permute-start = (bf16[768,768]{1,0:T(8,128)(2,1)}, bf16[768,768]{1,0:T(8,128)(2,1)}, u32[]{:S(2)}, u32[]{:S(2)}) collective-permute-start(bf16[768,768]{1,0:T(8,128)(2,1)} %bitcast.84), channel_id=1, source_target_pairs={{0,2},{2,0},{1,3},{3,1},{4,6},{6,4},{5,7},{7,5},{8,10},{10,8},{9,1... | collective-permute-start | bytes 3538952 | tf_op jit(solution)/shard_map/ppermute | solution.py:942
  9.1 15.3 %collective-permute-start.1 = (bf16[96,1408]{1,0:T(8,128)(2,1)S(1)}, bf16[96,1408]{1,0:T(8,128)(2,1)}, u32[]{:S(2)}, u32[]{:S(2)}) collective-permute-start(bf16[96,1408]{1,0:T(8,128)(2,1)S(1)} %get-tuple-element.218), channel_id=1, source_target_pairs={{0,1},{1,0},{2,3},{3,2},{4,5},{5,4},{6,7},{7,6},{8,9},{9,8},{10,11... | collective-permute-start | bytes 811016 | tf_op jit(solution)/shard_map/ppermute | solution.py:942
  9.2 15.2 %collective-permute-start.4 = (bf16[96,1408]{1,0:T(8,128)(2,1)}, bf16[96,1408]{1,0:T(8,128)(2,1)}, u32[]{:S(2)}, u32[]{:S(2)}) collective-permute-start(bf16[96,1408]{1,0:T(8,128)(2,1)} %get-tuple-element.219), channel_id=1, source_target_pairs={{0,1},{1,0},{2,3},{3,2},{4,5},{5,4},{6,7},{7,6},{8,9},{9,8},{10,11... | collective-permute-start | bytes 811016 | tf_op jit(solution)/shard_map/ppermute | solution.py:942
  17.4 23.7 %collective-permute-start.7 = (bf16[512,768]{1,0:T(8,128)(2,1)S(1)}, bf16[512,768]{1,0:T(8,128)(2,1)S(1)}, u32[]{:S(2)}, u32[]{:S(2)}) collective-permute-start(bf16[512,768]{1,0:T(8,128)(2,1)S(1)} %copy-done.7), channel_id=1, source_target_pairs={{0,1},{1,0},{2,3},{3,2},{4,5},{5,4},{6,7},{7,6},{8,9},{9,8},{10,11... | collective-permute-start | bytes 2359304 | tf_op jit(solution)/shard_map/ppermute | solution.py:942
  24.4 13.5 %collective-permute-start.3 = (bf16[96,1408]{1,0:T(8,128)(2,1)}, bf16[96,1408]{1,0:T(8,128)(2,1)S(1)}, u32[]{:S(2)}, u32[]{:S(2)}) collective-permute-start(bf16[96,1408]{1,0:T(8,128)(2,1)} %collective-permute-done.1), channel_id=1, source_target_pairs={{0,4},{4,0},{8,12},{12,8},{16,20},{20,16},{24,28},{28,24},{1,5},{5... | collective-permute-start | bytes 811016 | tf_op jit(solution)/shard_map/ppermute | solution.py:947
  25.9 11.3 %collective-permute-start.5 = (bf16[96,1408]{1,0:T(8,128)(2,1)}, bf16[96,1408]{1,0:T(8,128)(2,1)S(1)}, u32[]{:S(2)}, u32[]{:S(2)}) collective-permute-start(bf16[96,1408]{1,0:T(8,128)(2,1)} %collective-permute-done.4), channel_id=1, source_target_pairs={{0,8},{4,12},{8,0},{12,4},{16,24},{20,28},{24,16},{28,20},{1,9},{5... | collective-permute-start | bytes 811016 | tf_op jit(solution)/shard_map/ppermute | solution.py:947
  37.2 28.3 %collective-permute-start.12 = (bf16[2,96,3072]{2,1,0:T(8,128)(2,1)}, bf16[2,96,3072]{2,1,0:T(8,128)(2,1)}, u32[]{:S(2)}, u32[]{:S(2)}) collective-permute-start(bf16[2,96,3072]{2,1,0:T(8,128)(2,1)} %unit_columns.3), channel_id=1, source_target_pairs={{0,1},{1,0},{2,3},{3,2},{4,5},{5,4},{6,7},{7,6},{8,9},{9,8},{10,11... | collective-permute-start | bytes 3538952 | tf_op jit(solution)/shard_map/ppermute | solution.py:942
  40.0 12.2 %collective-permute-start.10 = (bf16[192,1408]{1,0:T(8,128)(2,1)S(1)}, bf16[192,1408]{1,0:T(8,128)(2,1)S(1)}, u32[]{:S(2)}, u32[]{:S(2)}) collective-permute-start(bf16[192,1408]{1,0:T(8,128)(2,1)S(1)} %pad_maximum_fusion.9.part0_ref), channel_id=1, source_target_pairs={{0,8},{4,12},{8,0},{12,4},{16,24},{20,28},{24,16},{28,20},{1,9},{5... | collective-permute-start | bytes 1622024 | tf_op jit(solution)/shard_map/ppermute | solution.py:947
  41.1 12.4 %collective-permute-start.11 = (bf16[192,1408]{1,0:T(8,128)(2,1)S(1)}, bf16[192,1408]{1,0:T(8,128)(2,1)S(1)}, u32[]{:S(2)}, u32[]{:S(2)}) collective-permute-start(bf16[192,1408]{1,0:T(8,128)(2,1)S(1)} %pad_maximum_fusion.10.part1_ref), channel_id=1, source_target_pairs={{0,4},{4,0},{8,12},{12,8},{16,20},{20,16},{24,28},{28,24},{1,5},{5... | collective-permute-start | bytes 1622024 | tf_op jit(solution)/shard_map/ppermute | solution.py:947
  43.6 9.9 %collective-permute-start.8 = (bf16[256,768]{1,0:T(8,128)(2,1)}, bf16[256,768]{1,0:T(8,128)(2,1)S(1)}, u32[]{:S(2)}, u32[]{:S(2)}) collective-permute-start(bf16[256,768]{1,0:T(8,128)(2,1)} %get-tuple-element.238), channel_id=1, source_target_pairs={{0,2},{2,0},{1,3},{3,1},{4,6},{6,4},{5,7},{7,5},{8,10},{10,8},{9,1... | collective-permute-start | bytes 1179656 | tf_op jit(solution)/shard_map/ppermute | solution.py:942
  43.6 9.9 %collective-permute-start.9 = (bf16[256,768]{1,0:T(8,128)(2,1)}, bf16[256,768]{1,0:T(8,128)(2,1)S(1)}, u32[]{:S(2)}, u32[]{:S(2)}) collective-permute-start(bf16[256,768]{1,0:T(8,128)(2,1)} %get-tuple-element.239), channel_id=1, source_target_pairs={{0,2},{2,0},{1,3},{3,1},{4,6},{6,4},{5,7},{7,5},{8,10},{10,8},{9,1... | collective-permute-start | bytes 1179656 | tf_op jit(solution)/shard_map/ppermute | solution.py:942
  66.8 17.9 %collective-permute-start.15 = (bf16[96,3072]{1,0:T(8,128)(2,1)S(1)}, bf16[96,3072]{1,0:T(8,128)(2,1)S(1)}, u32[]{:S(2)}, u32[]{:S(2)}) collective-permute-start(bf16[96,3072]{1,0:T(8,128)(2,1)S(1)} %get-tuple-element.245), channel_id=1, source_target_pairs={{0,8},{4,12},{8,0},{12,4},{16,24},{20,28},{24,16},{28,20},{1,9},{5... | collective-permute-start | bytes 1769480 | tf_op jit(solution)/shard_map/ppermute | solution.py:947
  70.7 14.1 %collective-permute-start.14 = (bf16[96,3072]{1,0:T(8,128)(2,1)S(1)}, bf16[96,3072]{1,0:T(8,128)(2,1)S(1)}, u32[]{:S(2)}, u32[]{:S(2)}) collective-permute-start(bf16[96,3072]{1,0:T(8,128)(2,1)S(1)} %get-tuple-element.244), channel_id=1, source_target_pairs={{0,4},{4,0},{8,12},{12,8},{16,20},{20,16},{24,28},{28,24},{1,5},{5... | collective-permute-start | bytes 1769480 | tf_op jit(solution)/shard_map/ppermute | solution.py:947
  82.7 18.4 %collective-permute-start.16 = (bf16[1024,128]{1,0:T(8,128)(2,1)}, bf16[1024,128]{1,0:T(8,128)(2,1)}, u32[]{:S(2)}, u32[]{:S(2)}) collective-permute-start(bf16[1024,128]{1,0:T(8,128)(2,1)} %get-tuple-element.266), channel_id=1, source_target_pairs={{0,1},{1,0},{2,3},{3,2},{4,5},{5,4},{6,7},{7,6},{8,9},{9,8},{10,11... | collective-permute-start | bytes 786440 | tf_op jit(solution)/shard_map/ppermute | solution.py:942
  83.3 17.8 %collective-permute-start.13 = (bf16[1024,256]{1,0:T(8,128)(2,1)}, bf16[1024,256]{1,0:T(8,128)(2,1)}, u32[]{:S(2)}, u32[]{:S(2)}) collective-permute-start(bf16[1024,256]{1,0:T(8,128)(2,1)} %get-tuple-element.249), channel_id=1, source_target_pairs={{0,1},{1,0},{2,3},{3,2},{4,5},{5,4},{6,7},{7,6},{8,9},{9,8},{10,11... | collective-permute-start | bytes 1572872 | tf_op jit(solution)/shard_map/ppermute | solution.py:942
  84.8 16.8 %collective-permute-start.17 = (bf16[1024,384]{1,0:T(8,128)(2,1)}, bf16[1024,384]{1,0:T(8,128)(2,1)}, u32[]{:S(2)}, u32[]{:S(2)}) collective-permute-start(bf16[1024,384]{1,0:T(8,128)(2,1)} %get-tuple-element.250.refs_0_), channel_id=1, source_target_pairs={{0,2},{2,0},{1,3},{3,1},{4,6},{6,4},{5,7},{7,5},{8,10},{10,8},{9,1... | collective-permute-start | bytes 2359304 | tf_op jit(solution)/shard_map/ppermute | solution.py:942
  85.2 35.1 %collective-permute-start.23 = (bf16[192,3072]{1,0:T(8,128)(2,1)S(1)}, bf16[192,3072]{1,0:T(8,128)(2,1)S(1)}, u32[]{:S(2)}, u32[]{:S(2)}) collective-permute-start(bf16[192,3072]{1,0:T(8,128)(2,1)S(1)} %pad_maximum_fusion.1.refs_0_.refs_4_.refs_6_), channel_id=1, source_target_pairs={{0,8},{4,12},{8,0},{12,4},{16,24},{20,28},{24,16},{28,20},{1,9},{5... | collective-permute-start | bytes 3538952 | tf_op jit(solution)/shard_map/ppermute | solution.py:947
  85.8 34.5 %collective-permute-start.24 = (bf16[192,3072]{1,0:T(8,128)(2,1)S(1)}, bf16[192,3072]{1,0:T(8,128)(2,1)}, u32[]{:S(2)}, u32[]{:S(2)}) collective-permute-start(bf16[192,3072]{1,0:T(8,128)(2,1)S(1)} %pad_maximum_fusion.2.refs_1_.refs_5_.refs_7_), channel_id=1, source_target_pairs={{0,4},{4,0},{8,12},{12,8},{16,20},{20,16},{24,28},{28,24},{1,5},{5... | collective-permute-start | bytes 3538952 | tf_op jit(solution)/shard_map/ppermute | solution.py:947
  104.1 16.5 %collective-permute-start.22 = (bf16[2,192,768]{2,1,0:T(8,128)(2,1)}, bf16[2,192,768]{2,1,0:T(8,128)(2,1)}, u32[]{:S(2)}, u32[]{:S(2)}) collective-permute-start(bf16[2,192,768]{2,1,0:T(8,128)(2,1)} %unit_rows.2), channel_id=1, source_target_pairs={{0,1},{1,0},{2,3},{3,2},{4,5},{5,4},{6,7},{7,6},{8,9},{9,8},{10,11... | collective-permute-start | bytes 1769480 | tf_op jit(solution)/shard_map/ppermute | solution.py:942
  104.6 37.5 %collective-permute-start.26 = (bf16[512,768]{1,0:T(8,128)(2,1)}, bf16[512,768]{1,0:T(8,128)(2,1)}, u32[]{:S(2)}, u32[]{:S(2)}) collective-permute-start(bf16[512,768]{1,0:T(8,128)(2,1)} %own_ref.1), channel_id=1, source_target_pairs={{0,1},{1,0},{2,3},{3,2},{4,5},{5,4},{6,7},{7,6},{8,9},{9,8},{10,11... | collective-permute-start | bytes 2359304 | tf_op jit(solution)/shard_map/ppermute | solution.py:942
  121.8 20.4 %collective-permute-start.27 = (bf16[192,768]{1,0:T(8,128)(2,1)S(1)}, bf16[192,768]{1,0:T(8,128)(2,1)S(1)}, u32[]{:S(2)}, u32[]{:S(2)}) collective-permute-start(bf16[192,768]{1,0:T(8,128)(2,1)S(1)} %get-tuple-element.278), channel_id=1, source_target_pairs={{0,8},{4,12},{8,0},{12,4},{16,24},{20,28},{24,16},{28,20},{1,9},{5... | collective-permute-start | bytes 884744 | tf_op jit(solution)/shard_map/ppermute | solution.py:947
  122.4 19.9 %collective-permute-start.25 = (bf16[192,768]{1,0:T(8,128)(2,1)S(1)}, bf16[192,768]{1,0:T(8,128)(2,1)S(1)}, u32[]{:S(2)}, u32[]{:S(2)}) collective-permute-start(bf16[192,768]{1,0:T(8,128)(2,1)S(1)} %get-tuple-element.277), channel_id=1, source_target_pairs={{0,4},{4,0},{8,12},{12,8},{16,20},{20,16},{24,28},{28,24},{1,5},{5... | collective-permute-start | bytes 884744 | tf_op jit(solution)/shard_map/ppermute | solution.py:947
  142.2 5.9 %collective-permute-start.29 = (bf16[512,768]{1,0:T(8,128)(2,1)}, bf16[512,768]{1,0:T(8,128)(2,1)}, u32[]{:S(2)}, u32[]{:S(2)}) collective-permute-start(bf16[512,768]{1,0:T(8,128)(2,1)} %collective-permute-done.26.far_ref), channel_id=1, source_target_pairs={{0,2},{2,0},{1,3},{3,1},{4,6},{6,4},{5,7},{7,5},{8,10},{10,8},{9,1... | collective-permute-start | bytes 2359304 | tf_op jit(solution)/shard_map/ppermute | solution.py:942
  143.7 4.4 collective-permute-start.28
  144.1 19.9 %collective-permute-start.31 = (bf16[384,768]{1,0:T(8,128)(2,1)S(1)}, bf16[384,768]{1,0:T(8,128)(2,1)}, u32[]{:S(2)}, u32[]{:S(2)}) collective-permute-start(bf16[384,768]{1,0:T(8,128)(2,1)S(1)} %pad_maximum_fusion.8.refs_1_.refs_5_), channel_id=1, source_target_pairs={{0,4},{4,0},{8,12},{12,8},{16,20},{20,16},{24,28},{28,24},{1,5},{5... | collective-permute-start | bytes 1769480 | tf_op jit(solution)/shard_map/ppermute | solution.py:947
  145.6 18.4 %collective-permute-start.30 = (bf16[384,768]{1,0:T(8,128)(2,1)S(1)}, bf16[384,768]{1,0:T(8,128)(2,1)}, u32[]{:S(2)}, u32[]{:S(2)}) collective-permute-start(bf16[384,768]{1,0:T(8,128)(2,1)S(1)} %pad_maximum_fusion.7.refs_0_.refs_4_), channel_id=1, source_target_pairs={{0,8},{4,12},{8,0},{12,4},{16,24},{20,28},{24,16},{28,20},{1,9},{5... | collective-permute-start | bytes 1769480 | tf_op jit(solution)/shard_map/ppermute | solution.py:947
  147.2 54.4 %collective-permute-start.34 = (bf16[768,1536]{1,0:T(8,128)(2,1)}, bf16[768,1536]{1,0:T(8,128)(2,1)S(1)}, u32[]{:S(2)}, u32[]{:S(2)}) collective-permute-start(bf16[768,1536]{1,0:T(8,128)(2,1)} %bitcast.35), channel_id=1, source_target_pairs={{0,1},{1,0},{2,3},{3,2},{4,5},{5,4},{6,7},{7,6},{8,9},{9,8},{10,11... | collective-permute-start | bytes 7077896 | tf_op jit(solution)/shard_map/ppermute | solution.py:942
  164.0 61.3 %collective-permute-start.32 = (bf16[4,192,1536]{2,1,0:T(8,128)(2,1)}, bf16[4,192,1536]{2,1,0:T(8,128)(2,1)}, u32[]{:S(2)}, u32[]{:S(2)}) collective-permute-start(bf16[4,192,1536]{2,1,0:T(8,128)(2,1)} %get-tuple-element.300), channel_id=1, source_target_pairs={{0,4},{4,0},{8,12},{12,8},{16,20},{20,16},{24,28},{28,24},{1,5},{5... | collective-permute-start | bytes 7077896 | tf_op jit(solution)/shard_map/ppermute | solution.py:947
  168.0 57.3 %collective-permute-start.33 = (bf16[768,768]{1,0:T(8,128)(2,1)}, bf16[768,768]{1,0:T(8,128)(2,1)S(1)}, u32[]{:S(2)}, u32[]{:S(2)}) collective-permute-start(bf16[768,768]{1,0:T(8,128)(2,1)} %bitcast.32), channel_id=1, source_target_pairs={{0,1},{1,0},{2,3},{3,2},{4,5},{5,4},{6,7},{7,6},{8,9},{9,8},{10,11... | collective-permute-start | bytes 3538952 | tf_op jit(solution)/shard_map/ppermute | solution.py:942
  199.6 76.6 %collective-permute-start.35 = (bf16[4,96,3072]{2,1,0:T(8,128)(2,1)}, bf16[4,96,3072]{2,1,0:T(8,128)(2,1)}, u32[]{:S(2)}, u32[]{:S(2)}) collective-permute-start(bf16[4,96,3072]{2,1,0:T(8,128)(2,1)} %get-tuple-element.319), channel_id=1, source_target_pairs={{0,4},{4,0},{8,12},{12,8},{16,20},{20,16},{24,28},{28,24},{1,5},{5... | collective-permute-start | bytes 7077896 | tf_op jit(solution)/shard_map/ppermute | solution.py:947
  229.6 42.1 %collective-permute-start.36 = (bf16[2,192,1536]{2,1,0:T(8,128)(2,1)}, bf16[2,192,1536]{2,1,0:T(8,128)(2,1)S(1)}, u32[]{:S(2)}, u32[]{:S(2)}) collective-permute-start(bf16[2,192,1536]{2,1,0:T(8,128)(2,1)} %get-tuple-element.321), channel_id=1, source_target_pairs={{0,8},{4,12},{8,0},{12,4},{16,24},{20,28},{24,16},{28,20},{1,9},{5... | collective-permute-start | bytes 3538952 | tf_op jit(solution)/shard_map/ppermute | solution.py:947
  230.0 93.7 %collective-permute-start.40 = (bf16[4,96,3072]{2,1,0:T(8,128)(2,1)}, bf16[4,96,3072]{2,1,0:T(8,128)(2,1)S(1)}, u32[]{:S(2)}, u32[]{:S(2)}) collective-permute-start(bf16[4,96,3072]{2,1,0:T(8,128)(2,1)} %get-tuple-element.342), channel_id=1, source_target_pairs={{0,4},{4,0},{8,12},{12,8},{16,20},{20,16},{24,28},{28,24},{1,5},{5... | collective-permute-start | bytes 7077896 | tf_op jit(solution)/shard_map/ppermute | solution.py:947
  280.4 38.8 %collective-permute-start.41 = (bf16[2,96,3072]{2,1,0:T(8,128)(2,1)}, bf16[2,96,3072]{2,1,0:T(8,128)(2,1)S(1)}, u32[]{:S(2)}, u32[]{:S(2)}) collective-permute-start(bf16[2,96,3072]{2,1,0:T(8,128)(2,1)} %get-tuple-element.344), channel_id=1, source_target_pairs={{0,8},{4,12},{8,0},{12,4},{16,24},{20,28},{24,16},{28,20},{1,9},{5... | collective-permute-start | bytes 3538952 | tf_op jit(solution)/shard_map/ppermute | solution.py:947
  282.0 3.7 collective-permute-start.38
  282.6 46.9 %collective-permute-start.39 = (bf16[1,192,1536]{2,1,0:T(8,128)(2,1)}, bf16[1,192,1536]{2,1,0:T(8,128)(2,1)S(1)}, u32[]{:S(2)}, u32[]{:S(2)}) collective-permute-start(bf16[1,192,1536]{2,1,0:T(8,128)(2,1)} %get-tuple-element.340), channel_id=1, source_target_pairs={{0,16},{4,20},{8,24},{12,28},{16,0},{20,4},{24,8},{28,12},{1,17},{... | collective-permute-start | bytes 1769480 | tf_op jit(solution)/shard_map/ppermute | solution.py:947
  290.8 41.4 %collective-permute-start.43 = (bf16[512,768]{1,0:T(8,128)(2,1)}, bf16[512,768]{1,0:T(8,128)(2,1)}, u32[]{:S(2)}, u32[]{:S(2)}) collective-permute-start(bf16[512,768]{1,0:T(8,128)(2,1)} %get-tuple-element.331), channel_id=1, source_target_pairs={{0,1},{1,0},{2,3},{3,2},{4,5},{5,4},{6,7},{7,6},{8,9},{9,8},{10,11... | collective-permute-start | bytes 2359304 | tf_op jit(solution)/shard_map/ppermute | solution.py:942
  291.6 40.6 %collective-permute-start.44 = (bf16[512,768]{1,0:T(8,128)(2,1)}, bf16[512,768]{1,0:T(8,128)(2,1)}, u32[]{:S(2)}, u32[]{:S(2)}) collective-permute-start(bf16[512,768]{1,0:T(8,128)(2,1)} %get-tuple-element.332), channel_id=1, source_target_pairs={{0,1},{1,0},{2,3},{3,2},{4,5},{5,4},{6,7},{7,6},{8,9},{9,8},{10,11... | collective-permute-start | bytes 2359304 | tf_op jit(solution)/shard_map/ppermute | solution.py:942
  330.7 32.9 %collective-permute-start.47 = (bf16[4,96,1536]{2,1,0:T(8,128)(2,1)}, bf16[4,96,1536]{2,1,0:T(8,128)(2,1)S(1)}, u32[]{:S(2)}, u32[]{:S(2)}) collective-permute-start(bf16[4,96,1536]{2,1,0:T(8,128)(2,1)} %get-tuple-element.360), channel_id=1, source_target_pairs={{0,4},{4,0},{8,12},{12,8},{16,20},{20,16},{24,28},{28,24},{1,5},{5... | collective-permute-start | bytes 3538952 | tf_op jit(solution)/shard_map/ppermute | solution.py:947
  332.2 7.7 %collective-permute-start.42 = (bf16[512,768]{1,0:T(8,128)(2,1)}, bf16[512,768]{1,0:T(8,128)(2,1)S(1)}, u32[]{:S(2)}, u32[]{:S(2)}) collective-permute-start(bf16[512,768]{1,0:T(8,128)(2,1)} %get-tuple-element.350), channel_id=1, source_target_pairs={{0,2},{2,0},{1,3},{3,1},{4,6},{6,4},{5,7},{7,5},{8,10},{10,8},{9,1... | collective-permute-start | bytes 2359304 | tf_op jit(solution)/shard_map/ppermute | solution.py:942
  368.0 62.5 %collective-permute-start.50 = (bf16[8,96,1536]{2,1,0:T(8,128)(2,1)}, bf16[8,96,1536]{2,1,0:T(8,128)(2,1)S(1)}, u32[]{:S(2)}, u32[]{:S(2)}) collective-permute-start(bf16[8,96,1536]{2,1,0:T(8,128)(2,1)} %get-tuple-element.372), channel_id=1, source_target_pairs={{0,4},{4,0},{8,12},{12,8},{16,20},{20,16},{24,28},{28,24},{1,5},{5... | collective-permute-start | bytes 7077896 | tf_op jit(solution)/shard_map/ppermute | solution.py:947
  368.6 31.2 %collective-permute-start.48 = (bf16[1024,640]{1,0:T(8,128)(2,1)}, bf16[1024,640]{1,0:T(8,128)(2,1)}, u32[]{:S(2)}, u32[]{:S(2)}) collective-permute-start(bf16[1024,640]{1,0:T(8,128)(2,1)} %get-tuple-element.363.query_ref), channel_id=1, source_target_pairs={{0,1},{1,0},{2,3},{3,2},{4,5},{5,4},{6,7},{7,6},{8,9},{9,8},{10,11... | collective-permute-start | bytes 3932168 | tf_op jit(solution)/shard_map/ppermute | solution.py:942
  369.4 41.7 %collective-permute-start.53 = (bf16[2,96,3072]{2,1,0:T(8,128)(2,1)}, bf16[2,96,3072]{2,1,0:T(8,128)(2,1)S(1)}, u32[]{:S(2)}, u32[]{:S(2)}) collective-permute-start(bf16[2,96,3072]{2,1,0:T(8,128)(2,1)} %get-tuple-element.378), channel_id=1, source_target_pairs={{0,8},{4,12},{8,0},{12,4},{16,24},{20,28},{24,16},{28,20},{1,9},{5... | collective-permute-start | bytes 3538952 | tf_op jit(solution)/shard_map/ppermute | solution.py:947
  369.4 53.3 %collective-permute-start.52 = (bf16[2,96,1536]{2,1,0:T(8,128)(2,1)}, bf16[2,96,1536]{2,1,0:T(8,128)(2,1)}, u32[]{:S(2)}, u32[]{:S(2)}) collective-permute-start(bf16[2,96,1536]{2,1,0:T(8,128)(2,1)} %get-tuple-element.376), channel_id=1, source_target_pairs={{0,8},{4,12},{8,0},{12,4},{16,24},{20,28},{24,16},{28,20},{1,9},{5... | collective-permute-start | bytes 1769480 | tf_op jit(solution)/shard_map/ppermute | solution.py:947
  371.4 54.1 %collective-permute-start.51 = (bf16[1,96,3072]{2,1,0:T(8,128)(2,1)}, bf16[1,96,3072]{2,1,0:T(8,128)(2,1)}, u32[]{:S(2)}, u32[]{:S(2)}) collective-permute-start(bf16[1,96,3072]{2,1,0:T(8,128)(2,1)} %get-tuple-element.374), channel_id=1, source_target_pairs={{0,16},{4,20},{8,24},{12,28},{16,0},{20,4},{24,8},{28,12},{1,17},{... | collective-permute-start | bytes 1769480 | tf_op jit(solution)/shard_map/ppermute | solution.py:947
  410.5 26.5 %collective-permute-start.54 = (bf16[512,768]{1,0:T(8,128)(2,1)}, bf16[512,768]{1,0:T(8,128)(2,1)}, u32[]{:S(2)}, u32[]{:S(2)}) collective-permute-start(bf16[512,768]{1,0:T(8,128)(2,1)} %get-tuple-element.387), channel_id=1, source_target_pairs={{0,2},{2,0},{1,3},{3,1},{4,6},{6,4},{5,7},{7,5},{8,10},{10,8},{9,1... | collective-permute-start | bytes 2359304 | tf_op jit(solution)/shard_map/ppermute | solution.py:942
  411.1 40.4 %collective-permute-start.49 = (bf16[4,96,1792]{2,1,0:T(8,128)(2,1)}, bf16[4,96,1792]{2,1,0:T(8,128)(2,1)}, u32[]{:S(2)}, u32[]{:S(2)}) collective-permute-start(bf16[4,96,1792]{2,1,0:T(8,128)(2,1)} %get-tuple-element.369), channel_id=1, source_target_pairs={{0,4},{4,0},{8,12},{12,8},{16,20},{20,16},{24,28},{28,24},{1,5},{5... | collective-permute-start | bytes 4128776 | tf_op jit(solution)/shard_map/ppermute | solution.py:947
  427.6 43.1 %collective-permute-start.59 = (bf16[1,96,1536]{2,1,0:T(8,128)(2,1)}, bf16[1,96,1536]{2,1,0:T(8,128)(2,1)S(1)}, u32[]{:S(2)}, u32[]{:S(2)}) collective-permute-start(bf16[1,96,1536]{2,1,0:T(8,128)(2,1)} %get-tuple-element.400), channel_id=1, source_target_pairs={{0,16},{4,20},{8,24},{12,28},{16,0},{20,4},{24,8},{28,12},{1,17},{... | collective-permute-start | bytes 884744 | tf_op jit(solution)/shard_map/ppermute | solution.py:947
  429.3 39.1 %collective-permute-start.60 = (bf16[1,96,3072]{2,1,0:T(8,128)(2,1)}, bf16[1,96,3072]{2,1,0:T(8,128)(2,1)}, u32[]{:S(2)}, u32[]{:S(2)}) collective-permute-start(bf16[1,96,3072]{2,1,0:T(8,128)(2,1)} %get-tuple-element.402), channel_id=1, source_target_pairs={{0,16},{4,20},{8,24},{12,28},{16,0},{20,4},{24,8},{28,12},{1,17},{... | collective-permute-start | bytes 1769480 | tf_op jit(solution)/shard_map/ppermute | solution.py:947
  440.6 3.7 collective-permute-start.55
  443.0 47.0 %collective-permute-start.58 = (bf16[4,96,1536]{2,1,0:T(8,128)(2,1)}, bf16[4,96,1536]{2,1,0:T(8,128)(2,1)S(1)}, u32[]{:S(2)}, u32[]{:S(2)}) collective-permute-start(bf16[4,96,1536]{2,1,0:T(8,128)(2,1)} %get-tuple-element.398), channel_id=1, source_target_pairs={{0,8},{4,12},{8,0},{12,4},{16,24},{20,28},{24,16},{28,20},{1,9},{5... | collective-permute-start | bytes 3538952 | tf_op jit(solution)/shard_map/ppermute | solution.py:947
  470.8 30.5 %collective-permute-start.71 = (bf16[96,768]{1,0:T(8,128)(2,1)S(1)}, bf16[96,768]{1,0:T(8,128)(2,1)}, u32[]{:S(2)}, u32[]{:S(2)}) collective-permute-start(bf16[96,768]{1,0:T(8,128)(2,1)S(1)} %slice.180), channel_id=1, source_target_pairs={{0,1},{1,0},{2,3},{3,2},{4,5},{5,4},{6,7},{7,6},{8,9},{9,8},{10,11... | collective-permute-start | bytes 442376 | tf_op jit(solution)/shard_map/ppermute | solution.py:942
  472.1 31.7 %collective-permute-start.70 = (bf16[192,768]{1,0:T(8,128)(2,1)}, bf16[192,768]{1,0:T(8,128)(2,1)S(1)}, u32[]{:S(2)}, u32[]{:S(2)}) collective-permute-start(bf16[192,768]{1,0:T(8,128)(2,1)} %slice.179), channel_id=1, source_target_pairs={{0,1},{1,0},{2,3},{3,2},{4,5},{5,4},{6,7},{7,6},{8,9},{9,8},{10,11... | collective-permute-start | bytes 884744 | tf_op jit(solution)/shard_map/ppermute | solution.py:942
  472.9 36.0 %collective-permute-start.56 = (bf16[2,96,1792]{2,1,0:T(8,128)(2,1)}, bf16[2,96,1792]{2,1,0:T(8,128)(2,1)}, u32[]{:S(2)}, u32[]{:S(2)}) collective-permute-start(bf16[2,96,1792]{2,1,0:T(8,128)(2,1)} %get-tuple-element.394), channel_id=1, source_target_pairs={{0,8},{4,12},{8,0},{12,4},{16,24},{20,28},{24,16},{28,20},{1,9},{5... | collective-permute-start | bytes 2064392 | tf_op jit(solution)/shard_map/ppermute | solution.py:947
  472.9 39.0 %collective-permute-start.62 = (bf16[512,768]{1,0:T(8,128)(2,1)}, bf16[512,768]{1,0:T(8,128)(2,1)}, u32[]{:S(2)}, u32[]{:S(2)}) collective-permute-start(bf16[512,768]{1,0:T(8,128)(2,1)} %add_convert_fusion), channel_id=1, source_target_pairs={{0,1},{1,0},{2,3},{3,2},{4,5},{5,4},{6,7},{7,6},{8,9},{9,8},{10,11... | collective-permute-start | bytes 2359304 | tf_op jit(solution)/shard_map/ppermute | solution.py:942
  494.3 33.5 %collective-permute-start.66 = (bf16[2,96,1536]{2,1,0:T(8,128)(2,1)}, bf16[2,96,1536]{2,1,0:T(8,128)(2,1)}, u32[]{:S(2)}, u32[]{:S(2)}) collective-permute-start(bf16[2,96,1536]{2,1,0:T(8,128)(2,1)} %get-tuple-element.416), channel_id=1, source_target_pairs={{0,16},{4,20},{8,24},{12,28},{16,0},{20,4},{24,8},{28,12},{1,17},{... | collective-permute-start | bytes 1769480 | tf_op jit(solution)/shard_map/ppermute | solution.py:947
  501.3 3.9 collective-permute-start.57
  503.7 35.1 %collective-permute-start.69 = (bf16[96,3072]{1,0:T(8,128)(2,1)S(1)}, bf16[96,3072]{1,0:T(8,128)(2,1)S(1)}, u32[]{:S(2)}, u32[]{:S(2)}) collective-permute-start(bf16[96,3072]{1,0:T(8,128)(2,1)S(1)} %bitcast.104), channel_id=1, source_target_pairs={{0,1},{1,0},{2,3},{3,2},{4,5},{5,4},{6,7},{7,6},{8,9},{9,8},{10,11... | collective-permute-start | bytes 1769480 | tf_op jit(solution)/shard_map/ppermute | solution.py:942
  505.2 6.9 %collective-permute-start.64 = (f32[2560]{0:T(1024)S(1)}, f32[2560]{0:T(1024)S(1)}, u32[]{:S(2)}, u32[]{:S(2)}) collective-permute-start(f32[2560]{0:T(1024)S(1)} %add.129), channel_id=1, source_target_pairs={{0,8},{4,12},{8,0},{12,4},{16,24},{20,28},{24,16},{28,20},{1,9},{5... | collective-permute-start | bytes 30728 | tf_op jit(solution)/shard_map/ppermute | solution.py:947
  511.9 24.8 %collective-permute-start.68 = (bf16[1,96,1792]{2,1,0:T(8,128)(2,1)}, bf16[1,96,1792]{2,1,0:T(8,128)(2,1)S(1)}, u32[]{:S(2)}, u32[]{:S(2)}) collective-permute-start(bf16[1,96,1792]{2,1,0:T(8,128)(2,1)} %get-tuple-element.422), channel_id=1, source_target_pairs={{0,16},{4,20},{8,24},{12,28},{16,0},{20,4},{24,8},{28,12},{1,17},{... | collective-permute-start | bytes 1032200 | tf_op jit(solution)/shard_map/ppermute | solution.py:947
  512.0 18.6 %collective-permute-start.61 = (bf16[512,768]{1,0:T(8,128)(2,1)S(1)}, bf16[512,768]{1,0:T(8,128)(2,1)S(1)}, u32[]{:S(2)}, u32[]{:S(2)}) collective-permute-start(bf16[512,768]{1,0:T(8,128)(2,1)S(1)} %copy-done.55), channel_id=1, source_target_pairs={{0,2},{2,0},{1,3},{3,1},{4,6},{6,4},{5,7},{7,5},{8,10},{10,8},{9,1... | collective-permute-start | bytes 2359304 | tf_op jit(solution)/shard_map/ppermute | solution.py:942
  512.0 23.9 %collective-permute-start.65 = (f32[2560]{0:T(1024)S(1)}, f32[2560]{0:T(1024)S(1)}, u32[]{:S(2)}, u32[]{:S(2)}) collective-permute-start(f32[2560]{0:T(1024)S(1)} %add.135), channel_id=1, source_target_pairs={{0,16},{4,20},{8,24},{12,28},{16,0},{20,4},{24,8},{28,12},{1,17},{... | collective-permute-start | bytes 30728 | tf_op jit(solution)/shard_map/ppermute | solution.py:947
  529.2 6.8 %collective-permute-start.67 = (bf16[96,1536]{1,0:T(8,128)(2,1)S(1)}, bf16[96,1536]{1,0:T(8,128)(2,1)S(1)}, u32[]{:S(2)}, u32[]{:S(2)}) collective-permute-start(bf16[96,1536]{1,0:T(8,128)(2,1)S(1)} %fusion.8), channel_id=1, source_target_pairs={{0,1},{1,0},{2,3},{3,2},{4,5},{5,4},{6,7},{7,6},{8,9},{9,8},{10,11... | collective-permute-start | bytes 884744 | tf_op jit(solution)/shard_map/ppermute | solution.py:942
  (65 other events, 317.0 us)

commit v6 on v5

--- a/solution.py
+++ b/solution.py
@@ -1222,9 +1222,9 @@
         table, line.step(second_normed), gate_up_own[1], gate_up_far[1]
     )
     line.mark(act1)
+    down_sum0.relay(line)
     down_far[1] = [line.step(down_far[1][0])]
     line.mark(*down_far[1])
-    down_sum0.relay(line)
     own_sum0 = Scatter(table, own_sent0, own_kept0, pair_first, line)
     d_gate1, d_up1 = activate_back(
         table, line.step(grad_full), down_own[1], down_far[1], gate_factor1, up_factor1

time: 556 us -> 553 us (level)
    ppermute x39, waiting for transfers between devices: 55.5 us -> 47.2 us  [swap(): return lax.ppermute(part, axis_name, [(0, 1), (1, 0)])]
    ppermute x33, waiting for transfers between devices: 53.5 us -> 59.1 us  [dp_swap(): return lax.ppermute(part, 'dp', [(i, i ^ 1 << bit) for i in range(count)])]
    unnamed x112 -> x110, local copies, waits for them, and re-layouts: 13.6 us -> 12.7 us
where the time goes in v6:
time: 553 us; the launch traced here: 542 us
  Pallas kernels  297 us (54%)
  waiting for transfers between devices  106 us (19%)
  starting transfers between devices  68 us (12%)
  local copies, waits for them, and re-layouts  36.6 us (7%)
  other arithmetic  33.1 us (6%)
    ppermute x33, waiting for transfers between devices, dp_swap(): return lax.ppermute(part, 'dp', [(i, i ^ 1 << bit) for i in range(count)])  59.1 us
    ppermute x39, waiting for transfers between devices, swap(): return lax.ppermute(part, axis_name, [(0, 1), (1, 0)])  47.2 us
    pallas_call x4, Pallas kernels, split_product(): pl.pallas_call(kernel, grid_spec=pltpu.PrefetchScalarGridSpec(num_scalar_...  45.3 us
    pallas_call x12, Pallas kernels, relay(): pl.pallas_call(relay_kernel, grid_spec=pltpu.PrefetchScalarGridSpec(num_s...  44.2 us
    ppermute x33, starting transfers between devices, dp_swap(): return lax.ppermute(part, 'dp', [(i, i ^ 1 << bit) for i in range(count)])  43.5 us
    pallas_call x2, Pallas kernels, activate(): pl.pallas_call(functools.partial(activate_kernel, width // 2), grid_spec=...  30.4 us
    pallas_call x1, Pallas kernels, normed_grad(): pl.pallas_call(functools.partial(normed_grad_kernel, halves, steps, tile,...  25.8 us
    ppermute x39, starting transfers between devices, swap(): return lax.ppermute(part, axis_name, [(0, 1), (1, 0)])  24.5 us
  transfers between devices with their start and end apart: 72, of which 21 were waited for; matrix products, arithmetic and copies ran while one was open for 10% of the time, Pallas kernels for 53%

profile of v6, /device:TPU:0, one launch (start us, length us, event | category | flops | bytes accessed | tf_op | source)
XLA Modules:
  0.0 542.4 jit_solution(4129247480965198521)
XLA Ops:
  2.0 3.0 collective-permute-start.2
  9.2 1.9 collective-permute-start.4
  11.9 3.1 fusion.9
  17.6 3.8 unit_columns.3
  21.4 3.0 collective-permute-done.4
  29.8 7.4 %unit_columns.4 = (bf16[8,96,3072]{2,1,0:T(8,128)(2,1)}, bf16[8,96,1536]{2,1,0:T(8,128)(2,1)}, bf16[8,96,1536]{2,1,0:T(8,128)(2,1)}) custom-call(s32[9]{0:T(128)} %get-tuple-element.467.table, bf16[768,8960]{1,0:T(8,128)(2,1)} %bitcast.73), custom_call_target="tpu_custom_call" | custom-call | flops 1 | bytes 1 | tf_op jit(solution)/shard_map/unit_columns/pallas_call | solution.py:103
  44.7 7.4 %unit_columns.5 = (bf16[8,96,3072]{2,1,0:T(8,128)(2,1)}, bf16[8,96,1536]{2,1,0:T(8,128)(2,1)}, bf16[8,96,1536]{2,1,0:T(8,128)(2,1)}) custom-call(s32[9]{0:T(128)} %get-tuple-element.466.table, bf16[768,8960]{1,0:T(8,128)(2,1)} %bitcast.74, ...), custom_call_target="tpu_custom_call", output_to_operand_aliasing={{0}: (2, {}), {1}: (3, {}), {2}: (4, {})} | custom-call | flops 1 | bytes 1 | tf_op jit(solution)/shard_map/unit_columns/pallas_call | solution.py:103
  54.5 8.5 %project.1 = (bf16[1024,1536]{1,0:T(8,128)(2,1)}, bf16[1024,768]{1,0:T(8,128)(2,1)}, f32[1024,128]{1,0:T(8,128)}, bf16[1024,384]{1,0:T(8,128)(2,1)}, bf16[1024,1...) custom-call(s32[5]{0:T(128)} %stack.39.table, bf16[512,768]{1,0:T(8,128)(2,1)} %own_ref, ...), custom_call_target="tpu_custom_call" | custom-call | flops 1 | bytes 1 | tf_op jit(solution)/shard_map/project/pallas_call | solution.py:244
  63.0 2.5 collective-permute-done.12
  72.2 10.5 %attend.1 = (bf16[1024,384]{1,0:T(8,128)(2,1)}, bf16[1024,256]{1,0:T(8,128)(2,1)}, bf16[1024,128]{1,0:T(8,128)(2,1)}) custom-call(bf16[1024,384]{1,0:T(8,128)(2,1)} %get-tuple-element.357.query_ref, bf16[1024,128]{1,0:T(8,128)(2,1)} %get-tuple-element.247.key_ref, bf16[1024,128]{1,0:T(8,128)(2,1)} %get-tuple-element.248.value_ref, ...), custom_call_target="tpu_custom_call" | custom-call | flops 1 | bytes 1 | tf_op jit(solution)/shard_map/attend/pallas_call | solution.py:334
  88.5 2.6 unit_rows.2
  91.0 7.0 %unit_rows.3 = (bf16[8,192,768]{2,1,0:T(8,128)(2,1)}, bf16[8,96,768]{2,1,0:T(8,128)(2,1)}) custom-call(s32[9]{0:T(128)} %pad_add_fusion.3.table, bf16[8,2,280,768]{3,2,1,0:T(8,128)(2,1)} %bitcast.79), custom_call_target="tpu_custom_call" | custom-call | flops 1 | bytes 1 | tf_op jit(solution)/shard_map/unit_rows/pallas_call | solution.py:136
  98.0 3.1 collective-permute-done.13.refs_2_
  101.7 2.0 collective-permute-done.19.refs_5_
  107.0 13.3 %residual.1 = (f32[1024,1536]{1,0:T(8,128)}, bf16[1024,1536]{1,0:T(8,128)(2,1)}, f32[1024,128]{1,0:T(8,128)}, bf16[1024,768]{1,0:T(8,128)(2,1)}) custom-call(s32[5]{0:T(128)} %stack.39.table, bf16[1024,1536]{1,0:T(8,128)(2,1)} %get-tuple-element.268.stream_ref, bf16[1024,384]{1,0:T(8,128)(2,1)} %get-tuple-element.250.refs_0_, ...), custom_call_target="tpu_custom_call" | custom-call | flops 1 | bytes 1 | tf_op jit(solution)/shard_map/residual/pallas_call | solution.py:467
  122.9 19.3 %activate.2 = (bf16[1024,1536]{1,0:T(8,128)(2,1)}, bf16[1024,1536]{1,0:T(8,128)(2,1)}, bf16[1024,1536]{1,0:T(8,128)(2,1)}) custom-call(s32[5]{0:T(128)} %stack.39.table, bf16[1024,1536]{1,0:T(8,128)(2,1)} %get-tuple-element.333.normed_ref.left_ref, bf16[768,3072]{1,0:T(8,128)(2,1)} %bitcast.75, bf16[768,3072]{1,0:T(8,128)(2,1)} %bitcast.76, ...), custom_call_target="tpu_custom_call" | custom-call | flops 1 | bytes 1 | tf_op jit(solution)/shard_map/activate/pallas_call | solution.py:521
  148.0 5.6 %join.1.refs_0_.grad_ref = bf16[1024,1536]{1,0:T(8,128)(2,1)} custom-call(s32[5]{0:T(128)} %stack.39.table, bf16[512,768]{1,0:T(8,128)(2,1)} %own_ref.1, bf16[512,768]{1,0:T(8,128)(2,1)} %collective-permute-done.28.near_ref, bf16[512,768]{1,0:T(8,128)(2,1)} %collective-permute-done.26.far_ref, bf16[512,768]{1,0:T(8,128)(2,1)} %collective-permute-done.29.far_near_ref), custom_call_target="tpu_custom_call" | custom-call | flops 1 | bytes 1 | tf_op jit(solution)/shard_map/join/pallas_call | solution.py:284
  153.6 10.4 %split_product.4 = (bf16[4,192,1536]{2,1,0:T(8,128)(2,1)}, bf16[4,192,1536]{2,1,0:T(8,128)(2,1)}) custom-call(s32[5]{0:T(128)} %stack.39.table, bf16[1024,1536]{1,0:T(8,128)(2,1)} %get-tuple-element.335.left_ref.refs_0_, bf16[1024,1536]{1,0:T(8,128)(2,1)} %join.1.refs_0_.grad_ref), custom_call_target="tpu_custom_call" | custom-call | flops 1 | bytes 1 | tf_op jit(solution)/shard_map/split_product/pallas_call | solution.py:657
  164.7 2.2 dynamic-slice_bitcast_fusion
  168.1 13.2 %activate_back.2 = (bf16[1024,1536]{1,0:T(8,128)(2,1)}, bf16[1024,1536]{1,0:T(8,128)(2,1)}) custom-call(s32[5]{0:T(128)} %stack.39.table, bf16[1024,1536]{1,0:T(8,128)(2,1)} %join.1.refs_0_.grad_ref, bf16[1536,768]{1,0:T(8,128)(2,1)} %bitcast.88, bf16[384,768]{1,0:T(8,128)(2,1)} %copy-done.11, bf16[384,768]{1,0:T(8,128)(2,1)} %copy-done.10, ...), custom_call_target="tpu_custom_call" | custom-call | flops 1 | bytes 1 | tf_op jit(solution)/shard_map/activate_back/pallas_call | solution.py:556
  181.3 17.3 %split_product.5 = (bf16[4,96,3072]{2,1,0:T(8,128)(2,1)}, bf16[4,96,3072]{2,1,0:T(8,128)(2,1)}, bf16[4,96,3072]{2,1,0:T(8,128)(2,1)}, bf16[4,96,3072]{2,1,0:T(8,128)(2,1)}) custom-call(s32[5]{0:T(128)} %stack.39.table, bf16[1024,1536]{1,0:T(8,128)(2,1)} %get-tuple-element.333.normed_ref.left_ref, bf16[1024,1536]{1,0:T(8,128)(2,1)} %get-tuple-element.314.refs_0_, ...), custom_call_target="tpu_custom_call" | custom-call | flops 1 | bytes 1 | tf_op jit(solution)/shard_map/split_product/pallas_call | solution.py:657
  202.6 11.2 %activate.3 = (bf16[1024,768]{1,0:T(8,128)(2,1)}, bf16[1024,768]{1,0:T(8,128)(2,1)}, bf16[1024,768]{1,0:T(8,128)(2,1)}) custom-call(s32[5]{0:T(128)} %stack.39.table, bf16[1024,1536]{1,0:T(8,128)(2,1)} %get-tuple-element.333.normed_ref.left_ref, bf16[768,1536]{1,0:T(8,128)(2,1)} %bitcast.81, bf16[768,1536]{1,0:T(8,128)(2,1)} %bitcast.82, ...), custom_call_target="tpu_custom_call" | custom-call | flops 1 | bytes 1 | tf_op jit(solution)/shard_map/activate/pallas_call | solution.py:521
  213.8 4.9 collective-permute-done.33.arrived_sent_ref.arrived_ref
  218.6 4.2 relay.12
  223.3 3.4 collective-permute-done.32.refs_0_.refs_8_
  227.8 8.5 %activate_back.3 = (bf16[1024,768]{1,0:T(8,128)(2,1)}, bf16[1024,768]{1,0:T(8,128)(2,1)}) custom-call(s32[5]{0:T(128)} %stack.39.table, bf16[1024,1536]{1,0:T(8,128)(2,1)} %join.1.refs_0_.grad_ref, bf16[768,768]{1,0:T(8,128)(2,1)} %bitcast.92, bf16[768,768]{1,0:T(8,128)(2,1)} %copy-done.13, bf16[1024,768]{1,0:T(8,128)(2,1)} %get-tuple-element.311.refs_1_, ...), custom_call_target="tpu_custom_call" | custom-call | flops 1 | bytes 1 | tf_op jit(solution)/shard_map/activate_back/pallas_call | solution.py:556
  236.3 25.8 %normed_grad.1 = (f32[512,1536]{1,0:T(8,128)}, bf16[512,768]{1,0:T(8,128)(2,1)}, bf16[512,768]{1,0:T(8,128)(2,1)}) custom-call(s32[5]{0:T(128)} %stack.39.table, bf16[1024,1536]{1,0:T(8,128)(2,1)} %get-tuple-element.314.refs_0_, bf16[1024,1536]{1,0:T(8,128)(2,1)} %get-tuple-element.302.refs_1_, bf16[1024,768]{1,0:T(8,128)(2,1)} %get-tuple-element.313.refs_2_.refs_0_, ...), custom_call_target="tpu_custom_call" | custom-call | flops 1 | bytes 1 | tf_op jit(solution)/shard_map/normed_grad/pallas_call | solution.py:766
  262.1 6.8 %split_product.6 = (bf16[4,96,1536]{2,1,0:T(8,128)(2,1)}, bf16[4,96,1536]{2,1,0:T(8,128)(2,1)}) custom-call(s32[5]{0:T(128)} %stack.39.table, bf16[1024,768]{1,0:T(8,128)(2,1)} %get-tuple-element.324.left_ref.refs_1_, bf16[1024,1536]{1,0:T(8,128)(2,1)} %join.1.refs_0_.grad_ref), custom_call_target="tpu_custom_call" | custom-call | flops 1 | bytes 1 | tf_op jit(solution)/shard_map/split_product/pallas_call | solution.py:657
  268.9 3.4 relay.13
  272.3 4.3 relay.14
  278.4 2.6 collective-permute-start.39
  281.7 5.0 chip_sum.1
  288.7 10.9 %split_product.7 = (bf16[8,96,1536]{2,1,0:T(8,128)(2,1)}, bf16[8,96,1536]{2,1,0:T(8,128)(2,1)}) custom-call(s32[5]{0:T(128)} %stack.39.table, bf16[1024,1536]{1,0:T(8,128)(2,1)} %get-tuple-element.333.normed_ref.left_ref, bf16[1024,768]{1,0:T(8,128)(2,1)} %get-tuple-element.313.refs_2_.refs_0_, bf16[1024,768]{1,0:T(8,128)(2,1)} %get-tuple-element.315.refs_3_.refs_1_), custom_call_target="tpu_custom_call" | custom-call | flops 1 | bytes 1 | tf_op jit(solution)/shard_map/split_product/pallas_call | solution.py:657
  299.5 15.1 %down.1 = (f32[512,1536]{1,0:T(8,128)}, bf16[512,768]{1,0:T(8,128)(2,1)}, bf16[512,768]{1,0:T(8,128)(2,1)}) custom-call(s32[5]{0:T(128)} %stack.39.table, bf16[1024,1536]{1,0:T(8,128)(2,1)} %get-tuple-element.335.left_ref.refs_0_, bf16[1024,768]{1,0:T(8,128)(2,1)} %get-tuple-element.324.left_ref.refs_1_, bf16[1536,768]{1,0:T(8,128)(2,1)} %bitcast.89, ...), custom_call_target="tpu_custom_call" | custom-call | flops 1 | bytes 1 | tf_op jit(solution)/shard_map/down/pallas_call | solution.py:604
  316.7 3.4 relay.15
  321.5 4.3 relay.16
  328.4 7.2 %norm_back.1 = (f32[512,768]{1,0:T(8,128)}, bf16[512,768]{1,0:T(8,128)(2,1)}, bf16[512,768]{1,0:T(8,128)(2,1)}, f32[1,768]{1,0:T(1,128)}) custom-call(s32[5]{0:T(128)} %stack.39.table, f32[512,1536]{1,0:T(8,128)} %get-tuple-element.352.chip_ref, bf16[512,768]{1,0:T(8,128)(2,1)} %collective-permute-done.43.far_own_ref, ...), custom_call_target="tpu_custom_call" | custom-call | flops 1 | bytes 1 | tf_op jit(solution)/shard_map/norm_back/pallas_call | solution.py:854
  336.2 2.5 add_convert_fusion
  340.4 19.4 %attend_back.1 = (bf16[1024,640]{1,0:T(8,128)(2,1)}, f32[1024,256]{1,0:T(8,128)}) custom-call(s32[5]{0:T(128)} %stack.39.table, bf16[1024,384]{1,0:T(8,128)(2,1)} %get-tuple-element.357.query_ref, bf16[1024,128]{1,0:T(8,128)(2,1)} %get-tuple-element.247.key_ref, bf16[1024,128]{1,0:T(8,128)(2,1)} %get-tuple-element.248.value_ref, ...), custom_call_target="tpu_custom_call" | custom-call | flops 1 | bytes 1 | tf_op jit(solution)/shard_map/attend_back/pallas_call | solution.py:404
  360.8 3.4 relay.17
  367.6 2.3 collective-permute-start.51
  370.0 26.1 %collective-permute-done.48.arrived_ref = bf16[1024,640]{1,0:T(8,128)(2,1)} collective-permute-done((bf16[1024,640]{1,0:T(8,128)(2,1)}, bf16[1024,640]{1,0:T(8,128)(2,1)}, u32[]{:S(2)}, u32[]{:S(2)}) %collective-permute-start.48) | collective-permute-done | bytes 1310752 | tf_op jit(solution)/shard_map/ppermute | solution.py:942
  396.1 10.7 %project_back.1 = (bf16[4,96,1792]{2,1,0:T(8,128)(2,1)}, bf16[4,96,1792]{2,1,0:T(8,128)(2,1)}, f32[512,768]{1,0:T(8,128)}, bf16[512,768]{1,0:T(8,128)(2,1)}, f32[1,1024]{1,0:T(1,128)}) custom-call(s32[5]{0:T(128)} %stack.39.table, bf16[1024,640]{1,0:T(8,128)(2,1)} %get-tuple-element.363.query_ref, f32[1024,256]{1,0:T(8,128)} %get-tuple-element.364.key_value_ref, ...), custom_call_target="tpu_custom_call" | custom-call | flops 1 | bytes 1 | tf_op jit(solution)/shard_map/project_back/pallas_call | solution.py:913
  413.6 3.5 relay.18
  419.0 2.8 relay.19
  421.7 2.0 convert_add_fusion.3
  428.1 5.1 relay.20
  433.3 2.3 fusion.6
  437.0 2.2 collective-permute-done.63
  440.6 7.0 %collective-permute-done.49.arrived_sent_ref.arrived_ref = bf16[4,96,1792]{2,1,0:T(8,128)(2,1)} collective-permute-done((bf16[4,96,1792]{2,1,0:T(8,128)(2,1)}, bf16[4,96,1792]{2,1,0:T(8,128)(2,1)}, u32[]{:S(2)}, u32[]{:S(2)}) %collective-permute-start.49) | collective-permute-done | bytes 1376288 | tf_op jit(solution)/shard_map/ppermute | solution.py:947
  447.6 3.5 relay.21
  451.1 13.5 %collective-permute-done.60 = bf16[1,96,3072]{2,1,0:T(8,128)(2,1)} collective-permute-done((bf16[1,96,3072]{2,1,0:T(8,128)(2,1)}, bf16[1,96,3072]{2,1,0:T(8,128)(2,1)}, u32[]{:S(2)}, u32[]{:S(2)}) %collective-permute-start.60) | collective-permute-done | bytes 589856 | tf_op jit(solution)/shard_map/ppermute | solution.py:947
  464.6 2.2 convert_add_fusion.2
  470.3 15.8 %collective-permute-done.58.arrived_sent_ref.arrived_ref = bf16[4,96,1536]{2,1,0:T(8,128)(2,1)S(1)} collective-permute-done((bf16[4,96,1536]{2,1,0:T(8,128)(2,1)}, bf16[4,96,1536]{2,1,0:T(8,128)(2,1)S(1)}, u32[]{:S(2)}, u32[]{:S(2)}) %collective-permute-start.58) | collective-permute-done | bytes 1179680 | tf_op jit(solution)/shard_map/ppermute | solution.py:947
  487.1 3.3 relay.22
  490.4 2.8 collective-permute-start.66
  493.2 3.3 fusion.5
  501.5 2.4 collective-permute-start.64
  505.3 3.0 relay.23
  508.4 2.9 collective-permute-start.65
  511.3 13.1 %collective-permute-done.66 = bf16[2,96,1536]{2,1,0:T(8,128)(2,1)} collective-permute-done((bf16[2,96,1536]{2,1,0:T(8,128)(2,1)}, bf16[2,96,1536]{2,1,0:T(8,128)(2,1)}, u32[]{:S(2)}, u32[]{:S(2)}) %collective-permute-start.66) | collective-permute-done | bytes 589856 | tf_op jit(solution)/shard_map/ppermute | solution.py:947
  526.9 3.0 fusion.7
  529.9 2.7 collective-permute-done.67.far1_ref
  536.4 5.6 %spread_columns.1 = f32[96,8960]{1,0:T(8,128)} custom-call(s32[5]{0:T(128)} %stack.39.table, f32[96,3072]{1,0:T(8,128)} %bitcast.94, f32[96,1536]{1,0:T(8,128)} %slice_bitcast_fusion.own1_ref, bf16[96,3072]{1,0:T(8,128)(2,1)} %copy-done.35, bf16[96,1536]{1,0:T(8,128)(2,1)} %copy-done.47), custom_call_target="tpu_custom_call" | custom-call | flops 1 | bytes 1 | tf_op jit(solution)/shard_map/spread_columns/pallas_call | solution.py:178
  (316 shorter events, 106.0 us)
Async XLA Ops:
  2.0 15.4 %collective-permute-start.2 = (f32[2,768]{1,0:T(2,128)S(1)}, f32[2,768]{1,0:T(2,128)S(1)}, u32[]{:S(2)}, u32[]{:S(2)}) collective-permute-start(f32[2,768]{1,0:T(2,128)S(1)} %pad_maximum_fusion.17), channel_id=1, source_target_pairs={{0,1},{1,0},{2,3},{3,2},{4,5},{5,4},{6,7},{7,6},{8,9},{9,8},{10,11... | collective-permute-start | bytes 18440 | tf_op jit(solution)/shard_map/ppermute | solution.py:942
  5.1 38.5 %collective-permute-start.6 = (bf16[512,768]{1,0:T(8,128)(2,1)}, bf16[512,768]{1,0:T(8,128)(2,1)}, u32[]{:S(2)}, u32[]{:S(2)}) collective-permute-start(bf16[512,768]{1,0:T(8,128)(2,1)} %own_ref), channel_id=1, source_target_pairs={{0,2},{2,0},{1,3},{3,1},{4,6},{6,4},{5,7},{7,5},{8,10},{10,8},{9,1... | collective-permute-start | bytes 2359304 | tf_op jit(solution)/shard_map/ppermute | solution.py:942
  5.1 38.5 %collective-permute-start = (bf16[768,768]{1,0:T(8,128)(2,1)}, bf16[768,768]{1,0:T(8,128)(2,1)}, u32[]{:S(2)}, u32[]{:S(2)}) collective-permute-start(bf16[768,768]{1,0:T(8,128)(2,1)} %bitcast.84), channel_id=1, source_target_pairs={{0,2},{2,0},{1,3},{3,1},{4,6},{6,4},{5,7},{7,5},{8,10},{10,8},{9,1... | collective-permute-start | bytes 3538952 | tf_op jit(solution)/shard_map/ppermute | solution.py:942
  9.1 15.3 %collective-permute-start.1 = (bf16[96,1408]{1,0:T(8,128)(2,1)S(1)}, bf16[96,1408]{1,0:T(8,128)(2,1)}, u32[]{:S(2)}, u32[]{:S(2)}) collective-permute-start(bf16[96,1408]{1,0:T(8,128)(2,1)S(1)} %get-tuple-element.218), channel_id=1, source_target_pairs={{0,1},{1,0},{2,3},{3,2},{4,5},{5,4},{6,7},{7,6},{8,9},{9,8},{10,11... | collective-permute-start | bytes 811016 | tf_op jit(solution)/shard_map/ppermute | solution.py:942
  9.2 15.2 %collective-permute-start.4 = (bf16[96,1408]{1,0:T(8,128)(2,1)}, bf16[96,1408]{1,0:T(8,128)(2,1)}, u32[]{:S(2)}, u32[]{:S(2)}) collective-permute-start(bf16[96,1408]{1,0:T(8,128)(2,1)} %get-tuple-element.219), channel_id=1, source_target_pairs={{0,1},{1,0},{2,3},{3,2},{4,5},{5,4},{6,7},{7,6},{8,9},{9,8},{10,11... | collective-permute-start | bytes 811016 | tf_op jit(solution)/shard_map/ppermute | solution.py:942
  17.5 23.6 %collective-permute-start.7 = (bf16[512,768]{1,0:T(8,128)(2,1)S(1)}, bf16[512,768]{1,0:T(8,128)(2,1)S(1)}, u32[]{:S(2)}, u32[]{:S(2)}) collective-permute-start(bf16[512,768]{1,0:T(8,128)(2,1)S(1)} %copy-done.7), channel_id=1, source_target_pairs={{0,1},{1,0},{2,3},{3,2},{4,5},{5,4},{6,7},{7,6},{8,9},{9,8},{10,11... | collective-permute-start | bytes 2359304 | tf_op jit(solution)/shard_map/ppermute | solution.py:942
  24.4 13.5 %collective-permute-start.3 = (bf16[96,1408]{1,0:T(8,128)(2,1)}, bf16[96,1408]{1,0:T(8,128)(2,1)S(1)}, u32[]{:S(2)}, u32[]{:S(2)}) collective-permute-start(bf16[96,1408]{1,0:T(8,128)(2,1)} %collective-permute-done.1), channel_id=1, source_target_pairs={{0,4},{4,0},{8,12},{12,8},{16,20},{20,16},{24,28},{28,24},{1,5},{5... | collective-permute-start | bytes 811016 | tf_op jit(solution)/shard_map/ppermute | solution.py:947
  25.9 11.4 %collective-permute-start.5 = (bf16[96,1408]{1,0:T(8,128)(2,1)}, bf16[96,1408]{1,0:T(8,128)(2,1)S(1)}, u32[]{:S(2)}, u32[]{:S(2)}) collective-permute-start(bf16[96,1408]{1,0:T(8,128)(2,1)} %collective-permute-done.4), channel_id=1, source_target_pairs={{0,8},{4,12},{8,0},{12,4},{16,24},{20,28},{24,16},{28,20},{1,9},{5... | collective-permute-start | bytes 811016 | tf_op jit(solution)/shard_map/ppermute | solution.py:947
  37.2 28.3 %collective-permute-start.12 = (bf16[2,96,3072]{2,1,0:T(8,128)(2,1)}, bf16[2,96,3072]{2,1,0:T(8,128)(2,1)}, u32[]{:S(2)}, u32[]{:S(2)}) collective-permute-start(bf16[2,96,3072]{2,1,0:T(8,128)(2,1)} %unit_columns.3), channel_id=1, source_target_pairs={{0,1},{1,0},{2,3},{3,2},{4,5},{5,4},{6,7},{7,6},{8,9},{9,8},{10,11... | collective-permute-start | bytes 3538952 | tf_op jit(solution)/shard_map/ppermute | solution.py:942
  40.0 12.1 %collective-permute-start.10 = (bf16[192,1408]{1,0:T(8,128)(2,1)S(1)}, bf16[192,1408]{1,0:T(8,128)(2,1)S(1)}, u32[]{:S(2)}, u32[]{:S(2)}) collective-permute-start(bf16[192,1408]{1,0:T(8,128)(2,1)S(1)} %pad_maximum_fusion.9.part0_ref), channel_id=1, source_target_pairs={{0,8},{4,12},{8,0},{12,4},{16,24},{20,28},{24,16},{28,20},{1,9},{5... | collective-permute-start | bytes 1622024 | tf_op jit(solution)/shard_map/ppermute | solution.py:947
  41.1 12.4 %collective-permute-start.11 = (bf16[192,1408]{1,0:T(8,128)(2,1)S(1)}, bf16[192,1408]{1,0:T(8,128)(2,1)S(1)}, u32[]{:S(2)}, u32[]{:S(2)}) collective-permute-start(bf16[192,1408]{1,0:T(8,128)(2,1)S(1)} %pad_maximum_fusion.10.part1_ref), channel_id=1, source_target_pairs={{0,4},{4,0},{8,12},{12,8},{16,20},{20,16},{24,28},{28,24},{1,5},{5... | collective-permute-start | bytes 1622024 | tf_op jit(solution)/shard_map/ppermute | solution.py:947
  43.6 9.9 %collective-permute-start.8 = (bf16[256,768]{1,0:T(8,128)(2,1)}, bf16[256,768]{1,0:T(8,128)(2,1)S(1)}, u32[]{:S(2)}, u32[]{:S(2)}) collective-permute-start(bf16[256,768]{1,0:T(8,128)(2,1)} %get-tuple-element.238), channel_id=1, source_target_pairs={{0,2},{2,0},{1,3},{3,1},{4,6},{6,4},{5,7},{7,5},{8,10},{10,8},{9,1... | collective-permute-start | bytes 1179656 | tf_op jit(solution)/shard_map/ppermute | solution.py:942
  43.6 9.9 %collective-permute-start.9 = (bf16[256,768]{1,0:T(8,128)(2,1)}, bf16[256,768]{1,0:T(8,128)(2,1)S(1)}, u32[]{:S(2)}, u32[]{:S(2)}) collective-permute-start(bf16[256,768]{1,0:T(8,128)(2,1)} %get-tuple-element.239), channel_id=1, source_target_pairs={{0,2},{2,0},{1,3},{3,1},{4,6},{6,4},{5,7},{7,5},{8,10},{10,8},{9,1... | collective-permute-start | bytes 1179656 | tf_op jit(solution)/shard_map/ppermute | solution.py:942
  66.8 17.9 %collective-permute-start.15 = (bf16[96,3072]{1,0:T(8,128)(2,1)S(1)}, bf16[96,3072]{1,0:T(8,128)(2,1)S(1)}, u32[]{:S(2)}, u32[]{:S(2)}) collective-permute-start(bf16[96,3072]{1,0:T(8,128)(2,1)S(1)} %get-tuple-element.245), channel_id=1, source_target_pairs={{0,8},{4,12},{8,0},{12,4},{16,24},{20,28},{24,16},{28,20},{1,9},{5... | collective-permute-start | bytes 1769480 | tf_op jit(solution)/shard_map/ppermute | solution.py:947
  70.7 14.1 %collective-permute-start.14 = (bf16[96,3072]{1,0:T(8,128)(2,1)S(1)}, bf16[96,3072]{1,0:T(8,128)(2,1)S(1)}, u32[]{:S(2)}, u32[]{:S(2)}) collective-permute-start(bf16[96,3072]{1,0:T(8,128)(2,1)S(1)} %get-tuple-element.244), channel_id=1, source_target_pairs={{0,4},{4,0},{8,12},{12,8},{16,20},{20,16},{24,28},{28,24},{1,5},{5... | collective-permute-start | bytes 1769480 | tf_op jit(solution)/shard_map/ppermute | solution.py:947
  82.7 18.4 %collective-permute-start.16 = (bf16[1024,128]{1,0:T(8,128)(2,1)}, bf16[1024,128]{1,0:T(8,128)(2,1)}, u32[]{:S(2)}, u32[]{:S(2)}) collective-permute-start(bf16[1024,128]{1,0:T(8,128)(2,1)} %get-tuple-element.266), channel_id=1, source_target_pairs={{0,1},{1,0},{2,3},{3,2},{4,5},{5,4},{6,7},{7,6},{8,9},{9,8},{10,11... | collective-permute-start | bytes 786440 | tf_op jit(solution)/shard_map/ppermute | solution.py:942
  83.3 17.8 %collective-permute-start.13 = (bf16[1024,256]{1,0:T(8,128)(2,1)}, bf16[1024,256]{1,0:T(8,128)(2,1)}, u32[]{:S(2)}, u32[]{:S(2)}) collective-permute-start(bf16[1024,256]{1,0:T(8,128)(2,1)} %get-tuple-element.249), channel_id=1, source_target_pairs={{0,1},{1,0},{2,3},{3,2},{4,5},{5,4},{6,7},{7,6},{8,9},{9,8},{10,11... | collective-permute-start | bytes 1572872 | tf_op jit(solution)/shard_map/ppermute | solution.py:942
  84.8 16.8 %collective-permute-start.17 = (bf16[1024,384]{1,0:T(8,128)(2,1)}, bf16[1024,384]{1,0:T(8,128)(2,1)}, u32[]{:S(2)}, u32[]{:S(2)}) collective-permute-start(bf16[1024,384]{1,0:T(8,128)(2,1)} %get-tuple-element.250.refs_0_), channel_id=1, source_target_pairs={{0,2},{2,0},{1,3},{3,1},{4,6},{6,4},{5,7},{7,5},{8,10},{10,8},{9,1... | collective-permute-start | bytes 2359304 | tf_op jit(solution)/shard_map/ppermute | solution.py:942
  85.2 35.1 %collective-permute-start.23 = (bf16[192,3072]{1,0:T(8,128)(2,1)S(1)}, bf16[192,3072]{1,0:T(8,128)(2,1)S(1)}, u32[]{:S(2)}, u32[]{:S(2)}) collective-permute-start(bf16[192,3072]{1,0:T(8,128)(2,1)S(1)} %pad_maximum_fusion.1.refs_0_.refs_4_.refs_6_), channel_id=1, source_target_pairs={{0,8},{4,12},{8,0},{12,4},{16,24},{20,28},{24,16},{28,20},{1,9},{5... | collective-permute-start | bytes 3538952 | tf_op jit(solution)/shard_map/ppermute | solution.py:947
  85.7 34.6 %collective-permute-start.24 = (bf16[192,3072]{1,0:T(8,128)(2,1)S(1)}, bf16[192,3072]{1,0:T(8,128)(2,1)}, u32[]{:S(2)}, u32[]{:S(2)}) collective-permute-start(bf16[192,3072]{1,0:T(8,128)(2,1)S(1)} %pad_maximum_fusion.2.refs_1_.refs_5_.refs_7_), channel_id=1, source_target_pairs={{0,4},{4,0},{8,12},{12,8},{16,20},{20,16},{24,28},{28,24},{1,5},{5... | collective-permute-start | bytes 3538952 | tf_op jit(solution)/shard_map/ppermute | solution.py:947
  104.1 16.5 %collective-permute-start.22 = (bf16[2,192,768]{2,1,0:T(8,128)(2,1)}, bf16[2,192,768]{2,1,0:T(8,128)(2,1)}, u32[]{:S(2)}, u32[]{:S(2)}) collective-permute-start(bf16[2,192,768]{2,1,0:T(8,128)(2,1)} %unit_rows.2), channel_id=1, source_target_pairs={{0,1},{1,0},{2,3},{3,2},{4,5},{5,4},{6,7},{7,6},{8,9},{9,8},{10,11... | collective-permute-start | bytes 1769480 | tf_op jit(solution)/shard_map/ppermute | solution.py:942
  104.6 37.5 %collective-permute-start.26 = (bf16[512,768]{1,0:T(8,128)(2,1)}, bf16[512,768]{1,0:T(8,128)(2,1)}, u32[]{:S(2)}, u32[]{:S(2)}) collective-permute-start(bf16[512,768]{1,0:T(8,128)(2,1)} %own_ref.1), channel_id=1, source_target_pairs={{0,1},{1,0},{2,3},{3,2},{4,5},{5,4},{6,7},{7,6},{8,9},{9,8},{10,11... | collective-permute-start | bytes 2359304 | tf_op jit(solution)/shard_map/ppermute | solution.py:942
  121.8 20.4 %collective-permute-start.27 = (bf16[192,768]{1,0:T(8,128)(2,1)S(1)}, bf16[192,768]{1,0:T(8,128)(2,1)S(1)}, u32[]{:S(2)}, u32[]{:S(2)}) collective-permute-start(bf16[192,768]{1,0:T(8,128)(2,1)S(1)} %get-tuple-element.278), channel_id=1, source_target_pairs={{0,8},{4,12},{8,0},{12,4},{16,24},{20,28},{24,16},{28,20},{1,9},{5... | collective-permute-start | bytes 884744 | tf_op jit(solution)/shard_map/ppermute | solution.py:947
  122.4 19.9 %collective-permute-start.25 = (bf16[192,768]{1,0:T(8,128)(2,1)S(1)}, bf16[192,768]{1,0:T(8,128)(2,1)S(1)}, u32[]{:S(2)}, u32[]{:S(2)}) collective-permute-start(bf16[192,768]{1,0:T(8,128)(2,1)S(1)} %get-tuple-element.277), channel_id=1, source_target_pairs={{0,4},{4,0},{8,12},{12,8},{16,20},{20,16},{24,28},{28,24},{1,5},{5... | collective-permute-start | bytes 884744 | tf_op jit(solution)/shard_map/ppermute | solution.py:947
  142.2 5.9 %collective-permute-start.29 = (bf16[512,768]{1,0:T(8,128)(2,1)}, bf16[512,768]{1,0:T(8,128)(2,1)}, u32[]{:S(2)}, u32[]{:S(2)}) collective-permute-start(bf16[512,768]{1,0:T(8,128)(2,1)} %collective-permute-done.26.far_ref), channel_id=1, source_target_pairs={{0,2},{2,0},{1,3},{3,1},{4,6},{6,4},{5,7},{7,5},{8,10},{10,8},{9,1... | collective-permute-start | bytes 2359304 | tf_op jit(solution)/shard_map/ppermute | solution.py:942
  143.7 4.4 collective-permute-start.28
  144.1 19.9 %collective-permute-start.31 = (bf16[384,768]{1,0:T(8,128)(2,1)S(1)}, bf16[384,768]{1,0:T(8,128)(2,1)}, u32[]{:S(2)}, u32[]{:S(2)}) collective-permute-start(bf16[384,768]{1,0:T(8,128)(2,1)S(1)} %pad_maximum_fusion.8.refs_1_.refs_5_), channel_id=1, source_target_pairs={{0,4},{4,0},{8,12},{12,8},{16,20},{20,16},{24,28},{28,24},{1,5},{5... | collective-permute-start | bytes 1769480 | tf_op jit(solution)/shard_map/ppermute | solution.py:947
  145.7 18.4 %collective-permute-start.30 = (bf16[384,768]{1,0:T(8,128)(2,1)S(1)}, bf16[384,768]{1,0:T(8,128)(2,1)}, u32[]{:S(2)}, u32[]{:S(2)}) collective-permute-start(bf16[384,768]{1,0:T(8,128)(2,1)S(1)} %pad_maximum_fusion.7.refs_0_.refs_4_), channel_id=1, source_target_pairs={{0,8},{4,12},{8,0},{12,4},{16,24},{20,28},{24,16},{28,20},{1,9},{5... | collective-permute-start | bytes 1769480 | tf_op jit(solution)/shard_map/ppermute | solution.py:947
  147.2 54.0 %collective-permute-start.34 = (bf16[768,1536]{1,0:T(8,128)(2,1)}, bf16[768,1536]{1,0:T(8,128)(2,1)S(1)}, u32[]{:S(2)}, u32[]{:S(2)}) collective-permute-start(bf16[768,1536]{1,0:T(8,128)(2,1)} %bitcast.35), channel_id=1, source_target_pairs={{0,1},{1,0},{2,3},{3,2},{4,5},{5,4},{6,7},{7,6},{8,9},{9,8},{10,11... | collective-permute-start | bytes 7077896 | tf_op jit(solution)/shard_map/ppermute | solution.py:942
  164.1 54.6 %collective-permute-start.33 = (bf16[4,192,1536]{2,1,0:T(8,128)(2,1)}, bf16[4,192,1536]{2,1,0:T(8,128)(2,1)}, u32[]{:S(2)}, u32[]{:S(2)}) collective-permute-start(bf16[4,192,1536]{2,1,0:T(8,128)(2,1)} %get-tuple-element.300), channel_id=1, source_target_pairs={{0,4},{4,0},{8,12},{12,8},{16,20},{20,16},{24,28},{28,24},{1,5},{5... | collective-permute-start | bytes 7077896 | tf_op jit(solution)/shard_map/ppermute | solution.py:947
  198.5 73.8 %collective-permute-start.35 = (bf16[4,96,3072]{2,1,0:T(8,128)(2,1)}, bf16[4,96,3072]{2,1,0:T(8,128)(2,1)}, u32[]{:S(2)}, u32[]{:S(2)}) collective-permute-start(bf16[4,96,3072]{2,1,0:T(8,128)(2,1)} %get-tuple-element.319), channel_id=1, source_target_pairs={{0,4},{4,0},{8,12},{12,8},{16,20},{20,16},{24,28},{28,24},{1,5},{5... | collective-permute-start | bytes 7077896 | tf_op jit(solution)/shard_map/ppermute | solution.py:947
  200.0 26.7 %collective-permute-start.32 = (bf16[768,768]{1,0:T(8,128)(2,1)}, bf16[768,768]{1,0:T(8,128)(2,1)S(1)}, u32[]{:S(2)}, u32[]{:S(2)}) collective-permute-start(bf16[768,768]{1,0:T(8,128)(2,1)} %bitcast.104), channel_id=1, source_target_pairs={{0,1},{1,0},{2,3},{3,2},{4,5},{5,4},{6,7},{7,6},{8,9},{9,8},{10,11... | collective-permute-start | bytes 3538952 | tf_op jit(solution)/shard_map/ppermute | solution.py:942
  222.9 46.0 %collective-permute-start.36 = (bf16[2,192,1536]{2,1,0:T(8,128)(2,1)}, bf16[2,192,1536]{2,1,0:T(8,128)(2,1)}, u32[]{:S(2)}, u32[]{:S(2)}) collective-permute-start(bf16[2,192,1536]{2,1,0:T(8,128)(2,1)} %get-tuple-element.321), channel_id=1, source_target_pairs={{0,8},{4,12},{8,0},{12,4},{16,24},{20,28},{24,16},{28,20},{1,9},{5... | collective-permute-start | bytes 3538952 | tf_op jit(solution)/shard_map/ppermute | solution.py:947
  226.7 93.4 %collective-permute-start.40 = (bf16[4,96,3072]{2,1,0:T(8,128)(2,1)}, bf16[4,96,3072]{2,1,0:T(8,128)(2,1)S(1)}, u32[]{:S(2)}, u32[]{:S(2)}) collective-permute-start(bf16[4,96,3072]{2,1,0:T(8,128)(2,1)} %get-tuple-element.342), channel_id=1, source_target_pairs={{0,4},{4,0},{8,12},{12,8},{16,20},{20,16},{24,28},{28,24},{1,5},{5... | collective-permute-start | bytes 7077896 | tf_op jit(solution)/shard_map/ppermute | solution.py:947
  276.6 39.1 %collective-permute-start.41 = (bf16[2,96,3072]{2,1,0:T(8,128)(2,1)}, bf16[2,96,3072]{2,1,0:T(8,128)(2,1)S(1)}, u32[]{:S(2)}, u32[]{:S(2)}) collective-permute-start(bf16[2,96,3072]{2,1,0:T(8,128)(2,1)} %get-tuple-element.344), channel_id=1, source_target_pairs={{0,8},{4,12},{8,0},{12,4},{16,24},{20,28},{24,16},{28,20},{1,9},{5... | collective-permute-start | bytes 3538952 | tf_op jit(solution)/shard_map/ppermute | solution.py:947
  277.9 3.7 collective-permute-start.38
  278.4 47.4 %collective-permute-start.39 = (bf16[1,192,1536]{2,1,0:T(8,128)(2,1)}, bf16[1,192,1536]{2,1,0:T(8,128)(2,1)S(1)}, u32[]{:S(2)}, u32[]{:S(2)}) collective-permute-start(bf16[1,192,1536]{2,1,0:T(8,128)(2,1)} %get-tuple-element.340), channel_id=1, source_target_pairs={{0,16},{4,20},{8,24},{12,28},{16,0},{20,4},{24,8},{28,12},{1,17},{... | collective-permute-start | bytes 1769480 | tf_op jit(solution)/shard_map/ppermute | solution.py:947
  286.6 41.8 %collective-permute-start.43 = (bf16[512,768]{1,0:T(8,128)(2,1)}, bf16[512,768]{1,0:T(8,128)(2,1)}, u32[]{:S(2)}, u32[]{:S(2)}) collective-permute-start(bf16[512,768]{1,0:T(8,128)(2,1)} %get-tuple-element.331), channel_id=1, source_target_pairs={{0,1},{1,0},{2,3},{3,2},{4,5},{5,4},{6,7},{7,6},{8,9},{9,8},{10,11... | collective-permute-start | bytes 2359304 | tf_op jit(solution)/shard_map/ppermute | solution.py:942
  287.5 40.9 %collective-permute-start.44 = (bf16[512,768]{1,0:T(8,128)(2,1)}, bf16[512,768]{1,0:T(8,128)(2,1)}, u32[]{:S(2)}, u32[]{:S(2)}) collective-permute-start(bf16[512,768]{1,0:T(8,128)(2,1)} %get-tuple-element.332), channel_id=1, source_target_pairs={{0,1},{1,0},{2,3},{3,2},{4,5},{5,4},{6,7},{7,6},{8,9},{9,8},{10,11... | collective-permute-start | bytes 2359304 | tf_op jit(solution)/shard_map/ppermute | solution.py:942
  327.1 32.7 %collective-permute-start.47 = (bf16[4,96,1536]{2,1,0:T(8,128)(2,1)}, bf16[4,96,1536]{2,1,0:T(8,128)(2,1)S(1)}, u32[]{:S(2)}, u32[]{:S(2)}) collective-permute-start(bf16[4,96,1536]{2,1,0:T(8,128)(2,1)} %get-tuple-element.360), channel_id=1, source_target_pairs={{0,4},{4,0},{8,12},{12,8},{16,20},{20,16},{24,28},{28,24},{1,5},{5... | collective-permute-start | bytes 3538952 | tf_op jit(solution)/shard_map/ppermute | solution.py:947
  328.4 7.8 %collective-permute-start.42 = (bf16[512,768]{1,0:T(8,128)(2,1)}, bf16[512,768]{1,0:T(8,128)(2,1)S(1)}, u32[]{:S(2)}, u32[]{:S(2)}) collective-permute-start(bf16[512,768]{1,0:T(8,128)(2,1)} %get-tuple-element.350), channel_id=1, source_target_pairs={{0,2},{2,0},{1,3},{3,1},{4,6},{6,4},{5,7},{7,5},{8,10},{10,8},{9,1... | collective-permute-start | bytes 2359304 | tf_op jit(solution)/shard_map/ppermute | solution.py:942
  364.2 62.5 %collective-permute-start.50 = (bf16[8,96,1536]{2,1,0:T(8,128)(2,1)}, bf16[8,96,1536]{2,1,0:T(8,128)(2,1)S(1)}, u32[]{:S(2)}, u32[]{:S(2)}) collective-permute-start(bf16[8,96,1536]{2,1,0:T(8,128)(2,1)} %get-tuple-element.372), channel_id=1, source_target_pairs={{0,4},{4,0},{8,12},{12,8},{16,20},{20,16},{24,28},{28,24},{1,5},{5... | collective-permute-start | bytes 7077896 | tf_op jit(solution)/shard_map/ppermute | solution.py:947
  365.0 31.1 %collective-permute-start.48 = (bf16[1024,640]{1,0:T(8,128)(2,1)}, bf16[1024,640]{1,0:T(8,128)(2,1)}, u32[]{:S(2)}, u32[]{:S(2)}) collective-permute-start(bf16[1024,640]{1,0:T(8,128)(2,1)} %get-tuple-element.363.query_ref), channel_id=1, source_target_pairs={{0,1},{1,0},{2,3},{3,2},{4,5},{5,4},{6,7},{7,6},{8,9},{9,8},{10,11... | collective-permute-start | bytes 3932168 | tf_op jit(solution)/shard_map/ppermute | solution.py:942
  365.6 41.7 %collective-permute-start.53 = (bf16[2,96,3072]{2,1,0:T(8,128)(2,1)}, bf16[2,96,3072]{2,1,0:T(8,128)(2,1)S(1)}, u32[]{:S(2)}, u32[]{:S(2)}) collective-permute-start(bf16[2,96,3072]{2,1,0:T(8,128)(2,1)} %get-tuple-element.378), channel_id=1, source_target_pairs={{0,8},{4,12},{8,0},{12,4},{16,24},{20,28},{24,16},{28,20},{1,9},{5... | collective-permute-start | bytes 3538952 | tf_op jit(solution)/shard_map/ppermute | solution.py:947
  365.8 53.1 %collective-permute-start.52 = (bf16[2,96,1536]{2,1,0:T(8,128)(2,1)}, bf16[2,96,1536]{2,1,0:T(8,128)(2,1)}, u32[]{:S(2)}, u32[]{:S(2)}) collective-permute-start(bf16[2,96,1536]{2,1,0:T(8,128)(2,1)} %get-tuple-element.376), channel_id=1, source_target_pairs={{0,8},{4,12},{8,0},{12,4},{16,24},{20,28},{24,16},{28,20},{1,9},{5... | collective-permute-start | bytes 1769480 | tf_op jit(solution)/shard_map/ppermute | solution.py:947
  367.6 54.1 %collective-permute-start.51 = (bf16[1,96,3072]{2,1,0:T(8,128)(2,1)}, bf16[1,96,3072]{2,1,0:T(8,128)(2,1)}, u32[]{:S(2)}, u32[]{:S(2)}) collective-permute-start(bf16[1,96,3072]{2,1,0:T(8,128)(2,1)} %get-tuple-element.374), channel_id=1, source_target_pairs={{0,16},{4,20},{8,24},{12,28},{16,0},{20,4},{24,8},{28,12},{1,17},{... | collective-permute-start | bytes 1769480 | tf_op jit(solution)/shard_map/ppermute | solution.py:947
  406.8 26.4 %collective-permute-start.54 = (bf16[512,768]{1,0:T(8,128)(2,1)}, bf16[512,768]{1,0:T(8,128)(2,1)}, u32[]{:S(2)}, u32[]{:S(2)}) collective-permute-start(bf16[512,768]{1,0:T(8,128)(2,1)} %get-tuple-element.387), channel_id=1, source_target_pairs={{0,2},{2,0},{1,3},{3,1},{4,6},{6,4},{5,7},{7,5},{8,10},{10,8},{9,1... | collective-permute-start | bytes 2359304 | tf_op jit(solution)/shard_map/ppermute | solution.py:942
  407.3 40.3 %collective-permute-start.49 = (bf16[4,96,1792]{2,1,0:T(8,128)(2,1)}, bf16[4,96,1792]{2,1,0:T(8,128)(2,1)}, u32[]{:S(2)}, u32[]{:S(2)}) collective-permute-start(bf16[4,96,1792]{2,1,0:T(8,128)(2,1)} %get-tuple-element.369), channel_id=1, source_target_pairs={{0,4},{4,0},{8,12},{12,8},{16,20},{20,16},{24,28},{28,24},{1,5},{5... | collective-permute-start | bytes 4128776 | tf_op jit(solution)/shard_map/ppermute | solution.py:947
  423.8 43.1 %collective-permute-start.59 = (bf16[1,96,1536]{2,1,0:T(8,128)(2,1)}, bf16[1,96,1536]{2,1,0:T(8,128)(2,1)S(1)}, u32[]{:S(2)}, u32[]{:S(2)}) collective-permute-start(bf16[1,96,1536]{2,1,0:T(8,128)(2,1)} %get-tuple-element.400), channel_id=1, source_target_pairs={{0,16},{4,20},{8,24},{12,28},{16,0},{20,4},{24,8},{28,12},{1,17},{... | collective-permute-start | bytes 884744 | tf_op jit(solution)/shard_map/ppermute | solution.py:947
  425.6 39.0 %collective-permute-start.60 = (bf16[1,96,3072]{2,1,0:T(8,128)(2,1)}, bf16[1,96,3072]{2,1,0:T(8,128)(2,1)}, u32[]{:S(2)}, u32[]{:S(2)}) collective-permute-start(bf16[1,96,3072]{2,1,0:T(8,128)(2,1)} %get-tuple-element.402), channel_id=1, source_target_pairs={{0,16},{4,20},{8,24},{12,28},{16,0},{20,4},{24,8},{28,12},{1,17},{... | collective-permute-start | bytes 1769480 | tf_op jit(solution)/shard_map/ppermute | solution.py:947
  436.9 3.7 collective-permute-start.55
  439.2 46.9 %collective-permute-start.58 = (bf16[4,96,1536]{2,1,0:T(8,128)(2,1)}, bf16[4,96,1536]{2,1,0:T(8,128)(2,1)S(1)}, u32[]{:S(2)}, u32[]{:S(2)}) collective-permute-start(bf16[4,96,1536]{2,1,0:T(8,128)(2,1)} %get-tuple-element.398), channel_id=1, source_target_pairs={{0,8},{4,12},{8,0},{12,4},{16,24},{20,28},{24,16},{28,20},{1,9},{5... | collective-permute-start | bytes 3538952 | tf_op jit(solution)/shard_map/ppermute | solution.py:947
  467.0 30.6 %collective-permute-start.71 = (bf16[96,768]{1,0:T(8,128)(2,1)S(1)}, bf16[96,768]{1,0:T(8,128)(2,1)}, u32[]{:S(2)}, u32[]{:S(2)}) collective-permute-start(bf16[96,768]{1,0:T(8,128)(2,1)S(1)} %slice.180), channel_id=1, source_target_pairs={{0,1},{1,0},{2,3},{3,2},{4,5},{5,4},{6,7},{7,6},{8,9},{9,8},{10,11... | collective-permute-start | bytes 442376 | tf_op jit(solution)/shard_map/ppermute | solution.py:942
  468.3 31.6 %collective-permute-start.70 = (bf16[192,768]{1,0:T(8,128)(2,1)}, bf16[192,768]{1,0:T(8,128)(2,1)S(1)}, u32[]{:S(2)}, u32[]{:S(2)}) collective-permute-start(bf16[192,768]{1,0:T(8,128)(2,1)} %slice.179), channel_id=1, source_target_pairs={{0,1},{1,0},{2,3},{3,2},{4,5},{5,4},{6,7},{7,6},{8,9},{9,8},{10,11... | collective-permute-start | bytes 884744 | tf_op jit(solution)/shard_map/ppermute | solution.py:942
  469.1 36.2 %collective-permute-start.56 = (bf16[2,96,1792]{2,1,0:T(8,128)(2,1)}, bf16[2,96,1792]{2,1,0:T(8,128)(2,1)}, u32[]{:S(2)}, u32[]{:S(2)}) collective-permute-start(bf16[2,96,1792]{2,1,0:T(8,128)(2,1)} %get-tuple-element.394), channel_id=1, source_target_pairs={{0,8},{4,12},{8,0},{12,4},{16,24},{20,28},{24,16},{28,20},{1,9},{5... | collective-permute-start | bytes 2064392 | tf_op jit(solution)/shard_map/ppermute | solution.py:947
  469.1 39.2 %collective-permute-start.62 = (bf16[512,768]{1,0:T(8,128)(2,1)}, bf16[512,768]{1,0:T(8,128)(2,1)}, u32[]{:S(2)}, u32[]{:S(2)}) collective-permute-start(bf16[512,768]{1,0:T(8,128)(2,1)} %add_convert_fusion), channel_id=1, source_target_pairs={{0,1},{1,0},{2,3},{3,2},{4,5},{5,4},{6,7},{7,6},{8,9},{9,8},{10,11... | collective-permute-start | bytes 2359304 | tf_op jit(solution)/shard_map/ppermute | solution.py:942
  490.4 34.0 %collective-permute-start.66 = (bf16[2,96,1536]{2,1,0:T(8,128)(2,1)}, bf16[2,96,1536]{2,1,0:T(8,128)(2,1)}, u32[]{:S(2)}, u32[]{:S(2)}) collective-permute-start(bf16[2,96,1536]{2,1,0:T(8,128)(2,1)} %get-tuple-element.416), channel_id=1, source_target_pairs={{0,16},{4,20},{8,24},{12,28},{16,0},{20,4},{24,8},{28,12},{1,17},{... | collective-permute-start | bytes 1769480 | tf_op jit(solution)/shard_map/ppermute | solution.py:947
  497.6 3.9 collective-permute-start.57
  499.9 35.6 %collective-permute-start.69 = (bf16[96,3072]{1,0:T(8,128)(2,1)S(1)}, bf16[96,3072]{1,0:T(8,128)(2,1)S(1)}, u32[]{:S(2)}, u32[]{:S(2)}) collective-permute-start(bf16[96,3072]{1,0:T(8,128)(2,1)S(1)} %bitcast.105), channel_id=1, source_target_pairs={{0,1},{1,0},{2,3},{3,2},{4,5},{5,4},{6,7},{7,6},{8,9},{9,8},{10,11... | collective-permute-start | bytes 1769480 | tf_op jit(solution)/shard_map/ppermute | solution.py:942
  501.5 6.9 %collective-permute-start.64 = (f32[2560]{0:T(1024)S(1)}, f32[2560]{0:T(1024)S(1)}, u32[]{:S(2)}, u32[]{:S(2)}) collective-permute-start(f32[2560]{0:T(1024)S(1)} %add.129), channel_id=1, source_target_pairs={{0,8},{4,12},{8,0},{12,4},{16,24},{20,28},{24,16},{28,20},{1,9},{5... | collective-permute-start | bytes 30728 | tf_op jit(solution)/shard_map/ppermute | solution.py:947
  508.3 25.0 %collective-permute-start.68 = (bf16[1,96,1792]{2,1,0:T(8,128)(2,1)}, bf16[1,96,1792]{2,1,0:T(8,128)(2,1)S(1)}, u32[]{:S(2)}, u32[]{:S(2)}) collective-permute-start(bf16[1,96,1792]{2,1,0:T(8,128)(2,1)} %get-tuple-element.422), channel_id=1, source_target_pairs={{0,16},{4,20},{8,24},{12,28},{16,0},{20,4},{24,8},{28,12},{1,17},{... | collective-permute-start | bytes 1032200 | tf_op jit(solution)/shard_map/ppermute | solution.py:947
  508.3 18.5 %collective-permute-start.61 = (bf16[512,768]{1,0:T(8,128)(2,1)S(1)}, bf16[512,768]{1,0:T(8,128)(2,1)S(1)}, u32[]{:S(2)}, u32[]{:S(2)}) collective-permute-start(bf16[512,768]{1,0:T(8,128)(2,1)S(1)} %copy-done.54), channel_id=1, source_target_pairs={{0,2},{2,0},{1,3},{3,1},{4,6},{6,4},{5,7},{7,5},{8,10},{10,8},{9,1... | collective-permute-start | bytes 2359304 | tf_op jit(solution)/shard_map/ppermute | solution.py:942
  508.4 24.2 %collective-permute-start.65 = (f32[2560]{0:T(1024)S(1)}, f32[2560]{0:T(1024)S(1)}, u32[]{:S(2)}, u32[]{:S(2)}) collective-permute-start(f32[2560]{0:T(1024)S(1)} %add.135), channel_id=1, source_target_pairs={{0,16},{4,20},{8,24},{12,28},{16,0},{20,4},{24,8},{28,12},{1,17},{... | collective-permute-start | bytes 30728 | tf_op jit(solution)/shard_map/ppermute | solution.py:947
  525.8 6.8 %collective-permute-start.67 = (bf16[96,1536]{1,0:T(8,128)(2,1)S(1)}, bf16[96,1536]{1,0:T(8,128)(2,1)S(1)}, u32[]{:S(2)}, u32[]{:S(2)}) collective-permute-start(bf16[96,1536]{1,0:T(8,128)(2,1)S(1)} %fusion.8), channel_id=1, source_target_pairs={{0,1},{1,0},{2,3},{3,2},{4,5},{5,4},{6,7},{7,6},{8,9},{9,8},{10,11... | collective-permute-start | bytes 884744 | tf_op jit(solution)/shard_map/ppermute | solution.py:942
  (64 other events, 312.6 us)
